TPU v7x, 32 devices: a whole 2x2x4 slice. The times are simulated.
32 devices in a mesh: section: 2 (over core), gx: 4 (over z), gy: 4 (over y, x).
Axes of the slice: x: 2, y: 2, z: 4, core: 2. Of those that a mesh axis runs over, the one named last changes fastest.
Arguments:
- rhs: float32 [4, 20, 20, 160], P('section', 'gx', 'gy'), may hold values from -6 to 6
- guess: float32 [4, 20, 20, 160], P('section', 'gx', 'gy'), may hold values from -6 to 6
- kappa: float32 [20, 20, 160], P('gx', 'gy'), may hold values from 0.1 to 10
- bc_flags: int32 [6, 4, 4, 32], P(None, 'gx', 'gy'), may hold values from 0 to 1
Outputs:
- solution: float32 [4, 20, 20, 160], P('section', 'gx', 'gy')
- residual: float32 [4, 20, 20, 160], P('section', 'gx', 'gy')
- arnoldi: float32 [3], replicated
Inputs may be any that keep to these rules, and one draw needn't show every extreme that they name: `bc_flags`: 1 selects the upwind flux, 0 the central flux, on that face of that element.
All inputs are finite; a program needn't handle non-finite values.
Results may differ from a plain program's by a relative error of at most 0.0003.
Values sent between devices are 32-bit elements; how exact they have to be, the bound alone decides.
No kernel may reach another device: no remote copies, remote signals or barrier semaphores. Data moves between devices by JAX's collectives and lax.ppermute only.
A program may use at most 64 MiB of HBM per device.

v0:
```python
from functools import partial
import math

import jax
import jax.numpy as jnp
import numpy as np
from jax import lax
from jax.experimental import pallas as pl
from jax.experimental.pallas import tpu as pltpu
from jax.sharding import PartitionSpec as P

ADVECT = (1.0, 0.7, 0.5)
DIFFUSE = 0.05
STEP_SIZE = 0.2
JACOBI_SCALE = 0.25
CHEB_LOW = 0.25
CHEB_HIGH = 2.0
LETTERS = "abcdef"


def extended(x, sides, width):
    for axis, dim in sides:
        peers, length = (lax.axis_size(axis), x.shape[dim])
        up = [(i, (i + 1) % peers) for i in range(peers)]
        down = [(j, i) for i, j in up]
        last = lax.slice_in_dim(x, length - width, length, axis=dim)
        leading = lax.slice_in_dim(x, 0, width, axis=dim)
        before = lax.ppermute(last, axis, up)
        after = lax.ppermute(leading, axis, down)
        x = jnp.concatenate([before, x, after], axis=dim)
    return x


def lobatto(count):
    if count == 5:
        inner = math.sqrt(3.0 / 7.0)
        return (
            np.array([-1.0, -inner, 0.0, inner, 1.0]),
            np.array([0.1, 49.0 / 90.0, 32.0 / 45.0, 49.0 / 90.0, 0.1]),
        )
    if count == 3:
        return (np.array([-1.0, 0.0, 1.0]), np.array([1.0 / 3.0, 4.0 / 3.0, 1.0 / 3.0]))
    return (np.array([-1.0, 1.0]), np.array([1.0, 1.0]))


def lagrange_table(nodes, points):
    table = np.ones((len(points), len(nodes)))
    for column in range(len(nodes)):
        for other in range(len(nodes)):
            if other != column:
                table[:, column] *= (points - nodes[other]) / (nodes[column] - nodes[other])
    return table


def slope_table(nodes):
    total = len(nodes)
    factor = np.array(
        [np.prod([nodes[i] - nodes[k] for k in range(total) if k != i]) for i in range(total)]
    )
    table = np.zeros((total, total))
    for row in range(total):
        for column in range(total):
            if row != column:
                table[row, column] = factor[row] / factor[column] / (nodes[row] - nodes[column])
        table[row, row] = -np.sum(table[row])
    return table


def element_matrix(count, direction):
    nodes, weights = lobatto(count)
    slopes = slope_table(nodes)
    stiffness = (1.0 / weights)[:, None] * (slopes.T @ (weights[:, None] * slopes))
    return ADVECT[direction] * slopes + DIFFUSE * stiffness


def legendre_pair(point, order):
    values = [1.0, point]
    slopes = [0.0, 1.0]
    for index in range(1, order):
        values.append(
            ((2 * index + 1) * point * values[index] - index * values[index - 1]) / (index + 1)
        )
        slopes.append(slopes[index - 1] + (2 * index + 1) * values[index])
    return (values, slopes)


def radau_nodes():
    starts = [0.0885879595127039, 0.4094668644407347, 0.7876594617608471]
    found = []
    for start in starts:
        point = start
        for sweep in range(30):
            values, slopes = legendre_pair(2.0 * point - 1.0, 4)
            change = (values[4] - values[3]) / (2.0 * (slopes[4] - slopes[3]))
            point = point - change
        found.append(point)
    found.append(1.0)
    return found


def poly_times(coefs, root):
    result = [0.0] * (len(coefs) + 1)
    for index in range(len(coefs)):
        result[index + 1] += coefs[index]
        result[index] -= root * coefs[index]
    return result


def radau_matrix():
    order = 4
    nodes = radau_nodes()
    matrix = np.zeros((order, order))
    for column in range(order):
        coefs = [1.0]
        denominator = 1.0
        for other in range(order):
            if other != column:
                coefs = poly_times(coefs, nodes[other])
                denominator *= nodes[column] - nodes[other]
        for row in range(order):
            upper_end = nodes[row]
            integral = 0.0
            for index in range(len(coefs)):
                integral += coefs[index] * upper_end ** (index + 1) / (index + 1)
            matrix[row, column] = integral / denominator
    return matrix


def node_einsum(table, field, axis):
    labels = LETTERS[: field.ndim]
    source = labels[: axis + 1] + "j" + labels[axis + 2 :]
    target = labels[: axis + 1] + "i" + labels[axis + 2 :]
    return jnp.einsum(
        "ij," + source + "->" + target,
        jnp.asarray(table, jnp.float32),
        field,
        precision=lax.Precision.HIGHEST,
    )


def apply_along(field, axis, count, table):
    shape = field.shape
    split = shape[:axis] + (shape[axis] // count, count) + shape[axis + 1 :]
    mapped = node_einsum(table, field.reshape(split), axis)
    return mapped.reshape(
        shape[:axis] + (mapped.shape[axis] * mapped.shape[axis + 1],) + shape[axis + 1 :]
    )


def line_part(field, axis, count, table, left_gain, right_gain, left_edge, right_edge):
    shape = field.shape
    elements = shape[axis] // count
    split = field.reshape(shape[:axis] + (elements, count) + shape[axis + 1 :])
    linear = node_einsum(table, split, axis)
    first = lax.index_in_dim(split, 0, axis + 1, keepdims=False)
    last = lax.index_in_dim(split, count - 1, axis + 1, keepdims=False)
    before = jnp.concatenate(
        [jnp.expand_dims(left_edge, axis), lax.slice_in_dim(last, 0, elements - 1, axis=axis)], axis
    )
    after = jnp.concatenate(
        [lax.slice_in_dim(first, 1, elements, axis=axis), jnp.expand_dims(right_edge, axis)], axis
    )
    front = jnp.expand_dims(left_gain * (first - before), axis + 1)
    back = jnp.expand_dims(right_gain * (last - after), axis + 1)
    if count > 2:
        middle_shape = list(front.shape)
        middle_shape[axis + 1] = count - 2
        pieces = [front, jnp.zeros(middle_shape, jnp.float32), back]
    else:
        pieces = [front, back]
    return (linear + jnp.concatenate(pieces, axis + 1)).reshape(shape)


def diag_along(shape, axis, count, table, left_gain, right_gain):
    elements = shape[axis] // count
    split = shape[:axis] + (elements, count) + shape[axis + 1 :]
    profile = [1] * len(split)
    profile[axis + 1] = count
    diagonal_entries = np.array([table[index, index] for index in range(count)])
    base = jnp.broadcast_to(jnp.asarray(diagonal_entries, jnp.float32).reshape(profile), split)
    front = jnp.expand_dims(left_gain, axis + 1)
    back = jnp.expand_dims(right_gain, axis + 1)
    if count > 2:
        middle_shape = list(front.shape)
        middle_shape[axis + 1] = count - 2
        pieces = [front, jnp.zeros(middle_shape, jnp.float32), back]
    else:
        pieces = [front, back]
    return (base + jnp.concatenate(pieces, axis + 1)).reshape(shape)


def level_kappa(kappa, count):
    if count == 5:
        return kappa
    picks = np.array([0, 2, 4]) if count == 3 else np.array([0, 4])
    extents = [extent // 5 for extent in kappa.shape]
    grouped = kappa.reshape(extents[0], 5, extents[1], 5, extents[2], 5)
    for axis in (1, 3, 5):
        grouped = jnp.take(grouped, picks, axis=axis)
    return grouped.reshape(extents[0] * count, extents[1] * count, extents[2] * count)


def face_plane(face, direction, count):
    plane = face.astype(jnp.float32)
    for axis in range(3):
        if axis != direction:
            plane = jnp.repeat(plane, count, axis=axis)
    return plane


def build_level(kappa, flags, count):
    nodes, weights = lobatto(count)
    kappa_level = level_kappa(kappa, count)
    tables, lefts, rights = ([], [], [])
    diagonal = kappa_level
    for direction in range(3):
        table = element_matrix(count, direction)
        lower = face_plane(flags[2 * direction], direction, count)
        upper = face_plane(flags[2 * direction + 1], direction, count)
        left_gain = (ADVECT[direction] * (1.0 + lower) / 2.0 + DIFFUSE * count * count) / float(
            weights[0]
        )
        right_gain = (DIFFUSE * count * count - ADVECT[direction] * (1.0 - upper) / 2.0) / float(
            weights[-1]
        )
        tables.append(table)
        lefts.append(left_gain)
        rights.append(right_gain)
        diagonal = diagonal + diag_along(
            kappa_level.shape, direction, count, table, left_gain, right_gain
        )
    scale = 1.0 / (1.0 + STEP_SIZE * JACOBI_SCALE * diagonal)
    return (count, tables, lefts, rights, kappa_level, scale)


def restrict(field, fine_count, coarse_count):
    fine_nodes, fine_weights = lobatto(fine_count)
    coarse_nodes, coarse_weights = lobatto(coarse_count)
    table = (
        (1.0 / coarse_weights)[:, None]
        * lagrange_table(coarse_nodes, fine_nodes).T
        * fine_weights[None, :]
    )
    for axis in range(field.ndim - 3, field.ndim):
        field = apply_along(field, axis, fine_count, table)
    return field


def prolong(field, coarse_count, fine_count):
    fine_nodes, fine_weights = lobatto(fine_count)
    coarse_nodes, coarse_weights = lobatto(coarse_count)
    table = lagrange_table(coarse_nodes, fine_nodes)
    for axis in range(field.ndim - 3, field.ndim):
        field = apply_along(field, axis, coarse_count, table)
    return field


def chebyshev(rhs, start, level, operator):
    centre = (CHEB_HIGH + CHEB_LOW) / 2.0
    radius = (CHEB_HIGH - CHEB_LOW) / 2.0
    ratio = centre / radius
    first_rho = 1.0 / ratio
    second_rho = 1.0 / (2.0 * ratio - first_rho)
    scale = level[5]
    if start is None:
        remain = rhs
    else:
        remain = rhs - operator(start, level)
    step = scale * remain / centre
    guess = step if start is None else start + step
    remain = remain - operator(step, level)
    step = second_rho * first_rho * step + 2.0 * second_rho / radius * scale * remain
    return guess + step


def vcycle(rhs, levels, operator):
    fine, middle, coarse = levels
    fine_x = chebyshev(rhs, None, fine, operator)
    middle_rhs = restrict(rhs - operator(fine_x, fine), 5, 3)
    middle_x = chebyshev(middle_rhs, None, middle, operator)
    coarse_rhs = restrict(middle_rhs - operator(middle_x, middle), 3, 2)
    coarse_x = chebyshev(coarse_rhs, None, coarse, operator)
    middle_x = chebyshev(middle_rhs, middle_x + prolong(coarse_x, 2, 3), middle, operator)
    return chebyshev(rhs, fine_x + prolong(middle_x, 3, 5), fine, operator)


def spatial(field, level):
    count, tables, lefts, rights, kappa_level, scale = level
    padded = extended(field, (("gx", 1), ("gy", 2)), 1)
    total = kappa_level * field
    total = total + line_part(
        field,
        1,
        count,
        tables[0],
        lefts[0],
        rights[0],
        padded[:, 0, 1:-1, :],
        padded[:, -1, 1:-1, :],
    )
    total = total + line_part(
        field,
        2,
        count,
        tables[1],
        lefts[1],
        rights[1],
        padded[:, 1:-1, 0, :],
        padded[:, 1:-1, -1, :],
    )
    total = total + line_part(
        field, 3, count, tables[2], lefts[2], rights[2], field[:, :, :, -1], field[:, :, :, 0]
    )
    return total


def apply_system(field, level, coupling):
    image = spatial(field, level)
    everyone = lax.all_gather(image, "section", axis=0, tiled=True)
    butcher = jnp.asarray(radau_matrix(), jnp.float32)
    rows = lax.dynamic_slice_in_dim(
        butcher, lax.axis_index("section") * field.shape[0], field.shape[0], 0
    )
    mixed = jnp.einsum("ij,jabc->iabc", rows, everyone, precision=lax.Precision.HIGHEST)
    return field + STEP_SIZE * mixed


def global_total(values):
    return lax.psum(values, ("section", "gx", "gy"))


def stepwise(rhs, guess, kappa, bc_flags):
    levels = [build_level(kappa, bc_flags, count) for count in (5, 3, 2)]
    section_operator = partial(apply_system, coupling=None)
    start_residual = rhs - section_operator(guess, levels[0])
    dofs = float(rhs.size * lax.axis_size("section") * lax.axis_size("gx") * lax.axis_size("gy"))
    beta = jnp.sqrt(global_total(jnp.sum(start_residual * start_residual).reshape(1))[0])
    basis = start_residual / beta
    precond = vcycle(basis, levels, section_operator)
    image = section_operator(precond, levels[0])
    upper = global_total(jnp.sum(image * basis).reshape(1))[0]
    remainder = image - upper * basis
    lower = jnp.sqrt(global_total(jnp.sum(remainder * remainder).reshape(1))[0])
    weight = beta * upper / (upper * upper + lower * lower)
    solution = guess + weight * precond
    residual = start_residual - weight * image
    arnoldi = jnp.stack([beta / math.sqrt(dofs), upper, lower]).astype(jnp.float32)
    return (solution, residual, arnoldi)


EZ = 32
COLS = 16
HALF = 64
PIECE = 96
FIELD = 1000
F32 = jnp.float32


def split_sections():
    matrix = radau_matrix()
    values, vectors = np.linalg.eig(matrix)
    order = [n for n in np.argsort(np.abs(values.imag), kind="stable") if values[n].imag > 0]
    bases = []
    for n in order:
        plane = np.stack([vectors[:, n].real, vectors[:, n].imag], axis=1)
        bases.append(np.linalg.qr(plane)[0])
    left, cross, right = np.linalg.svd(bases[0].T @ bases[1])
    bases = [bases[0] @ left, bases[1] @ right.T]
    for c in range(2):
        sign = np.sign(bases[0][np.argmax(np.abs(bases[0][:, c])), c])
        bases = [np.concatenate([b[:, :c], sign * b[:, c : c + 1], b[:, c + 1 :]], axis=1) for b in bases]
    whole = np.concatenate(bases, axis=1)
    back = np.linalg.inv(whole)
    return whole, back, back @ matrix, back @ matrix @ whole, cross


def iota(shape, dim):
    return lax.broadcasted_iota(jnp.int32, shape, dim)


def exact_dot(a, b):
    return lax.dot_general(
        a, b, (((1,), (0,)), ((), ())), precision=lax.Precision.HIGHEST, preferred_element_type=F32
    )


def choose(index, values):
    out = values[-1]
    for place in range(len(values) - 2, -1, -1):
        out = jnp.where(index == place, values[place], out)
    return out


def face_gains(flag, direction, side, count):
    nodes, weights = lobatto(count)
    c, nu = ADVECT[direction], DIFFUSE * count * count
    if side == 0:
        return (c * (1.0 + flag) / 2.0 + nu) * (1.0 / float(weights[0]))
    return (nu - c * (1.0 - flag) / 2.0) * (1.0 / float(weights[-1]))


def column_tables():
    kx, ky, kz = (element_matrix(5, d) for d in range(3))
    rows = np.zeros((64, 64))
    for s in range(2):
        for i in range(5):
            for j in range(5):
                r = s * 32 + i * 5 + j
                for m in range(5):
                    rows[r, s * 32 + m * 5 + j] += kx[i, m]
                    rows[r, s * 32 + i * 5 + m] += ky[j, m]
    lines = np.zeros((160, 320))
    for e in range(EZ):
        lines[e * 5 : e * 5 + 5, e * 5 : e * 5 + 5] = kz.T
        lines[(e - 1) % EZ * 5 + 4, 160 + e * 5] = 1.0
        lines[(e + 1) % EZ * 5, 160 + e * 5 + 4] = 1.0
    return rows.astype(np.float32), lines.astype(np.float32)


def pick_line(k):
    return (iota((160, 128), 0) == 5 * (iota((160, 128), 1) % EZ) + k).astype(F32)


def pair_factors(sec, table, own, s):
    upper = iota((32, 128), 1) < 64
    first = jnp.where(upper, float(table[0, s]), float(table[1, s]))
    second = jnp.where(upper, float(table[2, 2 + s]), float(table[3, 2 + s]))
    if not own:
        first = jnp.where(upper, float(table[2, s]), float(table[3, s]))
        second = jnp.where(upper, float(table[0, 2 + s]), float(table[1, 2 + s]))
    return jnp.where(sec == 0, first, second)


def pack_nodes(nodes):
    odd = iota((HALF, 128), 1) // EZ % 2 == 1
    return jnp.where(odd, nodes[HALF:, :], nodes[:HALF, :])


def fetch(pairs, sems):
    copies = [pltpu.make_async_copy(src, dst, sems.at[n]) for n, (src, dst) in enumerate(pairs)]
    for copy in copies:
        copy.start()
    for copy in copies:
        copy.wait()


def local_kernel(
    rhs_in, guess_in, kappa_in, flags_in, rows_in, lines_in, mine, theirs, faces,
    rhs, guess, kappa, flags, rows_t, lines_t, sems, x, kap, stack, own_nodes, other_nodes, krep,
):
    sec = lax.axis_index("section")
    fetch(
        [(rhs_in, rhs), (guess_in, guess), (kappa_in, kappa), (flags_in, flags), (rows_in, rows_t), (lines_in, lines_t)],
        sems,
    )
    x[...] = jnp.zeros_like(x)
    kap[...] = jnp.zeros_like(kap)
    stack[...] = jnp.zeros_like(stack)
    for i in range(5):
        kap[5 * i : 5 * i + 5, :] = kappa[i]
        for j in range(5):
            r = 5 * i + j
            value = guess[i, j]
            left = rhs[i, j] - value
            for s in range(2):
                x[s * 32 + r : s * 32 + r + 1, :] = value[s : s + 1]
                stack[s * 32 + r : s * 32 + r + 1, :] = left[s : s + 1]
    flag = flags[:, 0, 0, :].astype(F32)
    spread = (iota((EZ, 160), 1) // 5 == iota((EZ, 160), 0)).astype(F32)
    wide = exact_dot(flag, spread)
    gains = [face_gains(wide[d : d + 1, :], d // 2, d % 2, 5) for d in range(6)]
    row = iota((32, 160), 0)
    lane = iota((32, 160), 1) % 5
    none = jnp.zeros((32, 160), F32)
    gx = jnp.where(row < 5, gains[0], jnp.where((row >= 20) & (row < 25), gains[1], none))
    gy = jnp.where(row % 5 == 0, gains[2], jnp.where(row % 5 == 4, gains[3], none))
    gz = jnp.where(lane == 0, gains[4], jnp.where(lane == 4, gains[5], none))
    faces[0:32, :] = gx
    faces[32:64, :] = jnp.where(row < 25, gy, none)
    field = x[...]
    along = exact_dot(rows_t[...], field)
    across = exact_dot(field, lines_t[...])
    own = kap[...] + gx + gy + gz
    for s in range(2):
        r = slice(s * 32, s * 32 + 32)
        image = own * field[r] + along[r] + across[r, :160] - gz * across[r, 160:]
        stack[64 + s * 32 : 96 + s * 32, :] = image
    whole, back, back_matrix, blocks, cross = split_sections()
    own_nodes[...] = jnp.zeros_like(own_nodes)
    other_nodes[...] = jnp.zeros_like(other_nodes)
    krep[...] = jnp.zeros_like(krep)
    source = stack[...]
    coefs = kap[...]
    for k in range(5):
        pick = pick_line(k)
        parts = exact_dot(source, pick)
        for target, mark in ((own_nodes, True), (other_nodes, False)):
            total = jnp.zeros((32, 128), F32)
            for s in range(2):
                total = total + pair_factors(sec, back, mark, s) * parts[s * 32 : s * 32 + 32]
                factor = pair_factors(sec, -STEP_SIZE * back_matrix, mark, s)
                total = total + factor * parts[64 + s * 32 : 96 + s * 32]
            target[25 * k : 25 * k + 25, :] = total[:25]
        krep[25 * k : 25 * k + 25, :] = exact_dot(coefs, pick)[:25]
    repeat = (iota((EZ, 128), 1) % EZ == iota((EZ, 128), 0)).astype(F32)
    shown = exact_dot(flag, repeat)
    upper = iota((1, 128), 1) < 64
    for r in range(3):
        own_nodes[125 + r : 126 + r, :] = jnp.where(upper, shown[2 * r : 2 * r + 1], shown[2 * r + 1 : 2 * r + 2])
    mine[:HALF, :] = pack_nodes(own_nodes)
    theirs[...] = pack_nodes(other_nodes)
    mine[HALF:, :] = choose(iota((32, 128), 1) // EZ, [krep[32 * q : 32 * q + 32, :] for q in range(4)])


def halo_kernel(base_mine, base_theirs, faces, xb, xa, yb, ya, mine, theirs, nbx, nby, own_nodes, other_nodes):
    sec = lax.axis_index("section")
    for ref in (nbx, nby, own_nodes, other_nodes):
        ref[...] = jnp.zeros_like(ref)
    for m in range(5):
        for s in range(2):
            r = s * 32
            nbx[r + m : r + m + 1, :] = xb[4, m, s : s + 1, :]
            nbx[r + 20 + m : r + 21 + m, :] = xa[0, m, s : s + 1, :]
            nby[r + 5 * m : r + 5 * m + 1, :] = yb[m, 4, s : s + 1, :]
            nby[r + 5 * m + 4 : r + 5 * m + 5, :] = ya[m, 0, s : s + 1, :]
    gx, gy = faces[0:32, :], faces[32:64, :]
    for s in range(2):
        r = slice(s * 32, s * 32 + 32)
        nbx[r, :] = gx * nbx[r, :] + gy * nby[r, :]
    source = nbx[...]
    back_matrix = split_sections()[2]
    for k in range(5):
        parts = exact_dot(source, pick_line(k))
        for target, mark in ((own_nodes, True), (other_nodes, False)):
            total = jnp.zeros((32, 128), F32)
            for s in range(2):
                factor = pair_factors(sec, STEP_SIZE * back_matrix, mark, s)
                total = total + factor * parts[s * 32 : s * 32 + 32]
            target[25 * k : 25 * k + 25, :] = total[:25]
    mine[:HALF, :] = base_mine[:HALF, :] + pack_nodes(own_nodes)
    mine[HALF:, :] = base_mine[HALF:, :]
    theirs[...] = base_theirs[...] + pack_nodes(other_nodes)


VMEM = pl.BlockSpec(memory_space=pltpu.VMEM)
HBM = pl.BlockSpec(memory_space=pltpu.HBM)


def limit(mib):
    return pltpu.CompilerParams(vmem_limit_bytes=mib * 2**20)


def local_part(rhs, guess, kappa, flags):
    rows_t, lines_t = column_tables()
    operands = (rhs, guess, kappa, flags, jnp.asarray(rows_t), jnp.asarray(lines_t))
    return pl.pallas_call(
        local_kernel,
        out_shape=[
            jax.ShapeDtypeStruct((PIECE, 128), F32),
            jax.ShapeDtypeStruct((HALF, 128), F32),
            jax.ShapeDtypeStruct((64, 160), F32),
        ],
        in_specs=[HBM] * 6,
        out_specs=[VMEM] * 3,
        scratch_shapes=[pltpu.VMEM(o.shape, o.dtype) for o in operands]
        + [
            pltpu.SemaphoreType.DMA((6,)),
            pltpu.VMEM((64, 160), F32),
            pltpu.VMEM((32, 160), F32),
            pltpu.VMEM((128, 160), F32),
            pltpu.VMEM((128, 128), F32),
            pltpu.VMEM((128, 128), F32),
            pltpu.VMEM((128, 128), F32),
        ],
        compiler_params=limit(16),
        name="local_part",
    )(*operands)


def halo_part(base_mine, base_theirs, faces, halos):
    return pl.pallas_call(
        halo_kernel,
        out_shape=[
            jax.ShapeDtypeStruct((PIECE, 128), F32),
            jax.ShapeDtypeStruct((HALF, 128), F32),
        ],
        in_specs=[VMEM] * 7,
        out_specs=[VMEM] * 2,
        scratch_shapes=[pltpu.VMEM((64, 160), F32)] * 2 + [pltpu.VMEM((128, 128), F32)] * 2,
        compiler_params=limit(16),
        name="halo_part",
    )(base_mine, base_theirs, faces, *halos)


class Level:
    def __init__(self, count, refs):
        self.count = count
        self.f, self.diag, self.jac, self.x, self.dir, self.res, self.edge = refs
        self.tables = [element_matrix(count, d) for d in range(3)]
        self.gains = None


def tile(index):
    return pl.ds(index * 8, 8)


def cycle_kernel(block0, block1, block2, block3, fields, *scratch):
    sec = lax.axis_index("section")
    my_gx, my_gy = lax.axis_index("gx"), lax.axis_index("gy")
    levels = [Level(n, scratch[7 * p : 7 * p + 7]) for p, n in enumerate((5, 3, 2))]
    pieces, kap, half = scratch[21:24]
    fine, middle, coarse = levels
    lane = iota((8, 128), 1)
    sub = iota((8, 128), 0)
    group = lane // EZ
    odd = group % 2 == 1
    element = lane % EZ
    place = sub % 4
    low_half = sub < 4
    blocks = split_sections()[3]

    def lanes_of(upper, lower):
        return jnp.where(lane < 64, jnp.where(sec == 0, upper[0], upper[1]), jnp.where(sec == 0, lower[0], lower[1]))

    entry = [[[float(STEP_SIZE * blocks[2 * p + a, 2 * p + b]) for p in range(2)] for b in range(2)] for a in range(2)]
    same = lanes_of(entry[0][0], entry[1][1])
    swap = lanes_of(entry[0][1], entry[1][0])
    centre = (CHEB_HIGH + CHEB_LOW) / 2.0
    radius = (CHEB_HIGH - CHEB_LOW) / 2.0
    first_rho = radius / centre
    second_rho = 1.0 / (2.0 * centre / radius - first_rho)
    keep = 1.0 + second_rho * first_rho
    push = 2.0 * second_rho / radius * centre

    for b, block in enumerate((block0, block1, block2, block3)):
        gy = lax.rem(my_gy + 4 - b, 4)
        for a in range(4):
            column = lax.rem(my_gx + 4 - a, 4) * 4 + gy
            start = pl.multiple_of(column * PIECE, 8)
            pieces[pl.ds(start, PIECE), :] = block[a * PIECE : a * PIECE + PIECE, :]

    def rows_of(r, h):
        return pieces[pl.ds(8 * h * PIECE + r, 8, stride=PIECE), :]

    def place_nodes(r, last):
        low, high = rows_of(r, 0), rows_of(r, 1)
        fine.f[tile(r), :] = jnp.where(odd, pltpu.roll(high, 32, 1), low)
        if not last:
            fine.f[tile(64 + r), :] = jnp.where(odd, high, pltpu.roll(low, 96, 1))
        return low, high

    for r in range(61):
        place_nodes(r, False)
    flags = []
    for r in range(3):
        low, high = place_nodes(61 + r, True)
        turned = [[pltpu.roll(v, 32 * m, 1) if m else v for m in range(4)] for v in (low, high)]
        flags.append(choose(group, [turned[0][3], turned[1][0], turned[0][1], turned[1][2]]))
        flags.append(choose(group, [turned[0][1], turned[1][2], turned[0][3], turned[1][0]]))
    for r in range(32):
        turned = []
        for h in range(2):
            got = rows_of(HALF + r, h)
            turned.append([pltpu.roll(got, 32 * m, 1) if m else got for m in range(4)])
        for q in range(4):
            if q * 32 + r < 125:
                kap[tile(q * 32 + r), :] = choose(group, [turned[g % 2][(g - q) % 4] for g in range(4)])

    for level in levels:
        n = level.count
        picks = {5: (0, 1, 2, 3, 4), 3: (0, 2, 4), 2: (0, 4)}[n]
        level.gains = [face_gains(flags[d], d // 2, d % 2, n) for d in range(6)]
        terms = []
        for d in range(3):
            row = []
            for m in range(n):
                value = float(level.tables[d][m, m])
                if m == 0:
                    row.append(level.gains[2 * d] + value)
                elif m == n - 1:
                    row.append(level.gains[2 * d + 1] + value)
                else:
                    row.append(value)
            terms.append(row)
        for k in range(n):
            for i in range(n):
                both = terms[2][k] + terms[0][i]
                for j in range(n):
                    source = (picks[k] * 5 + picks[i]) * 5 + picks[j]
                    value = kap[tile(source), :] + (both + terms[1][j])
                    where = tile((k * n + i) * n + j)
                    level.diag[where, :] = value
                    scale = 1.0 / (1.0 + STEP_SIZE * JACOBI_SCALE * value)
                    level.jac[where, :] = scale * (1.0 / centre)
        level.edge[...] = jnp.zeros_like(level.edge)

    def apply(p, source, finish, carry):
        level = levels[p]
        n = level.count
        kx, ky, kz = level.tables
        for r in range(n * n):
            v = source[tile(r * n + n - 1), :]
            moved = jnp.where(place == 0, pltpu.roll(v, 5, 0), pltpu.roll(v, 1, 0))
            level.edge[tile(r * n), :] = level.gains[2] * moved
            v = source[tile(r * n), :]
            moved = jnp.where(place == 3, pltpu.roll(v, 3, 0), pltpu.roll(v, 7, 0))
            level.edge[tile(r * n + n - 1), :] = level.gains[3] * moved

        def at(r, j):
            return pl.ds(pl.multiple_of(j * 8, 8) + r * n * 8, 8)

        def plane(j, carry):
            sides = []
            for m in range(1, n):
                coef = choose(j, [float(ky[a, (a + m) % n]) for a in range(n)])
                sides.append((coef, jnp.where(j + m >= n, j + m - n, j + m)))
            v = [[source[at(k * n + i, j), :] for i in range(n)] for k in range(n)]

            def around(u):
                turned = pltpu.roll(u, 4, 0)
                return turned, jnp.where(odd, pltpu.roll(turned, 32, 1), pltpu.roll(turned, 96, 1))

            for k in range(n):
                left, left_far = around(v[k][n - 1])
                right, right_far = around(v[k][0])
                for i in range(n):
                    r = k * n + i
                    total = level.diag[at(r, j), :] * v[k][i] - level.edge[at(r, j), :]
                    for m in range(n):
                        if m != i:
                            total = total + float(kx[i, m]) * v[k][m]
                    for m in range(n):
                        if m != k:
                            total = total + float(kz[k, m]) * v[m][i]
                    for coef, far in sides:
                        total = total + coef * source[at(r, far), :]
                    if i == 0:
                        total = total - level.gains[0] * jnp.where(low_half, left_far, left)
                    if i == n - 1:
                        total = total - level.gains[1] * jnp.where(low_half, right, right_far)
                    if k == 0:
                        u = v[n - 1][i]
                        moved = jnp.where(element == 0, pltpu.roll(u, 97, 1), pltpu.roll(u, 1, 1))
                        total = total - level.gains[4] * moved
                    if k == n - 1:
                        u = v[0][i]
                        moved = jnp.where(element == EZ - 1, pltpu.roll(u, 31, 1), pltpu.roll(u, 127, 1))
                        total = total - level.gains[5] * moved
                    out = v[k][i] + (same * total + swap * pltpu.roll(total, 64, 1))
                    carry = finish(at(r, j), v[k][i], out, carry)
            return carry
        return lax.fori_loop(0, n, plane, carry)

    def smooth_first(p):
        level = levels[p]
        level.dir[...] = level.jac[...] * level.f[...]
        def finish(where, v, av, carry):
            level.x[where, :] = keep * v + push * level.jac[where, :] * (level.f[where, :] - av)
            return carry
        apply(p, level.dir, finish, 0)

    def defect(p):
        level = levels[p]
        def finish(where, v, av, carry):
            level.res[where, :] = level.f[where, :] - av
            return carry
        apply(p, level.x, finish, 0)

    def smooth_again(p):
        level = levels[p]
        def middle_step(where, v, av, carry):
            left = level.f[where, :] - av
            level.res[where, :] = left
            level.dir[where, :] = level.jac[where, :] * left
            return carry
        apply(p, level.x, middle_step, 0)
        def finish(where, v, av, carry):
            step = push * level.jac[where, :] * (level.res[where, :] - av)
            level.x[where, :] = level.x[where, :] + keep * v + step
            return carry
        apply(p, level.dir, finish, 0)

    def combine(weights, parts):
        total = None
        for weight, part in zip(weights, parts):
            if abs(weight) > 1e-14:
                term = part if abs(weight - 1.0) < 1e-14 else float(weight) * part
                total = term if total is None else total + term
        return total

    def change(table, source, target, add):
        m, n = table.shape
        for i in range(n):
            parts = [source[pl.ds((k * n + i) * n * 8, 8 * n), :] for k in range(n)]
            for k in range(m):
                half[pl.ds((k * n + i) * n * 8, 8 * n), :] = combine(table[k], parts)
        for k in range(m):
            parts = [half[pl.ds((k * n + i) * n * 8, 8 * n), :] for i in range(n)]
            for i in range(m):
                line = combine(table[i], parts)
                points = [line[8 * j : 8 * j + 8] for j in range(n)]
                for j in range(m):
                    value = combine(table[j], points)
                    where = tile((k * m + i) * m + j)
                    target[where, :] = target[where, :] + value if add else value

    def down(n, m):
        fine_nodes, fine_weights = lobatto(n)
        coarse_nodes, coarse_weights = lobatto(m)
        table = lagrange_table(coarse_nodes, fine_nodes)
        return (1.0 / coarse_weights)[:, None] * table.T * fine_weights[None, :]

    def up(m, n):
        return lagrange_table(lobatto(m)[0], lobatto(n)[0])

    smooth_first(0)
    defect(0)
    change(down(5, 3), fine.res, middle.f, False)
    smooth_first(1)
    defect(1)
    change(down(3, 2), middle.res, coarse.f, False)
    smooth_first(2)
    change(up(2, 3), coarse.x, middle.x, True)
    smooth_again(1)
    change(up(3, 5), middle.x, fine.x, True)
    smooth_again(0)

    def last(where, v, av, carry):
        fields[where, :] = av
        return carry
    apply(0, fine.x, last, 0)
    fields[FIELD : 2 * FIELD, :] = fine.f[...]
    column = (my_gx % 2) * 4 + my_gy
    fields[2 * FIELD : 2 * FIELD + 125, :] = fine.x[pl.ds(column, 125, stride=8), :]
    fields[2 * FIELD + 125 : 2 * FIELD + 128, :] = jnp.zeros((3, 128), F32)


def finish_kernel(own, other, guess, sol, res_out, arnoldi, cols, outs):
    sec = lax.axis_index("section")
    my_gx, my_gy = lax.axis_index("gx"), lax.axis_index("gy")
    whole, back, back_matrix, blocks, cross = split_sections()
    weights = jnp.where(iota((8, 128), 1) < 64, float(cross[0]), float(cross[1]))
    nothing = jnp.zeros((8, 128), F32)

    def product(a, b, c, d):
        return a * c + b * d + weights * (a * d + b * c)

    def sums(step, carry):
        uppers, sizes = carry
        for m in range(5):
            r = pl.multiple_of(step * 40, 8) + m * 8
            a, b = own[pl.ds(r, 8), :], other[pl.ds(r, 8), :]
            c, d = own[pl.ds(FIELD + r, 8), :], other[pl.ds(FIELD + r, 8), :]
            uppers = uppers + product(a, b, c, d)
            sizes = sizes + product(c, d, c, d)
        return uppers, sizes
    uppers, sizes = lax.fori_loop(0, 25, sums, (nothing, nothing))
    size = jnp.sum(sizes, keepdims=True)
    upper = jnp.sum(uppers, keepdims=True) / size

    def remainder(step, carry):
        for m in range(5):
            r = pl.multiple_of(step * 40, 8) + m * 8
            a = own[pl.ds(r, 8), :] - upper * own[pl.ds(FIELD + r, 8), :]
            b = other[pl.ds(r, 8), :] - upper * other[pl.ds(FIELD + r, 8), :]
            carry = carry + product(a, b, a, b)
        return carry
    rest = jnp.sum(lax.fori_loop(0, 25, remainder, nothing), keepdims=True)
    beta = jnp.sqrt(size)
    lower = jnp.sqrt(rest) / beta
    weight = upper / (upper * upper + lower * lower)
    entries = float(125 * EZ * COLS * 4)
    for place_out, value in enumerate((beta * (1.0 / math.sqrt(entries)), upper, lower)):
        arnoldi[place_out] = value[0, 0]

    lane = iota((32, 128), 1)
    here = lane // EZ % 2 == my_gx // 2
    factors = []
    for s in range(2):
        row = []
        for p in range(2):
            parts = []
            for mine in range(2):
                t = whole[2 * mine + s]
                pairs = [jnp.where(lane < 64, float(t[2 * q]), float(t[2 * q + 1])) for q in range(2)]
                parts.append(pairs[mine] if p == 0 else pairs[1 - mine])
            row.append(jnp.where(here, jnp.where(sec == 0, parts[0], parts[1]), 0.0))
        factors.append(row)
    column = (my_gx % 2) * 4 + my_gy
    cols[...] = jnp.zeros_like(cols)
    total = jnp.zeros((128, 160), F32)
    for k in range(5):
        for p, source in enumerate((own, other)):
            image = source[pl.ds(k * 200 + column, 25, stride=8), :]
            start = source[pl.ds(FIELD + k * 200 + column, 25, stride=8), :]
            for s in range(2):
                factor = factors[s][p][:25]
                z = weight * (factor * source[2 * FIELD + k * 25 : 2 * FIELD + k * 25 + 25, :])
                r = factor * (start - weight * image)
                if p == 0:
                    cols[s * 32 : s * 32 + 25, :] = z
                    cols[64 + s * 32 : 64 + s * 32 + 25, :] = r
                else:
                    cols[s * 32 : s * 32 + 25, :] += z
                    cols[64 + s * 32 : 64 + s * 32 + 25, :] += r
        hit = (iota((128, 160), 1) == 5 * (iota((128, 160), 0) % EZ) + k).astype(F32)
        total = total + exact_dot(cols[...], hit)
    outs[...] = total
    for i in range(5):
        for j in range(5):
            r = 5 * i + j
            for s in range(2):
                sol[i, j, s : s + 1, :] = guess[i, j, s : s + 1, :] + outs[s * 32 + r : s * 32 + r + 1, :]
                res_out[i, j, s : s + 1, :] = outs[64 + s * 32 + r : 64 + s * 32 + r + 1, :]


def cycle(blocks):
    scratch = []
    for n in (5, 3, 2):
        scratch += [pltpu.VMEM((n**3 * 8, 128), F32)] * 7
    scratch += [
        pltpu.VMEM((COLS * PIECE, 128), F32),
        pltpu.VMEM((FIELD, 128), F32),
        pltpu.VMEM((FIELD, 128), F32),
    ]
    return pl.pallas_call(
        cycle_kernel,
        out_shape=jax.ShapeDtypeStruct((2 * FIELD + 128, 128), F32),
        in_specs=[VMEM] * 4,
        out_specs=VMEM,
        scratch_shapes=scratch,
        compiler_params=limit(24),
        name="cycle",
    )(*blocks)


def finish(own, other, guess):
    return pl.pallas_call(
        finish_kernel,
        out_shape=[
            jax.ShapeDtypeStruct(guess.shape, F32),
            jax.ShapeDtypeStruct(guess.shape, F32),
            jax.ShapeDtypeStruct((3,), F32),
        ],
        in_specs=[VMEM] * 3,
        out_specs=[VMEM, VMEM, pl.BlockSpec(memory_space=pltpu.SMEM)],
        scratch_shapes=[pltpu.VMEM((128, 128), F32), pltpu.VMEM((128, 160), F32)],
        compiler_params=limit(24),
        name="finish",
    )(own, other, guess)


def turn(x, axis, offset):
    return lax.ppermute(x, axis, [(n, (n + offset) % 4) for n in range(4)])


def swap_cores(x):
    return lax.ppermute(x, "section", [(0, 1), (1, 0)])


def gathered_body(rhs, guess, kappa, bc_flags):
    rhs, guess = (jnp.transpose(v, (1, 2, 0, 3)) for v in (rhs, guess))
    halos = [turn(guess, axis, offset) for axis in ("gx", "gy") for offset in (1, 3)]
    base = local_part(rhs, guess, kappa, bc_flags)
    mine, theirs = halo_part(*base, halos)
    got = swap_cores(theirs)
    piece = jnp.concatenate([mine[:HALF] + got, mine[HALF:]])
    line = jnp.concatenate([piece] + [turn(piece, "gx", offset) for offset in (1, 2, 3)])
    blocks = [line] + [turn(line, "gy", offset) for offset in (1, 2, 3)]
    own = cycle(blocks)
    sol, res, arnoldi = finish(own, swap_cores(own), guess)
    sol, res = (jnp.transpose(v, (2, 0, 1, 3)) for v in (sol, res))
    return sol, res, arnoldi


def solution(mesh):
    placed = (
        P("section", "gx", "gy", None),
        P("section", "gx", "gy", None),
        P("gx", "gy", None),
        P(None, "gx", "gy", None),
    )
    sizes = (mesh.shape["section"], mesh.shape["gx"], mesh.shape["gy"])

    def step(rhs, guess, kappa, bc_flags):
        fits = sizes == (2, 4, 4) and rhs.shape == (4, 20, 20, 160)
        return jax.shard_map(
            gathered_body if fits else stepwise,
            mesh=mesh,
            in_specs=placed,
            out_specs=(P("section", "gx", "gy", None), P("section", "gx", "gy", None), P()),
            check_vma=False,
        )(rhs, guess, kappa, bc_flags)

    return step
```

profile of v0, /device:TPU:0, one launch (start us, length us, event | category | flops | bytes accessed | tf_op | source)
XLA Modules:
  0.0 52.5 jit_solution(14669378515472476462)
XLA Ops:
  0.6 3.9 %collective-permute-start.3 = (f32[5,5,2,160]{3,2,1,0:T(2,128)}, f32[5,5,2,160]{3,2,1,0:T(2,128)S(1)}, u32[]{:S(2)}, u32[]{:S(2)}) collective-permute-start(f32[5,5,2,160]{3,2,1,0:T(2,128)} %bitcast.4), channel_id=1, source_target_pairs={{0,3},{1,0},{2,1},{3,2},{4,7},{5,4},{6,5},{7,6},{8,11},{9,8},{10,9... | collective-permute-start | bytes 96008 | tf_op jit(solution)/shard_map/ppermute | solution.py:954
  4.6 0.0 collective-permute-start.2
  4.6 3.6 %collective-permute-start.1 = (f32[5,5,2,160]{3,2,1,0:T(2,128)}, f32[5,5,2,160]{3,2,1,0:T(2,128)S(1)}, u32[]{:S(2)}, u32[]{:S(2)}) collective-permute-start(f32[5,5,2,160]{3,2,1,0:T(2,128)} %bitcast.6), channel_id=1, source_target_pairs={{0,12},{4,0},{8,4},{12,8},{1,13},{5,1},{9,5},{13,9},{2,14},{6,2},{... | collective-permute-start | bytes 96008 | tf_op jit(solution)/shard_map/ppermute | solution.py:954
  8.2 0.0 collective-permute-start
  8.2 0.9 %copy-done = f32[160,320]{1,0:T(8,128)S(1)} copy-done((f32[160,320]{1,0:T(8,128)S(1)}, f32[160,320]{1,0:T(8,128)}, u32[]{:S(2)}) %copy-start) | copy-done | bytes 204824
  9.1 0.8 %copy-done.1 = f32[2,5,5,160]{3,0,2,1:T(2,128)S(1)} copy-done((f32[2,5,5,160]{3,0,2,1:T(2,128)S(1)}, f32[2,5,5,160]{3,0,2,1:T(2,128)}, u32[]{:S(2)}) %copy-start.1) | copy-done | bytes 32024
  9.9 0.8 %copy-done.3 = f32[2,5,5,160]{3,0,2,1:T(2,128)S(1)} copy-done((f32[2,5,5,160]{3,0,2,1:T(2,128)S(1)}, f32[2,5,5,160]{3,0,2,1:T(2,128)}, u32[]{:S(2)}) %copy-start.3) | copy-done | bytes 32024
  10.7 0.8 %copy-done.4 = f32[5,5,160]{2,1,0:T(8,128)S(1)} copy-done((f32[5,5,160]{2,1,0:T(8,128)S(1)}, f32[5,5,160]{2,1,0:T(8,128)}, u32[]{:S(2)}) %copy-start.4) | copy-done | bytes 16024
  11.5 0.8 %copy-done.5 = f32[64,64]{1,0:T(8,128)S(1)} copy-done((f32[64,64]{1,0:T(8,128)S(1)}, f32[64,64]{1,0:T(8,128)}, u32[]{:S(2)}) %copy-start.5) | copy-done | bytes 16408
  12.3 0.7 %copy-done.6 = s32[6,1,1,32]{3,2,1,0:T(1,128)S(1)} copy-done((s32[6,1,1,32]{3,2,1,0:T(1,128)S(1)}, s32[6,1,1,32]{3,2,1,0:T(1,128)}, u32[]{:S(2)}) %copy-start.6) | copy-done | bytes 792
  13.0 2.1 %local_part.1 = (f32[96,128]{1,0:T(8,128)S(1)}, f32[64,128]{1,0:T(8,128)S(1)}, f32[64,160]{1,0:T(8,128)S(1)}) custom-call(f32[5,5,2,160]{3,2,1,0:T(2,128)S(1)} %bitcast.10, f32[5,5,2,160]{3,2,1,0:T(2,128)S(1)} %bitcast.8, f32[5,5,160]{2,1,0:T(8,128)S(1)} %copy-done.4, s32[6,1,1,32]{3,2,1,0:T(1,128)S(1)} %copy-done.6, f32[64,64]{1,0:T(8,128)S(1)} %copy-done.5, ...), custom_call_target="tpu_custom_call" | custom-call | tf_op jit(solution)/shard_map/local_part/pallas_call | solution.py:556
  15.1 0.0 collective-permute-done.3.ya
  15.1 0.0 collective-permute-done.2.yb
  15.1 0.0 collective-permute-done.xb
  15.1 0.5 %halo_part.1 = (f32[96,128]{1,0:T(8,128)S(1)}, f32[64,128]{1,0:T(8,128)S(1)}) custom-call(f32[96,128]{1,0:T(8,128)S(1)} %get-tuple-element.11.base_mine, f32[64,128]{1,0:T(8,128)S(1)} %get-tuple-element.12.base_theirs, f32[64,160]{1,0:T(8,128)S(1)} %get-tuple-element.13.faces, f32[5,5,2,160]{3,2,1,0:T(2,128)S(1)} %collective-permute-done.xb, ...), custom_call_target="tpu_custom_call" | custom-call | tf_op jit(solution)/shard_map/halo_part/pallas_call | solution.py:581
  15.6 0.1 collective-permute-start.4
  15.7 1.2 %collective-permute-done.4 = f32[64,128]{1,0:T(8,128)S(1)} collective-permute-done((f32[64,128]{1,0:T(8,128)S(1)}, f32[64,128]{1,0:T(8,128)S(1)}, u32[]{:S(2)}, u32[]{:S(2)}) %collective-permute-start.4) | collective-permute-done | bytes 32800 | tf_op jit(solution)/shard_map/ppermute | solution.py:958
  16.9 0.0 copy-start.2
  17.0 0.1 collective-permute-start.5
  17.0 3.9 %collective-permute-start.7 = (f32[96,128]{1,0:T(8,128)S(1)}, f32[96,128]{1,0:T(8,128)S(1)}, u32[]{:S(2)}, u32[]{:S(2)}) collective-permute-start(f32[96,128]{1,0:T(8,128)S(1)} %pad_maximum_fusion), channel_id=1, source_target_pairs={{0,12},{4,0},{8,4},{12,8},{1,13},{5,1},{9,5},{13,9},{2,14},{6,2},{... | collective-permute-start | bytes 147464 | tf_op jit(solution)/shard_map/ppermute | solution.py:954
  20.9 0.5 collective-permute-start.6
  21.4 1.6 %collective-permute-done.5 = f32[96,128]{1,0:T(8,128)S(1)} collective-permute-done((f32[96,128]{1,0:T(8,128)S(1)}, f32[96,128]{1,0:T(8,128)S(1)}, u32[]{:S(2)}, u32[]{:S(2)}) %collective-permute-start.5) | collective-permute-done | bytes 49184 | tf_op jit(solution)/shard_map/ppermute | solution.py:954
  23.0 3.1 %collective-permute-done.6 = f32[96,128]{1,0:T(8,128)S(1)} collective-permute-done((f32[96,128]{1,0:T(8,128)S(1)}, f32[96,128]{1,0:T(8,128)S(1)}, u32[]{:S(2)}, u32[]{:S(2)}) %collective-permute-start.6) | collective-permute-done | bytes 49184 | tf_op jit(solution)/shard_map/ppermute | solution.py:954
  26.1 3.0 %collective-permute-start.10 = (f32[384,128]{1,0:T(8,128)S(1)}, f32[384,128]{1,0:T(8,128)S(1)}, u32[]{:S(2)}, u32[]{:S(2)}) collective-permute-start(f32[384,128]{1,0:T(8,128)S(1)} %constant_dynamic-update-slice_fusion.block0), channel_id=1, source_target_pairs={{0,3},{1,0},{2,1},{3,2},{4,7},{5,4},{6,5},{7,6},{8,11},{9,8},{10,9... | collective-permute-start | bytes 589832 | tf_op jit(solution)/shard_map/ppermute | solution.py:954
  29.1 0.5 collective-permute-start.9
  29.6 0.1 collective-permute-start.8
  29.7 4.6 %collective-permute-done.10.block3 = f32[384,128]{1,0:T(8,128)S(1)} collective-permute-done((f32[384,128]{1,0:T(8,128)S(1)}, f32[384,128]{1,0:T(8,128)S(1)}, u32[]{:S(2)}, u32[]{:S(2)}) %collective-permute-start.10) | collective-permute-done | bytes 196640 | tf_op jit(solution)/shard_map/ppermute | solution.py:954
  34.3 4.3 %collective-permute-done.9.block2 = f32[384,128]{1,0:T(8,128)S(1)} collective-permute-done((f32[384,128]{1,0:T(8,128)S(1)}, f32[384,128]{1,0:T(8,128)S(1)}, u32[]{:S(2)}, u32[]{:S(2)}) %collective-permute-start.9) | collective-permute-done | bytes 196640 | tf_op jit(solution)/shard_map/ppermute | solution.py:954
  38.6 8.6 %cycle.1.own = f32[2128,128]{1,0:T(8,128)S(1)} custom-call(f32[384,128]{1,0:T(8,128)S(1)} %constant_dynamic-update-slice_fusion.block0, f32[384,128]{1,0:T(8,128)S(1)} %collective-permute-done.8.block1, f32[384,128]{1,0:T(8,128)S(1)} %collective-permute-done.9.block2, f32[384,128]{1,0:T(8,128)S(1)} %collective-permute-done.10.block3), custom_call_target="tpu_custom_call" | custom-call | tf_op jit(solution)/shard_map/cycle/pallas_call | solution.py:926
  47.2 0.1 collective-permute-start.11
  47.3 2.7 %collective-permute-done.11.other = f32[2128,128]{1,0:T(8,128)S(1)} collective-permute-done((f32[2128,128]{1,0:T(8,128)S(1)}, f32[2128,128]{1,0:T(8,128)S(1)}, u32[]{:S(2)}, u32[]{:S(2)}) %collective-permute-start.11) | collective-permute-done | bytes 1089568 | tf_op jit(solution)/shard_map/ppermute | solution.py:958
  50.0 2.5 %finish.1 = (f32[5,5,2,160]{3,2,1,0:T(2,128)}, f32[5,5,2,160]{3,2,1,0:T(2,128)}, f32[3]{0:T(128)}) custom-call(f32[2128,128]{1,0:T(8,128)S(1)} %cycle.1.own, f32[2128,128]{1,0:T(8,128)S(1)} %collective-permute-done.11.other, f32[5,5,2,160]{3,2,1,0:T(2,128)S(1)} %bitcast.9), custom_call_target="tpu_custom_call" | custom-call | tf_op jit(solution)/shard_map/finish/pallas_call | solution.py:938
  (16 shorter events, 0.1 us)
Async XLA Ops:
  0.6 14.4 %collective-permute-start.3 = (f32[5,5,2,160]{3,2,1,0:T(2,128)}, f32[5,5,2,160]{3,2,1,0:T(2,128)S(1)}, u32[]{:S(2)}, u32[]{:S(2)}) collective-permute-start(f32[5,5,2,160]{3,2,1,0:T(2,128)} %bitcast.4), channel_id=1, source_target_pairs={{0,3},{1,0},{2,1},{3,2},{4,7},{5,4},{6,5},{7,6},{8,11},{9,8},{10,9... | collective-permute-start | bytes 96008 | tf_op jit(solution)/shard_map/ppermute | solution.py:954
  4.6 10.5 %collective-permute-start.2 = (f32[5,5,2,160]{3,2,1,0:T(2,128)}, f32[5,5,2,160]{3,2,1,0:T(2,128)S(1)}, u32[]{:S(2)}, u32[]{:S(2)}) collective-permute-start(f32[5,5,2,160]{3,2,1,0:T(2,128)} %bitcast.5), channel_id=1, source_target_pairs={{0,1},{1,2},{2,3},{3,0},{4,5},{5,6},{6,7},{7,4},{8,9},{9,10},{10,1... | collective-permute-start | bytes 96008 | tf_op jit(solution)/shard_map/ppermute | solution.py:954
  4.6 10.5 %collective-permute-start.1 = (f32[5,5,2,160]{3,2,1,0:T(2,128)}, f32[5,5,2,160]{3,2,1,0:T(2,128)S(1)}, u32[]{:S(2)}, u32[]{:S(2)}) collective-permute-start(f32[5,5,2,160]{3,2,1,0:T(2,128)} %bitcast.6), channel_id=1, source_target_pairs={{0,12},{4,0},{8,4},{12,8},{1,13},{5,1},{9,5},{13,9},{2,14},{6,2},{... | collective-permute-start | bytes 96008 | tf_op jit(solution)/shard_map/ppermute | solution.py:954
  8.2 6.9 %collective-permute-start = (f32[5,5,2,160]{3,2,1,0:T(2,128)}, f32[5,5,2,160]{3,2,1,0:T(2,128)S(1)}, u32[]{:S(2)}, u32[]{:S(2)}) collective-permute-start(f32[5,5,2,160]{3,2,1,0:T(2,128)} %bitcast.7), channel_id=1, source_target_pairs={{0,4},{4,8},{8,12},{12,0},{1,5},{5,9},{9,13},{13,1},{2,6},{6,10},{... | collective-permute-start | bytes 96008 | tf_op jit(solution)/shard_map/ppermute | solution.py:954
  8.2 0.9 %copy-start = (f32[160,320]{1,0:T(8,128)S(1)}, f32[160,320]{1,0:T(8,128)}, u32[]{:S(2)}) copy-start(f32[160,320]{1,0:T(8,128)} %constant.5.clone.lines_in) | copy-start | bytes 614404
  9.1 0.8 %copy-start.1 = (f32[2,5,5,160]{3,0,2,1:T(2,128)S(1)}, f32[2,5,5,160]{3,0,2,1:T(2,128)}, u32[]{:S(2)}) copy-start(f32[2,5,5,160]{3,0,2,1:T(2,128)} %param.7) | copy-start | bytes 96004
  9.9 0.8 %copy-start.3 = (f32[2,5,5,160]{3,0,2,1:T(2,128)S(1)}, f32[2,5,5,160]{3,0,2,1:T(2,128)}, u32[]{:S(2)}) copy-start(f32[2,5,5,160]{3,0,2,1:T(2,128)} %param.6) | copy-start | bytes 96004
  10.7 0.8 %copy-start.4 = (f32[5,5,160]{2,1,0:T(8,128)S(1)}, f32[5,5,160]{2,1,0:T(8,128)}, u32[]{:S(2)}) copy-start(f32[5,5,160]{2,1,0:T(8,128)} %kappa_in.1) | copy-start | bytes 48004
  11.5 0.8 %copy-start.5 = (f32[64,64]{1,0:T(8,128)S(1)}, f32[64,64]{1,0:T(8,128)}, u32[]{:S(2)}) copy-start(f32[64,64]{1,0:T(8,128)} %constant.4.clone.rows_in) | copy-start | bytes 49156
  12.3 0.7 %copy-start.6 = (s32[6,1,1,32]{3,2,1,0:T(1,128)S(1)}, s32[6,1,1,32]{3,2,1,0:T(1,128)}, u32[]{:S(2)}) copy-start(s32[6,1,1,32]{3,2,1,0:T(1,128)} %flags_in.1) | copy-start | bytes 2308
  15.6 1.3 %collective-permute-start.4 = (f32[64,128]{1,0:T(8,128)S(1)}, f32[64,128]{1,0:T(8,128)S(1)}, u32[]{:S(2)}, u32[]{:S(2)}) collective-permute-start(f32[64,128]{1,0:T(8,128)S(1)} %get-tuple-element.15), channel_id=1, source_target_pairs={{0,16},{16,0},{1,17},{17,1},{2,18},{18,2},{3,19},{19,3},{4,20},{20... | collective-permute-start | bytes 98312 | tf_op jit(solution)/shard_map/ppermute | solution.py:958
  16.9 33.1 %copy-start.2 = (f32[2,5,5,160]{3,0,2,1:T(2,128)S(1)}, f32[2,5,5,160]{3,0,2,1:T(2,128)}, u32[]{:S(2)}) copy-start(f32[2,5,5,160]{3,0,2,1:T(2,128)} %param.7) | copy-start | bytes 96004
  17.0 6.0 %collective-permute-start.5 = (f32[96,128]{1,0:T(8,128)S(1)}, f32[96,128]{1,0:T(8,128)S(1)}, u32[]{:S(2)}, u32[]{:S(2)}) collective-permute-start(f32[96,128]{1,0:T(8,128)S(1)} %pad_maximum_fusion), channel_id=1, source_target_pairs={{0,4},{4,8},{8,12},{12,0},{1,5},{5,9},{9,13},{13,1},{2,6},{6,10},{... | collective-permute-start | bytes 147464 | tf_op jit(solution)/shard_map/ppermute | solution.py:954
  17.0 9.0 %collective-permute-start.7 = (f32[96,128]{1,0:T(8,128)S(1)}, f32[96,128]{1,0:T(8,128)S(1)}, u32[]{:S(2)}, u32[]{:S(2)}) collective-permute-start(f32[96,128]{1,0:T(8,128)S(1)} %pad_maximum_fusion), channel_id=1, source_target_pairs={{0,12},{4,0},{8,4},{12,8},{1,13},{5,1},{9,5},{13,9},{2,14},{6,2},{... | collective-permute-start | bytes 147464 | tf_op jit(solution)/shard_map/ppermute | solution.py:954
  20.9 5.2 %collective-permute-start.6 = (f32[96,128]{1,0:T(8,128)S(1)}, f32[96,128]{1,0:T(8,128)S(1)}, u32[]{:S(2)}, u32[]{:S(2)}) collective-permute-start(f32[96,128]{1,0:T(8,128)S(1)} %pad_maximum_fusion), channel_id=1, source_target_pairs={{0,8},{4,12},{8,0},{12,4},{1,9},{5,13},{9,1},{13,5},{2,10},{6,14},... | collective-permute-start | bytes 147464 | tf_op jit(solution)/shard_map/ppermute | solution.py:954
  26.1 8.2 %collective-permute-start.10 = (f32[384,128]{1,0:T(8,128)S(1)}, f32[384,128]{1,0:T(8,128)S(1)}, u32[]{:S(2)}, u32[]{:S(2)}) collective-permute-start(f32[384,128]{1,0:T(8,128)S(1)} %constant_dynamic-update-slice_fusion.block0), channel_id=1, source_target_pairs={{0,3},{1,0},{2,1},{3,2},{4,7},{5,4},{6,5},{7,6},{8,11},{9,8},{10,9... | collective-permute-start | bytes 589832 | tf_op jit(solution)/shard_map/ppermute | solution.py:954
  29.1 9.5 %collective-permute-start.9 = (f32[384,128]{1,0:T(8,128)S(1)}, f32[384,128]{1,0:T(8,128)S(1)}, u32[]{:S(2)}, u32[]{:S(2)}) collective-permute-start(f32[384,128]{1,0:T(8,128)S(1)} %constant_dynamic-update-slice_fusion.block0), channel_id=1, source_target_pairs={{0,2},{1,3},{2,0},{3,1},{4,6},{5,7},{6,4},{7,5},{8,10},{9,11},{10,... | collective-permute-start | bytes 589832 | tf_op jit(solution)/shard_map/ppermute | solution.py:954
  29.6 9.0 %collective-permute-start.8 = (f32[384,128]{1,0:T(8,128)S(1)}, f32[384,128]{1,0:T(8,128)S(1)}, u32[]{:S(2)}, u32[]{:S(2)}) collective-permute-start(f32[384,128]{1,0:T(8,128)S(1)} %constant_dynamic-update-slice_fusion.block0), channel_id=1, source_target_pairs={{0,1},{1,2},{2,3},{3,0},{4,5},{5,6},{6,7},{7,4},{8,9},{9,10},{10,1... | collective-permute-start | bytes 589832 | tf_op jit(solution)/shard_map/ppermute | solution.py:954
  47.2 2.8 %collective-permute-start.11 = (f32[2128,128]{1,0:T(8,128)S(1)}, f32[2128,128]{1,0:T(8,128)S(1)}, u32[]{:S(2)}, u32[]{:S(2)}) collective-permute-start(f32[2128,128]{1,0:T(8,128)S(1)} %cycle.1.own), channel_id=1, source_target_pairs={{0,16},{16,0},{1,17},{17,1},{2,18},{18,2},{3,19},{19,3},{4,20},{20... | collective-permute-start | bytes 3268616 | tf_op jit(solution)/shard_map/ppermute | solution.py:958
where the time goes:
time: 52.9 us; the launch traced here: 52.5 us
  waiting for transfers between devices  17.4 us (33%)
  starting transfers between devices  15.7 us (30%)
  Pallas kernels  13.7 us (26%)
  local copies, waits for them, and re-layouts  4.79 us (9%)
  between operations  0.76 us (1%)
    ppermute x10, starting transfers between devices, turn(): return lax.ppermute(x, axis, [(n, (n + offset) % 4) for n in range(4)])  15.6 us
    ppermute x10, waiting for transfers between devices, turn(): return lax.ppermute(x, axis, [(n, (n + offset) % 4) for n in range(4)])  13.5 us
    pallas_call x1, Pallas kernels, cycle(): pl.pallas_call(cycle_kernel, out_shape=jax.ShapeDtypeStruct((2 * FIELD +...  8.64 us
    unnamed x16, local copies, waits for them, and re-layouts  4.79 us
    ppermute x2, waiting for transfers between devices, swap_cores(): return lax.ppermute(x, 'section', [(0, 1), (1, 0)])  3.9 us
    pallas_call x1, Pallas kernels, finish(): pl.pallas_call(finish_kernel, out_shape=[jax.ShapeDtypeStruct(guess.shape...  2.47 us
    pallas_call x1, Pallas kernels, local_part(): pl.pallas_call(local_kernel, out_shape=[jax.ShapeDtypeStruct((PIECE, 128)...  2.09 us
  transfers between devices with their start and end apart: 12, of which 6 were waited for; matrix products, arithmetic and copies ran while one was open for 0% of the time, Pallas kernels for 4%

commit v1 on v0

--- a/solution.py
+++ b/solution.py
@@ -445,7 +445,7 @@
 
 
 def local_kernel(
-    rhs_in, guess_in, kappa_in, flags_in, rows_in, lines_in, mine, theirs, faces,
+    rhs_in, guess_in, kappa_in, flags_in, rows_in, lines_in, base,
     rhs, guess, kappa, flags, rows_t, lines_t, sems, x, kap, stack, own_nodes, other_nodes, krep,
 ):
     sec = lax.axis_index("section")
@@ -475,8 +475,10 @@
     gx = jnp.where(row < 5, gains[0], jnp.where((row >= 20) & (row < 25), gains[1], none))
     gy = jnp.where(row % 5 == 0, gains[2], jnp.where(row % 5 == 4, gains[3], none))
     gz = jnp.where(lane == 0, gains[4], jnp.where(lane == 4, gains[5], none))
-    faces[0:32, :] = gx
-    faces[32:64, :] = jnp.where(row < 25, gy, none)
+    gy = jnp.where(row < 25, gy, none)
+    for place, gain in ((160, gx), (192, gy)):
+        base[place : place + 32, :] = gain[:, :128]
+        base[64 + place : 96 + place, :EZ] = gain[:, 128:]
     field = x[...]
     along = exact_dot(rows_t[...], field)
     across = exact_dot(field, lines_t[...])
@@ -507,27 +509,34 @@
     upper = iota((1, 128), 1) < 64
     for r in range(3):
         own_nodes[125 + r : 126 + r, :] = jnp.where(upper, shown[2 * r : 2 * r + 1], shown[2 * r + 1 : 2 * r + 2])
-    mine[:HALF, :] = pack_nodes(own_nodes)
-    theirs[...] = pack_nodes(other_nodes)
-    mine[HALF:, :] = choose(iota((32, 128), 1) // EZ, [krep[32 * q : 32 * q + 32, :] for q in range(4)])
-
-
-def halo_kernel(base_mine, base_theirs, faces, xb, xa, yb, ya, mine, theirs, nbx, nby, own_nodes, other_nodes):
+    base[:HALF, :] = pack_nodes(own_nodes)
+    base[PIECE : PIECE + HALF, :] = pack_nodes(other_nodes)
+    base[HALF:PIECE, :] = choose(iota((32, 128), 1) // EZ, [krep[32 * q : 32 * q + 32, :] for q in range(4)])
+
+
+def halo_kernel(base, x1, x3, y1, y3, mine, theirs, near, own_nodes, other_nodes):
     sec = lax.axis_index("section")
-    for ref in (nbx, nby, own_nodes, other_nodes):
+    even_x = lax.axis_index("gx") % 2 == 0
+    even_y = lax.axis_index("gy") % 2 == 0
+    for ref in (near, own_nodes, other_nodes):
         ref[...] = jnp.zeros_like(ref)
     for m in range(5):
         for s in range(2):
             r = s * 32
-            nbx[r + m : r + m + 1, :] = xb[4, m, s : s + 1, :]
-            nbx[r + 20 + m : r + 21 + m, :] = xa[0, m, s : s + 1, :]
-            nby[r + 5 * m : r + 5 * m + 1, :] = yb[m, 4, s : s + 1, :]
-            nby[r + 5 * m + 4 : r + 5 * m + 5, :] = ya[m, 0, s : s + 1, :]
-    gx, gy = faces[0:32, :], faces[32:64, :]
+            one = slice(s, s + 1)
+            near[r + m : r + m + 1, :] = jnp.where(even_x, x3[4, m, one, :], x1[4, m, one, :])
+            near[r + 20 + m : r + 21 + m, :] = jnp.where(even_x, x1[0, m, one, :], x3[0, m, one, :])
+            r += 64
+            near[r + 5 * m : r + 5 * m + 1, :] = jnp.where(even_y, y3[m, 4, one, :], y1[m, 4, one, :])
+            near[r + 5 * m + 4 : r + 5 * m + 5, :] = jnp.where(even_y, y1[m, 0, one, :], y3[m, 0, one, :])
+    gx, gy = (
+        jnp.concatenate([base[r : r + 32, :], base[64 + r : 96 + r, :EZ]], axis=1) for r in (160, 192)
+    )
+    parts_in = []
     for s in range(2):
-        r = slice(s * 32, s * 32 + 32)
-        nbx[r, :] = gx * nbx[r, :] + gy * nby[r, :]
-    source = nbx[...]
+        r = s * 32
+        parts_in.append(gx * near[r : r + 32, :] + gy * near[64 + r : 96 + r, :])
+    source = jnp.concatenate(parts_in, axis=0)
     back_matrix = split_sections()[2]
     for k in range(5):
         parts = exact_dot(source, pick_line(k))
@@ -537,9 +546,9 @@
                 factor = pair_factors(sec, STEP_SIZE * back_matrix, mark, s)
                 total = total + factor * parts[s * 32 : s * 32 + 32]
             target[25 * k : 25 * k + 25, :] = total[:25]
-    mine[:HALF, :] = base_mine[:HALF, :] + pack_nodes(own_nodes)
-    mine[HALF:, :] = base_mine[HALF:, :]
-    theirs[...] = base_theirs[...] + pack_nodes(other_nodes)
+    mine[:HALF, :] = base[:HALF, :] + pack_nodes(own_nodes)
+    mine[HALF:, :] = base[HALF:PIECE, :]
+    theirs[...] = base[PIECE : PIECE + HALF, :] + pack_nodes(other_nodes)
 
 
 VMEM = pl.BlockSpec(memory_space=pltpu.VMEM)
@@ -555,13 +564,9 @@
     operands = (rhs, guess, kappa, flags, jnp.asarray(rows_t), jnp.asarray(lines_t))
     return pl.pallas_call(
         local_kernel,
-        out_shape=[
-            jax.ShapeDtypeStruct((PIECE, 128), F32),
-            jax.ShapeDtypeStruct((HALF, 128), F32),
-            jax.ShapeDtypeStruct((64, 160), F32),
-        ],
+        out_shape=jax.ShapeDtypeStruct((288, 128), F32),
         in_specs=[HBM] * 6,
-        out_specs=[VMEM] * 3,
+        out_specs=VMEM,
         scratch_shapes=[pltpu.VMEM(o.shape, o.dtype) for o in operands]
         + [
             pltpu.SemaphoreType.DMA((6,)),
@@ -572,30 +577,30 @@
             pltpu.VMEM((128, 128), F32),
             pltpu.VMEM((128, 128), F32),
         ],
-        compiler_params=limit(16),
+        compiler_params=limit(60),
         name="local_part",
     )(*operands)
 
 
-def halo_part(base_mine, base_theirs, faces, halos):
+def halo_part(base, halos):
     return pl.pallas_call(
         halo_kernel,
         out_shape=[
             jax.ShapeDtypeStruct((PIECE, 128), F32),
             jax.ShapeDtypeStruct((HALF, 128), F32),
         ],
-        in_specs=[VMEM] * 7,
+        in_specs=[VMEM] * 5,
         out_specs=[VMEM] * 2,
-        scratch_shapes=[pltpu.VMEM((64, 160), F32)] * 2 + [pltpu.VMEM((128, 128), F32)] * 2,
+        scratch_shapes=[pltpu.VMEM((128, 160), F32)] + [pltpu.VMEM((128, 128), F32)] * 2,
         compiler_params=limit(16),
         name="halo_part",
-    )(base_mine, base_theirs, faces, *halos)
+    )(base, *halos)
 
 
 class Level:
     def __init__(self, count, refs):
         self.count = count
-        self.f, self.diag, self.jac, self.x, self.dir, self.res, self.edge = refs
+        self.diag, self.jac, self.x, self.dir, self.res, self.f = refs
         self.tables = [element_matrix(count, d) for d in range(3)]
         self.gains = None
 
@@ -604,12 +609,35 @@
     return pl.ds(index * 8, 8)
 
 
-def cycle_kernel(block0, block1, block2, block3, fields, *scratch):
+def rows_of(pieces, size, r, h):
+    return pieces[pl.ds(8 * h * size + r, 8, stride=size), :]
+
+
+def place_pieces(blocks, pieces, first, size):
+    my_gx, my_gy = lax.axis_index("gx"), lax.axis_index("gy")
+    for b, block in enumerate(blocks):
+        for a in range(4):
+            column = (my_gx ^ a) * 4 + (my_gy ^ b)
+            start = pl.multiple_of(column * size, 8)
+            pieces[pl.ds(start, size), :] = block[a * PIECE + first : a * PIECE + first + size, :]
+
+
+def assemble_kernel(block0, block1, block2, block3, field, pieces):
+    place_pieces((block0, block1, block2, block3), pieces, 0, HALF)
+    odd = iota((8, 128), 1) // EZ % 2 == 1
+    for r in range(HALF):
+        low, high = rows_of(pieces, HALF, r, 0), rows_of(pieces, HALF, r, 1)
+        field[tile(r), :] = jnp.where(odd, pltpu.roll(high, 32, 1), low)
+        field[tile(HALF + r), :] = jnp.where(odd, high, pltpu.roll(low, 96, 1))
+
+
+def cycle_kernel(block0, block1, block2, block3, assembled, fields, *scratch):
     sec = lax.axis_index("section")
     my_gx, my_gy = lax.axis_index("gx"), lax.axis_index("gy")
-    levels = [Level(n, scratch[7 * p : 7 * p + 7]) for p, n in enumerate((5, 3, 2))]
-    pieces, kap, half = scratch[21:24]
+    levels = [Level(n, scratch[6 * p : 6 * p + 6]) for p, n in enumerate((5, 3, 2))]
+    pieces, kap, half = scratch[18:21]
     fine, middle, coarse = levels
+    fine.f = assembled
     lane = iota((8, 128), 1)
     sub = iota((8, 128), 0)
     group = lane // EZ
@@ -632,35 +660,16 @@
     keep = 1.0 + second_rho * first_rho
     push = 2.0 * second_rho / radius * centre
 
-    for b, block in enumerate((block0, block1, block2, block3)):
-        gy = lax.rem(my_gy + 4 - b, 4)
-        for a in range(4):
-            column = lax.rem(my_gx + 4 - a, 4) * 4 + gy
-            start = pl.multiple_of(column * PIECE, 8)
-            pieces[pl.ds(start, PIECE), :] = block[a * PIECE : a * PIECE + PIECE, :]
-
-    def rows_of(r, h):
-        return pieces[pl.ds(8 * h * PIECE + r, 8, stride=PIECE), :]
-
-    def place_nodes(r, last):
-        low, high = rows_of(r, 0), rows_of(r, 1)
-        fine.f[tile(r), :] = jnp.where(odd, pltpu.roll(high, 32, 1), low)
-        if not last:
-            fine.f[tile(64 + r), :] = jnp.where(odd, high, pltpu.roll(low, 96, 1))
-        return low, high
-
-    for r in range(61):
-        place_nodes(r, False)
     flags = []
     for r in range(3):
-        low, high = place_nodes(61 + r, True)
-        turned = [[pltpu.roll(v, 32 * m, 1) if m else v for m in range(4)] for v in (low, high)]
-        flags.append(choose(group, [turned[0][3], turned[1][0], turned[0][1], turned[1][2]]))
-        flags.append(choose(group, [turned[0][1], turned[1][2], turned[0][3], turned[1][0]]))
+        got = assembled[tile(125 + r), :]
+        across = pltpu.roll(got, 64, 1)
+        flags += [jnp.where(lane < 64, got, across), jnp.where(lane < 64, across, got)]
+    place_pieces((block0, block1, block2, block3), pieces, HALF, 32)
     for r in range(32):
         turned = []
         for h in range(2):
-            got = rows_of(HALF + r, h)
+            got = rows_of(pieces, 32, r, h)
             turned.append([pltpu.roll(got, 32 * m, 1) if m else got for m in range(4)])
         for q in range(4):
             if q * 32 + r < 125:
@@ -692,52 +701,45 @@
                     level.diag[where, :] = value
                     scale = 1.0 / (1.0 + STEP_SIZE * JACOBI_SCALE * value)
                     level.jac[where, :] = scale * (1.0 / centre)
-        level.edge[...] = jnp.zeros_like(level.edge)
 
     def apply(p, source, finish, carry):
         level = levels[p]
         n = level.count
         kx, ky, kz = level.tables
-        for r in range(n * n):
-            v = source[tile(r * n + n - 1), :]
-            moved = jnp.where(place == 0, pltpu.roll(v, 5, 0), pltpu.roll(v, 1, 0))
-            level.edge[tile(r * n), :] = level.gains[2] * moved
-            v = source[tile(r * n), :]
-            moved = jnp.where(place == 3, pltpu.roll(v, 3, 0), pltpu.roll(v, 7, 0))
-            level.edge[tile(r * n + n - 1), :] = level.gains[3] * moved
-
-        def at(r, j):
-            return pl.ds(pl.multiple_of(j * 8, 8) + r * n * 8, 8)
-
-        def plane(j, carry):
-            sides = []
-            for m in range(1, n):
-                coef = choose(j, [float(ky[a, (a + m) % n]) for a in range(n)])
-                sides.append((coef, jnp.where(j + m >= n, j + m - n, j + m)))
-            v = [[source[at(k * n + i, j), :] for i in range(n)] for k in range(n)]
-
-            def around(u):
-                turned = pltpu.roll(u, 4, 0)
-                return turned, jnp.where(odd, pltpu.roll(turned, 32, 1), pltpu.roll(turned, 96, 1))
-
+
+        def around(u):
+            turned = pltpu.roll(u, 4, 0)
+            return turned, jnp.where(odd, pltpu.roll(turned, 32, 1), pltpu.roll(turned, 96, 1))
+
+        for j in range(n):
+            v = [[source[tile((k * n + i) * n + j), :] for i in range(n)] for k in range(n)]
             for k in range(n):
                 left, left_far = around(v[k][n - 1])
                 right, right_far = around(v[k][0])
                 for i in range(n):
-                    r = k * n + i
-                    total = level.diag[at(r, j), :] * v[k][i] - level.edge[at(r, j), :]
+                    base = (k * n + i) * n
+                    total = level.diag[tile(base + j), :] * v[k][i]
                     for m in range(n):
                         if m != i:
                             total = total + float(kx[i, m]) * v[k][m]
                     for m in range(n):
                         if m != k:
                             total = total + float(kz[k, m]) * v[m][i]
-                    for coef, far in sides:
-                        total = total + coef * source[at(r, far), :]
+                    for m in range(n):
+                        if m != j:
+                            total = total + float(ky[j, m]) * source[tile(base + m), :]
                     if i == 0:
                         total = total - level.gains[0] * jnp.where(low_half, left_far, left)
                     if i == n - 1:
                         total = total - level.gains[1] * jnp.where(low_half, right, right_far)
+                    if j == 0:
+                        u = source[tile(base + n - 1), :]
+                        moved = jnp.where(place == 0, pltpu.roll(u, 5, 0), pltpu.roll(u, 1, 0))
+                        total = total - level.gains[2] * moved
+                    if j == n - 1:
+                        u = source[tile(base), :]
+                        moved = jnp.where(place == 3, pltpu.roll(u, 3, 0), pltpu.roll(u, 7, 0))
+                        total = total - level.gains[3] * moved
                     if k == 0:
                         u = v[n - 1][i]
                         moved = jnp.where(element == 0, pltpu.roll(u, 97, 1), pltpu.roll(u, 1, 1))
@@ -747,13 +749,13 @@
                         moved = jnp.where(element == EZ - 1, pltpu.roll(u, 31, 1), pltpu.roll(u, 127, 1))
                         total = total - level.gains[5] * moved
                     out = v[k][i] + (same * total + swap * pltpu.roll(total, 64, 1))
-                    carry = finish(at(r, j), v[k][i], out, carry)
-            return carry
-        return lax.fori_loop(0, n, plane, carry)
+                    carry = finish(tile(base + j), v[k][i], out, carry)
+        return carry
 
     def smooth_first(p):
         level = levels[p]
-        level.dir[...] = level.jac[...] * level.f[...]
+        rows = 8 * level.count**3
+        level.dir[...] = level.jac[...] * level.f[:rows, :]
         def finish(where, v, av, carry):
             level.x[where, :] = keep * v + push * level.jac[where, :] * (level.f[where, :] - av)
             return carry
@@ -829,49 +831,29 @@
         fields[where, :] = av
         return carry
     apply(0, fine.x, last, 0)
-    fields[FIELD : 2 * FIELD, :] = fine.f[...]
     column = (my_gx % 2) * 4 + my_gy
-    fields[2 * FIELD : 2 * FIELD + 125, :] = fine.x[pl.ds(column, 125, stride=8), :]
-    fields[2 * FIELD + 125 : 2 * FIELD + 128, :] = jnp.zeros((3, 128), F32)
-
-
-def finish_kernel(own, other, guess, sol, res_out, arnoldi, cols, outs):
+    fields[FIELD : FIELD + 125, :] = fine.x[pl.ds(column, 125, stride=8), :]
+    fields[FIELD + 125 : FIELD + 128, :] = jnp.zeros((3, 128), F32)
+
+
+def split_dot(a, b):
+    high = a.astype(jnp.bfloat16)
+    rest = a - high.astype(F32)
+    middle = rest.astype(jnp.bfloat16)
+    low = (rest - middle.astype(F32)).astype(jnp.bfloat16)
+    b = b.astype(jnp.bfloat16)
+    return sum(
+        lax.dot_general(part, b, (((1,), (0,)), ((), ())), preferred_element_type=F32)
+        for part in (low, middle, high)
+    )
+
+
+def finish_kernel(own, other, own_start, other_start, guess, sol, res_out, arnoldi, cols, outs):
     sec = lax.axis_index("section")
     my_gx, my_gy = lax.axis_index("gx"), lax.axis_index("gy")
     whole, back, back_matrix, blocks, cross = split_sections()
     weights = jnp.where(iota((8, 128), 1) < 64, float(cross[0]), float(cross[1]))
     nothing = jnp.zeros((8, 128), F32)
-
-    def product(a, b, c, d):
-        return a * c + b * d + weights * (a * d + b * c)
-
-    def sums(step, carry):
-        uppers, sizes = carry
-        for m in range(5):
-            r = pl.multiple_of(step * 40, 8) + m * 8
-            a, b = own[pl.ds(r, 8), :], other[pl.ds(r, 8), :]
-            c, d = own[pl.ds(FIELD + r, 8), :], other[pl.ds(FIELD + r, 8), :]
-            uppers = uppers + product(a, b, c, d)
-            sizes = sizes + product(c, d, c, d)
-        return uppers, sizes
-    uppers, sizes = lax.fori_loop(0, 25, sums, (nothing, nothing))
-    size = jnp.sum(sizes, keepdims=True)
-    upper = jnp.sum(uppers, keepdims=True) / size
-
-    def remainder(step, carry):
-        for m in range(5):
-            r = pl.multiple_of(step * 40, 8) + m * 8
-            a = own[pl.ds(r, 8), :] - upper * own[pl.ds(FIELD + r, 8), :]
-            b = other[pl.ds(r, 8), :] - upper * other[pl.ds(FIELD + r, 8), :]
-            carry = carry + product(a, b, a, b)
-        return carry
-    rest = jnp.sum(lax.fori_loop(0, 25, remainder, nothing), keepdims=True)
-    beta = jnp.sqrt(size)
-    lower = jnp.sqrt(rest) / beta
-    weight = upper / (upper * upper + lower * lower)
-    entries = float(125 * EZ * COLS * 4)
-    for place_out, value in enumerate((beta * (1.0 / math.sqrt(entries)), upper, lower)):
-        arnoldi[place_out] = value[0, 0]
 
     lane = iota((32, 128), 1)
     here = lane // EZ % 2 == my_gx // 2
@@ -884,28 +866,47 @@
                 t = whole[2 * mine + s]
                 pairs = [jnp.where(lane < 64, float(t[2 * q]), float(t[2 * q + 1])) for q in range(2)]
                 parts.append(pairs[mine] if p == 0 else pairs[1 - mine])
-            row.append(jnp.where(here, jnp.where(sec == 0, parts[0], parts[1]), 0.0))
+            row.append(jnp.where(here, jnp.where(sec == 0, parts[0], parts[1]), 0.0)[:25])
         factors.append(row)
     column = (my_gx % 2) * 4 + my_gy
     cols[...] = jnp.zeros_like(cols)
-    total = jnp.zeros((128, 160), F32)
+    total = jnp.zeros((192, 160), F32)
     for k in range(5):
-        for p, source in enumerate((own, other)):
-            image = source[pl.ds(k * 200 + column, 25, stride=8), :]
-            start = source[pl.ds(FIELD + k * 200 + column, 25, stride=8), :]
+        where = pl.ds(k * 200 + column, 25, stride=8)
+        shown = [[ref[FIELD + k * 25 : FIELD + k * 25 + 25, :] for ref in (own, other)]]
+        shown.append([ref[where, :] for ref in (own_start, other_start)])
+        shown.append([ref[where, :] for ref in (own, other)])
+        for f, (a, b) in enumerate(shown):
             for s in range(2):
-                factor = factors[s][p][:25]
-                z = weight * (factor * source[2 * FIELD + k * 25 : 2 * FIELD + k * 25 + 25, :])
-                r = factor * (start - weight * image)
-                if p == 0:
-                    cols[s * 32 : s * 32 + 25, :] = z
-                    cols[64 + s * 32 : 64 + s * 32 + 25, :] = r
-                else:
-                    cols[s * 32 : s * 32 + 25, :] += z
-                    cols[64 + s * 32 : 64 + s * 32 + 25, :] += r
+                r = f * 64 + s * 32
+                cols[r : r + 25, :] = factors[s][0] * a + factors[s][1] * b
         hit = (iota((128, 160), 1) == 5 * (iota((128, 160), 0) % EZ) + k).astype(F32)
-        total = total + exact_dot(cols[...], hit)
-    outs[...] = total
+        total = total + split_dot(cols[...], hit)
+
+    def product(a, b, c, d):
+        return (a * c + b * d) + weights * (a * d + b * c)
+
+    uppers, sizes = [nothing] * 5, [nothing] * 5
+    for r in range(125):
+        a, b, c, d = (ref[tile(r), :] for ref in (own, other, own_start, other_start))
+        uppers[r % 5] = uppers[r % 5] + product(a, b, c, d)
+        sizes[r % 5] = sizes[r % 5] + product(c, d, c, d)
+    size = jnp.sum(sum(sizes), keepdims=True)
+    upper = jnp.sum(sum(uppers), keepdims=True) / size
+    rests = [nothing] * 5
+    for r in range(125):
+        a, b, c, d = (ref[tile(r), :] for ref in (own, other, own_start, other_start))
+        a, b = a - upper * c, b - upper * d
+        rests[r % 5] = rests[r % 5] + product(a, b, a, b)
+    rest = jnp.sum(sum(rests), keepdims=True)
+    beta = jnp.sqrt(size)
+    lower = jnp.sqrt(rest) / beta
+    weight = upper / (upper * upper + lower * lower)
+    entries = float(125 * EZ * COLS * 4)
+    for place_out, value in enumerate((beta * (1.0 / math.sqrt(entries)), upper, lower)):
+        arnoldi[place_out] = value[0, 0]
+    outs[:64, :] = weight * total[:64]
+    outs[64:, :] = total[64:128] - weight * total[128:]
     for i in range(5):
         for j in range(5):
             r = 5 * i + j
@@ -914,27 +915,39 @@
                 res_out[i, j, s : s + 1, :] = outs[64 + s * 32 + r : 64 + s * 32 + r + 1, :]
 
 
-def cycle(blocks):
+def assemble(blocks):
+    return pl.pallas_call(
+        assemble_kernel,
+        out_shape=jax.ShapeDtypeStruct((128 * 8, 128), F32),
+        in_specs=[VMEM] * 4,
+        out_specs=VMEM,
+        scratch_shapes=[pltpu.VMEM((COLS * HALF, 128), F32)],
+        compiler_params=limit(16),
+        name="assemble",
+    )(*blocks)
+
+
+def cycle(blocks, assembled):
     scratch = []
     for n in (5, 3, 2):
-        scratch += [pltpu.VMEM((n**3 * 8, 128), F32)] * 7
+        scratch += [pltpu.VMEM((n**3 * 8, 128), F32)] * 6
     scratch += [
-        pltpu.VMEM((COLS * PIECE, 128), F32),
+        pltpu.VMEM((COLS * 32, 128), F32),
         pltpu.VMEM((FIELD, 128), F32),
         pltpu.VMEM((FIELD, 128), F32),
     ]
     return pl.pallas_call(
         cycle_kernel,
-        out_shape=jax.ShapeDtypeStruct((2 * FIELD + 128, 128), F32),
-        in_specs=[VMEM] * 4,
+        out_shape=jax.ShapeDtypeStruct((FIELD + 128, 128), F32),
+        in_specs=[VMEM] * 5,
         out_specs=VMEM,
         scratch_shapes=scratch,
         compiler_params=limit(24),
         name="cycle",
-    )(*blocks)
-
-
-def finish(own, other, guess):
+    )(*blocks, assembled)
+
+
+def finish(own, other, own_start, other_start, guess):
     return pl.pallas_call(
         finish_kernel,
         out_shape=[
@@ -942,33 +955,31 @@
             jax.ShapeDtypeStruct(guess.shape, F32),
             jax.ShapeDtypeStruct((3,), F32),
         ],
-        in_specs=[VMEM] * 3,
+        in_specs=[VMEM] * 5,
         out_specs=[VMEM, VMEM, pl.BlockSpec(memory_space=pltpu.SMEM)],
-        scratch_shapes=[pltpu.VMEM((128, 128), F32), pltpu.VMEM((128, 160), F32)],
+        scratch_shapes=[pltpu.VMEM((192, 128), F32), pltpu.VMEM((128, 160), F32)],
         compiler_params=limit(24),
         name="finish",
-    )(own, other, guess)
-
-
-def turn(x, axis, offset):
-    return lax.ppermute(x, axis, [(n, (n + offset) % 4) for n in range(4)])
-
-
-def swap_cores(x):
-    return lax.ppermute(x, "section", [(0, 1), (1, 0)])
+    )(own, other, own_start, other_start, guess)
+
+
+def exchange(x, axis, bits):
+    return lax.ppermute(x, axis, [(n, n ^ bits) for n in range(lax.axis_size(axis))])
 
 
 def gathered_body(rhs, guess, kappa, bc_flags):
     rhs, guess = (jnp.transpose(v, (1, 2, 0, 3)) for v in (rhs, guess))
-    halos = [turn(guess, axis, offset) for axis in ("gx", "gy") for offset in (1, 3)]
+    halos = [exchange(guess, axis, bits) for axis in ("gx", "gy") for bits in (1, 3)]
     base = local_part(rhs, guess, kappa, bc_flags)
-    mine, theirs = halo_part(*base, halos)
-    got = swap_cores(theirs)
+    mine, theirs = halo_part(base, halos)
+    got = exchange(theirs, "section", 1)
     piece = jnp.concatenate([mine[:HALF] + got, mine[HALF:]])
-    line = jnp.concatenate([piece] + [turn(piece, "gx", offset) for offset in (1, 2, 3)])
-    blocks = [line] + [turn(line, "gy", offset) for offset in (1, 2, 3)]
-    own = cycle(blocks)
-    sol, res, arnoldi = finish(own, swap_cores(own), guess)
+    line = jnp.concatenate([piece] + [exchange(piece, "gx", bits) for bits in (1, 2, 3)])
+    blocks = [line] + [exchange(line, "gy", bits) for bits in (1, 2, 3)]
+    start = assemble(blocks)
+    other_start = exchange(start, "section", 1)
+    own = cycle(blocks, start)
+    sol, res, arnoldi = finish(own, exchange(own, "section", 1), start, other_start, guess)
     sol, res = (jnp.transpose(v, (2, 0, 1, 3)) for v in (sol, res))
     return sol, res, arnoldi
 

time: 52.9 us -> 71.8 us (1.36)
  Pallas kernels: 13.7 us -> 36.2 us
  local copies, waits for them, and re-layouts: 4.79 us -> 0.94 us
    pallas_call x2 -> x3, Pallas kernels: 10.7 us -> 33.9 us  [the longest x1 30.2 us: cycle(): pl.pallas_call(cycle_kernel, out_shape=jax.ShapeDtypeStruct((FIELD + 128,...]
    unnamed x16 -> x6, local copies, waits for them, and re-layouts: 4.79 us -> 0.93 us
    ppermute x12 -> x13, waiting for transfers between devices: 17.4 us -> 17.9 us  [exchange(): lax.ppermute(x, axis, [(n, n ^ bits) for n in range(lax.axis_size(axis))])]
    ppermute x12 -> x13, starting transfers between devices: 15.7 us -> 15.9 us  [exchange(): lax.ppermute(x, axis, [(n, n ^ bits) for n in range(lax.axis_size(axis))])]
  transfers between devices with their start and end apart: 12 -> 13, of which waited for: 6 -> 7; matrix products, arithmetic and copies ran while one was open for 0% -> 0% of each run, Pallas kernels for 4% -> 5%
where the time goes in v1:
time: 71.8 us; the launch traced here: 71.6 us
  Pallas kernels  36.2 us (50%)
  waiting for transfers between devices  17.9 us (25%)
  starting transfers between devices  15.9 us (22%)
  local copies, waits for them, and re-layouts  0.94 us (1%)
  between operations  0.73 us (1%)
    pallas_call x1, Pallas kernels, cycle(): pl.pallas_call(cycle_kernel, out_shape=jax.ShapeDtypeStruct((FIELD + 128,...  30.2 us
    ppermute x13, waiting for transfers between devices, exchange(): lax.ppermute(x, axis, [(n, n ^ bits) for n in range(lax.axis_size(axis))])  17.9 us
    ppermute x13, starting transfers between devices, exchange(): lax.ppermute(x, axis, [(n, n ^ bits) for n in range(lax.axis_size(axis))])  15.9 us
    pallas_call x1, Pallas kernels, local_part(): pl.pallas_call(local_kernel, out_shape=jax.ShapeDtypeStruct((288, 128), F...  3.3 us
    pallas_call x1, Pallas kernels, finish(): pl.pallas_call(finish_kernel, out_shape=[jax.ShapeDtypeStruct(guess.shape...  1.78 us
  transfers between devices with their start and end apart: 13, of which 7 were waited for; matrix products, arithmetic and copies ran while one was open for 0% of the time, Pallas kernels for 5%

profile of v1, /device:TPU:0, one launch (start us, length us, event | category | flops | bytes accessed | tf_op | source)
XLA Modules:
  0.0 71.6 jit_solution(11058458162532600685)
XLA Ops:
  0.6 4.0 %collective-permute-start.3 = (f32[5,5,2,160]{3,2,1,0:T(2,128)}, f32[5,5,2,160]{3,2,1,0:T(2,128)S(1)}, u32[]{:S(2)}, u32[]{:S(2)}) collective-permute-start(f32[5,5,2,160]{3,2,1,0:T(2,128)} %bitcast.4), channel_id=1, source_target_pairs={{0,3},{1,2},{2,1},{3,0},{4,7},{5,6},{6,5},{7,4},{8,11},{9,10},{10,... | collective-permute-start | bytes 96008 | tf_op jit(solution)/shard_map/ppermute | solution.py:967
  4.6 0.5 collective-permute-start.2
  5.1 3.6 %collective-permute-start.1 = (f32[5,5,2,160]{3,2,1,0:T(2,128)}, f32[5,5,2,160]{3,2,1,0:T(2,128)S(1)}, u32[]{:S(2)}, u32[]{:S(2)}) collective-permute-start(f32[5,5,2,160]{3,2,1,0:T(2,128)} %bitcast.6), channel_id=1, source_target_pairs={{0,12},{4,8},{8,4},{12,0},{1,13},{5,9},{9,5},{13,1},{2,14},{6,10},... | collective-permute-start | bytes 96008 | tf_op jit(solution)/shard_map/ppermute | solution.py:967
  8.7 0.0 collective-permute-start
  8.7 3.3 %local_part.1.base = f32[288,128]{1,0:T(8,128)} custom-call(f32[5,5,2,160]{3,2,1,0:T(2,128)} %bitcast.10, f32[5,5,2,160]{3,2,1,0:T(2,128)} %bitcast.8, f32[5,5,160]{2,1,0:T(8,128)} %kappa_in.1, s32[6,1,1,32]{3,2,1,0:T(1,128)} %flags_in.1, f32[64,64]{1,0:T(8,128)} %constant.4.clone.rows_in, f32[160,320]{1,0:T(8,128)} %constant.5.clone.lines_in), custom_call_target="tpu_custom_call" | custom-call | tf_op jit(solution)/shard_map/local_part/pallas_call | solution.py:565
  12.0 0.0 collective-permute-done.3.y3
  12.1 0.0 collective-permute-done.2.y1
  12.1 0.0 collective-permute-done.1.x3
  12.1 1.0 %collective-permute-done.x1 = f32[5,5,2,160]{3,2,1,0:T(2,128)S(1)} collective-permute-done((f32[5,5,2,160]{3,2,1,0:T(2,128)}, f32[5,5,2,160]{3,2,1,0:T(2,128)S(1)}, u32[]{:S(2)}, u32[]{:S(2)}) %collective-permute-start) | collective-permute-done | bytes 32032 | tf_op jit(solution)/shard_map/ppermute | solution.py:967
  13.1 0.9 %copy-done = f32[288,128]{1,0:T(8,128)S(1)} copy-done((f32[288,128]{1,0:T(8,128)S(1)}, f32[288,128]{1,0:T(8,128)}, u32[]{:S(2)}) %copy-start) | copy-done | bytes 147480
  14.0 0.5 halo_part.1
  14.5 0.1 collective-permute-start.4
  14.6 1.2 %collective-permute-done.4 = f32[64,128]{1,0:T(8,128)S(1)} collective-permute-done((f32[64,128]{1,0:T(8,128)S(1)}, f32[64,128]{1,0:T(8,128)S(1)}, u32[]{:S(2)}, u32[]{:S(2)}) %collective-permute-start.4) | collective-permute-done | bytes 32800 | tf_op jit(solution)/shard_map/ppermute | solution.py:967
  15.8 1.1 %collective-permute-start.5 = (f32[96,128]{1,0:T(8,128)S(1)}, f32[96,128]{1,0:T(8,128)S(1)}, u32[]{:S(2)}, u32[]{:S(2)}) collective-permute-start(f32[96,128]{1,0:T(8,128)S(1)} %pad_maximum_fusion), channel_id=1, source_target_pairs={{0,4},{4,0},{8,12},{12,8},{1,5},{5,1},{9,13},{13,9},{2,6},{6,2},{1... | collective-permute-start | bytes 147464 | tf_op jit(solution)/shard_map/ppermute | solution.py:967
  16.9 0.8 %collective-permute-start.7 = (f32[96,128]{1,0:T(8,128)S(1)}, f32[96,128]{1,0:T(8,128)S(1)}, u32[]{:S(2)}, u32[]{:S(2)}) collective-permute-start(f32[96,128]{1,0:T(8,128)S(1)} %pad_maximum_fusion), channel_id=1, source_target_pairs={{0,12},{4,8},{8,4},{12,0},{1,13},{5,9},{9,5},{13,1},{2,14},{6,10},... | collective-permute-start | bytes 147464 | tf_op jit(solution)/shard_map/ppermute | solution.py:967
  17.8 1.6 %collective-permute-start.6 = (f32[96,128]{1,0:T(8,128)S(1)}, f32[96,128]{1,0:T(8,128)S(1)}, u32[]{:S(2)}, u32[]{:S(2)}) collective-permute-start(f32[96,128]{1,0:T(8,128)S(1)} %pad_maximum_fusion), channel_id=1, source_target_pairs={{0,8},{4,12},{8,0},{12,4},{1,9},{5,13},{9,1},{13,5},{2,10},{6,14},... | collective-permute-start | bytes 147464 | tf_op jit(solution)/shard_map/ppermute | solution.py:967
  19.4 0.6 collective-permute-done.5
  20.0 4.6 %collective-permute-done.6 = f32[96,128]{1,0:T(8,128)S(1)} collective-permute-done((f32[96,128]{1,0:T(8,128)S(1)}, f32[96,128]{1,0:T(8,128)S(1)}, u32[]{:S(2)}, u32[]{:S(2)}) %collective-permute-start.6) | collective-permute-done | bytes 49184 | tf_op jit(solution)/shard_map/ppermute | solution.py:967
  24.6 0.0 collective-permute-done.7
  24.6 1.5 %collective-permute-start.10 = (f32[384,128]{1,0:T(8,128)S(1)}, f32[384,128]{1,0:T(8,128)S(1)}, u32[]{:S(2)}, u32[]{:S(2)}) collective-permute-start(f32[384,128]{1,0:T(8,128)S(1)} %constant_dynamic-update-slice_fusion.block0), channel_id=1, source_target_pairs={{0,3},{1,2},{2,1},{3,0},{4,7},{5,6},{6,5},{7,4},{8,11},{9,10},{10,... | collective-permute-start | bytes 589832 | tf_op jit(solution)/shard_map/ppermute | solution.py:967
  26.1 1.5 %collective-permute-start.9 = (f32[384,128]{1,0:T(8,128)S(1)}, f32[384,128]{1,0:T(8,128)S(1)}, u32[]{:S(2)}, u32[]{:S(2)}) collective-permute-start(f32[384,128]{1,0:T(8,128)S(1)} %constant_dynamic-update-slice_fusion.block0), channel_id=1, source_target_pairs={{0,2},{1,3},{2,0},{3,1},{4,6},{5,7},{6,4},{7,5},{8,10},{9,11},{10,... | collective-permute-start | bytes 589832 | tf_op jit(solution)/shard_map/ppermute | solution.py:967
  27.6 0.5 collective-permute-start.8
  28.2 5.2 %collective-permute-done.10.block3 = f32[384,128]{1,0:T(8,128)S(1)} collective-permute-done((f32[384,128]{1,0:T(8,128)S(1)}, f32[384,128]{1,0:T(8,128)S(1)}, u32[]{:S(2)}, u32[]{:S(2)}) %collective-permute-start.10) | collective-permute-done | bytes 196640 | tf_op jit(solution)/shard_map/ppermute | solution.py:967
  33.4 3.0 %collective-permute-done.9.block2 = f32[384,128]{1,0:T(8,128)S(1)} collective-permute-done((f32[384,128]{1,0:T(8,128)S(1)}, f32[384,128]{1,0:T(8,128)S(1)}, u32[]{:S(2)}, u32[]{:S(2)}) %collective-permute-start.9) | collective-permute-done | bytes 196640 | tf_op jit(solution)/shard_map/ppermute | solution.py:967
  36.4 0.4 assemble.1.assembled.own_start
  36.8 0.0 copy-start.1
  36.8 30.2 %cycle.1.own = f32[1128,128]{1,0:T(8,128)S(1)} custom-call(f32[384,128]{1,0:T(8,128)S(1)} %constant_dynamic-update-slice_fusion.block0, f32[384,128]{1,0:T(8,128)S(1)} %collective-permute-done.8.block1, f32[384,128]{1,0:T(8,128)S(1)} %collective-permute-done.9.block2, f32[384,128]{1,0:T(8,128)S(1)} %collective-permute-done.10.block3, ...), custom_call_target="tpu_custom_call" | custom-call | tf_op jit(solution)/shard_map/cycle/pallas_call | solution.py:939
  67.0 0.1 collective-permute-start.11
  67.1 0.5 collective-permute-start.12
  67.6 2.2 %collective-permute-done.12.other_start = f32[1024,128]{1,0:T(8,128)S(1)} collective-permute-done((f32[1024,128]{1,0:T(8,128)S(1)}, f32[1024,128]{1,0:T(8,128)S(1)}, u32[]{:S(2)}, u32[]{:S(2)}) %collective-permute-start.12) | collective-permute-done | bytes 524320 | tf_op jit(solution)/shard_map/ppermute | solution.py:967
  69.8 0.0 collective-permute-done.11.other
  69.8 1.8 %finish.1 = (f32[5,5,2,160]{3,2,1,0:T(2,128)}, f32[5,5,2,160]{3,2,1,0:T(2,128)}, f32[3]{0:T(128)}) custom-call(f32[1128,128]{1,0:T(8,128)S(1)} %cycle.1.own, f32[1128,128]{1,0:T(8,128)S(1)} %collective-permute-done.11.other, f32[1024,128]{1,0:T(8,128)S(1)} %assemble.1.assembled.own_start, f32[1024,128]{1,0:T(8,128)S(1)} %collective-permute-done.12.other_start, ...), custom_call_target="tpu_custom_call" | custom-call | tf_op jit(solution)/shard_map/finish/pallas_call | solution.py:951
  (9 shorter events, 0.0 us)
Async XLA Ops:
  0.6 11.4 %collective-permute-start.3 = (f32[5,5,2,160]{3,2,1,0:T(2,128)}, f32[5,5,2,160]{3,2,1,0:T(2,128)S(1)}, u32[]{:S(2)}, u32[]{:S(2)}) collective-permute-start(f32[5,5,2,160]{3,2,1,0:T(2,128)} %bitcast.4), channel_id=1, source_target_pairs={{0,3},{1,2},{2,1},{3,0},{4,7},{5,6},{6,5},{7,4},{8,11},{9,10},{10,... | collective-permute-start | bytes 96008 | tf_op jit(solution)/shard_map/ppermute | solution.py:967
  4.6 7.5 %collective-permute-start.2 = (f32[5,5,2,160]{3,2,1,0:T(2,128)}, f32[5,5,2,160]{3,2,1,0:T(2,128)S(1)}, u32[]{:S(2)}, u32[]{:S(2)}) collective-permute-start(f32[5,5,2,160]{3,2,1,0:T(2,128)} %bitcast.5), channel_id=1, source_target_pairs={{0,1},{1,0},{2,3},{3,2},{4,5},{5,4},{6,7},{7,6},{8,9},{9,8},{10,11... | collective-permute-start | bytes 96008 | tf_op jit(solution)/shard_map/ppermute | solution.py:967
  5.1 6.9 %collective-permute-start.1 = (f32[5,5,2,160]{3,2,1,0:T(2,128)}, f32[5,5,2,160]{3,2,1,0:T(2,128)S(1)}, u32[]{:S(2)}, u32[]{:S(2)}) collective-permute-start(f32[5,5,2,160]{3,2,1,0:T(2,128)} %bitcast.6), channel_id=1, source_target_pairs={{0,12},{4,8},{8,4},{12,0},{1,13},{5,9},{9,5},{13,1},{2,14},{6,10},... | collective-permute-start | bytes 96008 | tf_op jit(solution)/shard_map/ppermute | solution.py:967
  8.7 4.3 %collective-permute-start = (f32[5,5,2,160]{3,2,1,0:T(2,128)}, f32[5,5,2,160]{3,2,1,0:T(2,128)S(1)}, u32[]{:S(2)}, u32[]{:S(2)}) collective-permute-start(f32[5,5,2,160]{3,2,1,0:T(2,128)} %bitcast.7), channel_id=1, source_target_pairs={{0,4},{4,0},{8,12},{12,8},{1,5},{5,1},{9,13},{13,9},{2,6},{6,2},{1... | collective-permute-start | bytes 96008 | tf_op jit(solution)/shard_map/ppermute | solution.py:967
  13.1 0.9 %copy-start = (f32[288,128]{1,0:T(8,128)S(1)}, f32[288,128]{1,0:T(8,128)}, u32[]{:S(2)}) copy-start(f32[288,128]{1,0:T(8,128)} %local_part.1.base) | copy-start | bytes 442372
  14.5 1.3 %collective-permute-start.4 = (f32[64,128]{1,0:T(8,128)S(1)}, f32[64,128]{1,0:T(8,128)S(1)}, u32[]{:S(2)}, u32[]{:S(2)}) collective-permute-start(f32[64,128]{1,0:T(8,128)S(1)} %get-tuple-element.9), channel_id=1, source_target_pairs={{0,16},{16,0},{1,17},{17,1},{2,18},{18,2},{3,19},{19,3},{4,20},{20... | collective-permute-start | bytes 98312 | tf_op jit(solution)/shard_map/ppermute | solution.py:967
  15.8 4.2 %collective-permute-start.5 = (f32[96,128]{1,0:T(8,128)S(1)}, f32[96,128]{1,0:T(8,128)S(1)}, u32[]{:S(2)}, u32[]{:S(2)}) collective-permute-start(f32[96,128]{1,0:T(8,128)S(1)} %pad_maximum_fusion), channel_id=1, source_target_pairs={{0,4},{4,0},{8,12},{12,8},{1,5},{5,1},{9,13},{13,9},{2,6},{6,2},{1... | collective-permute-start | bytes 147464 | tf_op jit(solution)/shard_map/ppermute | solution.py:967
  16.9 7.7 %collective-permute-start.7 = (f32[96,128]{1,0:T(8,128)S(1)}, f32[96,128]{1,0:T(8,128)S(1)}, u32[]{:S(2)}, u32[]{:S(2)}) collective-permute-start(f32[96,128]{1,0:T(8,128)S(1)} %pad_maximum_fusion), channel_id=1, source_target_pairs={{0,12},{4,8},{8,4},{12,0},{1,13},{5,9},{9,5},{13,1},{2,14},{6,10},... | collective-permute-start | bytes 147464 | tf_op jit(solution)/shard_map/ppermute | solution.py:967
  17.8 6.8 %collective-permute-start.6 = (f32[96,128]{1,0:T(8,128)S(1)}, f32[96,128]{1,0:T(8,128)S(1)}, u32[]{:S(2)}, u32[]{:S(2)}) collective-permute-start(f32[96,128]{1,0:T(8,128)S(1)} %pad_maximum_fusion), channel_id=1, source_target_pairs={{0,8},{4,12},{8,0},{12,4},{1,9},{5,13},{9,1},{13,5},{2,10},{6,14},... | collective-permute-start | bytes 147464 | tf_op jit(solution)/shard_map/ppermute | solution.py:967
  24.6 8.8 %collective-permute-start.10 = (f32[384,128]{1,0:T(8,128)S(1)}, f32[384,128]{1,0:T(8,128)S(1)}, u32[]{:S(2)}, u32[]{:S(2)}) collective-permute-start(f32[384,128]{1,0:T(8,128)S(1)} %constant_dynamic-update-slice_fusion.block0), channel_id=1, source_target_pairs={{0,3},{1,2},{2,1},{3,0},{4,7},{5,6},{6,5},{7,4},{8,11},{9,10},{10,... | collective-permute-start | bytes 589832 | tf_op jit(solution)/shard_map/ppermute | solution.py:967
  26.1 10.3 %collective-permute-start.9 = (f32[384,128]{1,0:T(8,128)S(1)}, f32[384,128]{1,0:T(8,128)S(1)}, u32[]{:S(2)}, u32[]{:S(2)}) collective-permute-start(f32[384,128]{1,0:T(8,128)S(1)} %constant_dynamic-update-slice_fusion.block0), channel_id=1, source_target_pairs={{0,2},{1,3},{2,0},{3,1},{4,6},{5,7},{6,4},{7,5},{8,10},{9,11},{10,... | collective-permute-start | bytes 589832 | tf_op jit(solution)/shard_map/ppermute | solution.py:967
  27.6 8.8 %collective-permute-start.8 = (f32[384,128]{1,0:T(8,128)S(1)}, f32[384,128]{1,0:T(8,128)S(1)}, u32[]{:S(2)}, u32[]{:S(2)}) collective-permute-start(f32[384,128]{1,0:T(8,128)S(1)} %constant_dynamic-update-slice_fusion.block0), channel_id=1, source_target_pairs={{0,1},{1,0},{2,3},{3,2},{4,5},{5,4},{6,7},{7,6},{8,9},{9,8},{10,11... | collective-permute-start | bytes 589832 | tf_op jit(solution)/shard_map/ppermute | solution.py:967
  36.8 33.0 %copy-start.1 = (f32[2,5,5,160]{3,0,2,1:T(2,128)S(1)}, f32[2,5,5,160]{3,0,2,1:T(2,128)}, u32[]{:S(2)}) copy-start(f32[2,5,5,160]{3,0,2,1:T(2,128)} %param.7) | copy-start | bytes 96004
  67.0 2.8 %collective-permute-start.11 = (f32[1128,128]{1,0:T(8,128)S(1)}, f32[1128,128]{1,0:T(8,128)S(1)}, u32[]{:S(2)}, u32[]{:S(2)}) collective-permute-start(f32[1128,128]{1,0:T(8,128)S(1)} %cycle.1.own), channel_id=1, source_target_pairs={{0,16},{16,0},{1,17},{17,1},{2,18},{18,2},{3,19},{19,3},{4,20},{20... | collective-permute-start | bytes 1732616 | tf_op jit(solution)/shard_map/ppermute | solution.py:967
  67.1 2.7 %collective-permute-start.12 = (f32[1024,128]{1,0:T(8,128)S(1)}, f32[1024,128]{1,0:T(8,128)S(1)}, u32[]{:S(2)}, u32[]{:S(2)}) collective-permute-start(f32[1024,128]{1,0:T(8,128)S(1)} %assemble.1.assembled.own_start), channel_id=1, source_target_pairs={{0,16},{16,0},{1,17},{17,1},{2,18},{18,2},{3,19},{19,3},{4,20},{20... | collective-permute-start | bytes 1572872 | tf_op jit(solution)/shard_map/ppermute | solution.py:967

commit v2 on v1

--- a/solution.py
+++ b/solution.py
@@ -600,7 +600,8 @@
 class Level:
     def __init__(self, count, refs):
         self.count = count
-        self.diag, self.jac, self.x, self.dir, self.res, self.f = refs
+        self.size = 8 * count**3
+        self.diag, self.jac, self.held, self.edge = refs
         self.tables = [element_matrix(count, d) for d in range(3)]
         self.gains = None
 
@@ -631,13 +632,15 @@
         field[tile(HALF + r), :] = jnp.where(odd, high, pltpu.roll(low, 96, 1))
 
 
+def at(offset, static):
+    return pl.ds(pl.multiple_of(offset, 8) + static, 8)
+
+
 def cycle_kernel(block0, block1, block2, block3, assembled, fields, *scratch):
     sec = lax.axis_index("section")
     my_gx, my_gy = lax.axis_index("gx"), lax.axis_index("gy")
-    levels = [Level(n, scratch[6 * p : 6 * p + 6]) for p, n in enumerate((5, 3, 2))]
-    pieces, kap, half = scratch[18:21]
-    fine, middle, coarse = levels
-    fine.f = assembled
+    levels = [Level(n, scratch[4 * p : 4 * p + 4]) for p, n in enumerate((5, 3, 2))]
+    pieces, kap, half, terms = scratch[12:16]
     lane = iota((8, 128), 1)
     sub = iota((8, 128), 0)
     group = lane // EZ
@@ -666,80 +669,106 @@
         across = pltpu.roll(got, 64, 1)
         flags += [jnp.where(lane < 64, got, across), jnp.where(lane < 64, across, got)]
     place_pieces((block0, block1, block2, block3), pieces, HALF, 32)
-    for r in range(32):
+
+    def place_kappa(r, carry):
         turned = []
         for h in range(2):
             got = rows_of(pieces, 32, r, h)
             turned.append([pltpu.roll(got, 32 * m, 1) if m else got for m in range(4)])
         for q in range(4):
-            if q * 32 + r < 125:
-                kap[tile(q * 32 + r), :] = choose(group, [turned[g % 2][(g - q) % 4] for g in range(4)])
+            kap[at(r * 8, q * 256), :] = choose(group, [turned[g % 2][(g - q) % 4] for g in range(4)])
+        return carry
+    lax.fori_loop(0, 32, place_kappa, 0, unroll=2)
 
     for level in levels:
         n = level.count
-        picks = {5: (0, 1, 2, 3, 4), 3: (0, 2, 4), 2: (0, 4)}[n]
+        stride = 4 // (n - 1)
         level.gains = [face_gains(flags[d], d // 2, d % 2, n) for d in range(6)]
-        terms = []
         for d in range(3):
-            row = []
             for m in range(n):
-                value = float(level.tables[d][m, m])
+                value = jnp.full((8, 128), float(level.tables[d][m, m]), F32)
                 if m == 0:
-                    row.append(level.gains[2 * d] + value)
-                elif m == n - 1:
-                    row.append(level.gains[2 * d + 1] + value)
-                else:
-                    row.append(value)
-            terms.append(row)
-        for k in range(n):
-            for i in range(n):
-                both = terms[2][k] + terms[0][i]
-                for j in range(n):
-                    source = (picks[k] * 5 + picks[i]) * 5 + picks[j]
-                    value = kap[tile(source), :] + (both + terms[1][j])
-                    where = tile((k * n + i) * n + j)
-                    level.diag[where, :] = value
-                    scale = 1.0 / (1.0 + STEP_SIZE * JACOBI_SCALE * value)
-                    level.jac[where, :] = scale * (1.0 / centre)
-
-    def apply(p, source, finish, carry):
-        level = levels[p]
+                    value = value + level.gains[2 * d]
+                if m == n - 1:
+                    value = value + level.gains[2 * d + 1]
+                terms[tile(5 * d + m), :] = value
+
+        def diagonals(r, carry, level=level, n=n, stride=stride):
+            k = r // n
+            i = r - k * n
+            both = terms[at(i * 8, 0), :] + terms[at(k * 8, 80), :]
+            for j in range(n):
+                source = at((k * 25 + i * 5) * 8 * stride, j * stride * 8)
+                value = kap[source, :] + (both + terms[tile(5 + j), :])
+                level.diag[at(r * n * 8, j * 8), :] = value
+                scale = 1.0 / (1.0 + STEP_SIZE * JACOBI_SCALE * value)
+                level.jac[at(r * n * 8, j * 8), :] = scale * (1.0 / centre)
+            return carry
+        lax.fori_loop(0, n * n, diagonals, 0)
+        level.edge[...] = jnp.zeros_like(level.edge)
+
+    def begin(level, source):
         n = level.count
+
+        def start(r, carry):
+            for j in range(n):
+                where = at(r * n * 8, j * 8)
+                f = source[where, :]
+                level.held[where, :] = f
+                level.held[at(r * n * 8, level.size + j * 8), :] = f
+                level.held[at(r * n * 8, 2 * level.size + j * 8), :] = jnp.zeros_like(f)
+                level.held[at(r * n * 8, 3 * level.size + j * 8), :] = level.jac[where, :] * f
+            return carry
+        lax.fori_loop(0, n * n, start, 0)
+
+    def apply(level, smooth):
+        n, size, held = level.count, level.size, level.held
         kx, ky, kz = level.tables
+        source = jnp.where(smooth, 3 * size, 2 * size)
+        right_side = jnp.where(smooth, size, 0)
+        first_out = jnp.where(smooth, 2 * size, size)
+        second_out = jnp.where(smooth, 4 * size, 3 * size)
+
+        def faces(r, carry):
+            v = held[at(source + r * n * 8, (n - 1) * 8), :]
+            moved = jnp.where(place == 0, pltpu.roll(v, 5, 0), pltpu.roll(v, 1, 0))
+            level.edge[at(r * n * 8, 0), :] = level.gains[2] * moved
+            v = held[at(source + r * n * 8, 0), :]
+            moved = jnp.where(place == 3, pltpu.roll(v, 3, 0), pltpu.roll(v, 7, 0))
+            level.edge[at(r * n * 8, (n - 1) * 8), :] = level.gains[3] * moved
+            return carry
+        lax.fori_loop(0, n * n, faces, 0, unroll=n)
 
         def around(u):
             turned = pltpu.roll(u, 4, 0)
             return turned, jnp.where(odd, pltpu.roll(turned, 32, 1), pltpu.roll(turned, 96, 1))
 
-        for j in range(n):
-            v = [[source[tile((k * n + i) * n + j), :] for i in range(n)] for k in range(n)]
+        def plane(j, carry):
+            sides = []
+            for m in range(1, n):
+                coef = choose(j, [float(ky[a, (a + m) % n]) for a in range(n)])
+                far = jnp.where(j + m >= n, j + m - n, j + m)
+                sides.append((coef, source + far * 8))
+            here = source + j * 8
+            v = [[held[at(here, (k * n + i) * n * 8), :] for i in range(n)] for k in range(n)]
             for k in range(n):
                 left, left_far = around(v[k][n - 1])
                 right, right_far = around(v[k][0])
                 for i in range(n):
-                    base = (k * n + i) * n
-                    total = level.diag[tile(base + j), :] * v[k][i]
+                    base = (k * n + i) * n * 8
+                    total = level.diag[at(j * 8, base), :] * v[k][i] - level.edge[at(j * 8, base), :]
                     for m in range(n):
                         if m != i:
                             total = total + float(kx[i, m]) * v[k][m]
                     for m in range(n):
                         if m != k:
                             total = total + float(kz[k, m]) * v[m][i]
-                    for m in range(n):
-                        if m != j:
-                            total = total + float(ky[j, m]) * source[tile(base + m), :]
+                    for coef, far in sides:
+                        total = total + coef * held[at(far, base), :]
                     if i == 0:
                         total = total - level.gains[0] * jnp.where(low_half, left_far, left)
                     if i == n - 1:
                         total = total - level.gains[1] * jnp.where(low_half, right, right_far)
-                    if j == 0:
-                        u = source[tile(base + n - 1), :]
-                        moved = jnp.where(place == 0, pltpu.roll(u, 5, 0), pltpu.roll(u, 1, 0))
-                        total = total - level.gains[2] * moved
-                    if j == n - 1:
-                        u = source[tile(base), :]
-                        moved = jnp.where(place == 3, pltpu.roll(u, 3, 0), pltpu.roll(u, 7, 0))
-                        total = total - level.gains[3] * moved
                     if k == 0:
                         u = v[n - 1][i]
                         moved = jnp.where(element == 0, pltpu.roll(u, 97, 1), pltpu.roll(u, 1, 1))
@@ -748,39 +777,15 @@
                         u = v[0][i]
                         moved = jnp.where(element == EZ - 1, pltpu.roll(u, 31, 1), pltpu.roll(u, 127, 1))
                         total = total - level.gains[5] * moved
-                    out = v[k][i] + (same * total + swap * pltpu.roll(total, 64, 1))
-                    carry = finish(tile(base + j), v[k][i], out, carry)
-        return carry
-
-    def smooth_first(p):
-        level = levels[p]
-        rows = 8 * level.count**3
-        level.dir[...] = level.jac[...] * level.f[:rows, :]
-        def finish(where, v, av, carry):
-            level.x[where, :] = keep * v + push * level.jac[where, :] * (level.f[where, :] - av)
+                    image = v[k][i] + (same * total + swap * pltpu.roll(total, 64, 1))
+                    left_over = held[at(right_side + j * 8, base), :] - image
+                    scaled = level.jac[at(j * 8, base), :] * left_over
+                    x = held[at(j * 8, 2 * size + base), :]
+                    first = jnp.where(smooth, x + keep * v[k][i] + push * scaled, left_over)
+                    held[at(first_out + j * 8, base), :] = first
+                    held[at(second_out + j * 8, base), :] = scaled
             return carry
-        apply(p, level.dir, finish, 0)
-
-    def defect(p):
-        level = levels[p]
-        def finish(where, v, av, carry):
-            level.res[where, :] = level.f[where, :] - av
-            return carry
-        apply(p, level.x, finish, 0)
-
-    def smooth_again(p):
-        level = levels[p]
-        def middle_step(where, v, av, carry):
-            left = level.f[where, :] - av
-            level.res[where, :] = left
-            level.dir[where, :] = level.jac[where, :] * left
-            return carry
-        apply(p, level.x, middle_step, 0)
-        def finish(where, v, av, carry):
-            step = push * level.jac[where, :] * (level.res[where, :] - av)
-            level.x[where, :] = level.x[where, :] + keep * v + step
-            return carry
-        apply(p, level.dir, finish, 0)
+        lax.fori_loop(0, n, plane, 0)
 
     def combine(weights, parts):
         total = None
@@ -790,21 +795,29 @@
                 total = term if total is None else total + term
         return total
 
-    def change(table, source, target, add):
+    def change(table, source, source_base, target, target_base, add):
         m, n = table.shape
-        for i in range(n):
-            parts = [source[pl.ds((k * n + i) * n * 8, 8 * n), :] for k in range(n)]
+
+        def outer(i, carry):
+            parts = [
+                source[pl.ds(pl.multiple_of(i * n * 8, 8) + source_base + k * n * n * 8, 8 * n), :] for k in range(n)
+            ]
             for k in range(m):
-                half[pl.ds((k * n + i) * n * 8, 8 * n), :] = combine(table[k], parts)
-        for k in range(m):
-            parts = [half[pl.ds((k * n + i) * n * 8, 8 * n), :] for i in range(n)]
+                half[pl.ds(pl.multiple_of(i * n * 8, 8) + k * n * n * 8, 8 * n), :] = combine(table[k], parts)
+            return carry
+        lax.fori_loop(0, n, outer, 0)
+
+        def inner(k, carry):
+            parts = [half[pl.ds(pl.multiple_of(k * n * n * 8, 8) + i * n * 8, 8 * n), :] for i in range(n)]
             for i in range(m):
                 line = combine(table[i], parts)
                 points = [line[8 * j : 8 * j + 8] for j in range(n)]
                 for j in range(m):
                     value = combine(table[j], points)
-                    where = tile((k * m + i) * m + j)
+                    where = at(k * m * m * 8, target_base + (i * m + j) * 8)
                     target[where, :] = target[where, :] + value if add else value
+            return carry
+        lax.fori_loop(0, m, inner, 0)
 
     def down(n, m):
         fine_nodes, fine_weights = lobatto(n)
@@ -815,24 +828,37 @@
     def up(m, n):
         return lagrange_table(lobatto(m)[0], lobatto(n)[0])
 
-    smooth_first(0)
-    defect(0)
-    change(down(5, 3), fine.res, middle.f, False)
-    smooth_first(1)
-    defect(1)
-    change(down(3, 2), middle.res, coarse.f, False)
-    smooth_first(2)
-    change(up(2, 3), coarse.x, middle.x, True)
-    smooth_again(1)
-    change(up(3, 5), middle.x, fine.x, True)
-    smooth_again(0)
-
-    def last(where, v, av, carry):
-        fields[where, :] = av
+    def solve(p):
+        level = levels[p]
+        if p == 2:
+            apply(level, True)
+            return
+        below = levels[p + 1]
+
+        def step(t, carry):
+            apply(level, (t == 0) | (t == 3))
+
+            @pl.when(t == 1)
+            def _():
+                n, m = level.count, below.count
+                change(down(n, m), level.held, level.size, below.held, 0, False)
+                begin(below, below.held)
+                solve(p + 1)
+                change(up(m, n), below.held, 2 * below.size, level.held, 2 * level.size, True)
+            return carry
+        lax.fori_loop(0, 5 if p == 0 else 4, step, 0)
+
+    begin(levels[0], assembled)
+    solve(0)
+    fine = levels[0]
+
+    def give(r, carry):
+        for m in range(5):
+            fields[at(r * 40, m * 8), :] = fine.held[at(r * 40, fine.size + m * 8), :]
         return carry
-    apply(0, fine.x, last, 0)
+    lax.fori_loop(0, 25, give, 0)
     column = (my_gx % 2) * 4 + my_gy
-    fields[FIELD : FIELD + 125, :] = fine.x[pl.ds(column, 125, stride=8), :]
+    fields[FIELD : FIELD + 125, :] = fine.held[pl.ds(2 * fine.size + column, 125, stride=8), :]
     fields[FIELD + 125 : FIELD + 128, :] = jnp.zeros((3, 128), F32)
 
 
@@ -875,7 +901,7 @@
         where = pl.ds(k * 200 + column, 25, stride=8)
         shown = [[ref[FIELD + k * 25 : FIELD + k * 25 + 25, :] for ref in (own, other)]]
         shown.append([ref[where, :] for ref in (own_start, other_start)])
-        shown.append([ref[where, :] for ref in (own, other)])
+        shown.append([b[where, :] - a[where, :] for a, b in ((own, own_start), (other, other_start))])
         for f, (a, b) in enumerate(shown):
             for s in range(2):
                 r = f * 64 + s * 32
@@ -889,6 +915,7 @@
     uppers, sizes = [nothing] * 5, [nothing] * 5
     for r in range(125):
         a, b, c, d = (ref[tile(r), :] for ref in (own, other, own_start, other_start))
+        a, b = c - a, d - b
         uppers[r % 5] = uppers[r % 5] + product(a, b, c, d)
         sizes[r % 5] = sizes[r % 5] + product(c, d, c, d)
     size = jnp.sum(sum(sizes), keepdims=True)
@@ -896,6 +923,7 @@
     rests = [nothing] * 5
     for r in range(125):
         a, b, c, d = (ref[tile(r), :] for ref in (own, other, own_start, other_start))
+        a, b = c - a, d - b
         a, b = a - upper * c, b - upper * d
         rests[r % 5] = rests[r % 5] + product(a, b, a, b)
     rest = jnp.sum(sum(rests), keepdims=True)
@@ -930,11 +958,12 @@
 def cycle(blocks, assembled):
     scratch = []
     for n in (5, 3, 2):
-        scratch += [pltpu.VMEM((n**3 * 8, 128), F32)] * 6
+        scratch += [pltpu.VMEM((n**3 * 8 * copies, 128), F32) for copies in (1, 1, 5, 1)]
     scratch += [
         pltpu.VMEM((COLS * 32, 128), F32),
+        pltpu.VMEM((128 * 8, 128), F32),
         pltpu.VMEM((FIELD, 128), F32),
-        pltpu.VMEM((FIELD, 128), F32),
+        pltpu.VMEM((15 * 8, 128), F32),
     ]
     return pl.pallas_call(
         cycle_kernel,
@@ -943,6 +972,7 @@
         out_specs=VMEM,
         scratch_shapes=scratch,
         compiler_params=limit(24),
+        cost_estimate=pl.CostEstimate(flops=40_000_000, bytes_accessed=30_000_000, transcendentals=0),
         name="cycle",
     )(*blocks, assembled)
 
@@ -978,7 +1008,7 @@
     blocks = [line] + [exchange(line, "gy", bits) for bits in (1, 2, 3)]
     start = assemble(blocks)
     other_start = exchange(start, "section", 1)
-    own = cycle(blocks, start)
+    own, other_start = lax.optimization_barrier((cycle(blocks, start), other_start))
     sol, res, arnoldi = finish(own, exchange(own, "section", 1), start, other_start, guess)
     sol, res = (jnp.transpose(v, (2, 0, 1, 3)) for v in (sol, res))
     return sol, res, arnoldi

time: 71.8 us -> 110 us (1.53)
  Pallas kernels: 36.2 us -> 74.5 us
    pallas_call x1, Pallas kernels: 30.2 us -> 68.4 us  [cycle(): pl.pallas_call(cycle_kernel, out_shape=jax.ShapeDtypeStruct((FIELD + 128,...]
  transfers between devices with their start and end apart: 13 -> 13, of which waited for: 7 -> 7; matrix products, arithmetic and copies ran while one was open for 0% -> 0% of each run, Pallas kernels for 5% -> 66%
where the time goes in v2:
time: 110 us; the launch traced here: 109 us
  Pallas kernels  74.5 us (68%)
  waiting for transfers between devices  17.3 us (16%)
  starting transfers between devices  15.9 us (14%)
    pallas_call x1, Pallas kernels, cycle(): pl.pallas_call(cycle_kernel, out_shape=jax.ShapeDtypeStruct((FIELD + 128,...  68.4 us
    ppermute x13, waiting for transfers between devices, exchange(): lax.ppermute(x, axis, [(n, n ^ bits) for n in range(lax.axis_size(axis))])  17.3 us
    ppermute x13, starting transfers between devices, exchange(): lax.ppermute(x, axis, [(n, n ^ bits) for n in range(lax.axis_size(axis))])  15.9 us
    pallas_call x1, Pallas kernels, local_part(): pl.pallas_call(local_kernel, out_shape=jax.ShapeDtypeStruct((288, 128), F...  3.3 us
  transfers between devices with their start and end apart: 13, of which 7 were waited for; matrix products, arithmetic and copies ran while one was open for 0% of the time, Pallas kernels for 66%

profile of v2, /device:TPU:0, one launch (start us, length us, event | category | flops | bytes accessed | tf_op | source)
XLA Modules:
  0.0 109.3 jit_solution(8222703020443232532)
XLA Ops:
  0.6 4.0 %collective-permute-start.3 = (f32[5,5,2,160]{3,2,1,0:T(2,128)}, f32[5,5,2,160]{3,2,1,0:T(2,128)S(1)}, u32[]{:S(2)}, u32[]{:S(2)}) collective-permute-start(f32[5,5,2,160]{3,2,1,0:T(2,128)} %bitcast.4), channel_id=1, source_target_pairs={{0,3},{1,2},{2,1},{3,0},{4,7},{5,6},{6,5},{7,4},{8,11},{9,10},{10,... | collective-permute-start | bytes 96008 | tf_op jit(solution)/shard_map/ppermute | solution.py:997
  4.6 0.5 collective-permute-start.2
  5.1 3.6 %collective-permute-start.1 = (f32[5,5,2,160]{3,2,1,0:T(2,128)}, f32[5,5,2,160]{3,2,1,0:T(2,128)S(1)}, u32[]{:S(2)}, u32[]{:S(2)}) collective-permute-start(f32[5,5,2,160]{3,2,1,0:T(2,128)} %bitcast.6), channel_id=1, source_target_pairs={{0,12},{4,8},{8,4},{12,0},{1,13},{5,9},{9,5},{13,1},{2,14},{6,10},... | collective-permute-start | bytes 96008 | tf_op jit(solution)/shard_map/ppermute | solution.py:997
  8.7 0.0 collective-permute-start
  8.7 3.3 %local_part.1.base = f32[288,128]{1,0:T(8,128)} custom-call(f32[5,5,2,160]{3,2,1,0:T(2,128)} %bitcast.10, f32[5,5,2,160]{3,2,1,0:T(2,128)} %bitcast.8, f32[5,5,160]{2,1,0:T(8,128)} %kappa_in.1, s32[6,1,1,32]{3,2,1,0:T(1,128)} %flags_in.1, f32[64,64]{1,0:T(8,128)} %constant.4.clone.rows_in, f32[160,320]{1,0:T(8,128)} %constant.5.clone.lines_in), custom_call_target="tpu_custom_call" | custom-call | tf_op jit(solution)/shard_map/local_part/pallas_call | solution.py:565
  12.0 0.0 collective-permute-done.3.y3
  12.1 0.0 collective-permute-done.2.y1
  12.1 0.0 collective-permute-done.1.x3
  12.1 1.0 collective-permute-done.x1
  13.1 0.9 copy-done
  14.0 0.5 halo_part.1
  14.5 0.1 collective-permute-start.4
  14.6 1.2 %collective-permute-done.4 = f32[64,128]{1,0:T(8,128)S(1)} collective-permute-done((f32[64,128]{1,0:T(8,128)S(1)}, f32[64,128]{1,0:T(8,128)S(1)}, u32[]{:S(2)}, u32[]{:S(2)}) %collective-permute-start.4) | collective-permute-done | bytes 32800 | tf_op jit(solution)/shard_map/ppermute | solution.py:997
  15.8 1.1 %collective-permute-start.5 = (f32[96,128]{1,0:T(8,128)S(1)}, f32[96,128]{1,0:T(8,128)S(1)}, u32[]{:S(2)}, u32[]{:S(2)}) collective-permute-start(f32[96,128]{1,0:T(8,128)S(1)} %pad_maximum_fusion), channel_id=1, source_target_pairs={{0,4},{4,0},{8,12},{12,8},{1,5},{5,1},{9,13},{13,9},{2,6},{6,2},{1... | collective-permute-start | bytes 147464 | tf_op jit(solution)/shard_map/ppermute | solution.py:997
  16.9 0.8 collective-permute-start.7
  17.8 1.6 %collective-permute-start.6 = (f32[96,128]{1,0:T(8,128)S(1)}, f32[96,128]{1,0:T(8,128)S(1)}, u32[]{:S(2)}, u32[]{:S(2)}) collective-permute-start(f32[96,128]{1,0:T(8,128)S(1)} %pad_maximum_fusion), channel_id=1, source_target_pairs={{0,8},{4,12},{8,0},{12,4},{1,9},{5,13},{9,1},{13,5},{2,10},{6,14},... | collective-permute-start | bytes 147464 | tf_op jit(solution)/shard_map/ppermute | solution.py:997
  19.4 0.6 collective-permute-done.5
  20.0 4.6 %collective-permute-done.6 = f32[96,128]{1,0:T(8,128)S(1)} collective-permute-done((f32[96,128]{1,0:T(8,128)S(1)}, f32[96,128]{1,0:T(8,128)S(1)}, u32[]{:S(2)}, u32[]{:S(2)}) %collective-permute-start.6) | collective-permute-done | bytes 49184 | tf_op jit(solution)/shard_map/ppermute | solution.py:997
  24.6 0.0 collective-permute-done.7
  24.6 1.5 %collective-permute-start.10 = (f32[384,128]{1,0:T(8,128)S(1)}, f32[384,128]{1,0:T(8,128)S(1)}, u32[]{:S(2)}, u32[]{:S(2)}) collective-permute-start(f32[384,128]{1,0:T(8,128)S(1)} %constant_dynamic-update-slice_fusion.block0), channel_id=1, source_target_pairs={{0,3},{1,2},{2,1},{3,0},{4,7},{5,6},{6,5},{7,4},{8,11},{9,10},{10,... | collective-permute-start | bytes 589832 | tf_op jit(solution)/shard_map/ppermute | solution.py:997
  26.1 1.5 %collective-permute-start.9 = (f32[384,128]{1,0:T(8,128)S(1)}, f32[384,128]{1,0:T(8,128)S(1)}, u32[]{:S(2)}, u32[]{:S(2)}) collective-permute-start(f32[384,128]{1,0:T(8,128)S(1)} %constant_dynamic-update-slice_fusion.block0), channel_id=1, source_target_pairs={{0,2},{1,3},{2,0},{3,1},{4,6},{5,7},{6,4},{7,5},{8,10},{9,11},{10,... | collective-permute-start | bytes 589832 | tf_op jit(solution)/shard_map/ppermute | solution.py:997
  27.6 0.5 collective-permute-start.8
  28.2 5.2 %collective-permute-done.10.block3 = f32[384,128]{1,0:T(8,128)S(1)} collective-permute-done((f32[384,128]{1,0:T(8,128)S(1)}, f32[384,128]{1,0:T(8,128)S(1)}, u32[]{:S(2)}, u32[]{:S(2)}) %collective-permute-start.10) | collective-permute-done | bytes 196640 | tf_op jit(solution)/shard_map/ppermute | solution.py:997
  33.4 3.0 %collective-permute-done.9.block2 = f32[384,128]{1,0:T(8,128)S(1)} collective-permute-done((f32[384,128]{1,0:T(8,128)S(1)}, f32[384,128]{1,0:T(8,128)S(1)}, u32[]{:S(2)}, u32[]{:S(2)}) %collective-permute-start.9) | collective-permute-done | bytes 196640 | tf_op jit(solution)/shard_map/ppermute | solution.py:997
  36.4 0.0 collective-permute-done.8.block1
  36.4 0.4 assemble.1.assembled.own_start
  36.8 0.0 copy-start.1
  36.8 0.1 collective-permute-start.11
  36.9 68.4 %cycle.1.own = f32[1128,128]{1,0:T(8,128)S(1)} custom-call(f32[384,128]{1,0:T(8,128)S(1)} %constant_dynamic-update-slice_fusion.block0, f32[384,128]{1,0:T(8,128)S(1)} %collective-permute-done.8.block1, f32[384,128]{1,0:T(8,128)S(1)} %collective-permute-done.9.block2, f32[384,128]{1,0:T(8,128)S(1)} %collective-permute-done.10.block3, ...), custom_call_target="tpu_custom_call" | custom-call | flops 40000000 | bytes 30000000 | tf_op jit(solution)/shard_map/cycle/pallas_call | solution.py:968
  105.4 0.6 collective-permute-start.12
  105.9 1.6 %collective-permute-done.12.other = f32[1128,128]{1,0:T(8,128)S(1)} collective-permute-done((f32[1128,128]{1,0:T(8,128)S(1)}, f32[1128,128]{1,0:T(8,128)S(1)}, u32[]{:S(2)}, u32[]{:S(2)}) %collective-permute-start.12) | collective-permute-done | bytes 577568 | tf_op jit(solution)/shard_map/ppermute | solution.py:997
  107.5 1.8 %finish.1 = (f32[5,5,2,160]{3,2,1,0:T(2,128)}, f32[5,5,2,160]{3,2,1,0:T(2,128)}, f32[3]{0:T(128)}) custom-call(f32[1128,128]{1,0:T(8,128)S(1)} %cycle.1.own, f32[1128,128]{1,0:T(8,128)S(1)} %collective-permute-done.12.other, f32[1024,128]{1,0:T(8,128)S(1)} %assemble.1.assembled.own_start, f32[1024,128]{1,0:T(8,128)S(1)} %collective-permute-done.11.other_start, ...), custom_call_target="tpu_custom_call" | custom-call | tf_op jit(solution)/shard_map/finish/pallas_call | solution.py:981
  (9 shorter events, 0.0 us)
Async XLA Ops:
  0.6 11.4 %collective-permute-start.3 = (f32[5,5,2,160]{3,2,1,0:T(2,128)}, f32[5,5,2,160]{3,2,1,0:T(2,128)S(1)}, u32[]{:S(2)}, u32[]{:S(2)}) collective-permute-start(f32[5,5,2,160]{3,2,1,0:T(2,128)} %bitcast.4), channel_id=1, source_target_pairs={{0,3},{1,2},{2,1},{3,0},{4,7},{5,6},{6,5},{7,4},{8,11},{9,10},{10,... | collective-permute-start | bytes 96008 | tf_op jit(solution)/shard_map/ppermute | solution.py:997
  4.6 7.5 %collective-permute-start.2 = (f32[5,5,2,160]{3,2,1,0:T(2,128)}, f32[5,5,2,160]{3,2,1,0:T(2,128)S(1)}, u32[]{:S(2)}, u32[]{:S(2)}) collective-permute-start(f32[5,5,2,160]{3,2,1,0:T(2,128)} %bitcast.5), channel_id=1, source_target_pairs={{0,1},{1,0},{2,3},{3,2},{4,5},{5,4},{6,7},{7,6},{8,9},{9,8},{10,11... | collective-permute-start | bytes 96008 | tf_op jit(solution)/shard_map/ppermute | solution.py:997
  5.1 6.9 %collective-permute-start.1 = (f32[5,5,2,160]{3,2,1,0:T(2,128)}, f32[5,5,2,160]{3,2,1,0:T(2,128)S(1)}, u32[]{:S(2)}, u32[]{:S(2)}) collective-permute-start(f32[5,5,2,160]{3,2,1,0:T(2,128)} %bitcast.6), channel_id=1, source_target_pairs={{0,12},{4,8},{8,4},{12,0},{1,13},{5,9},{9,5},{13,1},{2,14},{6,10},... | collective-permute-start | bytes 96008 | tf_op jit(solution)/shard_map/ppermute | solution.py:997
  8.7 4.3 %collective-permute-start = (f32[5,5,2,160]{3,2,1,0:T(2,128)}, f32[5,5,2,160]{3,2,1,0:T(2,128)S(1)}, u32[]{:S(2)}, u32[]{:S(2)}) collective-permute-start(f32[5,5,2,160]{3,2,1,0:T(2,128)} %bitcast.7), channel_id=1, source_target_pairs={{0,4},{4,0},{8,12},{12,8},{1,5},{5,1},{9,13},{13,9},{2,6},{6,2},{1... | collective-permute-start | bytes 96008 | tf_op jit(solution)/shard_map/ppermute | solution.py:997
  13.1 0.9 copy-start
  14.5 1.3 %collective-permute-start.4 = (f32[64,128]{1,0:T(8,128)S(1)}, f32[64,128]{1,0:T(8,128)S(1)}, u32[]{:S(2)}, u32[]{:S(2)}) collective-permute-start(f32[64,128]{1,0:T(8,128)S(1)} %get-tuple-element.11), channel_id=1, source_target_pairs={{0,16},{16,0},{1,17},{17,1},{2,18},{18,2},{3,19},{19,3},{4,20},{20... | collective-permute-start | bytes 98312 | tf_op jit(solution)/shard_map/ppermute | solution.py:997
  15.8 4.2 %collective-permute-start.5 = (f32[96,128]{1,0:T(8,128)S(1)}, f32[96,128]{1,0:T(8,128)S(1)}, u32[]{:S(2)}, u32[]{:S(2)}) collective-permute-start(f32[96,128]{1,0:T(8,128)S(1)} %pad_maximum_fusion), channel_id=1, source_target_pairs={{0,4},{4,0},{8,12},{12,8},{1,5},{5,1},{9,13},{13,9},{2,6},{6,2},{1... | collective-permute-start | bytes 147464 | tf_op jit(solution)/shard_map/ppermute | solution.py:997
  16.9 7.7 %collective-permute-start.7 = (f32[96,128]{1,0:T(8,128)S(1)}, f32[96,128]{1,0:T(8,128)S(1)}, u32[]{:S(2)}, u32[]{:S(2)}) collective-permute-start(f32[96,128]{1,0:T(8,128)S(1)} %pad_maximum_fusion), channel_id=1, source_target_pairs={{0,12},{4,8},{8,4},{12,0},{1,13},{5,9},{9,5},{13,1},{2,14},{6,10},... | collective-permute-start | bytes 147464 | tf_op jit(solution)/shard_map/ppermute | solution.py:997
  17.8 6.8 %collective-permute-start.6 = (f32[96,128]{1,0:T(8,128)S(1)}, f32[96,128]{1,0:T(8,128)S(1)}, u32[]{:S(2)}, u32[]{:S(2)}) collective-permute-start(f32[96,128]{1,0:T(8,128)S(1)} %pad_maximum_fusion), channel_id=1, source_target_pairs={{0,8},{4,12},{8,0},{12,4},{1,9},{5,13},{9,1},{13,5},{2,10},{6,14},... | collective-permute-start | bytes 147464 | tf_op jit(solution)/shard_map/ppermute | solution.py:997
  24.6 8.8 %collective-permute-start.10 = (f32[384,128]{1,0:T(8,128)S(1)}, f32[384,128]{1,0:T(8,128)S(1)}, u32[]{:S(2)}, u32[]{:S(2)}) collective-permute-start(f32[384,128]{1,0:T(8,128)S(1)} %constant_dynamic-update-slice_fusion.block0), channel_id=1, source_target_pairs={{0,3},{1,2},{2,1},{3,0},{4,7},{5,6},{6,5},{7,4},{8,11},{9,10},{10,... | collective-permute-start | bytes 589832 | tf_op jit(solution)/shard_map/ppermute | solution.py:997
  26.1 10.3 %collective-permute-start.9 = (f32[384,128]{1,0:T(8,128)S(1)}, f32[384,128]{1,0:T(8,128)S(1)}, u32[]{:S(2)}, u32[]{:S(2)}) collective-permute-start(f32[384,128]{1,0:T(8,128)S(1)} %constant_dynamic-update-slice_fusion.block0), channel_id=1, source_target_pairs={{0,2},{1,3},{2,0},{3,1},{4,6},{5,7},{6,4},{7,5},{8,10},{9,11},{10,... | collective-permute-start | bytes 589832 | tf_op jit(solution)/shard_map/ppermute | solution.py:997
  27.6 8.8 %collective-permute-start.8 = (f32[384,128]{1,0:T(8,128)S(1)}, f32[384,128]{1,0:T(8,128)S(1)}, u32[]{:S(2)}, u32[]{:S(2)}) collective-permute-start(f32[384,128]{1,0:T(8,128)S(1)} %constant_dynamic-update-slice_fusion.block0), channel_id=1, source_target_pairs={{0,1},{1,0},{2,3},{3,2},{4,5},{5,4},{6,7},{7,6},{8,9},{9,8},{10,11... | collective-permute-start | bytes 589832 | tf_op jit(solution)/shard_map/ppermute | solution.py:997
  36.8 70.7 %copy-start.1 = (f32[2,5,5,160]{3,0,2,1:T(2,128)S(1)}, f32[2,5,5,160]{3,0,2,1:T(2,128)}, u32[]{:S(2)}) copy-start(f32[2,5,5,160]{3,0,2,1:T(2,128)} %param.7) | copy-start | bytes 96004
  36.8 68.5 %collective-permute-start.11 = (f32[1024,128]{1,0:T(8,128)S(1)}, f32[1024,128]{1,0:T(8,128)S(1)}, u32[]{:S(2)}, u32[]{:S(2)}) collective-permute-start(f32[1024,128]{1,0:T(8,128)S(1)} %assemble.1.assembled.own_start), channel_id=1, source_target_pairs={{0,16},{16,0},{1,17},{17,1},{2,18},{18,2},{3,19},{19,3},{4,20},{20... | collective-permute-start | bytes 1572872 | tf_op jit(solution)/shard_map/ppermute | solution.py:997
  105.4 2.2 %collective-permute-start.12 = (f32[1128,128]{1,0:T(8,128)S(1)}, f32[1128,128]{1,0:T(8,128)S(1)}, u32[]{:S(2)}, u32[]{:S(2)}) collective-permute-start(f32[1128,128]{1,0:T(8,128)S(1)} %cycle.1.own), channel_id=1, source_target_pairs={{0,16},{16,0},{1,17},{17,1},{2,18},{18,2},{3,19},{19,3},{4,20},{20... | collective-permute-start | bytes 1732616 | tf_op jit(solution)/shard_map/ppermute | solution.py:997

commit v3 on v2

--- a/solution.py
+++ b/solution.py
@@ -600,8 +600,7 @@
 class Level:
     def __init__(self, count, refs):
         self.count = count
-        self.size = 8 * count**3
-        self.diag, self.jac, self.held, self.edge = refs
+        self.diag, self.jac, self.x, self.dir, self.res, self.edge, self.f = refs
         self.tables = [element_matrix(count, d) for d in range(3)]
         self.gains = None
 
@@ -632,15 +631,21 @@
         field[tile(HALF + r), :] = jnp.where(odd, high, pltpu.roll(low, 96, 1))
 
 
-def at(offset, static):
-    return pl.ds(pl.multiple_of(offset, 8) + static, 8)
+def load(ref, first, count):
+    start = first * 8 if isinstance(first, int) else pl.multiple_of(first * 8, 8)
+    return ref[pl.ds(start, count * 8), :].reshape(count, 8, 128)
+
+
+def store(ref, first, value):
+    start = first * 8 if isinstance(first, int) else pl.multiple_of(first * 8, 8)
+    ref[pl.ds(start, value.shape[0] * 8), :] = value.reshape(value.shape[0] * 8, 128)
 
 
 def cycle_kernel(block0, block1, block2, block3, assembled, fields, *scratch):
     sec = lax.axis_index("section")
     my_gx, my_gy = lax.axis_index("gx"), lax.axis_index("gy")
-    levels = [Level(n, scratch[4 * p : 4 * p + 4]) for p, n in enumerate((5, 3, 2))]
-    pieces, kap, half, terms = scratch[12:16]
+    levels = [Level(n, scratch[7 * p : 7 * p + 7]) for p, n in enumerate((5, 3, 2))]
+    pieces, kap, half, terms = scratch[21:25]
     lane = iota((8, 128), 1)
     sub = iota((8, 128), 0)
     group = lane // EZ
@@ -670,120 +675,119 @@
         flags += [jnp.where(lane < 64, got, across), jnp.where(lane < 64, across, got)]
     place_pieces((block0, block1, block2, block3), pieces, HALF, 32)
 
-    def place_kappa(r, carry):
+    for r in range(32):
         turned = []
         for h in range(2):
             got = rows_of(pieces, 32, r, h)
             turned.append([pltpu.roll(got, 32 * m, 1) if m else got for m in range(4)])
         for q in range(4):
-            kap[at(r * 8, q * 256), :] = choose(group, [turned[g % 2][(g - q) % 4] for g in range(4)])
-        return carry
-    lax.fori_loop(0, 32, place_kappa, 0, unroll=2)
+            kap[tile(q * 32 + r), :] = choose(group, [turned[g % 2][(g - q) % 4] for g in range(4)])
 
     for level in levels:
         n = level.count
         stride = 4 // (n - 1)
         level.gains = [face_gains(flags[d], d // 2, d % 2, n) for d in range(6)]
+        rows = []
         for d in range(3):
-            for m in range(n):
-                value = jnp.full((8, 128), float(level.tables[d][m, m]), F32)
-                if m == 0:
-                    value = value + level.gains[2 * d]
-                if m == n - 1:
-                    value = value + level.gains[2 * d + 1]
-                terms[tile(5 * d + m), :] = value
-
-        def diagonals(r, carry, level=level, n=n, stride=stride):
-            k = r // n
-            i = r - k * n
-            both = terms[at(i * 8, 0), :] + terms[at(k * 8, 80), :]
-            for j in range(n):
-                source = at((k * 25 + i * 5) * 8 * stride, j * stride * 8)
-                value = kap[source, :] + (both + terms[tile(5 + j), :])
-                level.diag[at(r * n * 8, j * 8), :] = value
+            row = [jnp.full((8, 128), float(level.tables[d][m, m]), F32) for m in range(n)]
+            row[0] = row[0] + level.gains[2 * d]
+            row[n - 1] = row[n - 1] + level.gains[2 * d + 1]
+            rows.append(row)
+        for m in range(n):
+            terms[tile(m), :] = rows[2][m]
+
+        def diagonals(k, carry, level=level, n=n, stride=stride, rows=rows):
+            along = jnp.stack(rows[1])
+            for i in range(n):
+                line = load(kap, k * 25 * stride + i * stride * 5, 5)
+                line = jnp.stack([line[j * stride] for j in range(n)])
+                value = line + (along + (load(terms, k, 1) + rows[0][i]))
                 scale = 1.0 / (1.0 + STEP_SIZE * JACOBI_SCALE * value)
-                level.jac[at(r * n * 8, j * 8), :] = scale * (1.0 / centre)
+                store(level.diag, (k * n + i) * n, value)
+                store(level.jac, (k * n + i) * n, scale * (1.0 / centre))
             return carry
-        lax.fori_loop(0, n * n, diagonals, 0)
+        lax.fori_loop(0, n, diagonals, 0)
         level.edge[...] = jnp.zeros_like(level.edge)
 
     def begin(level, source):
         n = level.count
 
-        def start(r, carry):
-            for j in range(n):
-                where = at(r * n * 8, j * 8)
-                f = source[where, :]
-                level.held[where, :] = f
-                level.held[at(r * n * 8, level.size + j * 8), :] = f
-                level.held[at(r * n * 8, 2 * level.size + j * 8), :] = jnp.zeros_like(f)
-                level.held[at(r * n * 8, 3 * level.size + j * 8), :] = level.jac[where, :] * f
+        def start(k, carry):
+            first = k * n * n
+            f = load(source, first, n * n)
+            store(level.dir, first, load(level.jac, first, n * n) * f)
+            store(level.res, first, f)
+            store(level.x, first, jnp.zeros_like(f))
             return carry
-        lax.fori_loop(0, n * n, start, 0)
+        lax.fori_loop(0, n, start, 0)
 
     def apply(level, smooth):
-        n, size, held = level.count, level.size, level.held
+        n = level.count
         kx, ky, kz = level.tables
-        source = jnp.where(smooth, 3 * size, 2 * size)
-        right_side = jnp.where(smooth, size, 0)
-        first_out = jnp.where(smooth, 2 * size, size)
-        second_out = jnp.where(smooth, 4 * size, 3 * size)
-
-        def faces(r, carry):
-            v = held[at(source + r * n * 8, (n - 1) * 8), :]
-            moved = jnp.where(place == 0, pltpu.roll(v, 5, 0), pltpu.roll(v, 1, 0))
-            level.edge[at(r * n * 8, 0), :] = level.gains[2] * moved
-            v = held[at(source + r * n * 8, 0), :]
-            moved = jnp.where(place == 3, pltpu.roll(v, 3, 0), pltpu.roll(v, 7, 0))
-            level.edge[at(r * n * 8, (n - 1) * 8), :] = level.gains[3] * moved
-            return carry
-        lax.fori_loop(0, n * n, faces, 0, unroll=n)
+        source = level.dir if smooth else level.x
+        for i in range(n):
+            v = load(source, ((n - 1) * n + i) * n, n)
+            moved = jnp.where(element == 0, pltpu.roll(v, 97, 2), pltpu.roll(v, 1, 2))
+            store(level.edge, i * n, level.gains[4] * moved)
+            v = load(source, i * n, n)
+            moved = jnp.where(element == EZ - 1, pltpu.roll(v, 31, 2), pltpu.roll(v, 127, 2))
+            store(level.edge, ((n - 1) * n + i) * n, level.gains[5] * moved)
 
         def around(u):
-            turned = pltpu.roll(u, 4, 0)
-            return turned, jnp.where(odd, pltpu.roll(turned, 32, 1), pltpu.roll(turned, 96, 1))
-
-        def plane(j, carry):
+            turned = pltpu.roll(u, 4, 1)
+            return turned, jnp.where(odd, pltpu.roll(turned, 32, 2), pltpu.roll(turned, 96, 2))
+
+        def plane(k, carry):
             sides = []
             for m in range(1, n):
-                coef = choose(j, [float(ky[a, (a + m) % n]) for a in range(n)])
-                far = jnp.where(j + m >= n, j + m - n, j + m)
-                sides.append((coef, source + far * 8))
-            here = source + j * 8
-            v = [[held[at(here, (k * n + i) * n * 8), :] for i in range(n)] for k in range(n)]
-            for k in range(n):
-                left, left_far = around(v[k][n - 1])
-                right, right_far = around(v[k][0])
-                for i in range(n):
-                    base = (k * n + i) * n * 8
-                    total = level.diag[at(j * 8, base), :] * v[k][i] - level.edge[at(j * 8, base), :]
+                coef = choose(k, [float(kz[a, (a + m) % n]) for a in range(n)])
+                sides.append((coef, jnp.where(k + m >= n, k + m - n, k + m) * (n * n)))
+            here = k * (n * n)
+            v = [load(source, here + i * n, n) for i in range(n)]
+            left, left_far = around(v[n - 1])
+            right, right_far = around(v[0])
+            waiting = []
+            for i in range(n):
+                first = here + i * n
+                total = load(level.diag, first, n) * v[i] - load(level.edge, first, n)
+                for m in range(n):
+                    if m != i:
+                        total = total + float(kx[i, m]) * v[m]
+                for coef, far in sides:
+                    total = total + coef * load(source, far + i * n, n)
+                lines = []
+                for j in range(n):
+                    line = None
                     for m in range(n):
-                        if m != i:
-                            total = total + float(kx[i, m]) * v[k][m]
-                    for m in range(n):
-                        if m != k:
-                            total = total + float(kz[k, m]) * v[m][i]
-                    for coef, far in sides:
-                        total = total + coef * held[at(far, base), :]
-                    if i == 0:
-                        total = total - level.gains[0] * jnp.where(low_half, left_far, left)
-                    if i == n - 1:
-                        total = total - level.gains[1] * jnp.where(low_half, right, right_far)
-                    if k == 0:
-                        u = v[n - 1][i]
-                        moved = jnp.where(element == 0, pltpu.roll(u, 97, 1), pltpu.roll(u, 1, 1))
-                        total = total - level.gains[4] * moved
-                    if k == n - 1:
-                        u = v[0][i]
-                        moved = jnp.where(element == EZ - 1, pltpu.roll(u, 31, 1), pltpu.roll(u, 127, 1))
-                        total = total - level.gains[5] * moved
-                    image = v[k][i] + (same * total + swap * pltpu.roll(total, 64, 1))
-                    left_over = held[at(right_side + j * 8, base), :] - image
-                    scaled = level.jac[at(j * 8, base), :] * left_over
-                    x = held[at(j * 8, 2 * size + base), :]
-                    first = jnp.where(smooth, x + keep * v[k][i] + push * scaled, left_over)
-                    held[at(first_out + j * 8, base), :] = first
-                    held[at(second_out + j * 8, base), :] = scaled
+                        if m != j:
+                            term = float(ky[j, m]) * v[i][m]
+                            line = term if line is None else line + term
+                    if j == 0:
+                        u = v[i][n - 1]
+                        moved = jnp.where(place == 0, pltpu.roll(u, 5, 0), pltpu.roll(u, 1, 0))
+                        line = line - level.gains[2] * moved
+                    if j == n - 1:
+                        u = v[i][0]
+                        moved = jnp.where(place == 3, pltpu.roll(u, 3, 0), pltpu.roll(u, 7, 0))
+                        line = line - level.gains[3] * moved
+                    lines.append(line)
+                total = total + jnp.stack(lines)
+                if i == 0:
+                    total = total - level.gains[0] * jnp.where(low_half, left_far, left)
+                if i == n - 1:
+                    total = total - level.gains[1] * jnp.where(low_half, right, right_far)
+                image = v[i] + (same * total + swap * pltpu.roll(total, 64, 2))
+                if smooth:
+                    scaled = load(level.jac, first, n) * (load(level.res, first, n) - image)
+                    waiting.append((level.x, first, load(level.x, first, n) + keep * v[i] + push * scaled))
+                else:
+                    rest = load(level.f, first, n) - image
+                    waiting.append((level.res, first, rest))
+                    waiting.append((level.dir, first, load(level.jac, first, n) * rest))
+                if i % 2 == 1 or i == n - 1:
+                    for place_out in waiting:
+                        store(*place_out)
+                    waiting = []
             return carry
         lax.fori_loop(0, n, plane, 0)
 
@@ -795,27 +799,23 @@
                 total = term if total is None else total + term
         return total
 
-    def change(table, source, source_base, target, target_base, add):
+    def change(table, source, target, add):
         m, n = table.shape
 
         def outer(i, carry):
-            parts = [
-                source[pl.ds(pl.multiple_of(i * n * 8, 8) + source_base + k * n * n * 8, 8 * n), :] for k in range(n)
-            ]
+            parts = [load(source, i * n + k * n * n, n) for k in range(n)]
             for k in range(m):
-                half[pl.ds(pl.multiple_of(i * n * 8, 8) + k * n * n * 8, 8 * n), :] = combine(table[k], parts)
+                store(half, i * n + k * n * n, combine(table[k], parts))
             return carry
         lax.fori_loop(0, n, outer, 0)
 
         def inner(k, carry):
-            parts = [half[pl.ds(pl.multiple_of(k * n * n * 8, 8) + i * n * 8, 8 * n), :] for i in range(n)]
+            parts = [load(half, k * n * n + i * n, n) for i in range(n)]
             for i in range(m):
                 line = combine(table[i], parts)
-                points = [line[8 * j : 8 * j + 8] for j in range(n)]
-                for j in range(m):
-                    value = combine(table[j], points)
-                    where = at(k * m * m * 8, target_base + (i * m + j) * 8)
-                    target[where, :] = target[where, :] + value if add else value
+                value = jnp.stack([combine(table[j], [line[a] for a in range(n)]) for j in range(m)])
+                first = k * m * m + i * m
+                store(target, first, load(target, first, m) + value if add else value)
             return carry
         lax.fori_loop(0, m, inner, 0)
 
@@ -836,29 +836,35 @@
         below = levels[p + 1]
 
         def step(t, carry):
-            apply(level, (t == 0) | (t == 3))
-
-            @pl.when(t == 1)
+            @pl.when(t != 1)
+            def _():
+                apply(level, True)
+
+            @pl.when((t != 2) | (p == 0))
+            def _():
+                apply(level, False)
+
+            @pl.when(t == 0)
             def _():
                 n, m = level.count, below.count
-                change(down(n, m), level.held, level.size, below.held, 0, False)
-                begin(below, below.held)
+                change(down(n, m), level.res, below.f, False)
+                begin(below, below.f)
                 solve(p + 1)
-                change(up(m, n), below.held, 2 * below.size, level.held, 2 * level.size, True)
+                change(up(m, n), below.x, level.x, True)
             return carry
-        lax.fori_loop(0, 5 if p == 0 else 4, step, 0)
-
-    begin(levels[0], assembled)
+        lax.fori_loop(0, 3, step, 0)
+
+    fine = levels[0]
+    fine.f = assembled
+    begin(fine, assembled)
     solve(0)
-    fine = levels[0]
-
-    def give(r, carry):
-        for m in range(5):
-            fields[at(r * 40, m * 8), :] = fine.held[at(r * 40, fine.size + m * 8), :]
+
+    def give(k, carry):
+        store(fields, k * 25, load(fine.res, k * 25, 25))
         return carry
-    lax.fori_loop(0, 25, give, 0)
+    lax.fori_loop(0, 5, give, 0)
     column = (my_gx % 2) * 4 + my_gy
-    fields[FIELD : FIELD + 125, :] = fine.held[pl.ds(2 * fine.size + column, 125, stride=8), :]
+    fields[FIELD : FIELD + 125, :] = fine.x[pl.ds(column, 125, stride=8), :]
     fields[FIELD + 125 : FIELD + 128, :] = jnp.zeros((3, 128), F32)
 
 
@@ -958,7 +964,7 @@
 def cycle(blocks, assembled):
     scratch = []
     for n in (5, 3, 2):
-        scratch += [pltpu.VMEM((n**3 * 8 * copies, 128), F32) for copies in (1, 1, 5, 1)]
+        scratch += [pltpu.VMEM((n**3 * 8, 128), F32)] * 7
     scratch += [
         pltpu.VMEM((COLS * 32, 128), F32),
         pltpu.VMEM((128 * 8, 128), F32),

time: 110 us -> 50.9 us (0.46)
  Pallas kernels: 74.5 us -> 15.9 us
    pallas_call x1, Pallas kernels: 68.4 us -> 9.85 us  [cycle(): pl.pallas_call(cycle_kernel, out_shape=jax.ShapeDtypeStruct((FIELD + 128,...]
  transfers between devices with their start and end apart: 13 -> 13, of which waited for: 7 -> 7; matrix products, arithmetic and copies ran while one was open for 0% -> 0% of each run, Pallas kernels for 66% -> 26%
where the time goes in v3:
time: 50.9 us; the launch traced here: 50.8 us
  waiting for transfers between devices  17.3 us (34%)
  starting transfers between devices  15.9 us (31%)
  Pallas kernels  15.9 us (31%)
  local copies, waits for them, and re-layouts  0.94 us (2%)
  between operations  0.74 us (1%)
    ppermute x13, waiting for transfers between devices, exchange(): lax.ppermute(x, axis, [(n, n ^ bits) for n in range(lax.axis_size(axis))])  17.3 us
    ppermute x13, starting transfers between devices, exchange(): lax.ppermute(x, axis, [(n, n ^ bits) for n in range(lax.axis_size(axis))])  15.9 us
    pallas_call x1, Pallas kernels, cycle(): pl.pallas_call(cycle_kernel, out_shape=jax.ShapeDtypeStruct((FIELD + 128,...  9.85 us
    pallas_call x1, Pallas kernels, local_part(): pl.pallas_call(local_kernel, out_shape=jax.ShapeDtypeStruct((288, 128), F...  3.3 us
    pallas_call x1, Pallas kernels, finish(): pl.pallas_call(finish_kernel, out_shape=[jax.ShapeDtypeStruct(guess.shape...  1.82 us
  transfers between devices with their start and end apart: 13, of which 7 were waited for; matrix products, arithmetic and copies ran while one was open for 0% of the time, Pallas kernels for 26%

profile of v3, /device:TPU:0, one launch (start us, length us, event | category | flops | bytes accessed | tf_op | source)
XLA Modules:
  0.0 50.8 jit_solution(1160313120944416054)
XLA Ops:
  0.6 4.0 %collective-permute-start.3 = (f32[5,5,2,160]{3,2,1,0:T(2,128)}, f32[5,5,2,160]{3,2,1,0:T(2,128)S(1)}, u32[]{:S(2)}, u32[]{:S(2)}) collective-permute-start(f32[5,5,2,160]{3,2,1,0:T(2,128)} %bitcast.4), channel_id=1, source_target_pairs={{0,3},{1,2},{2,1},{3,0},{4,7},{5,6},{6,5},{7,4},{8,11},{9,10},{10,... | collective-permute-start | bytes 96008 | tf_op jit(solution)/shard_map/ppermute | solution.py:1003
  4.6 0.5 %collective-permute-start.2 = (f32[5,5,2,160]{3,2,1,0:T(2,128)}, f32[5,5,2,160]{3,2,1,0:T(2,128)S(1)}, u32[]{:S(2)}, u32[]{:S(2)}) collective-permute-start(f32[5,5,2,160]{3,2,1,0:T(2,128)} %bitcast.5), channel_id=1, source_target_pairs={{0,1},{1,0},{2,3},{3,2},{4,5},{5,4},{6,7},{7,6},{8,9},{9,8},{10,11... | collective-permute-start | bytes 96008 | tf_op jit(solution)/shard_map/ppermute | solution.py:1003
  5.1 3.6 %collective-permute-start.1 = (f32[5,5,2,160]{3,2,1,0:T(2,128)}, f32[5,5,2,160]{3,2,1,0:T(2,128)S(1)}, u32[]{:S(2)}, u32[]{:S(2)}) collective-permute-start(f32[5,5,2,160]{3,2,1,0:T(2,128)} %bitcast.6), channel_id=1, source_target_pairs={{0,12},{4,8},{8,4},{12,0},{1,13},{5,9},{9,5},{13,1},{2,14},{6,10},... | collective-permute-start | bytes 96008 | tf_op jit(solution)/shard_map/ppermute | solution.py:1003
  8.7 0.0 collective-permute-start
  8.7 3.3 %local_part.1.base = f32[288,128]{1,0:T(8,128)} custom-call(f32[5,5,2,160]{3,2,1,0:T(2,128)} %bitcast.10, f32[5,5,2,160]{3,2,1,0:T(2,128)} %bitcast.8, f32[5,5,160]{2,1,0:T(8,128)} %kappa_in.1, s32[6,1,1,32]{3,2,1,0:T(1,128)} %flags_in.1, f32[64,64]{1,0:T(8,128)} %constant.4.clone.rows_in, f32[160,320]{1,0:T(8,128)} %constant.5.clone.lines_in), custom_call_target="tpu_custom_call" | custom-call | tf_op jit(solution)/shard_map/local_part/pallas_call | solution.py:565
  12.0 0.0 collective-permute-done.3.y3
  12.1 0.0 collective-permute-done.2.y1
  12.1 0.0 collective-permute-done.1.x3
  12.1 1.0 %collective-permute-done.x1 = f32[5,5,2,160]{3,2,1,0:T(2,128)S(1)} collective-permute-done((f32[5,5,2,160]{3,2,1,0:T(2,128)}, f32[5,5,2,160]{3,2,1,0:T(2,128)S(1)}, u32[]{:S(2)}, u32[]{:S(2)}) %collective-permute-start) | collective-permute-done | bytes 32032 | tf_op jit(solution)/shard_map/ppermute | solution.py:1003
  13.1 0.9 %copy-done = f32[288,128]{1,0:T(8,128)S(1)} copy-done((f32[288,128]{1,0:T(8,128)S(1)}, f32[288,128]{1,0:T(8,128)}, u32[]{:S(2)}) %copy-start) | copy-done | bytes 147480
  14.0 0.5 %halo_part.1 = (f32[96,128]{1,0:T(8,128)S(1)}, f32[64,128]{1,0:T(8,128)S(1)}) custom-call(f32[288,128]{1,0:T(8,128)S(1)} %copy-done, f32[5,5,2,160]{3,2,1,0:T(2,128)S(1)} %collective-permute-done.x1, f32[5,5,2,160]{3,2,1,0:T(2,128)S(1)} %collective-permute-done.1.x3, f32[5,5,2,160]{3,2,1,0:T(2,128)S(1)} %collective-permute-done.2.y1, ...), custom_call_target="tpu_custom_call" | custom-call | tf_op jit(solution)/shard_map/halo_part/pallas_call | solution.py:586
  14.5 0.1 collective-permute-start.4
  14.6 1.2 %collective-permute-done.4 = f32[64,128]{1,0:T(8,128)S(1)} collective-permute-done((f32[64,128]{1,0:T(8,128)S(1)}, f32[64,128]{1,0:T(8,128)S(1)}, u32[]{:S(2)}, u32[]{:S(2)}) %collective-permute-start.4) | collective-permute-done | bytes 32800 | tf_op jit(solution)/shard_map/ppermute | solution.py:1003
  15.8 1.1 %collective-permute-start.5 = (f32[96,128]{1,0:T(8,128)S(1)}, f32[96,128]{1,0:T(8,128)S(1)}, u32[]{:S(2)}, u32[]{:S(2)}) collective-permute-start(f32[96,128]{1,0:T(8,128)S(1)} %pad_maximum_fusion), channel_id=1, source_target_pairs={{0,4},{4,0},{8,12},{12,8},{1,5},{5,1},{9,13},{13,9},{2,6},{6,2},{1... | collective-permute-start | bytes 147464 | tf_op jit(solution)/shard_map/ppermute | solution.py:1003
  16.9 0.8 %collective-permute-start.7 = (f32[96,128]{1,0:T(8,128)S(1)}, f32[96,128]{1,0:T(8,128)S(1)}, u32[]{:S(2)}, u32[]{:S(2)}) collective-permute-start(f32[96,128]{1,0:T(8,128)S(1)} %pad_maximum_fusion), channel_id=1, source_target_pairs={{0,12},{4,8},{8,4},{12,0},{1,13},{5,9},{9,5},{13,1},{2,14},{6,10},... | collective-permute-start | bytes 147464 | tf_op jit(solution)/shard_map/ppermute | solution.py:1003
  17.8 1.6 %collective-permute-start.6 = (f32[96,128]{1,0:T(8,128)S(1)}, f32[96,128]{1,0:T(8,128)S(1)}, u32[]{:S(2)}, u32[]{:S(2)}) collective-permute-start(f32[96,128]{1,0:T(8,128)S(1)} %pad_maximum_fusion), channel_id=1, source_target_pairs={{0,8},{4,12},{8,0},{12,4},{1,9},{5,13},{9,1},{13,5},{2,10},{6,14},... | collective-permute-start | bytes 147464 | tf_op jit(solution)/shard_map/ppermute | solution.py:1003
  19.4 0.6 %collective-permute-done.5 = f32[96,128]{1,0:T(8,128)S(1)} collective-permute-done((f32[96,128]{1,0:T(8,128)S(1)}, f32[96,128]{1,0:T(8,128)S(1)}, u32[]{:S(2)}, u32[]{:S(2)}) %collective-permute-start.5) | collective-permute-done | bytes 49184 | tf_op jit(solution)/shard_map/ppermute | solution.py:1003
  20.0 4.6 %collective-permute-done.6 = f32[96,128]{1,0:T(8,128)S(1)} collective-permute-done((f32[96,128]{1,0:T(8,128)S(1)}, f32[96,128]{1,0:T(8,128)S(1)}, u32[]{:S(2)}, u32[]{:S(2)}) %collective-permute-start.6) | collective-permute-done | bytes 49184 | tf_op jit(solution)/shard_map/ppermute | solution.py:1003
  24.6 0.0 collective-permute-done.7
  24.6 1.5 %collective-permute-start.10 = (f32[384,128]{1,0:T(8,128)S(1)}, f32[384,128]{1,0:T(8,128)S(1)}, u32[]{:S(2)}, u32[]{:S(2)}) collective-permute-start(f32[384,128]{1,0:T(8,128)S(1)} %constant_dynamic-update-slice_fusion.block0), channel_id=1, source_target_pairs={{0,3},{1,2},{2,1},{3,0},{4,7},{5,6},{6,5},{7,4},{8,11},{9,10},{10,... | collective-permute-start | bytes 589832 | tf_op jit(solution)/shard_map/ppermute | solution.py:1003
  26.1 1.5 %collective-permute-start.9 = (f32[384,128]{1,0:T(8,128)S(1)}, f32[384,128]{1,0:T(8,128)S(1)}, u32[]{:S(2)}, u32[]{:S(2)}) collective-permute-start(f32[384,128]{1,0:T(8,128)S(1)} %constant_dynamic-update-slice_fusion.block0), channel_id=1, source_target_pairs={{0,2},{1,3},{2,0},{3,1},{4,6},{5,7},{6,4},{7,5},{8,10},{9,11},{10,... | collective-permute-start | bytes 589832 | tf_op jit(solution)/shard_map/ppermute | solution.py:1003
  27.6 0.5 %collective-permute-start.8 = (f32[384,128]{1,0:T(8,128)S(1)}, f32[384,128]{1,0:T(8,128)S(1)}, u32[]{:S(2)}, u32[]{:S(2)}) collective-permute-start(f32[384,128]{1,0:T(8,128)S(1)} %constant_dynamic-update-slice_fusion.block0), channel_id=1, source_target_pairs={{0,1},{1,0},{2,3},{3,2},{4,5},{5,4},{6,7},{7,6},{8,9},{9,8},{10,11... | collective-permute-start | bytes 589832 | tf_op jit(solution)/shard_map/ppermute | solution.py:1003
  28.2 5.2 %collective-permute-done.10.block3 = f32[384,128]{1,0:T(8,128)S(1)} collective-permute-done((f32[384,128]{1,0:T(8,128)S(1)}, f32[384,128]{1,0:T(8,128)S(1)}, u32[]{:S(2)}, u32[]{:S(2)}) %collective-permute-start.10) | collective-permute-done | bytes 196640 | tf_op jit(solution)/shard_map/ppermute | solution.py:1003
  33.4 3.0 %collective-permute-done.9.block2 = f32[384,128]{1,0:T(8,128)S(1)} collective-permute-done((f32[384,128]{1,0:T(8,128)S(1)}, f32[384,128]{1,0:T(8,128)S(1)}, u32[]{:S(2)}, u32[]{:S(2)}) %collective-permute-start.9) | collective-permute-done | bytes 196640 | tf_op jit(solution)/shard_map/ppermute | solution.py:1003
  36.4 0.4 assemble.1.assembled.own_start
  36.8 0.0 copy-start.1
  36.8 0.1 collective-permute-start.11
  36.9 9.9 %cycle.1.own = f32[1128,128]{1,0:T(8,128)S(1)} custom-call(f32[384,128]{1,0:T(8,128)S(1)} %constant_dynamic-update-slice_fusion.block0, f32[384,128]{1,0:T(8,128)S(1)} %collective-permute-done.8.block1, f32[384,128]{1,0:T(8,128)S(1)} %collective-permute-done.9.block2, f32[384,128]{1,0:T(8,128)S(1)} %collective-permute-done.10.block3, ...), custom_call_target="tpu_custom_call" | custom-call | flops 40000000 | bytes 30000000 | tf_op jit(solution)/shard_map/cycle/pallas_call | solution.py:974
  46.8 0.0 collective-permute-done.11.other_start
  46.8 0.6 %collective-permute-start.12 = (f32[1128,128]{1,0:T(8,128)S(1)}, f32[1128,128]{1,0:T(8,128)S(1)}, u32[]{:S(2)}, u32[]{:S(2)}) collective-permute-start(f32[1128,128]{1,0:T(8,128)S(1)} %cycle.1.own), channel_id=1, source_target_pairs={{0,16},{16,0},{1,17},{17,1},{2,18},{18,2},{3,19},{19,3},{4,20},{20... | collective-permute-start | bytes 1732616 | tf_op jit(solution)/shard_map/ppermute | solution.py:1003
  47.4 1.6 %collective-permute-done.12.other = f32[1128,128]{1,0:T(8,128)S(1)} collective-permute-done((f32[1128,128]{1,0:T(8,128)S(1)}, f32[1128,128]{1,0:T(8,128)S(1)}, u32[]{:S(2)}, u32[]{:S(2)}) %collective-permute-start.12) | collective-permute-done | bytes 577568 | tf_op jit(solution)/shard_map/ppermute | solution.py:1003
  49.0 1.8 %finish.1 = (f32[5,5,2,160]{3,2,1,0:T(2,128)}, f32[5,5,2,160]{3,2,1,0:T(2,128)}, f32[3]{0:T(128)}) custom-call(f32[1128,128]{1,0:T(8,128)S(1)} %cycle.1.own, f32[1128,128]{1,0:T(8,128)S(1)} %collective-permute-done.12.other, f32[1024,128]{1,0:T(8,128)S(1)} %assemble.1.assembled.own_start, f32[1024,128]{1,0:T(8,128)S(1)} %collective-permute-done.11.other_start, ...), custom_call_target="tpu_custom_call" | custom-call | tf_op jit(solution)/shard_map/finish/pallas_call | solution.py:987
  (9 shorter events, 0.0 us)
Async XLA Ops:
  0.6 11.4 %collective-permute-start.3 = (f32[5,5,2,160]{3,2,1,0:T(2,128)}, f32[5,5,2,160]{3,2,1,0:T(2,128)S(1)}, u32[]{:S(2)}, u32[]{:S(2)}) collective-permute-start(f32[5,5,2,160]{3,2,1,0:T(2,128)} %bitcast.4), channel_id=1, source_target_pairs={{0,3},{1,2},{2,1},{3,0},{4,7},{5,6},{6,5},{7,4},{8,11},{9,10},{10,... | collective-permute-start | bytes 96008 | tf_op jit(solution)/shard_map/ppermute | solution.py:1003
  4.6 7.5 %collective-permute-start.2 = (f32[5,5,2,160]{3,2,1,0:T(2,128)}, f32[5,5,2,160]{3,2,1,0:T(2,128)S(1)}, u32[]{:S(2)}, u32[]{:S(2)}) collective-permute-start(f32[5,5,2,160]{3,2,1,0:T(2,128)} %bitcast.5), channel_id=1, source_target_pairs={{0,1},{1,0},{2,3},{3,2},{4,5},{5,4},{6,7},{7,6},{8,9},{9,8},{10,11... | collective-permute-start | bytes 96008 | tf_op jit(solution)/shard_map/ppermute | solution.py:1003
  5.1 6.9 %collective-permute-start.1 = (f32[5,5,2,160]{3,2,1,0:T(2,128)}, f32[5,5,2,160]{3,2,1,0:T(2,128)S(1)}, u32[]{:S(2)}, u32[]{:S(2)}) collective-permute-start(f32[5,5,2,160]{3,2,1,0:T(2,128)} %bitcast.6), channel_id=1, source_target_pairs={{0,12},{4,8},{8,4},{12,0},{1,13},{5,9},{9,5},{13,1},{2,14},{6,10},... | collective-permute-start | bytes 96008 | tf_op jit(solution)/shard_map/ppermute | solution.py:1003
  8.7 4.3 %collective-permute-start = (f32[5,5,2,160]{3,2,1,0:T(2,128)}, f32[5,5,2,160]{3,2,1,0:T(2,128)S(1)}, u32[]{:S(2)}, u32[]{:S(2)}) collective-permute-start(f32[5,5,2,160]{3,2,1,0:T(2,128)} %bitcast.7), channel_id=1, source_target_pairs={{0,4},{4,0},{8,12},{12,8},{1,5},{5,1},{9,13},{13,9},{2,6},{6,2},{1... | collective-permute-start | bytes 96008 | tf_op jit(solution)/shard_map/ppermute | solution.py:1003
  13.1 0.9 %copy-start = (f32[288,128]{1,0:T(8,128)S(1)}, f32[288,128]{1,0:T(8,128)}, u32[]{:S(2)}) copy-start(f32[288,128]{1,0:T(8,128)} %local_part.1.base) | copy-start | bytes 442372
  14.5 1.3 %collective-permute-start.4 = (f32[64,128]{1,0:T(8,128)S(1)}, f32[64,128]{1,0:T(8,128)S(1)}, u32[]{:S(2)}, u32[]{:S(2)}) collective-permute-start(f32[64,128]{1,0:T(8,128)S(1)} %get-tuple-element.11), channel_id=1, source_target_pairs={{0,16},{16,0},{1,17},{17,1},{2,18},{18,2},{3,19},{19,3},{4,20},{20... | collective-permute-start | bytes 98312 | tf_op jit(solution)/shard_map/ppermute | solution.py:1003
  15.8 4.2 %collective-permute-start.5 = (f32[96,128]{1,0:T(8,128)S(1)}, f32[96,128]{1,0:T(8,128)S(1)}, u32[]{:S(2)}, u32[]{:S(2)}) collective-permute-start(f32[96,128]{1,0:T(8,128)S(1)} %pad_maximum_fusion), channel_id=1, source_target_pairs={{0,4},{4,0},{8,12},{12,8},{1,5},{5,1},{9,13},{13,9},{2,6},{6,2},{1... | collective-permute-start | bytes 147464 | tf_op jit(solution)/shard_map/ppermute | solution.py:1003
  16.9 7.7 %collective-permute-start.7 = (f32[96,128]{1,0:T(8,128)S(1)}, f32[96,128]{1,0:T(8,128)S(1)}, u32[]{:S(2)}, u32[]{:S(2)}) collective-permute-start(f32[96,128]{1,0:T(8,128)S(1)} %pad_maximum_fusion), channel_id=1, source_target_pairs={{0,12},{4,8},{8,4},{12,0},{1,13},{5,9},{9,5},{13,1},{2,14},{6,10},... | collective-permute-start | bytes 147464 | tf_op jit(solution)/shard_map/ppermute | solution.py:1003
  17.8 6.8 %collective-permute-start.6 = (f32[96,128]{1,0:T(8,128)S(1)}, f32[96,128]{1,0:T(8,128)S(1)}, u32[]{:S(2)}, u32[]{:S(2)}) collective-permute-start(f32[96,128]{1,0:T(8,128)S(1)} %pad_maximum_fusion), channel_id=1, source_target_pairs={{0,8},{4,12},{8,0},{12,4},{1,9},{5,13},{9,1},{13,5},{2,10},{6,14},... | collective-permute-start | bytes 147464 | tf_op jit(solution)/shard_map/ppermute | solution.py:1003
  24.6 8.8 %collective-permute-start.10 = (f32[384,128]{1,0:T(8,128)S(1)}, f32[384,128]{1,0:T(8,128)S(1)}, u32[]{:S(2)}, u32[]{:S(2)}) collective-permute-start(f32[384,128]{1,0:T(8,128)S(1)} %constant_dynamic-update-slice_fusion.block0), channel_id=1, source_target_pairs={{0,3},{1,2},{2,1},{3,0},{4,7},{5,6},{6,5},{7,4},{8,11},{9,10},{10,... | collective-permute-start | bytes 589832 | tf_op jit(solution)/shard_map/ppermute | solution.py:1003
  26.1 10.3 %collective-permute-start.9 = (f32[384,128]{1,0:T(8,128)S(1)}, f32[384,128]{1,0:T(8,128)S(1)}, u32[]{:S(2)}, u32[]{:S(2)}) collective-permute-start(f32[384,128]{1,0:T(8,128)S(1)} %constant_dynamic-update-slice_fusion.block0), channel_id=1, source_target_pairs={{0,2},{1,3},{2,0},{3,1},{4,6},{5,7},{6,4},{7,5},{8,10},{9,11},{10,... | collective-permute-start | bytes 589832 | tf_op jit(solution)/shard_map/ppermute | solution.py:1003
  27.6 8.8 %collective-permute-start.8 = (f32[384,128]{1,0:T(8,128)S(1)}, f32[384,128]{1,0:T(8,128)S(1)}, u32[]{:S(2)}, u32[]{:S(2)}) collective-permute-start(f32[384,128]{1,0:T(8,128)S(1)} %constant_dynamic-update-slice_fusion.block0), channel_id=1, source_target_pairs={{0,1},{1,0},{2,3},{3,2},{4,5},{5,4},{6,7},{7,6},{8,9},{9,8},{10,11... | collective-permute-start | bytes 589832 | tf_op jit(solution)/shard_map/ppermute | solution.py:1003
  36.8 12.1 %copy-start.1 = (f32[2,5,5,160]{3,0,2,1:T(2,128)S(1)}, f32[2,5,5,160]{3,0,2,1:T(2,128)}, u32[]{:S(2)}) copy-start(f32[2,5,5,160]{3,0,2,1:T(2,128)} %param.7) | copy-start | bytes 96004
  36.8 9.9 %collective-permute-start.11 = (f32[1024,128]{1,0:T(8,128)S(1)}, f32[1024,128]{1,0:T(8,128)S(1)}, u32[]{:S(2)}, u32[]{:S(2)}) collective-permute-start(f32[1024,128]{1,0:T(8,128)S(1)} %assemble.1.assembled.own_start), channel_id=1, source_target_pairs={{0,16},{16,0},{1,17},{17,1},{2,18},{18,2},{3,19},{19,3},{4,20},{20... | collective-permute-start | bytes 1572872 | tf_op jit(solution)/shard_map/ppermute | solution.py:1003
  46.8 2.2 %collective-permute-start.12 = (f32[1128,128]{1,0:T(8,128)S(1)}, f32[1128,128]{1,0:T(8,128)S(1)}, u32[]{:S(2)}, u32[]{:S(2)}) collective-permute-start(f32[1128,128]{1,0:T(8,128)S(1)} %cycle.1.own), channel_id=1, source_target_pairs={{0,16},{16,0},{1,17},{17,1},{2,18},{18,2},{3,19},{19,3},{4,20},{20... | collective-permute-start | bytes 1732616 | tf_op jit(solution)/shard_map/ppermute | solution.py:1003

commit v4 on v3

--- a/solution.py
+++ b/solution.py
@@ -384,6 +384,18 @@
     )
 
 
+def split_dot(a, b):
+    high = a.astype(jnp.bfloat16)
+    rest = a - high.astype(F32)
+    middle = rest.astype(jnp.bfloat16)
+    low = (rest - middle.astype(F32)).astype(jnp.bfloat16)
+    b = b.astype(jnp.bfloat16)
+    return sum(
+        lax.dot_general(part, b, (((1,), (0,)), ((), ())), preferred_element_type=F32)
+        for part in (low, middle, high)
+    )
+
+
 def choose(index, values):
     out = values[-1]
     for place in range(len(values) - 2, -1, -1):
@@ -467,7 +479,7 @@
                 stack[s * 32 + r : s * 32 + r + 1, :] = left[s : s + 1]
     flag = flags[:, 0, 0, :].astype(F32)
     spread = (iota((EZ, 160), 1) // 5 == iota((EZ, 160), 0)).astype(F32)
-    wide = exact_dot(flag, spread)
+    wide = split_dot(flag, spread)
     gains = [face_gains(wide[d : d + 1, :], d // 2, d % 2, 5) for d in range(6)]
     row = iota((32, 160), 0)
     lane = iota((32, 160), 1) % 5
@@ -491,11 +503,10 @@
     own_nodes[...] = jnp.zeros_like(own_nodes)
     other_nodes[...] = jnp.zeros_like(other_nodes)
     krep[...] = jnp.zeros_like(krep)
+    stack[128:, :] = kap[...]
     source = stack[...]
-    coefs = kap[...]
     for k in range(5):
-        pick = pick_line(k)
-        parts = exact_dot(source, pick)
+        parts = split_dot(source, pick_line(k))
         for target, mark in ((own_nodes, True), (other_nodes, False)):
             total = jnp.zeros((32, 128), F32)
             for s in range(2):
@@ -503,9 +514,9 @@
                 factor = pair_factors(sec, -STEP_SIZE * back_matrix, mark, s)
                 total = total + factor * parts[64 + s * 32 : 96 + s * 32]
             target[25 * k : 25 * k + 25, :] = total[:25]
-        krep[25 * k : 25 * k + 25, :] = exact_dot(coefs, pick)[:25]
+        krep[25 * k : 25 * k + 25, :] = parts[128:153]
     repeat = (iota((EZ, 128), 1) % EZ == iota((EZ, 128), 0)).astype(F32)
-    shown = exact_dot(flag, repeat)
+    shown = split_dot(flag, repeat)
     upper = iota((1, 128), 1) < 64
     for r in range(3):
         own_nodes[125 + r : 126 + r, :] = jnp.where(upper, shown[2 * r : 2 * r + 1], shown[2 * r + 1 : 2 * r + 2])
@@ -539,7 +550,7 @@
     source = jnp.concatenate(parts_in, axis=0)
     back_matrix = split_sections()[2]
     for k in range(5):
-        parts = exact_dot(source, pick_line(k))
+        parts = split_dot(source, pick_line(k))
         for target, mark in ((own_nodes, True), (other_nodes, False)):
             total = jnp.zeros((32, 128), F32)
             for s in range(2):
@@ -572,7 +583,7 @@
             pltpu.SemaphoreType.DMA((6,)),
             pltpu.VMEM((64, 160), F32),
             pltpu.VMEM((32, 160), F32),
-            pltpu.VMEM((128, 160), F32),
+            pltpu.VMEM((160, 160), F32),
             pltpu.VMEM((128, 128), F32),
             pltpu.VMEM((128, 128), F32),
             pltpu.VMEM((128, 128), F32),
@@ -600,7 +611,7 @@
 class Level:
     def __init__(self, count, refs):
         self.count = count
-        self.diag, self.jac, self.x, self.dir, self.res, self.edge, self.f = refs
+        self.diag, self.jac, self.x, self.dir, self.res, self.f = refs
         self.tables = [element_matrix(count, d) for d in range(3)]
         self.gains = None
 
@@ -644,8 +655,8 @@
 def cycle_kernel(block0, block1, block2, block3, assembled, fields, *scratch):
     sec = lax.axis_index("section")
     my_gx, my_gy = lax.axis_index("gx"), lax.axis_index("gy")
-    levels = [Level(n, scratch[7 * p : 7 * p + 7]) for p, n in enumerate((5, 3, 2))]
-    pieces, kap, half, terms = scratch[21:25]
+    levels = [Level(n, scratch[6 * p : 6 * p + 6]) for p, n in enumerate((5, 3, 2))]
+    pieces, kap, half, terms = scratch[18:22]
     lane = iota((8, 128), 1)
     sub = iota((8, 128), 0)
     group = lane // EZ
@@ -707,7 +718,6 @@
                 store(level.jac, (k * n + i) * n, scale * (1.0 / centre))
             return carry
         lax.fori_loop(0, n, diagonals, 0)
-        level.edge[...] = jnp.zeros_like(level.edge)
 
     def begin(level, source):
         n = level.count
@@ -725,36 +735,26 @@
         n = level.count
         kx, ky, kz = level.tables
         source = level.dir if smooth else level.x
-        for i in range(n):
-            v = load(source, ((n - 1) * n + i) * n, n)
-            moved = jnp.where(element == 0, pltpu.roll(v, 97, 2), pltpu.roll(v, 1, 2))
-            store(level.edge, i * n, level.gains[4] * moved)
-            v = load(source, i * n, n)
-            moved = jnp.where(element == EZ - 1, pltpu.roll(v, 31, 2), pltpu.roll(v, 127, 2))
-            store(level.edge, ((n - 1) * n + i) * n, level.gains[5] * moved)
 
         def around(u):
             turned = pltpu.roll(u, 4, 1)
             return turned, jnp.where(odd, pltpu.roll(turned, 32, 2), pltpu.roll(turned, 96, 2))
 
-        def plane(k, carry):
-            sides = []
-            for m in range(1, n):
-                coef = choose(k, [float(kz[a, (a + m) % n]) for a in range(n)])
-                sides.append((coef, jnp.where(k + m >= n, k + m - n, k + m) * (n * n)))
-            here = k * (n * n)
+        for k in range(n):
+            here = k * n * n
             v = [load(source, here + i * n, n) for i in range(n)]
             left, left_far = around(v[n - 1])
             right, right_far = around(v[0])
             waiting = []
             for i in range(n):
                 first = here + i * n
-                total = load(level.diag, first, n) * v[i] - load(level.edge, first, n)
+                total = load(level.diag, first, n) * v[i]
                 for m in range(n):
                     if m != i:
                         total = total + float(kx[i, m]) * v[m]
-                for coef, far in sides:
-                    total = total + coef * load(source, far + i * n, n)
+                for m in range(n):
+                    if m != k:
+                        total = total + float(kz[k, m]) * load(source, (m * n + i) * n, n)
                 lines = []
                 for j in range(n):
                     line = None
@@ -776,6 +776,14 @@
                     total = total - level.gains[0] * jnp.where(low_half, left_far, left)
                 if i == n - 1:
                     total = total - level.gains[1] * jnp.where(low_half, right, right_far)
+                if k == 0:
+                    u = load(source, ((n - 1) * n + i) * n, n)
+                    moved = jnp.where(element == 0, pltpu.roll(u, 97, 2), pltpu.roll(u, 1, 2))
+                    total = total - level.gains[4] * moved
+                if k == n - 1:
+                    u = load(source, i * n, n)
+                    moved = jnp.where(element == EZ - 1, pltpu.roll(u, 31, 2), pltpu.roll(u, 127, 2))
+                    total = total - level.gains[5] * moved
                 image = v[i] + (same * total + swap * pltpu.roll(total, 64, 2))
                 if smooth:
                     scaled = load(level.jac, first, n) * (load(level.res, first, n) - image)
@@ -788,8 +796,6 @@
                     for place_out in waiting:
                         store(*place_out)
                     waiting = []
-            return carry
-        lax.fori_loop(0, n, plane, 0)
 
     def combine(weights, parts):
         total = None
@@ -866,18 +872,6 @@
     column = (my_gx % 2) * 4 + my_gy
     fields[FIELD : FIELD + 125, :] = fine.x[pl.ds(column, 125, stride=8), :]
     fields[FIELD + 125 : FIELD + 128, :] = jnp.zeros((3, 128), F32)
-
-
-def split_dot(a, b):
-    high = a.astype(jnp.bfloat16)
-    rest = a - high.astype(F32)
-    middle = rest.astype(jnp.bfloat16)
-    low = (rest - middle.astype(F32)).astype(jnp.bfloat16)
-    b = b.astype(jnp.bfloat16)
-    return sum(
-        lax.dot_general(part, b, (((1,), (0,)), ((), ())), preferred_element_type=F32)
-        for part in (low, middle, high)
-    )
 
 
 def finish_kernel(own, other, own_start, other_start, guess, sol, res_out, arnoldi, cols, outs):
@@ -964,7 +958,7 @@
 def cycle(blocks, assembled):
     scratch = []
     for n in (5, 3, 2):
-        scratch += [pltpu.VMEM((n**3 * 8, 128), F32)] * 7
+        scratch += [pltpu.VMEM((n**3 * 8, 128), F32)] * 6
     scratch += [
         pltpu.VMEM((COLS * 32, 128), F32),
         pltpu.VMEM((128 * 8, 128), F32),

time: 50.9 us -> 47.3 us (0.929)
  Pallas kernels: 15.9 us -> 12.2 us
    pallas_call x1, Pallas kernels: 9.85 us -> 6.84 us  [cycle(): pl.pallas_call(cycle_kernel, out_shape=jax.ShapeDtypeStruct((FIELD + 128,...]
    pallas_call x1, Pallas kernels: 3.3 us -> 2.77 us  [local_part(): pl.pallas_call(local_kernel, out_shape=jax.ShapeDtypeStruct((288, 128), F...]
  transfers between devices with their start and end apart: 13 -> 13, of which waited for: 7 -> 7; matrix products, arithmetic and copies ran while one was open for 0% -> 0% of each run, Pallas kernels for 26% -> 20%
where the time goes in v4:
time: 47.3 us; the launch traced here: 47.2 us
  waiting for transfers between devices  17.4 us (37%)
  starting transfers between devices  15.9 us (34%)
  Pallas kernels  12.2 us (26%)
  local copies, waits for them, and re-layouts  0.94 us (2%)
  between operations  0.74 us (2%)
    ppermute x13, waiting for transfers between devices, exchange(): lax.ppermute(x, axis, [(n, n ^ bits) for n in range(lax.axis_size(axis))])  17.4 us
    ppermute x13, starting transfers between devices, exchange(): lax.ppermute(x, axis, [(n, n ^ bits) for n in range(lax.axis_size(axis))])  15.9 us
    pallas_call x1, Pallas kernels, cycle(): pl.pallas_call(cycle_kernel, out_shape=jax.ShapeDtypeStruct((FIELD + 128,...  6.84 us
    pallas_call x1, Pallas kernels, local_part(): pl.pallas_call(local_kernel, out_shape=jax.ShapeDtypeStruct((288, 128), F...  2.77 us
    pallas_call x1, Pallas kernels, finish(): pl.pallas_call(finish_kernel, out_shape=[jax.ShapeDtypeStruct(guess.shape...  1.81 us
  transfers between devices with their start and end apart: 13, of which 7 were waited for; matrix products, arithmetic and copies ran while one was open for 0% of the time, Pallas kernels for 20%

profile of v4, /device:TPU:0, one launch (start us, length us, event | category | flops | bytes accessed | tf_op | source)
XLA Modules:
  0.0 47.2 jit_solution(17835930583812679464)
XLA Ops:
  0.6 4.0 %collective-permute-start.3 = (f32[5,5,2,160]{3,2,1,0:T(2,128)}, f32[5,5,2,160]{3,2,1,0:T(2,128)S(1)}, u32[]{:S(2)}, u32[]{:S(2)}) collective-permute-start(f32[5,5,2,160]{3,2,1,0:T(2,128)} %bitcast.4), channel_id=1, source_target_pairs={{0,3},{1,2},{2,1},{3,0},{4,7},{5,6},{6,5},{7,4},{8,11},{9,10},{10,... | collective-permute-start | bytes 96008 | tf_op jit(solution)/shard_map/ppermute | solution.py:997
  4.6 0.5 %collective-permute-start.2 = (f32[5,5,2,160]{3,2,1,0:T(2,128)}, f32[5,5,2,160]{3,2,1,0:T(2,128)S(1)}, u32[]{:S(2)}, u32[]{:S(2)}) collective-permute-start(f32[5,5,2,160]{3,2,1,0:T(2,128)} %bitcast.5), channel_id=1, source_target_pairs={{0,1},{1,0},{2,3},{3,2},{4,5},{5,4},{6,7},{7,6},{8,9},{9,8},{10,11... | collective-permute-start | bytes 96008 | tf_op jit(solution)/shard_map/ppermute | solution.py:997
  5.1 3.6 %collective-permute-start.1 = (f32[5,5,2,160]{3,2,1,0:T(2,128)}, f32[5,5,2,160]{3,2,1,0:T(2,128)S(1)}, u32[]{:S(2)}, u32[]{:S(2)}) collective-permute-start(f32[5,5,2,160]{3,2,1,0:T(2,128)} %bitcast.6), channel_id=1, source_target_pairs={{0,12},{4,8},{8,4},{12,0},{1,13},{5,9},{9,5},{13,1},{2,14},{6,10},... | collective-permute-start | bytes 96008 | tf_op jit(solution)/shard_map/ppermute | solution.py:997
  8.7 0.0 collective-permute-start
  8.7 2.8 %local_part.1.base = f32[288,128]{1,0:T(8,128)} custom-call(f32[5,5,2,160]{3,2,1,0:T(2,128)} %bitcast.10, f32[5,5,2,160]{3,2,1,0:T(2,128)} %bitcast.8, f32[5,5,160]{2,1,0:T(8,128)} %kappa_in.1, s32[6,1,1,32]{3,2,1,0:T(1,128)} %flags_in.1, f32[64,64]{1,0:T(8,128)} %constant.4.clone.rows_in, f32[160,320]{1,0:T(8,128)} %constant.5.clone.lines_in), custom_call_target="tpu_custom_call" | custom-call | tf_op jit(solution)/shard_map/local_part/pallas_call | solution.py:576
  11.5 0.0 collective-permute-done.3.y3
  11.5 0.0 collective-permute-done.2.y1
  11.5 1.5 %collective-permute-done.x1 = f32[5,5,2,160]{3,2,1,0:T(2,128)S(1)} collective-permute-done((f32[5,5,2,160]{3,2,1,0:T(2,128)}, f32[5,5,2,160]{3,2,1,0:T(2,128)S(1)}, u32[]{:S(2)}, u32[]{:S(2)}) %collective-permute-start) | collective-permute-done | bytes 32032 | tf_op jit(solution)/shard_map/ppermute | solution.py:997
  13.1 0.9 %copy-done = f32[288,128]{1,0:T(8,128)S(1)} copy-done((f32[288,128]{1,0:T(8,128)S(1)}, f32[288,128]{1,0:T(8,128)}, u32[]{:S(2)}) %copy-start) | copy-done | bytes 147480
  14.0 0.4 halo_part.1
  14.3 0.1 collective-permute-start.4
  14.4 1.2 %collective-permute-done.4 = f32[64,128]{1,0:T(8,128)S(1)} collective-permute-done((f32[64,128]{1,0:T(8,128)S(1)}, f32[64,128]{1,0:T(8,128)S(1)}, u32[]{:S(2)}, u32[]{:S(2)}) %collective-permute-start.4) | collective-permute-done | bytes 32800 | tf_op jit(solution)/shard_map/ppermute | solution.py:997
  15.6 0.6 %collective-permute-start.5 = (f32[96,128]{1,0:T(8,128)S(1)}, f32[96,128]{1,0:T(8,128)S(1)}, u32[]{:S(2)}, u32[]{:S(2)}) collective-permute-start(f32[96,128]{1,0:T(8,128)S(1)} %pad_maximum_fusion), channel_id=1, source_target_pairs={{0,4},{4,0},{8,12},{12,8},{1,5},{5,1},{9,13},{13,9},{2,6},{6,2},{1... | collective-permute-start | bytes 147464 | tf_op jit(solution)/shard_map/ppermute | solution.py:997
  16.2 1.3 %collective-permute-start.7 = (f32[96,128]{1,0:T(8,128)S(1)}, f32[96,128]{1,0:T(8,128)S(1)}, u32[]{:S(2)}, u32[]{:S(2)}) collective-permute-start(f32[96,128]{1,0:T(8,128)S(1)} %pad_maximum_fusion), channel_id=1, source_target_pairs={{0,12},{4,8},{8,4},{12,0},{1,13},{5,9},{9,5},{13,1},{2,14},{6,10},... | collective-permute-start | bytes 147464 | tf_op jit(solution)/shard_map/ppermute | solution.py:997
  17.6 1.6 %collective-permute-start.6 = (f32[96,128]{1,0:T(8,128)S(1)}, f32[96,128]{1,0:T(8,128)S(1)}, u32[]{:S(2)}, u32[]{:S(2)}) collective-permute-start(f32[96,128]{1,0:T(8,128)S(1)} %pad_maximum_fusion), channel_id=1, source_target_pairs={{0,8},{4,12},{8,0},{12,4},{1,9},{5,13},{9,1},{13,5},{2,10},{6,14},... | collective-permute-start | bytes 147464 | tf_op jit(solution)/shard_map/ppermute | solution.py:997
  19.2 0.6 %collective-permute-done.5 = f32[96,128]{1,0:T(8,128)S(1)} collective-permute-done((f32[96,128]{1,0:T(8,128)S(1)}, f32[96,128]{1,0:T(8,128)S(1)}, u32[]{:S(2)}, u32[]{:S(2)}) %collective-permute-start.5) | collective-permute-done | bytes 49184 | tf_op jit(solution)/shard_map/ppermute | solution.py:997
  19.8 4.4 %collective-permute-done.6 = f32[96,128]{1,0:T(8,128)S(1)} collective-permute-done((f32[96,128]{1,0:T(8,128)S(1)}, f32[96,128]{1,0:T(8,128)S(1)}, u32[]{:S(2)}, u32[]{:S(2)}) %collective-permute-start.6) | collective-permute-done | bytes 49184 | tf_op jit(solution)/shard_map/ppermute | solution.py:997
  24.2 0.0 collective-permute-done.7
  24.2 1.5 %collective-permute-start.10 = (f32[384,128]{1,0:T(8,128)S(1)}, f32[384,128]{1,0:T(8,128)S(1)}, u32[]{:S(2)}, u32[]{:S(2)}) collective-permute-start(f32[384,128]{1,0:T(8,128)S(1)} %constant_dynamic-update-slice_fusion.block0), channel_id=1, source_target_pairs={{0,3},{1,2},{2,1},{3,0},{4,7},{5,6},{6,5},{7,4},{8,11},{9,10},{10,... | collective-permute-start | bytes 589832 | tf_op jit(solution)/shard_map/ppermute | solution.py:997
  25.7 1.5 %collective-permute-start.9 = (f32[384,128]{1,0:T(8,128)S(1)}, f32[384,128]{1,0:T(8,128)S(1)}, u32[]{:S(2)}, u32[]{:S(2)}) collective-permute-start(f32[384,128]{1,0:T(8,128)S(1)} %constant_dynamic-update-slice_fusion.block0), channel_id=1, source_target_pairs={{0,2},{1,3},{2,0},{3,1},{4,6},{5,7},{6,4},{7,5},{8,10},{9,11},{10,... | collective-permute-start | bytes 589832 | tf_op jit(solution)/shard_map/ppermute | solution.py:997
  27.3 0.5 %collective-permute-start.8 = (f32[384,128]{1,0:T(8,128)S(1)}, f32[384,128]{1,0:T(8,128)S(1)}, u32[]{:S(2)}, u32[]{:S(2)}) collective-permute-start(f32[384,128]{1,0:T(8,128)S(1)} %constant_dynamic-update-slice_fusion.block0), channel_id=1, source_target_pairs={{0,1},{1,0},{2,3},{3,2},{4,5},{5,4},{6,7},{7,6},{8,9},{9,8},{10,11... | collective-permute-start | bytes 589832 | tf_op jit(solution)/shard_map/ppermute | solution.py:997
  27.8 5.3 %collective-permute-done.10.block3 = f32[384,128]{1,0:T(8,128)S(1)} collective-permute-done((f32[384,128]{1,0:T(8,128)S(1)}, f32[384,128]{1,0:T(8,128)S(1)}, u32[]{:S(2)}, u32[]{:S(2)}) %collective-permute-start.10) | collective-permute-done | bytes 196640 | tf_op jit(solution)/shard_map/ppermute | solution.py:997
  33.1 2.8 %collective-permute-done.9.block2 = f32[384,128]{1,0:T(8,128)S(1)} collective-permute-done((f32[384,128]{1,0:T(8,128)S(1)}, f32[384,128]{1,0:T(8,128)S(1)}, u32[]{:S(2)}, u32[]{:S(2)}) %collective-permute-start.9) | collective-permute-done | bytes 196640 | tf_op jit(solution)/shard_map/ppermute | solution.py:997
  35.8 0.0 collective-permute-done.8.block1
  35.8 0.4 assemble.1.assembled.own_start
  36.2 0.0 copy-start.1
  36.3 0.1 collective-permute-start.11
  36.3 6.8 %cycle.1.own = f32[1128,128]{1,0:T(8,128)S(1)} custom-call(f32[384,128]{1,0:T(8,128)S(1)} %constant_dynamic-update-slice_fusion.block0, f32[384,128]{1,0:T(8,128)S(1)} %collective-permute-done.8.block1, f32[384,128]{1,0:T(8,128)S(1)} %collective-permute-done.9.block2, f32[384,128]{1,0:T(8,128)S(1)} %collective-permute-done.10.block3, ...), custom_call_target="tpu_custom_call" | custom-call | flops 40000000 | bytes 30000000 | tf_op jit(solution)/shard_map/cycle/pallas_call | solution.py:968
  43.2 0.0 collective-permute-done.11.other_start
  43.2 0.6 %collective-permute-start.12 = (f32[1128,128]{1,0:T(8,128)S(1)}, f32[1128,128]{1,0:T(8,128)S(1)}, u32[]{:S(2)}, u32[]{:S(2)}) collective-permute-start(f32[1128,128]{1,0:T(8,128)S(1)} %cycle.1.own), channel_id=1, source_target_pairs={{0,16},{16,0},{1,17},{17,1},{2,18},{18,2},{3,19},{19,3},{4,20},{20... | collective-permute-start | bytes 1732616 | tf_op jit(solution)/shard_map/ppermute | solution.py:997
  43.8 1.6 %collective-permute-done.12.other = f32[1128,128]{1,0:T(8,128)S(1)} collective-permute-done((f32[1128,128]{1,0:T(8,128)S(1)}, f32[1128,128]{1,0:T(8,128)S(1)}, u32[]{:S(2)}, u32[]{:S(2)}) %collective-permute-start.12) | collective-permute-done | bytes 577568 | tf_op jit(solution)/shard_map/ppermute | solution.py:997
  45.4 1.8 %finish.1 = (f32[5,5,2,160]{3,2,1,0:T(2,128)}, f32[5,5,2,160]{3,2,1,0:T(2,128)}, f32[3]{0:T(128)}) custom-call(f32[1128,128]{1,0:T(8,128)S(1)} %cycle.1.own, f32[1128,128]{1,0:T(8,128)S(1)} %collective-permute-done.12.other, f32[1024,128]{1,0:T(8,128)S(1)} %assemble.1.assembled.own_start, f32[1024,128]{1,0:T(8,128)S(1)} %collective-permute-done.11.other_start, ...), custom_call_target="tpu_custom_call" | custom-call | tf_op jit(solution)/shard_map/finish/pallas_call | solution.py:981
  (9 shorter events, 0.0 us)
Async XLA Ops:
  0.6 10.9 %collective-permute-start.3 = (f32[5,5,2,160]{3,2,1,0:T(2,128)}, f32[5,5,2,160]{3,2,1,0:T(2,128)S(1)}, u32[]{:S(2)}, u32[]{:S(2)}) collective-permute-start(f32[5,5,2,160]{3,2,1,0:T(2,128)} %bitcast.4), channel_id=1, source_target_pairs={{0,3},{1,2},{2,1},{3,0},{4,7},{5,6},{6,5},{7,4},{8,11},{9,10},{10,... | collective-permute-start | bytes 96008 | tf_op jit(solution)/shard_map/ppermute | solution.py:997
  4.6 6.9 %collective-permute-start.2 = (f32[5,5,2,160]{3,2,1,0:T(2,128)}, f32[5,5,2,160]{3,2,1,0:T(2,128)S(1)}, u32[]{:S(2)}, u32[]{:S(2)}) collective-permute-start(f32[5,5,2,160]{3,2,1,0:T(2,128)} %bitcast.5), channel_id=1, source_target_pairs={{0,1},{1,0},{2,3},{3,2},{4,5},{5,4},{6,7},{7,6},{8,9},{9,8},{10,11... | collective-permute-start | bytes 96008 | tf_op jit(solution)/shard_map/ppermute | solution.py:997
  5.1 6.4 %collective-permute-start.1 = (f32[5,5,2,160]{3,2,1,0:T(2,128)}, f32[5,5,2,160]{3,2,1,0:T(2,128)S(1)}, u32[]{:S(2)}, u32[]{:S(2)}) collective-permute-start(f32[5,5,2,160]{3,2,1,0:T(2,128)} %bitcast.6), channel_id=1, source_target_pairs={{0,12},{4,8},{8,4},{12,0},{1,13},{5,9},{9,5},{13,1},{2,14},{6,10},... | collective-permute-start | bytes 96008 | tf_op jit(solution)/shard_map/ppermute | solution.py:997
  8.7 4.3 %collective-permute-start = (f32[5,5,2,160]{3,2,1,0:T(2,128)}, f32[5,5,2,160]{3,2,1,0:T(2,128)S(1)}, u32[]{:S(2)}, u32[]{:S(2)}) collective-permute-start(f32[5,5,2,160]{3,2,1,0:T(2,128)} %bitcast.7), channel_id=1, source_target_pairs={{0,4},{4,0},{8,12},{12,8},{1,5},{5,1},{9,13},{13,9},{2,6},{6,2},{1... | collective-permute-start | bytes 96008 | tf_op jit(solution)/shard_map/ppermute | solution.py:997
  13.1 0.9 %copy-start = (f32[288,128]{1,0:T(8,128)S(1)}, f32[288,128]{1,0:T(8,128)}, u32[]{:S(2)}) copy-start(f32[288,128]{1,0:T(8,128)} %local_part.1.base) | copy-start | bytes 442372
  14.3 1.3 %collective-permute-start.4 = (f32[64,128]{1,0:T(8,128)S(1)}, f32[64,128]{1,0:T(8,128)S(1)}, u32[]{:S(2)}, u32[]{:S(2)}) collective-permute-start(f32[64,128]{1,0:T(8,128)S(1)} %get-tuple-element.11), channel_id=1, source_target_pairs={{0,16},{16,0},{1,17},{17,1},{2,18},{18,2},{3,19},{19,3},{4,20},{20... | collective-permute-start | bytes 98312 | tf_op jit(solution)/shard_map/ppermute | solution.py:997
  15.6 4.2 %collective-permute-start.5 = (f32[96,128]{1,0:T(8,128)S(1)}, f32[96,128]{1,0:T(8,128)S(1)}, u32[]{:S(2)}, u32[]{:S(2)}) collective-permute-start(f32[96,128]{1,0:T(8,128)S(1)} %pad_maximum_fusion), channel_id=1, source_target_pairs={{0,4},{4,0},{8,12},{12,8},{1,5},{5,1},{9,13},{13,9},{2,6},{6,2},{1... | collective-permute-start | bytes 147464 | tf_op jit(solution)/shard_map/ppermute | solution.py:997
  16.2 8.0 %collective-permute-start.7 = (f32[96,128]{1,0:T(8,128)S(1)}, f32[96,128]{1,0:T(8,128)S(1)}, u32[]{:S(2)}, u32[]{:S(2)}) collective-permute-start(f32[96,128]{1,0:T(8,128)S(1)} %pad_maximum_fusion), channel_id=1, source_target_pairs={{0,12},{4,8},{8,4},{12,0},{1,13},{5,9},{9,5},{13,1},{2,14},{6,10},... | collective-permute-start | bytes 147464 | tf_op jit(solution)/shard_map/ppermute | solution.py:997
  17.6 6.6 %collective-permute-start.6 = (f32[96,128]{1,0:T(8,128)S(1)}, f32[96,128]{1,0:T(8,128)S(1)}, u32[]{:S(2)}, u32[]{:S(2)}) collective-permute-start(f32[96,128]{1,0:T(8,128)S(1)} %pad_maximum_fusion), channel_id=1, source_target_pairs={{0,8},{4,12},{8,0},{12,4},{1,9},{5,13},{9,1},{13,5},{2,10},{6,14},... | collective-permute-start | bytes 147464 | tf_op jit(solution)/shard_map/ppermute | solution.py:997
  24.2 8.8 %collective-permute-start.10 = (f32[384,128]{1,0:T(8,128)S(1)}, f32[384,128]{1,0:T(8,128)S(1)}, u32[]{:S(2)}, u32[]{:S(2)}) collective-permute-start(f32[384,128]{1,0:T(8,128)S(1)} %constant_dynamic-update-slice_fusion.block0), channel_id=1, source_target_pairs={{0,3},{1,2},{2,1},{3,0},{4,7},{5,6},{6,5},{7,4},{8,11},{9,10},{10,... | collective-permute-start | bytes 589832 | tf_op jit(solution)/shard_map/ppermute | solution.py:997
  25.7 10.1 %collective-permute-start.9 = (f32[384,128]{1,0:T(8,128)S(1)}, f32[384,128]{1,0:T(8,128)S(1)}, u32[]{:S(2)}, u32[]{:S(2)}) collective-permute-start(f32[384,128]{1,0:T(8,128)S(1)} %constant_dynamic-update-slice_fusion.block0), channel_id=1, source_target_pairs={{0,2},{1,3},{2,0},{3,1},{4,6},{5,7},{6,4},{7,5},{8,10},{9,11},{10,... | collective-permute-start | bytes 589832 | tf_op jit(solution)/shard_map/ppermute | solution.py:997
  27.3 8.6 %collective-permute-start.8 = (f32[384,128]{1,0:T(8,128)S(1)}, f32[384,128]{1,0:T(8,128)S(1)}, u32[]{:S(2)}, u32[]{:S(2)}) collective-permute-start(f32[384,128]{1,0:T(8,128)S(1)} %constant_dynamic-update-slice_fusion.block0), channel_id=1, source_target_pairs={{0,1},{1,0},{2,3},{3,2},{4,5},{5,4},{6,7},{7,6},{8,9},{9,8},{10,11... | collective-permute-start | bytes 589832 | tf_op jit(solution)/shard_map/ppermute | solution.py:997
  36.2 9.1 %copy-start.1 = (f32[2,5,5,160]{3,0,2,1:T(2,128)S(1)}, f32[2,5,5,160]{3,0,2,1:T(2,128)}, u32[]{:S(2)}) copy-start(f32[2,5,5,160]{3,0,2,1:T(2,128)} %param.7) | copy-start | bytes 96004
  36.3 6.9 %collective-permute-start.11 = (f32[1024,128]{1,0:T(8,128)S(1)}, f32[1024,128]{1,0:T(8,128)S(1)}, u32[]{:S(2)}, u32[]{:S(2)}) collective-permute-start(f32[1024,128]{1,0:T(8,128)S(1)} %assemble.1.assembled.own_start), channel_id=1, source_target_pairs={{0,16},{16,0},{1,17},{17,1},{2,18},{18,2},{3,19},{19,3},{4,20},{20... | collective-permute-start | bytes 1572872 | tf_op jit(solution)/shard_map/ppermute | solution.py:997
  43.2 2.2 %collective-permute-start.12 = (f32[1128,128]{1,0:T(8,128)S(1)}, f32[1128,128]{1,0:T(8,128)S(1)}, u32[]{:S(2)}, u32[]{:S(2)}) collective-permute-start(f32[1128,128]{1,0:T(8,128)S(1)} %cycle.1.own), channel_id=1, source_target_pairs={{0,16},{16,0},{1,17},{17,1},{2,18},{18,2},{3,19},{19,3},{4,20},{20... | collective-permute-start | bytes 1732616 | tf_op jit(solution)/shard_map/ppermute | solution.py:997

commit v5 on v4

--- a/solution.py
+++ b/solution.py
@@ -625,16 +625,15 @@
 
 
 def place_pieces(blocks, pieces, first, size):
-    my_gx, my_gy = lax.axis_index("gx"), lax.axis_index("gy")
-    for b, block in enumerate(blocks):
-        for a in range(4):
-            column = (my_gx ^ a) * 4 + (my_gy ^ b)
-            start = pl.multiple_of(column * size, 8)
-            pieces[pl.ds(start, size), :] = block[a * PIECE + first : a * PIECE + first + size, :]
-
-
-def assemble_kernel(block0, block1, block2, block3, field, pieces):
-    place_pieces((block0, block1, block2, block3), pieces, 0, HALF)
+    for gy in range(4):
+        for gx in range(4):
+            source = (gy * 4 + gx) * PIECE + first
+            target = (gx * 4 + gy) * size
+            pieces[target : target + size, :] = blocks[source : source + size, :]
+
+
+def assemble_kernel(blocks, field, pieces):
+    place_pieces(blocks, pieces, 0, HALF)
     odd = iota((8, 128), 1) // EZ % 2 == 1
     for r in range(HALF):
         low, high = rows_of(pieces, HALF, r, 0), rows_of(pieces, HALF, r, 1)
@@ -652,7 +651,7 @@
     ref[pl.ds(start, value.shape[0] * 8), :] = value.reshape(value.shape[0] * 8, 128)
 
 
-def cycle_kernel(block0, block1, block2, block3, assembled, fields, *scratch):
+def cycle_kernel(gathered, assembled, fields, *scratch):
     sec = lax.axis_index("section")
     my_gx, my_gy = lax.axis_index("gx"), lax.axis_index("gy")
     levels = [Level(n, scratch[6 * p : 6 * p + 6]) for p, n in enumerate((5, 3, 2))]
@@ -684,7 +683,7 @@
         got = assembled[tile(125 + r), :]
         across = pltpu.roll(got, 64, 1)
         flags += [jnp.where(lane < 64, got, across), jnp.where(lane < 64, across, got)]
-    place_pieces((block0, block1, block2, block3), pieces, HALF, 32)
+    place_pieces(gathered, pieces, HALF, 32)
 
     for r in range(32):
         turned = []
@@ -947,12 +946,12 @@
     return pl.pallas_call(
         assemble_kernel,
         out_shape=jax.ShapeDtypeStruct((128 * 8, 128), F32),
-        in_specs=[VMEM] * 4,
+        in_specs=[VMEM],
         out_specs=VMEM,
         scratch_shapes=[pltpu.VMEM((COLS * HALF, 128), F32)],
         compiler_params=limit(16),
         name="assemble",
-    )(*blocks)
+    )(blocks)
 
 
 def cycle(blocks, assembled):
@@ -968,13 +967,13 @@
     return pl.pallas_call(
         cycle_kernel,
         out_shape=jax.ShapeDtypeStruct((FIELD + 128, 128), F32),
-        in_specs=[VMEM] * 5,
+        in_specs=[VMEM] * 2,
         out_specs=VMEM,
         scratch_shapes=scratch,
         compiler_params=limit(24),
         cost_estimate=pl.CostEstimate(flops=40_000_000, bytes_accessed=30_000_000, transcendentals=0),
         name="cycle",
-    )(*blocks, assembled)
+    )(blocks, assembled)
 
 
 def finish(own, other, own_start, other_start, guess):
@@ -997,6 +996,12 @@
     return lax.ppermute(x, axis, [(n, n ^ bits) for n in range(lax.axis_size(axis))])
 
 
+def spread(x, axis):
+    copies = jnp.broadcast_to(x, (lax.axis_size(axis),) + x.shape)
+    got = lax.all_to_all(copies, axis, split_axis=0, concat_axis=0)
+    return got.reshape((-1,) + x.shape[1:])
+
+
 def gathered_body(rhs, guess, kappa, bc_flags):
     rhs, guess = (jnp.transpose(v, (1, 2, 0, 3)) for v in (rhs, guess))
     halos = [exchange(guess, axis, bits) for axis in ("gx", "gy") for bits in (1, 3)]
@@ -1004,8 +1009,7 @@
     mine, theirs = halo_part(base, halos)
     got = exchange(theirs, "section", 1)
     piece = jnp.concatenate([mine[:HALF] + got, mine[HALF:]])
-    line = jnp.concatenate([piece] + [exchange(piece, "gx", bits) for bits in (1, 2, 3)])
-    blocks = [line] + [exchange(line, "gy", bits) for bits in (1, 2, 3)]
+    blocks = spread(spread(piece, "gx"), "gy")
     start = assemble(blocks)
     other_start = exchange(start, "section", 1)
     own, other_start = lax.optimization_barrier((cycle(blocks, start), other_start))

time: 47.3 us -> 50.3 us (1.063)
  blocking collectives: 0 us -> 23 us
  waiting for transfers between devices: 17.4 us -> 4.33 us
  starting transfers between devices: 15.9 us -> 8.8 us
    all_to_all x0 -> x2, blocking collectives: none -> 23 us  [spread(): got = lax.all_to_all(copies, axis, split_axis=0, concat_axis=0)]
    ppermute x13 -> x7, waiting for transfers between devices: 17.4 us -> 4.33 us  [exchange(): lax.ppermute(x, axis, [(n, n ^ bits) for n in range(lax.axis_size(axis))])]
    ppermute x13 -> x7, starting transfers between devices: 15.9 us -> 8.8 us  [exchange(): lax.ppermute(x, axis, [(n, n ^ bits) for n in range(lax.axis_size(axis))])]
  transfers between devices with their start and end apart: 13 -> 7, of which waited for: 7 -> 3; matrix products, arithmetic and copies ran while one was open for 0% -> 0% of each run, Pallas kernels for 20% -> 19%
where the time goes in v5:
time: 50.3 us; the launch traced here: 50.1 us
  blocking collectives  23 us (46%)
  Pallas kernels  12.2 us (24%)
  starting transfers between devices  8.8 us (17%)
  waiting for transfers between devices  4.33 us (9%)
  local copies, waits for them, and re-layouts  0.99 us (2%)
  between operations  0.74 us (1%)
    all_to_all x2, blocking collectives, spread(): got = lax.all_to_all(copies, axis, split_axis=0, concat_axis=0)  23 us
    ppermute x7, starting transfers between devices, exchange(): lax.ppermute(x, axis, [(n, n ^ bits) for n in range(lax.axis_size(axis))])  8.8 us
    pallas_call x1, Pallas kernels, cycle(): pl.pallas_call(cycle_kernel, out_shape=jax.ShapeDtypeStruct((FIELD + 128,...  6.83 us
    ppermute x7, waiting for transfers between devices, exchange(): lax.ppermute(x, axis, [(n, n ^ bits) for n in range(lax.axis_size(axis))])  4.33 us
    pallas_call x1, Pallas kernels, local_part(): pl.pallas_call(local_kernel, out_shape=jax.ShapeDtypeStruct((288, 128), F...  2.75 us
    pallas_call x1, Pallas kernels, finish(): pl.pallas_call(finish_kernel, out_shape=[jax.ShapeDtypeStruct(guess.shape...  1.82 us
  transfers between devices with their start and end apart: 7, of which 3 were waited for; matrix products, arithmetic and copies ran while one was open for 0% of the time, Pallas kernels for 19%

profile of v5, /device:TPU:0, one launch (start us, length us, event | category | flops | bytes accessed | tf_op | source)
XLA Modules:
  0.0 50.1 jit_solution(1392248496276284361)
XLA Ops:
  0.6 4.0 %collective-permute-start.3 = (f32[5,5,2,160]{3,2,1,0:T(2,128)}, f32[5,5,2,160]{3,2,1,0:T(2,128)S(1)}, u32[]{:S(2)}, u32[]{:S(2)}) collective-permute-start(f32[5,5,2,160]{3,2,1,0:T(2,128)} %bitcast.8), channel_id=1, source_target_pairs={{0,3},{1,2},{2,1},{3,0},{4,7},{5,6},{6,5},{7,4},{8,11},{9,10},{10,... | collective-permute-start | bytes 96008 | tf_op jit(solution)/shard_map/ppermute | solution.py:996
  4.6 0.5 %collective-permute-start.2 = (f32[5,5,2,160]{3,2,1,0:T(2,128)}, f32[5,5,2,160]{3,2,1,0:T(2,128)S(1)}, u32[]{:S(2)}, u32[]{:S(2)}) collective-permute-start(f32[5,5,2,160]{3,2,1,0:T(2,128)} %bitcast.9), channel_id=1, source_target_pairs={{0,1},{1,0},{2,3},{3,2},{4,5},{5,4},{6,7},{7,6},{8,9},{9,8},{10,11... | collective-permute-start | bytes 96008 | tf_op jit(solution)/shard_map/ppermute | solution.py:996
  5.1 3.6 %collective-permute-start.1 = (f32[5,5,2,160]{3,2,1,0:T(2,128)}, f32[5,5,2,160]{3,2,1,0:T(2,128)S(1)}, u32[]{:S(2)}, u32[]{:S(2)}) collective-permute-start(f32[5,5,2,160]{3,2,1,0:T(2,128)} %bitcast.10), channel_id=1, source_target_pairs={{0,12},{4,8},{8,4},{12,0},{1,13},{5,9},{9,5},{13,1},{2,14},{6,10},... | collective-permute-start | bytes 96008 | tf_op jit(solution)/shard_map/ppermute | solution.py:996
  8.7 0.0 collective-permute-start
  8.7 2.8 %local_part.1.base = f32[288,128]{1,0:T(8,128)} custom-call(f32[5,5,2,160]{3,2,1,0:T(2,128)} %bitcast.15, f32[5,5,2,160]{3,2,1,0:T(2,128)} %bitcast.12, f32[5,5,160]{2,1,0:T(8,128)} %kappa_in.1, s32[6,1,1,32]{3,2,1,0:T(1,128)} %flags_in.1, f32[64,64]{1,0:T(8,128)} %constant.4.clone.rows_in, f32[160,320]{1,0:T(8,128)} %constant.5.clone.lines_in), custom_call_target="tpu_custom_call" | custom-call | tf_op jit(solution)/shard_map/local_part/pallas_call | solution.py:576
  11.5 0.0 collective-permute-done.3.y3
  11.5 0.0 collective-permute-done.2.y1
  11.5 0.0 collective-permute-done.1.x3
  11.5 1.5 %collective-permute-done.x1 = f32[5,5,2,160]{3,2,1,0:T(2,128)S(1)} collective-permute-done((f32[5,5,2,160]{3,2,1,0:T(2,128)}, f32[5,5,2,160]{3,2,1,0:T(2,128)S(1)}, u32[]{:S(2)}, u32[]{:S(2)}) %collective-permute-start) | collective-permute-done | bytes 32032 | tf_op jit(solution)/shard_map/ppermute | solution.py:996
  13.1 0.0 copy-start
  13.1 0.9 %copy-done = f32[288,128]{1,0:T(8,128)S(1)} copy-done((f32[288,128]{1,0:T(8,128)S(1)}, f32[288,128]{1,0:T(8,128)}, u32[]{:S(2)}) %copy-start) | copy-done | bytes 147480
  14.0 0.4 halo_part.1
  14.3 0.1 collective-permute-start.4
  14.4 1.2 %collective-permute-done.4 = f32[64,128]{1,0:T(8,128)S(1)} collective-permute-done((f32[64,128]{1,0:T(8,128)S(1)}, f32[64,128]{1,0:T(8,128)S(1)}, u32[]{:S(2)}, u32[]{:S(2)}) %collective-permute-start.4) | collective-permute-done | bytes 32800 | tf_op jit(solution)/shard_map/ppermute | solution.py:996
  15.6 10.7 %all_to_all.10 = f32[4,96,128]{2,1,0:T(8,128)S(1)} all-to-all(f32[4,96,128]{2,1,0:T(8,128)S(1)} %broadcast_in_dim.6), channel_id=1, replica_groups=mesh['section'=2,'gx'=4,'gy'=4] {'gx'}, dimensions={0} | all-to-all | bytes 393216 | tf_op jit(solution)/shard_map/all_to_all | solution.py:1001
  26.3 0.1 broadcast_in_dim.7
  26.4 12.3 %all_to_all.11 = f32[4,384,128]{2,1,0:T(8,128)S(1)} all-to-all(f32[4,384,128]{2,1,0:T(8,128)S(1)} %broadcast_in_dim.7), channel_id=1, replica_groups=mesh['section'=2,'gx'=4,'gy'=4] {'gy'}, dimensions={0} | all-to-all | bytes 1572864 | tf_op jit(solution)/shard_map/all_to_all | solution.py:1001
  38.7 0.4 assemble.1.assembled.own_start
  39.2 0.0 copy-start.1
  39.2 0.1 collective-permute-start.5
  39.3 6.8 %cycle.1.own = f32[1128,128]{1,0:T(8,128)S(1)} custom-call(f32[1536,128]{1,0:T(8,128)S(1)} %bitcast.7, f32[1024,128]{1,0:T(8,128)S(1)} %assemble.1.assembled.own_start), custom_call_target="tpu_custom_call" | custom-call | flops 40000000 | bytes 30000000 | tf_op jit(solution)/shard_map/cycle/pallas_call | solution.py:967
  46.1 0.0 collective-permute-done.5.other_start
  46.1 0.6 %collective-permute-start.6 = (f32[1128,128]{1,0:T(8,128)S(1)}, f32[1128,128]{1,0:T(8,128)S(1)}, u32[]{:S(2)}, u32[]{:S(2)}) collective-permute-start(f32[1128,128]{1,0:T(8,128)S(1)} %cycle.1.own), channel_id=1, source_target_pairs={{0,16},{16,0},{1,17},{17,1},{2,18},{18,2},{3,19},{19,3},{4,20},{20... | collective-permute-start | bytes 1732616 | tf_op jit(solution)/shard_map/ppermute | solution.py:996
  46.7 1.6 %collective-permute-done.6.other = f32[1128,128]{1,0:T(8,128)S(1)} collective-permute-done((f32[1128,128]{1,0:T(8,128)S(1)}, f32[1128,128]{1,0:T(8,128)S(1)}, u32[]{:S(2)}, u32[]{:S(2)}) %collective-permute-start.6) | collective-permute-done | bytes 577568 | tf_op jit(solution)/shard_map/ppermute | solution.py:996
  48.3 0.0 copy-done.1
  48.3 1.8 %finish.1 = (f32[5,5,2,160]{3,2,1,0:T(2,128)}, f32[5,5,2,160]{3,2,1,0:T(2,128)}, f32[3]{0:T(128)}) custom-call(f32[1128,128]{1,0:T(8,128)S(1)} %cycle.1.own, f32[1128,128]{1,0:T(8,128)S(1)} %collective-permute-done.6.other, f32[1024,128]{1,0:T(8,128)S(1)} %assemble.1.assembled.own_start, f32[1024,128]{1,0:T(8,128)S(1)} %collective-permute-done.5.other_start, ...), custom_call_target="tpu_custom_call" | custom-call | tf_op jit(solution)/shard_map/finish/pallas_call | solution.py:980
  (4 shorter events, 0.0 us)
Async XLA Ops:
  0.6 10.9 %collective-permute-start.3 = (f32[5,5,2,160]{3,2,1,0:T(2,128)}, f32[5,5,2,160]{3,2,1,0:T(2,128)S(1)}, u32[]{:S(2)}, u32[]{:S(2)}) collective-permute-start(f32[5,5,2,160]{3,2,1,0:T(2,128)} %bitcast.8), channel_id=1, source_target_pairs={{0,3},{1,2},{2,1},{3,0},{4,7},{5,6},{6,5},{7,4},{8,11},{9,10},{10,... | collective-permute-start | bytes 96008 | tf_op jit(solution)/shard_map/ppermute | solution.py:996
  4.6 6.9 %collective-permute-start.2 = (f32[5,5,2,160]{3,2,1,0:T(2,128)}, f32[5,5,2,160]{3,2,1,0:T(2,128)S(1)}, u32[]{:S(2)}, u32[]{:S(2)}) collective-permute-start(f32[5,5,2,160]{3,2,1,0:T(2,128)} %bitcast.9), channel_id=1, source_target_pairs={{0,1},{1,0},{2,3},{3,2},{4,5},{5,4},{6,7},{7,6},{8,9},{9,8},{10,11... | collective-permute-start | bytes 96008 | tf_op jit(solution)/shard_map/ppermute | solution.py:996
  5.1 6.4 %collective-permute-start.1 = (f32[5,5,2,160]{3,2,1,0:T(2,128)}, f32[5,5,2,160]{3,2,1,0:T(2,128)S(1)}, u32[]{:S(2)}, u32[]{:S(2)}) collective-permute-start(f32[5,5,2,160]{3,2,1,0:T(2,128)} %bitcast.10), channel_id=1, source_target_pairs={{0,12},{4,8},{8,4},{12,0},{1,13},{5,9},{9,5},{13,1},{2,14},{6,10},... | collective-permute-start | bytes 96008 | tf_op jit(solution)/shard_map/ppermute | solution.py:996
  8.7 4.3 %collective-permute-start = (f32[5,5,2,160]{3,2,1,0:T(2,128)}, f32[5,5,2,160]{3,2,1,0:T(2,128)S(1)}, u32[]{:S(2)}, u32[]{:S(2)}) collective-permute-start(f32[5,5,2,160]{3,2,1,0:T(2,128)} %bitcast.11), channel_id=1, source_target_pairs={{0,4},{4,0},{8,12},{12,8},{1,5},{5,1},{9,13},{13,9},{2,6},{6,2},{1... | collective-permute-start | bytes 96008 | tf_op jit(solution)/shard_map/ppermute | solution.py:996
  13.1 0.9 %copy-start = (f32[288,128]{1,0:T(8,128)S(1)}, f32[288,128]{1,0:T(8,128)}, u32[]{:S(2)}) copy-start(f32[288,128]{1,0:T(8,128)} %local_part.1.base) | copy-start | bytes 442372
  14.3 1.3 %collective-permute-start.4 = (f32[64,128]{1,0:T(8,128)S(1)}, f32[64,128]{1,0:T(8,128)S(1)}, u32[]{:S(2)}, u32[]{:S(2)}) collective-permute-start(f32[64,128]{1,0:T(8,128)S(1)} %get-tuple-element.11), channel_id=1, source_target_pairs={{0,16},{16,0},{1,17},{17,1},{2,18},{18,2},{3,19},{19,3},{4,20},{20... | collective-permute-start | bytes 98312 | tf_op jit(solution)/shard_map/ppermute | solution.py:996
  39.2 9.1 %copy-start.1 = (f32[2,5,5,160]{3,0,2,1:T(2,128)S(1)}, f32[2,5,5,160]{3,0,2,1:T(2,128)}, u32[]{:S(2)}) copy-start(f32[2,5,5,160]{3,0,2,1:T(2,128)} %param.7) | copy-start | bytes 96004
  39.2 6.9 %collective-permute-start.5 = (f32[1024,128]{1,0:T(8,128)S(1)}, f32[1024,128]{1,0:T(8,128)S(1)}, u32[]{:S(2)}, u32[]{:S(2)}) collective-permute-start(f32[1024,128]{1,0:T(8,128)S(1)} %assemble.1.assembled.own_start), channel_id=1, source_target_pairs={{0,16},{16,0},{1,17},{17,1},{2,18},{18,2},{3,19},{19,3},{4,20},{20... | collective-permute-start | bytes 1572872 | tf_op jit(solution)/shard_map/ppermute | solution.py:996
  46.1 2.2 %collective-permute-start.6 = (f32[1128,128]{1,0:T(8,128)S(1)}, f32[1128,128]{1,0:T(8,128)S(1)}, u32[]{:S(2)}, u32[]{:S(2)}) collective-permute-start(f32[1128,128]{1,0:T(8,128)S(1)} %cycle.1.own), channel_id=1, source_target_pairs={{0,16},{16,0},{1,17},{17,1},{2,18},{18,2},{3,19},{19,3},{4,20},{20... | collective-permute-start | bytes 1732616 | tf_op jit(solution)/shard_map/ppermute | solution.py:996

commit v6 on v4

--- a/solution.py
+++ b/solution.py
@@ -351,7 +351,9 @@
 EZ = 32
 COLS = 16
 HALF = 64
-PIECE = 96
+TRACE = 40
+PIECE = HALF + TRACE
+COEFS = 40
 FIELD = 1000
 F32 = jnp.float32
 
@@ -444,8 +446,17 @@
 
 
 def pack_nodes(nodes):
-    odd = iota((HALF, 128), 1) // EZ % 2 == 1
-    return jnp.where(odd, nodes[HALF:, :], nodes[:HALF, :])
+    half = nodes.shape[0] // 2
+    odd = iota((half, 128), 1) // EZ % 2 == 1
+    return jnp.where(odd, nodes[half:, :], nodes[:half, :])
+
+
+def face_place(i, j):
+    if i == 0:
+        return j
+    if i == 4:
+        return 11 + j
+    return 3 + 2 * i + (0 if j == 0 else 1)
 
 
 def fetch(pairs, sems):
@@ -456,9 +467,28 @@
         copy.wait()
 
 
+def coefs_kernel(kappa_in, flags_in, out, kappa, flags, sems, kap, krep):
+    fetch([(kappa_in, kappa), (flags_in, flags)], sems)
+    kap[...] = jnp.zeros_like(kap)
+    for i in range(5):
+        kap[5 * i : 5 * i + 5, :] = kappa[i]
+    coefs = kap[...]
+    krep[...] = jnp.zeros_like(krep)
+    for k in range(5):
+        krep[25 * k : 25 * k + 25, :] = split_dot(coefs, pick_line(k))[:25]
+    out[:32, :] = choose(iota((32, 128), 1) // EZ, [krep[32 * q : 32 * q + 32, :] for q in range(4)])
+    flag = flags[:, 0, 0, :].astype(F32)
+    repeat = (iota((EZ, 128), 1) % EZ == iota((EZ, 128), 0)).astype(F32)
+    shown = split_dot(flag, repeat)
+    group = iota((1, 128), 1) // EZ
+    out[32:40, :] = jnp.zeros((8, 128), F32)
+    out[32:33, :] = choose(group, [shown[d : d + 1] for d in range(4)])
+    out[33:34, :] = choose(group, [shown[4:5], shown[5:6]])
+
+
 def local_kernel(
-    rhs_in, guess_in, kappa_in, flags_in, rows_in, lines_in, base,
-    rhs, guess, kappa, flags, rows_t, lines_t, sems, x, kap, stack, own_nodes, other_nodes, krep,
+    rhs_in, guess_in, kappa_in, flags_in, rows_in, lines_in, mine, theirs,
+    rhs, guess, kappa, flags, rows_t, lines_t, sems, x, kap, stack, nodes, traces,
 ):
     sec = lax.axis_index("section")
     fetch(
@@ -487,10 +517,6 @@
     gx = jnp.where(row < 5, gains[0], jnp.where((row >= 20) & (row < 25), gains[1], none))
     gy = jnp.where(row % 5 == 0, gains[2], jnp.where(row % 5 == 4, gains[3], none))
     gz = jnp.where(lane == 0, gains[4], jnp.where(lane == 4, gains[5], none))
-    gy = jnp.where(row < 25, gy, none)
-    for place, gain in ((160, gx), (192, gy)):
-        base[place : place + 32, :] = gain[:, :128]
-        base[64 + place : 96 + place, :EZ] = gain[:, 128:]
     field = x[...]
     along = exact_dot(rows_t[...], field)
     across = exact_dot(field, lines_t[...])
@@ -499,67 +525,31 @@
         r = slice(s * 32, s * 32 + 32)
         image = own * field[r] + along[r] + across[r, :160] - gz * across[r, 160:]
         stack[64 + s * 32 : 96 + s * 32, :] = image
-    whole, back, back_matrix, blocks, cross = split_sections()
-    own_nodes[...] = jnp.zeros_like(own_nodes)
-    other_nodes[...] = jnp.zeros_like(other_nodes)
-    krep[...] = jnp.zeros_like(krep)
-    stack[128:, :] = kap[...]
+    stack[128:, :] = field
     source = stack[...]
+    back, back_matrix = split_sections()[1:3]
+    nodes[...] = jnp.zeros_like(nodes)
     for k in range(5):
         parts = split_dot(source, pick_line(k))
-        for target, mark in ((own_nodes, True), (other_nodes, False)):
+        for p, mark in enumerate((True, False)):
             total = jnp.zeros((32, 128), F32)
+            trace = jnp.zeros((32, 128), F32)
             for s in range(2):
                 total = total + pair_factors(sec, back, mark, s) * parts[s * 32 : s * 32 + 32]
-                factor = pair_factors(sec, -STEP_SIZE * back_matrix, mark, s)
-                total = total + factor * parts[64 + s * 32 : 96 + s * 32]
-            target[25 * k : 25 * k + 25, :] = total[:25]
-        krep[25 * k : 25 * k + 25, :] = parts[128:153]
-    repeat = (iota((EZ, 128), 1) % EZ == iota((EZ, 128), 0)).astype(F32)
-    shown = split_dot(flag, repeat)
-    upper = iota((1, 128), 1) < 64
-    for r in range(3):
-        own_nodes[125 + r : 126 + r, :] = jnp.where(upper, shown[2 * r : 2 * r + 1], shown[2 * r + 1 : 2 * r + 2])
-    base[:HALF, :] = pack_nodes(own_nodes)
-    base[PIECE : PIECE + HALF, :] = pack_nodes(other_nodes)
-    base[HALF:PIECE, :] = choose(iota((32, 128), 1) // EZ, [krep[32 * q : 32 * q + 32, :] for q in range(4)])
-
-
-def halo_kernel(base, x1, x3, y1, y3, mine, theirs, near, own_nodes, other_nodes):
-    sec = lax.axis_index("section")
-    even_x = lax.axis_index("gx") % 2 == 0
-    even_y = lax.axis_index("gy") % 2 == 0
-    for ref in (near, own_nodes, other_nodes):
-        ref[...] = jnp.zeros_like(ref)
-    for m in range(5):
-        for s in range(2):
-            r = s * 32
-            one = slice(s, s + 1)
-            near[r + m : r + m + 1, :] = jnp.where(even_x, x3[4, m, one, :], x1[4, m, one, :])
-            near[r + 20 + m : r + 21 + m, :] = jnp.where(even_x, x1[0, m, one, :], x3[0, m, one, :])
-            r += 64
-            near[r + 5 * m : r + 5 * m + 1, :] = jnp.where(even_y, y3[m, 4, one, :], y1[m, 4, one, :])
-            near[r + 5 * m + 4 : r + 5 * m + 5, :] = jnp.where(even_y, y1[m, 0, one, :], y3[m, 0, one, :])
-    gx, gy = (
-        jnp.concatenate([base[r : r + 32, :], base[64 + r : 96 + r, :EZ]], axis=1) for r in (160, 192)
-    )
-    parts_in = []
-    for s in range(2):
-        r = s * 32
-        parts_in.append(gx * near[r : r + 32, :] + gy * near[64 + r : 96 + r, :])
-    source = jnp.concatenate(parts_in, axis=0)
-    back_matrix = split_sections()[2]
-    for k in range(5):
-        parts = split_dot(source, pick_line(k))
-        for target, mark in ((own_nodes, True), (other_nodes, False)):
-            total = jnp.zeros((32, 128), F32)
-            for s in range(2):
                 factor = pair_factors(sec, STEP_SIZE * back_matrix, mark, s)
-                total = total + factor * parts[s * 32 : s * 32 + 32]
-            target[25 * k : 25 * k + 25, :] = total[:25]
-    mine[:HALF, :] = base[:HALF, :] + pack_nodes(own_nodes)
-    mine[HALF:, :] = base[HALF:PIECE, :]
-    theirs[...] = base[PIECE : PIECE + HALF, :] + pack_nodes(other_nodes)
+                total = total - factor * parts[64 + s * 32 : 96 + s * 32]
+                trace = trace + factor * parts[128 + s * 32 : 160 + s * 32]
+            nodes[128 * p + 25 * k : 128 * p + 25 * k + 25, :] = total[:25]
+            start = 80 * p + 16 * k
+            traces[start : start + 5, :] = trace[:5]
+            for i in range(1, 4):
+                for j in (0, 4):
+                    r = start + face_place(i, j)
+                    traces[r : r + 1, :] = trace[5 * i + j : 5 * i + j + 1]
+            traces[start + 11 : start + 16, :] = trace[20:25]
+    for p, out in enumerate((mine, theirs)):
+        out[:HALF, :] = pack_nodes(nodes[128 * p : 128 * p + 128, :])
+        out[HALF:, :] = pack_nodes(traces[80 * p : 80 * p + 80, :])
 
 
 VMEM = pl.BlockSpec(memory_space=pltpu.VMEM)
@@ -568,6 +558,20 @@
 
 def limit(mib):
     return pltpu.CompilerParams(vmem_limit_bytes=mib * 2**20)
+
+
+def coefs_part(kappa, flags):
+    operands = (kappa, flags)
+    return pl.pallas_call(
+        coefs_kernel,
+        out_shape=jax.ShapeDtypeStruct((COEFS, 128), F32),
+        in_specs=[HBM] * 2,
+        out_specs=VMEM,
+        scratch_shapes=[pltpu.VMEM(o.shape, o.dtype) for o in operands]
+        + [pltpu.SemaphoreType.DMA((2,)), pltpu.VMEM((32, 160), F32), pltpu.VMEM((128, 128), F32)],
+        compiler_params=limit(60),
+        name="coefs_part",
+    )(*operands)
 
 
 def local_part(rhs, guess, kappa, flags):
@@ -575,45 +579,30 @@
     operands = (rhs, guess, kappa, flags, jnp.asarray(rows_t), jnp.asarray(lines_t))
     return pl.pallas_call(
         local_kernel,
-        out_shape=jax.ShapeDtypeStruct((288, 128), F32),
+        out_shape=[jax.ShapeDtypeStruct((PIECE, 128), F32)] * 2,
         in_specs=[HBM] * 6,
-        out_specs=VMEM,
+        out_specs=[VMEM] * 2,
         scratch_shapes=[pltpu.VMEM(o.shape, o.dtype) for o in operands]
         + [
             pltpu.SemaphoreType.DMA((6,)),
             pltpu.VMEM((64, 160), F32),
             pltpu.VMEM((32, 160), F32),
-            pltpu.VMEM((160, 160), F32),
-            pltpu.VMEM((128, 128), F32),
-            pltpu.VMEM((128, 128), F32),
-            pltpu.VMEM((128, 128), F32),
+            pltpu.VMEM((192, 160), F32),
+            pltpu.VMEM((256, 128), F32),
+            pltpu.VMEM((160, 128), F32),
         ],
         compiler_params=limit(60),
+        cost_estimate=pl.CostEstimate(flops=20_000_000, bytes_accessed=8_000_000, transcendentals=0),
         name="local_part",
     )(*operands)
-
-
-def halo_part(base, halos):
-    return pl.pallas_call(
-        halo_kernel,
-        out_shape=[
-            jax.ShapeDtypeStruct((PIECE, 128), F32),
-            jax.ShapeDtypeStruct((HALF, 128), F32),
-        ],
-        in_specs=[VMEM] * 5,
-        out_specs=[VMEM] * 2,
-        scratch_shapes=[pltpu.VMEM((128, 160), F32)] + [pltpu.VMEM((128, 128), F32)] * 2,
-        compiler_params=limit(16),
-        name="halo_part",
-    )(base, *halos)
 
 
 class Level:
     def __init__(self, count, refs):
         self.count = count
-        self.diag, self.jac, self.x, self.dir, self.res, self.f = refs
+        self.x, self.dir, self.res, self.f = refs
         self.tables = [element_matrix(count, d) for d in range(3)]
-        self.gains = None
+        self.gains = self.diag = self.jac = None
 
 
 def tile(index):
@@ -624,22 +613,79 @@
     return pieces[pl.ds(8 * h * size + r, 8, stride=size), :]
 
 
-def place_pieces(blocks, pieces, first, size):
+def place_pieces(blocks, stride, pieces, first, size):
     my_gx, my_gy = lax.axis_index("gx"), lax.axis_index("gy")
     for b, block in enumerate(blocks):
         for a in range(4):
             column = (my_gx ^ a) * 4 + (my_gy ^ b)
             start = pl.multiple_of(column * size, 8)
-            pieces[pl.ds(start, size), :] = block[a * PIECE + first : a * PIECE + first + size, :]
-
-
-def assemble_kernel(block0, block1, block2, block3, field, pieces):
-    place_pieces((block0, block1, block2, block3), pieces, 0, HALF)
-    odd = iota((8, 128), 1) // EZ % 2 == 1
-    for r in range(HALF):
-        low, high = rows_of(pieces, HALF, r, 0), rows_of(pieces, HALF, r, 1)
-        field[tile(r), :] = jnp.where(odd, pltpu.roll(high, 32, 1), low)
-        field[tile(HALF + r), :] = jnp.where(odd, high, pltpu.roll(low, 96, 1))
+            pieces[pl.ds(start, size), :] = block[a * stride + first : a * stride + first + size, :]
+
+
+class Lanes:
+    def __init__(self):
+        self.lane = iota((8, 128), 1)
+        sub = iota((8, 128), 0)
+        self.group = self.lane // EZ
+        self.odd = self.group % 2 == 1
+        self.element = self.lane % EZ
+        self.place = sub % 4
+        self.low_half = sub < 4
+
+    def around(self, u):
+        turned = pltpu.roll(u, 4, u.ndim - 2)
+        far = jnp.where(self.odd, pltpu.roll(turned, 32, u.ndim - 1), pltpu.roll(turned, 96, u.ndim - 1))
+        return turned, far
+
+    def x_before(self, u):
+        turned, far = self.around(u)
+        return jnp.where(self.low_half, far, turned)
+
+    def x_after(self, u):
+        turned, far = self.around(u)
+        return jnp.where(self.low_half, turned, far)
+
+    def y_before(self, u):
+        return jnp.where(self.place == 0, pltpu.roll(u, 5, 0), pltpu.roll(u, 1, 0))
+
+    def y_after(self, u):
+        return jnp.where(self.place == 3, pltpu.roll(u, 3, 0), pltpu.roll(u, 7, 0))
+
+    def z_before(self, u):
+        return jnp.where(self.element == 0, pltpu.roll(u, 97, u.ndim - 1), pltpu.roll(u, 1, u.ndim - 1))
+
+    def z_after(self, u):
+        last = self.element == EZ - 1
+        return jnp.where(last, pltpu.roll(u, 31, u.ndim - 1), pltpu.roll(u, 127, u.ndim - 1))
+
+
+def assemble_kernel(block0, block1, block2, block3, coefs, field, pieces, edges, traces):
+    blocks = (block0, block1, block2, block3)
+    place_pieces(blocks, PIECE, pieces, 0, HALF)
+    place_pieces(blocks, PIECE, edges, HALF, TRACE)
+    lanes = Lanes()
+
+    def widen(source, size, target):
+        for r in range(size):
+            low, high = rows_of(source, size, r, 0), rows_of(source, size, r, 1)
+            target[tile(r), :] = jnp.where(lanes.odd, pltpu.roll(high, 32, 1), low)
+            target[tile(size + r), :] = jnp.where(lanes.odd, high, pltpu.roll(low, 96, 1))
+
+    widen(edges, TRACE, traces)
+    widen(pieces, HALF, field)
+    gains = [coefs[tile(GAINS[0] + d), :] for d in range(4)]
+    for k in range(5):
+        def trace(i, j, k=k):
+            return traces[tile(k * 16 + face_place(i, j)), :]
+
+        for m in range(5):
+            for where, term in (
+                (m, gains[0] * lanes.x_before(trace(4, m))),
+                (20 + m, gains[1] * lanes.x_after(trace(0, m))),
+                (5 * m, gains[2] * lanes.y_before(trace(m, 4))),
+                (5 * m + 4, gains[3] * lanes.y_after(trace(m, 0))),
+            ):
+                field[tile(k * 25 + where), :] = field[tile(k * 25 + where), :] + term
 
 
 def load(ref, first, count):
@@ -652,18 +698,59 @@
     ref[pl.ds(start, value.shape[0] * 8), :] = value.reshape(value.shape[0] * 8, 128)
 
 
-def cycle_kernel(block0, block1, block2, block3, assembled, fields, *scratch):
+DIAGS = (0, 250, 304)
+GAINS = (320, 326, 332)
+REGISTERS = 338
+CENTRE = (CHEB_HIGH + CHEB_LOW) / 2.0
+RADIUS = (CHEB_HIGH - CHEB_LOW) / 2.0
+
+
+def setup_kernel(block0, block1, block2, block3, coefs, pieces, kap):
+    place_pieces((block0, block1, block2, block3), COEFS, pieces, 0, COEFS)
+    lanes = Lanes()
+    group = lanes.group
+
+    def widen(r):
+        turned = []
+        for h in range(2):
+            got = rows_of(pieces, COEFS, r, h)
+            turned.append([pltpu.roll(got, 32 * m, 1) if m else got for m in range(4)])
+        return [choose(group, [turned[g % 2][(g - q) % 4] for g in range(4)]) for q in range(4)]
+
+    for r in range(32):
+        for q, part in enumerate(widen(r)):
+            kap[tile(q * 32 + r), :] = part
+    flags = widen(32) + widen(33)[:2]
+    for p, n in enumerate((5, 3, 2)):
+        stride = 4 // (n - 1)
+        gains = [face_gains(flags[d], d // 2, d % 2, n) for d in range(6)]
+        rows = []
+        for d in range(3):
+            coefs[tile(GAINS[p] + 2 * d), :] = gains[2 * d]
+            coefs[tile(GAINS[p] + 2 * d + 1), :] = gains[2 * d + 1]
+            table = element_matrix(n, d)
+            row = [jnp.full((8, 128), float(table[m, m]), F32) for m in range(n)]
+            row[0] = row[0] + gains[2 * d]
+            row[n - 1] = row[n - 1] + gains[2 * d + 1]
+            rows.append(row)
+        along = jnp.stack(rows[1])
+        for k in range(n):
+            for i in range(n):
+                line = load(kap, k * 25 * stride + i * stride * 5, 5)
+                line = jnp.stack([line[j * stride] for j in range(n)])
+                value = line + (along + (rows[2][k] + rows[0][i]))
+                scale = 1.0 / (1.0 + STEP_SIZE * JACOBI_SCALE * value)
+                store(coefs, DIAGS[p] + (k * n + i) * n, value)
+                store(coefs, DIAGS[p] + n**3 + (k * n + i) * n, scale * (1.0 / CENTRE))
+
+
+def cycle_kernel(coefs, assembled, fields, *scratch):
     sec = lax.axis_index("section")
     my_gx, my_gy = lax.axis_index("gx"), lax.axis_index("gy")
-    levels = [Level(n, scratch[6 * p : 6 * p + 6]) for p, n in enumerate((5, 3, 2))]
-    pieces, kap, half, terms = scratch[18:22]
-    lane = iota((8, 128), 1)
-    sub = iota((8, 128), 0)
-    group = lane // EZ
-    odd = group % 2 == 1
-    element = lane % EZ
-    place = sub % 4
-    low_half = sub < 4
+    levels = [Level(n, scratch[4 * p : 4 * p + 4]) for p, n in enumerate((5, 3, 2))]
+    half = scratch[12]
+    lanes = Lanes()
+    lane = lanes.lane
     blocks = split_sections()[3]
 
     def lanes_of(upper, lower):
@@ -672,83 +759,36 @@
     entry = [[[float(STEP_SIZE * blocks[2 * p + a, 2 * p + b]) for p in range(2)] for b in range(2)] for a in range(2)]
     same = lanes_of(entry[0][0], entry[1][1])
     swap = lanes_of(entry[0][1], entry[1][0])
-    centre = (CHEB_HIGH + CHEB_LOW) / 2.0
-    radius = (CHEB_HIGH - CHEB_LOW) / 2.0
-    first_rho = radius / centre
-    second_rho = 1.0 / (2.0 * centre / radius - first_rho)
+    first_rho = RADIUS / CENTRE
+    second_rho = 1.0 / (2.0 * CENTRE / RADIUS - first_rho)
     keep = 1.0 + second_rho * first_rho
-    push = 2.0 * second_rho / radius * centre
-
-    flags = []
-    for r in range(3):
-        got = assembled[tile(125 + r), :]
-        across = pltpu.roll(got, 64, 1)
-        flags += [jnp.where(lane < 64, got, across), jnp.where(lane < 64, across, got)]
-    place_pieces((block0, block1, block2, block3), pieces, HALF, 32)
-
-    for r in range(32):
-        turned = []
-        for h in range(2):
-            got = rows_of(pieces, 32, r, h)
-            turned.append([pltpu.roll(got, 32 * m, 1) if m else got for m in range(4)])
-        for q in range(4):
-            kap[tile(q * 32 + r), :] = choose(group, [turned[g % 2][(g - q) % 4] for g in range(4)])
-
-    for level in levels:
-        n = level.count
-        stride = 4 // (n - 1)
-        level.gains = [face_gains(flags[d], d // 2, d % 2, n) for d in range(6)]
-        rows = []
-        for d in range(3):
-            row = [jnp.full((8, 128), float(level.tables[d][m, m]), F32) for m in range(n)]
-            row[0] = row[0] + level.gains[2 * d]
-            row[n - 1] = row[n - 1] + level.gains[2 * d + 1]
-            rows.append(row)
-        for m in range(n):
-            terms[tile(m), :] = rows[2][m]
-
-        def diagonals(k, carry, level=level, n=n, stride=stride, rows=rows):
-            along = jnp.stack(rows[1])
-            for i in range(n):
-                line = load(kap, k * 25 * stride + i * stride * 5, 5)
-                line = jnp.stack([line[j * stride] for j in range(n)])
-                value = line + (along + (load(terms, k, 1) + rows[0][i]))
-                scale = 1.0 / (1.0 + STEP_SIZE * JACOBI_SCALE * value)
-                store(level.diag, (k * n + i) * n, value)
-                store(level.jac, (k * n + i) * n, scale * (1.0 / centre))
-            return carry
-        lax.fori_loop(0, n, diagonals, 0)
+    push = 2.0 * second_rho / RADIUS * CENTRE
+    for p, level in enumerate(levels):
+        size = level.count**3
+        level.gains = [coefs[tile(GAINS[p] + d), :] for d in range(6)]
+        level.diag = lambda first, count, p=p: load(coefs, DIAGS[p] + first, count)
+        level.jac = lambda first, count, p=p, size=size: load(coefs, DIAGS[p] + size + first, count)
 
     def begin(level, source):
         n = level.count
-
-        def start(k, carry):
-            first = k * n * n
-            f = load(source, first, n * n)
-            store(level.dir, first, load(level.jac, first, n * n) * f)
+        for first in range(0, n**3, n):
+            f = load(source, first, n)
+            store(level.dir, first, level.jac(first, n) * f)
             store(level.res, first, f)
             store(level.x, first, jnp.zeros_like(f))
-            return carry
-        lax.fori_loop(0, n, start, 0)
 
     def apply(level, smooth):
         n = level.count
         kx, ky, kz = level.tables
+        gains = level.gains
         source = level.dir if smooth else level.x
-
-        def around(u):
-            turned = pltpu.roll(u, 4, 1)
-            return turned, jnp.where(odd, pltpu.roll(turned, 32, 2), pltpu.roll(turned, 96, 2))
-
         for k in range(n):
             here = k * n * n
             v = [load(source, here + i * n, n) for i in range(n)]
-            left, left_far = around(v[n - 1])
-            right, right_far = around(v[0])
             waiting = []
             for i in range(n):
                 first = here + i * n
-                total = load(level.diag, first, n) * v[i]
+                total = level.diag(first, n) * v[i]
                 for m in range(n):
                     if m != i:
                         total = total + float(kx[i, m]) * v[m]
@@ -763,35 +803,27 @@
                             term = float(ky[j, m]) * v[i][m]
                             line = term if line is None else line + term
                     if j == 0:
-                        u = v[i][n - 1]
-                        moved = jnp.where(place == 0, pltpu.roll(u, 5, 0), pltpu.roll(u, 1, 0))
-                        line = line - level.gains[2] * moved
+                        line = line - gains[2] * lanes.y_before(v[i][n - 1])
                     if j == n - 1:
-                        u = v[i][0]
-                        moved = jnp.where(place == 3, pltpu.roll(u, 3, 0), pltpu.roll(u, 7, 0))
-                        line = line - level.gains[3] * moved
+                        line = line - gains[3] * lanes.y_after(v[i][0])
                     lines.append(line)
                 total = total + jnp.stack(lines)
                 if i == 0:
-                    total = total - level.gains[0] * jnp.where(low_half, left_far, left)
+                    total = total - gains[0] * lanes.x_before(v[n - 1])
                 if i == n - 1:
-                    total = total - level.gains[1] * jnp.where(low_half, right, right_far)
+                    total = total - gains[1] * lanes.x_after(v[0])
                 if k == 0:
-                    u = load(source, ((n - 1) * n + i) * n, n)
-                    moved = jnp.where(element == 0, pltpu.roll(u, 97, 2), pltpu.roll(u, 1, 2))
-                    total = total - level.gains[4] * moved
+                    total = total - gains[4] * lanes.z_before(load(source, ((n - 1) * n + i) * n, n))
                 if k == n - 1:
-                    u = load(source, i * n, n)
-                    moved = jnp.where(element == EZ - 1, pltpu.roll(u, 31, 2), pltpu.roll(u, 127, 2))
-                    total = total - level.gains[5] * moved
+                    total = total - gains[5] * lanes.z_after(load(source, i * n, n))
                 image = v[i] + (same * total + swap * pltpu.roll(total, 64, 2))
                 if smooth:
-                    scaled = load(level.jac, first, n) * (load(level.res, first, n) - image)
+                    scaled = level.jac(first, n) * (load(level.res, first, n) - image)
                     waiting.append((level.x, first, load(level.x, first, n) + keep * v[i] + push * scaled))
                 else:
                     rest = load(level.f, first, n) - image
                     waiting.append((level.res, first, rest))
-                    waiting.append((level.dir, first, load(level.jac, first, n) * rest))
+                    waiting.append((level.dir, first, level.jac(first, n) * rest))
                 if i % 2 == 1 or i == n - 1:
                     for place_out in waiting:
                         store(*place_out)
@@ -807,23 +839,17 @@
 
     def change(table, source, target, add):
         m, n = table.shape
-
-        def outer(i, carry):
+        for i in range(n):
             parts = [load(source, i * n + k * n * n, n) for k in range(n)]
             for k in range(m):
                 store(half, i * n + k * n * n, combine(table[k], parts))
-            return carry
-        lax.fori_loop(0, n, outer, 0)
-
-        def inner(k, carry):
+        for k in range(m):
             parts = [load(half, k * n * n + i * n, n) for i in range(n)]
             for i in range(m):
                 line = combine(table[i], parts)
                 value = jnp.stack([combine(table[j], [line[a] for a in range(n)]) for j in range(m)])
                 first = k * m * m + i * m
                 store(target, first, load(target, first, m) + value if add else value)
-            return carry
-        lax.fori_loop(0, m, inner, 0)
 
     def down(n, m):
         fine_nodes, fine_weights = lobatto(n)
@@ -865,10 +891,8 @@
     begin(fine, assembled)
     solve(0)
 
-    def give(k, carry):
-        store(fields, k * 25, load(fine.res, k * 25, 25))
-        return carry
-    lax.fori_loop(0, 5, give, 0)
+    for first in range(0, 125, 5):
+        store(fields, first, load(fine.res, first, 5))
     column = (my_gx % 2) * 4 + my_gy
     fields[FIELD : FIELD + 125, :] = fine.x[pl.ds(column, 125, stride=8), :]
     fields[FIELD + 125 : FIELD + 128, :] = jnp.zeros((3, 128), F32)
@@ -943,38 +967,50 @@
                 res_out[i, j, s : s + 1, :] = outs[64 + s * 32 + r : 64 + s * 32 + r + 1, :]
 
 
-def assemble(blocks):
+def setup(blocks):
+    return pl.pallas_call(
+        setup_kernel,
+        out_shape=jax.ShapeDtypeStruct((REGISTERS * 8, 128), F32),
+        in_specs=[VMEM] * 4,
+        out_specs=VMEM,
+        scratch_shapes=[pltpu.VMEM((COLS * COEFS, 128), F32), pltpu.VMEM((128 * 8, 128), F32)],
+        compiler_params=limit(16),
+        cost_estimate=pl.CostEstimate(flops=4_000_000, bytes_accessed=4_000_000, transcendentals=0),
+        name="setup",
+    )(*blocks)
+
+
+def assemble(blocks, coefs):
     return pl.pallas_call(
         assemble_kernel,
         out_shape=jax.ShapeDtypeStruct((128 * 8, 128), F32),
-        in_specs=[VMEM] * 4,
+        in_specs=[VMEM] * 5,
         out_specs=VMEM,
-        scratch_shapes=[pltpu.VMEM((COLS * HALF, 128), F32)],
+        scratch_shapes=[
+            pltpu.VMEM((COLS * HALF, 128), F32),
+            pltpu.VMEM((COLS * TRACE, 128), F32),
+            pltpu.VMEM((80 * 8, 128), F32),
+        ],
         compiler_params=limit(16),
         name="assemble",
-    )(*blocks)
-
-
-def cycle(blocks, assembled):
+    )(*blocks, coefs)
+
+
+def cycle(coefs, assembled):
     scratch = []
     for n in (5, 3, 2):
-        scratch += [pltpu.VMEM((n**3 * 8, 128), F32)] * 6
-    scratch += [
-        pltpu.VMEM((COLS * 32, 128), F32),
-        pltpu.VMEM((128 * 8, 128), F32),
-        pltpu.VMEM((FIELD, 128), F32),
-        pltpu.VMEM((15 * 8, 128), F32),
-    ]
+        scratch += [pltpu.VMEM((n**3 * 8, 128), F32)] * 4
+    scratch += [pltpu.VMEM((FIELD, 128), F32)]
     return pl.pallas_call(
         cycle_kernel,
         out_shape=jax.ShapeDtypeStruct((FIELD + 128, 128), F32),
-        in_specs=[VMEM] * 5,
+        in_specs=[VMEM] * 2,
         out_specs=VMEM,
         scratch_shapes=scratch,
         compiler_params=limit(24),
         cost_estimate=pl.CostEstimate(flops=40_000_000, bytes_accessed=30_000_000, transcendentals=0),
         name="cycle",
-    )(*blocks, assembled)
+    )(coefs, assembled)
 
 
 def finish(own, other, own_start, other_start, guess):
@@ -999,16 +1035,21 @@
 
 def gathered_body(rhs, guess, kappa, bc_flags):
     rhs, guess = (jnp.transpose(v, (1, 2, 0, 3)) for v in (rhs, guess))
-    halos = [exchange(guess, axis, bits) for axis in ("gx", "gy") for bits in (1, 3)]
-    base = local_part(rhs, guess, kappa, bc_flags)
-    mine, theirs = halo_part(base, halos)
-    got = exchange(theirs, "section", 1)
-    piece = jnp.concatenate([mine[:HALF] + got, mine[HALF:]])
-    line = jnp.concatenate([piece] + [exchange(piece, "gx", bits) for bits in (1, 2, 3)])
+    coefs = coefs_part(kappa, bc_flags)
+    coefs_line = jnp.concatenate([coefs] + [exchange(coefs, "gx", bits) for bits in (1, 2, 3)])
+    mine, theirs = local_part(rhs, guess, kappa, bc_flags)
+    piece = mine + exchange(theirs, "section", 1)
+    piece, coefs_line = lax.optimization_barrier((piece, coefs_line))
+    parts = [exchange(piece, "gx", bits) for bits in (1, 2, 3)]
+    others = [exchange(coefs_line, "gy", bits) for bits in (1, 2, 3)]
+    parts, others = lax.optimization_barrier((parts, others))
+    coefs_blocks = [coefs_line] + others
+    line = jnp.concatenate([piece] + parts)
     blocks = [line] + [exchange(line, "gy", bits) for bits in (1, 2, 3)]
-    start = assemble(blocks)
+    all_coefs = setup(coefs_blocks)
+    start = assemble(blocks, all_coefs)
     other_start = exchange(start, "section", 1)
-    own, other_start = lax.optimization_barrier((cycle(blocks, start), other_start))
+    own, other_start = lax.optimization_barrier((cycle(all_coefs, start), other_start))
     sol, res, arnoldi = finish(own, exchange(own, "section", 1), start, other_start, guess)
     sol, res = (jnp.transpose(v, (2, 0, 1, 3)) for v in (sol, res))
     return sol, res, arnoldi

time: 47.3 us -> 48.3 us (1.021)
  waiting for transfers between devices: 17.4 us -> 13.7 us
  starting transfers between devices: 15.9 us -> 17.9 us
  Pallas kernels: 12.2 us -> 14.1 us
  other arithmetic: 0.01 us -> 1.56 us
  local copies, waits for them, and re-layouts: 0.94 us -> 0.03 us
    ppermute x13 -> x15, waiting for transfers between devices: 17.4 us -> 13.7 us  [exchange(): lax.ppermute(x, axis, [(n, n ^ bits) for n in range(lax.axis_size(axis))])]
    ppermute x13 -> x15, starting transfers between devices: 15.9 us -> 17.9 us  [exchange(): lax.ppermute(x, axis, [(n, n ^ bits) for n in range(lax.axis_size(axis))])]
    pallas_call x2 -> x3, Pallas kernels: 3.14 us -> 4.98 us  [the longest x1 2.81 us: local_part(): pl.pallas_call(local_kernel, out_shape=[jax.ShapeDtypeStruct((PIECE, 128)...]
    unnamed x6 -> x5, local copies, waits for them, and re-layouts: 0.93 us -> 0.02 us
    add x0 -> x1, other arithmetic: none -> 0.82 us  [gathered_body(): piece = mine + exchange(theirs, 'section', 1)]
    concatenate x1, other arithmetic: 0.01 us -> 0.74 us  [gathered_body(): jnp.concatenate([coefs] + [exchange(coefs, 'gx', bits) for bits in (1, 2,...]
  transfers between devices with their start and end apart: 13 -> 15, of which waited for: 7 -> 10; matrix products, arithmetic and copies ran while one was open for 0% -> 2% of each run, Pallas kernels for 20% -> 21%
where the time goes in v6:
time: 48.3 us; the launch traced here: 48 us
  starting transfers between devices  17.9 us (37%)
  Pallas kernels  14.1 us (29%)
  waiting for transfers between devices  13.7 us (28%)
  other arithmetic  1.56 us (3%)
  between operations  0.74 us (2%)
    ppermute x15, starting transfers between devices, exchange(): lax.ppermute(x, axis, [(n, n ^ bits) for n in range(lax.axis_size(axis))])  17.9 us
    ppermute x15, waiting for transfers between devices, exchange(): lax.ppermute(x, axis, [(n, n ^ bits) for n in range(lax.axis_size(axis))])  13.7 us
    pallas_call x1, Pallas kernels, cycle(): pl.pallas_call(cycle_kernel, out_shape=jax.ShapeDtypeStruct((FIELD + 128,...  6.71 us
    pallas_call x1, Pallas kernels, local_part(): pl.pallas_call(local_kernel, out_shape=[jax.ShapeDtypeStruct((PIECE, 128)...  2.81 us
    pallas_call x1, Pallas kernels, finish(): pl.pallas_call(finish_kernel, out_shape=[jax.ShapeDtypeStruct(guess.shape...  1.78 us
    pallas_call x1, Pallas kernels, coefs_part(): pl.pallas_call(coefs_kernel, out_shape=jax.ShapeDtypeStruct((COEFS, 128),...  1.75 us
  transfers between devices with their start and end apart: 15, of which 10 were waited for; matrix products, arithmetic and copies ran while one was open for 2% of the time, Pallas kernels for 21%

profile of v6, /device:TPU:0, one launch (start us, length us, event | category | flops | bytes accessed | tf_op | source)
XLA Modules:
  0.0 48.0 jit_solution(5565745217890277602)
XLA Ops:
  0.6 1.7 %coefs_part.1 = f32[40,128]{1,0:T(8,128)} custom-call(f32[5,5,160]{2,1,0:T(8,128)} %kappa_in.3, s32[6,1,1,32]{3,2,1,0:T(1,128)} %flags_in.3), custom_call_target="tpu_custom_call" | custom-call | tf_op jit(solution)/shard_map/coefs_part/pallas_call | solution.py:565
  2.4 5.1 %collective-permute-start.3 = (f32[40,128]{1,0:T(8,128)}, f32[40,128]{1,0:T(8,128)S(1)}, u32[]{:S(2)}, u32[]{:S(2)}) collective-permute-start(f32[40,128]{1,0:T(8,128)} %coefs_part.1), channel_id=1, source_target_pairs={{0,12},{4,8},{8,4},{12,0},{1,13},{5,9},{9,5},{13,1},{2,14},{6,10},... | collective-permute-start | bytes 61448 | tf_op jit(solution)/shard_map/ppermute | solution.py:1033
  7.5 0.6 %collective-permute-start.1 = (f32[40,128]{1,0:T(8,128)}, f32[40,128]{1,0:T(8,128)S(1)}, u32[]{:S(2)}, u32[]{:S(2)}) collective-permute-start(f32[40,128]{1,0:T(8,128)} %coefs_part.1), channel_id=1, source_target_pairs={{0,4},{4,0},{8,12},{12,8},{1,5},{5,1},{9,13},{13,9},{2,6},{6,2},{1... | collective-permute-start | bytes 61448 | tf_op jit(solution)/shard_map/ppermute | solution.py:1033
  8.1 2.8 %local_part.1 = (f32[104,128]{1,0:T(8,128)}, f32[104,128]{1,0:T(8,128)}) custom-call(f32[5,5,2,160]{3,2,1,0:T(2,128)} %bitcast.6, f32[5,5,2,160]{3,2,1,0:T(2,128)} %bitcast.4, f32[5,5,160]{2,1,0:T(8,128)} %kappa_in.3, s32[6,1,1,32]{3,2,1,0:T(1,128)} %flags_in.3, f32[64,64]{1,0:T(8,128)} %constant.4.clone.rows_in, f32[160,320]{1,0:T(8,128)} %constant.5.clone.lines_in), custom_call_target="tpu_custom_call" | custom-call | flops 20000000 | bytes 8000000 | tf_op jit(solution)/shard_map/local_part/pallas_call | solution.py:580
  11.0 0.1 collective-permute-start
  11.1 1.3 %collective-permute-done.2 = f32[40,128]{1,0:T(8,128)S(1)} collective-permute-done((f32[40,128]{1,0:T(8,128)}, f32[40,128]{1,0:T(8,128)S(1)}, u32[]{:S(2)}, u32[]{:S(2)}) %collective-permute-start.2) | collective-permute-done | bytes 20512 | tf_op jit(solution)/shard_map/ppermute | solution.py:1033
  12.4 0.7 %pad_maximum_fusion.block0 = f32[160,128]{1,0:T(8,128)S(1)} fusion(f32[40,128]{1,0:T(8,128)S(1)} %collective-permute-done.3, f32[40,128]{1,0:T(8,128)S(1)} %collective-permute-done.2, f32[40,128]{1,0:T(8,128)S(1)} %collective-permute-done.1, f32[40,128]{1,0:T(8,128)} %coefs_part.1), kind=kLoop, calls=%fused_computation | loop fusion | flops 61440 | bytes 163840 | tf_op jit(solution)/shard_map/concatenate | solution.py:1039
  13.1 0.8 %add.3 = f32[104,128]{1,0:T(8,128)S(1)} add(f32[104,128]{1,0:T(8,128)} %get-tuple-element.18, f32[104,128]{1,0:T(8,128)S(1)} %collective-permute-done) | non-fusion elementwise | flops 13312 | bytes 159744 | tf_op jit(solution)/shard_map/add | solution.py:1041
  14.0 3.1 %collective-permute-start.6 = (f32[104,128]{1,0:T(8,128)S(1)}, f32[104,128]{1,0:T(8,128)S(1)}, u32[]{:S(2)}, u32[]{:S(2)}) collective-permute-start(f32[104,128]{1,0:T(8,128)S(1)} %add.3), channel_id=1, source_target_pairs={{0,12},{4,8},{8,4},{12,0},{1,13},{5,9},{9,5},{13,1},{2,14},{6,10},... | collective-permute-start | bytes 159752 | tf_op jit(solution)/shard_map/ppermute | solution.py:1033
  17.0 1.3 %collective-permute-start.4 = (f32[104,128]{1,0:T(8,128)S(1)}, f32[104,128]{1,0:T(8,128)S(1)}, u32[]{:S(2)}, u32[]{:S(2)}) collective-permute-start(f32[104,128]{1,0:T(8,128)S(1)} %add.3), channel_id=1, source_target_pairs={{0,4},{4,0},{8,12},{12,8},{1,5},{5,1},{9,13},{13,9},{2,6},{6,2},{1... | collective-permute-start | bytes 159752 | tf_op jit(solution)/shard_map/ppermute | solution.py:1033
  18.4 2.4 %collective-permute-start.9 = (f32[160,128]{1,0:T(8,128)S(1)}, f32[160,128]{1,0:T(8,128)S(1)}, u32[]{:S(2)}, u32[]{:S(2)}) collective-permute-start(f32[160,128]{1,0:T(8,128)S(1)} %pad_maximum_fusion.block0), channel_id=1, source_target_pairs={{0,3},{1,2},{2,1},{3,0},{4,7},{5,6},{6,5},{7,4},{8,11},{9,10},{10,... | collective-permute-start | bytes 245768 | tf_op jit(solution)/shard_map/ppermute | solution.py:1033
  20.8 0.5 %collective-permute-start.8 = (f32[160,128]{1,0:T(8,128)S(1)}, f32[160,128]{1,0:T(8,128)S(1)}, u32[]{:S(2)}, u32[]{:S(2)}) collective-permute-start(f32[160,128]{1,0:T(8,128)S(1)} %pad_maximum_fusion.block0), channel_id=1, source_target_pairs={{0,2},{1,3},{2,0},{3,1},{4,6},{5,7},{6,4},{7,5},{8,10},{9,11},{10,... | collective-permute-start | bytes 245768 | tf_op jit(solution)/shard_map/ppermute | solution.py:1033
  21.3 0.5 %collective-permute-start.7 = (f32[160,128]{1,0:T(8,128)S(1)}, f32[160,128]{1,0:T(8,128)S(1)}, u32[]{:S(2)}, u32[]{:S(2)}) collective-permute-start(f32[160,128]{1,0:T(8,128)S(1)} %pad_maximum_fusion.block0), channel_id=1, source_target_pairs={{0,1},{1,0},{2,3},{3,2},{4,5},{5,4},{6,7},{7,6},{8,9},{9,8},{10,11... | collective-permute-start | bytes 245768 | tf_op jit(solution)/shard_map/ppermute | solution.py:1033
  21.9 0.4 collective-permute-done.5
  22.2 0.1 collective-permute-done.4
  22.3 1.9 %collective-permute-done.9.block3 = f32[160,128]{1,0:T(8,128)S(1)} collective-permute-done((f32[160,128]{1,0:T(8,128)S(1)}, f32[160,128]{1,0:T(8,128)S(1)}, u32[]{:S(2)}, u32[]{:S(2)}) %collective-permute-start.9) | collective-permute-done | bytes 81952 | tf_op jit(solution)/shard_map/ppermute | solution.py:1033
  24.2 1.0 %collective-permute-done.8.block2 = f32[160,128]{1,0:T(8,128)S(1)} collective-permute-done((f32[160,128]{1,0:T(8,128)S(1)}, f32[160,128]{1,0:T(8,128)S(1)}, u32[]{:S(2)}, u32[]{:S(2)}) %collective-permute-start.8) | collective-permute-done | bytes 81952 | tf_op jit(solution)/shard_map/ppermute | solution.py:1033
  25.2 0.5 %collective-permute-done.7.block1 = f32[160,128]{1,0:T(8,128)S(1)} collective-permute-done((f32[160,128]{1,0:T(8,128)S(1)}, f32[160,128]{1,0:T(8,128)S(1)}, u32[]{:S(2)}, u32[]{:S(2)}) %collective-permute-start.7) | collective-permute-done | bytes 81952 | tf_op jit(solution)/shard_map/ppermute | solution.py:1033
  25.8 1.6 %collective-permute-start.12 = (f32[416,128]{1,0:T(8,128)S(1)}, f32[416,128]{1,0:T(8,128)S(1)}, u32[]{:S(2)}, u32[]{:S(2)}) collective-permute-start(f32[416,128]{1,0:T(8,128)S(1)} %constant_dynamic-update-slice_fusion.block0), channel_id=1, source_target_pairs={{0,3},{1,2},{2,1},{3,0},{4,7},{5,6},{6,5},{7,4},{8,11},{9,10},{10,... | collective-permute-start | bytes 638984 | tf_op jit(solution)/shard_map/ppermute | solution.py:1033
  27.3 0.6 %collective-permute-start.11 = (f32[416,128]{1,0:T(8,128)S(1)}, f32[416,128]{1,0:T(8,128)S(1)}, u32[]{:S(2)}, u32[]{:S(2)}) collective-permute-start(f32[416,128]{1,0:T(8,128)S(1)} %constant_dynamic-update-slice_fusion.block0), channel_id=1, source_target_pairs={{0,2},{1,3},{2,0},{3,1},{4,6},{5,7},{6,4},{7,5},{8,10},{9,11},{10,... | collective-permute-start | bytes 638984 | tf_op jit(solution)/shard_map/ppermute | solution.py:1033
  27.9 1.4 %collective-permute-start.10 = (f32[416,128]{1,0:T(8,128)S(1)}, f32[416,128]{1,0:T(8,128)S(1)}, u32[]{:S(2)}, u32[]{:S(2)}) collective-permute-start(f32[416,128]{1,0:T(8,128)S(1)} %constant_dynamic-update-slice_fusion.block0), channel_id=1, source_target_pairs={{0,1},{1,0},{2,3},{3,2},{4,5},{5,4},{6,7},{7,6},{8,9},{9,8},{10,11... | collective-permute-start | bytes 638984 | tf_op jit(solution)/shard_map/ppermute | solution.py:1033
  29.3 0.4 setup.1.coefs
  29.8 4.4 %collective-permute-done.12.block3 = f32[416,128]{1,0:T(8,128)S(1)} collective-permute-done((f32[416,128]{1,0:T(8,128)S(1)}, f32[416,128]{1,0:T(8,128)S(1)}, u32[]{:S(2)}, u32[]{:S(2)}) %collective-permute-start.12) | collective-permute-done | bytes 213024 | tf_op jit(solution)/shard_map/ppermute | solution.py:1033
  34.2 2.1 %collective-permute-done.11.block2 = f32[416,128]{1,0:T(8,128)S(1)} collective-permute-done((f32[416,128]{1,0:T(8,128)S(1)}, f32[416,128]{1,0:T(8,128)S(1)}, u32[]{:S(2)}, u32[]{:S(2)}) %collective-permute-start.11) | collective-permute-done | bytes 213024 | tf_op jit(solution)/shard_map/ppermute | solution.py:1033
  36.3 0.2 collective-permute-done.10.block1
  36.5 0.6 %assemble.1.assembled.own_start = f32[1024,128]{1,0:T(8,128)S(1)} custom-call(f32[416,128]{1,0:T(8,128)S(1)} %constant_dynamic-update-slice_fusion.block0, f32[416,128]{1,0:T(8,128)S(1)} %collective-permute-done.10.block1, f32[416,128]{1,0:T(8,128)S(1)} %collective-permute-done.11.block2, f32[416,128]{1,0:T(8,128)S(1)} %collective-permute-done.12.block3, ...), custom_call_target="tpu_custom_call" | custom-call | tf_op jit(solution)/shard_map/assemble/pallas_call | solution.py:984
  37.2 0.0 copy-start
  37.2 0.1 collective-permute-start.13
  37.3 6.7 %cycle.1.own = f32[1128,128]{1,0:T(8,128)S(1)} custom-call(f32[2704,128]{1,0:T(8,128)S(1)} %setup.1.coefs, f32[1024,128]{1,0:T(8,128)S(1)} %assemble.1.assembled.own_start), custom_call_target="tpu_custom_call" | custom-call | flops 40000000 | bytes 30000000 | tf_op jit(solution)/shard_map/cycle/pallas_call | solution.py:1004
  44.0 0.6 %collective-permute-start.14 = (f32[1128,128]{1,0:T(8,128)S(1)}, f32[1128,128]{1,0:T(8,128)S(1)}, u32[]{:S(2)}, u32[]{:S(2)}) collective-permute-start(f32[1128,128]{1,0:T(8,128)S(1)} %cycle.1.own), channel_id=1, source_target_pairs={{0,16},{16,0},{1,17},{17,1},{2,18},{18,2},{3,19},{19,3},{4,20},{20... | collective-permute-start | bytes 1732616 | tf_op jit(solution)/shard_map/ppermute | solution.py:1033
  44.6 1.6 %collective-permute-done.14.other = f32[1128,128]{1,0:T(8,128)S(1)} collective-permute-done((f32[1128,128]{1,0:T(8,128)S(1)}, f32[1128,128]{1,0:T(8,128)S(1)}, u32[]{:S(2)}, u32[]{:S(2)}) %collective-permute-start.14) | collective-permute-done | bytes 577568 | tf_op jit(solution)/shard_map/ppermute | solution.py:1033
  46.2 1.8 %finish.1 = (f32[5,5,2,160]{3,2,1,0:T(2,128)}, f32[5,5,2,160]{3,2,1,0:T(2,128)}, f32[3]{0:T(128)}) custom-call(f32[1128,128]{1,0:T(8,128)S(1)} %cycle.1.own, f32[1128,128]{1,0:T(8,128)S(1)} %collective-permute-done.14.other, f32[1024,128]{1,0:T(8,128)S(1)} %assemble.1.assembled.own_start, f32[1024,128]{1,0:T(8,128)S(1)} %collective-permute-done.13.other_start, ...), custom_call_target="tpu_custom_call" | custom-call | tf_op jit(solution)/shard_map/finish/pallas_call | solution.py:1017
  (12 shorter events, 0.0 us)
Async XLA Ops:
  2.4 8.7 %collective-permute-start.3 = (f32[40,128]{1,0:T(8,128)}, f32[40,128]{1,0:T(8,128)S(1)}, u32[]{:S(2)}, u32[]{:S(2)}) collective-permute-start(f32[40,128]{1,0:T(8,128)} %coefs_part.1), channel_id=1, source_target_pairs={{0,12},{4,8},{8,4},{12,0},{1,13},{5,9},{9,5},{13,1},{2,14},{6,10},... | collective-permute-start | bytes 61448 | tf_op jit(solution)/shard_map/ppermute | solution.py:1033
  7.5 4.9 %collective-permute-start.2 = (f32[40,128]{1,0:T(8,128)}, f32[40,128]{1,0:T(8,128)S(1)}, u32[]{:S(2)}, u32[]{:S(2)}) collective-permute-start(f32[40,128]{1,0:T(8,128)} %coefs_part.1), channel_id=1, source_target_pairs={{0,8},{4,12},{8,0},{12,4},{1,9},{5,13},{9,1},{13,5},{2,10},{6,14},... | collective-permute-start | bytes 61448 | tf_op jit(solution)/shard_map/ppermute | solution.py:1033
  7.5 4.9 %collective-permute-start.1 = (f32[40,128]{1,0:T(8,128)}, f32[40,128]{1,0:T(8,128)S(1)}, u32[]{:S(2)}, u32[]{:S(2)}) collective-permute-start(f32[40,128]{1,0:T(8,128)} %coefs_part.1), channel_id=1, source_target_pairs={{0,4},{4,0},{8,12},{12,8},{1,5},{5,1},{9,13},{13,9},{2,6},{6,2},{1... | collective-permute-start | bytes 61448 | tf_op jit(solution)/shard_map/ppermute | solution.py:1033
  11.0 2.2 %collective-permute-start = (f32[104,128]{1,0:T(8,128)}, f32[104,128]{1,0:T(8,128)S(1)}, u32[]{:S(2)}, u32[]{:S(2)}) collective-permute-start(f32[104,128]{1,0:T(8,128)} %get-tuple-element.19), channel_id=1, source_target_pairs={{0,16},{16,0},{1,17},{17,1},{2,18},{18,2},{3,19},{19,3},{4,20},{20... | collective-permute-start | bytes 159752 | tf_op jit(solution)/shard_map/ppermute | solution.py:1033
  14.0 7.3 %collective-permute-start.6 = (f32[104,128]{1,0:T(8,128)S(1)}, f32[104,128]{1,0:T(8,128)S(1)}, u32[]{:S(2)}, u32[]{:S(2)}) collective-permute-start(f32[104,128]{1,0:T(8,128)S(1)} %add.3), channel_id=1, source_target_pairs={{0,12},{4,8},{8,4},{12,0},{1,13},{5,9},{9,5},{13,1},{2,14},{6,10},... | collective-permute-start | bytes 159752 | tf_op jit(solution)/shard_map/ppermute | solution.py:1033
  17.0 5.2 %collective-permute-start.5 = (f32[104,128]{1,0:T(8,128)S(1)}, f32[104,128]{1,0:T(8,128)S(1)}, u32[]{:S(2)}, u32[]{:S(2)}) collective-permute-start(f32[104,128]{1,0:T(8,128)S(1)} %add.3), channel_id=1, source_target_pairs={{0,8},{4,12},{8,0},{12,4},{1,9},{5,13},{9,1},{13,5},{2,10},{6,14},... | collective-permute-start | bytes 159752 | tf_op jit(solution)/shard_map/ppermute | solution.py:1033
  17.0 5.2 %collective-permute-start.4 = (f32[104,128]{1,0:T(8,128)S(1)}, f32[104,128]{1,0:T(8,128)S(1)}, u32[]{:S(2)}, u32[]{:S(2)}) collective-permute-start(f32[104,128]{1,0:T(8,128)S(1)} %add.3), channel_id=1, source_target_pairs={{0,4},{4,0},{8,12},{12,8},{1,5},{5,1},{9,13},{13,9},{2,6},{6,2},{1... | collective-permute-start | bytes 159752 | tf_op jit(solution)/shard_map/ppermute | solution.py:1033
  18.4 5.9 %collective-permute-start.9 = (f32[160,128]{1,0:T(8,128)S(1)}, f32[160,128]{1,0:T(8,128)S(1)}, u32[]{:S(2)}, u32[]{:S(2)}) collective-permute-start(f32[160,128]{1,0:T(8,128)S(1)} %pad_maximum_fusion.block0), channel_id=1, source_target_pairs={{0,3},{1,2},{2,1},{3,0},{4,7},{5,6},{6,5},{7,4},{8,11},{9,10},{10,... | collective-permute-start | bytes 245768 | tf_op jit(solution)/shard_map/ppermute | solution.py:1033
  20.8 4.4 %collective-permute-start.8 = (f32[160,128]{1,0:T(8,128)S(1)}, f32[160,128]{1,0:T(8,128)S(1)}, u32[]{:S(2)}, u32[]{:S(2)}) collective-permute-start(f32[160,128]{1,0:T(8,128)S(1)} %pad_maximum_fusion.block0), channel_id=1, source_target_pairs={{0,2},{1,3},{2,0},{3,1},{4,6},{5,7},{6,4},{7,5},{8,10},{9,11},{10,... | collective-permute-start | bytes 245768 | tf_op jit(solution)/shard_map/ppermute | solution.py:1033
  21.3 4.4 %collective-permute-start.7 = (f32[160,128]{1,0:T(8,128)S(1)}, f32[160,128]{1,0:T(8,128)S(1)}, u32[]{:S(2)}, u32[]{:S(2)}) collective-permute-start(f32[160,128]{1,0:T(8,128)S(1)} %pad_maximum_fusion.block0), channel_id=1, source_target_pairs={{0,1},{1,0},{2,3},{3,2},{4,5},{5,4},{6,7},{7,6},{8,9},{9,8},{10,11... | collective-permute-start | bytes 245768 | tf_op jit(solution)/shard_map/ppermute | solution.py:1033
  25.8 8.4 %collective-permute-start.12 = (f32[416,128]{1,0:T(8,128)S(1)}, f32[416,128]{1,0:T(8,128)S(1)}, u32[]{:S(2)}, u32[]{:S(2)}) collective-permute-start(f32[416,128]{1,0:T(8,128)S(1)} %constant_dynamic-update-slice_fusion.block0), channel_id=1, source_target_pairs={{0,3},{1,2},{2,1},{3,0},{4,7},{5,6},{6,5},{7,4},{8,11},{9,10},{10,... | collective-permute-start | bytes 638984 | tf_op jit(solution)/shard_map/ppermute | solution.py:1033
  27.3 9.0 %collective-permute-start.11 = (f32[416,128]{1,0:T(8,128)S(1)}, f32[416,128]{1,0:T(8,128)S(1)}, u32[]{:S(2)}, u32[]{:S(2)}) collective-permute-start(f32[416,128]{1,0:T(8,128)S(1)} %constant_dynamic-update-slice_fusion.block0), channel_id=1, source_target_pairs={{0,2},{1,3},{2,0},{3,1},{4,6},{5,7},{6,4},{7,5},{8,10},{9,11},{10,... | collective-permute-start | bytes 638984 | tf_op jit(solution)/shard_map/ppermute | solution.py:1033
  27.9 8.7 %collective-permute-start.10 = (f32[416,128]{1,0:T(8,128)S(1)}, f32[416,128]{1,0:T(8,128)S(1)}, u32[]{:S(2)}, u32[]{:S(2)}) collective-permute-start(f32[416,128]{1,0:T(8,128)S(1)} %constant_dynamic-update-slice_fusion.block0), channel_id=1, source_target_pairs={{0,1},{1,0},{2,3},{3,2},{4,5},{5,4},{6,7},{7,6},{8,9},{9,8},{10,11... | collective-permute-start | bytes 638984 | tf_op jit(solution)/shard_map/ppermute | solution.py:1033
  37.2 9.0 %copy-start = (f32[2,5,5,160]{3,0,2,1:T(2,128)S(1)}, f32[2,5,5,160]{3,0,2,1:T(2,128)}, u32[]{:S(2)}) copy-start(f32[2,5,5,160]{3,0,2,1:T(2,128)} %param.7) | copy-start | bytes 96004
  37.2 6.8 %collective-permute-start.13 = (f32[1024,128]{1,0:T(8,128)S(1)}, f32[1024,128]{1,0:T(8,128)S(1)}, u32[]{:S(2)}, u32[]{:S(2)}) collective-permute-start(f32[1024,128]{1,0:T(8,128)S(1)} %assemble.1.assembled.own_start), channel_id=1, source_target_pairs={{0,16},{16,0},{1,17},{17,1},{2,18},{18,2},{3,19},{19,3},{4,20},{20... | collective-permute-start | bytes 1572872 | tf_op jit(solution)/shard_map/ppermute | solution.py:1033
  44.0 2.2 %collective-permute-start.14 = (f32[1128,128]{1,0:T(8,128)S(1)}, f32[1128,128]{1,0:T(8,128)S(1)}, u32[]{:S(2)}, u32[]{:S(2)}) collective-permute-start(f32[1128,128]{1,0:T(8,128)S(1)} %cycle.1.own), channel_id=1, source_target_pairs={{0,16},{16,0},{1,17},{17,1},{2,18},{18,2},{3,19},{19,3},{4,20},{20... | collective-permute-start | bytes 1732616 | tf_op jit(solution)/shard_map/ppermute | solution.py:1033

commit v7 on v6

--- a/solution.py
+++ b/solution.py
@@ -352,8 +352,8 @@
 COLS = 16
 HALF = 64
 TRACE = 40
-PIECE = HALF + TRACE
-COEFS = 40
+KAPPA = HALF + TRACE
+PIECE = KAPPA + 32
 FIELD = 1000
 F32 = jnp.float32
 
@@ -467,28 +467,9 @@
         copy.wait()
 
 
-def coefs_kernel(kappa_in, flags_in, out, kappa, flags, sems, kap, krep):
-    fetch([(kappa_in, kappa), (flags_in, flags)], sems)
-    kap[...] = jnp.zeros_like(kap)
-    for i in range(5):
-        kap[5 * i : 5 * i + 5, :] = kappa[i]
-    coefs = kap[...]
-    krep[...] = jnp.zeros_like(krep)
-    for k in range(5):
-        krep[25 * k : 25 * k + 25, :] = split_dot(coefs, pick_line(k))[:25]
-    out[:32, :] = choose(iota((32, 128), 1) // EZ, [krep[32 * q : 32 * q + 32, :] for q in range(4)])
-    flag = flags[:, 0, 0, :].astype(F32)
-    repeat = (iota((EZ, 128), 1) % EZ == iota((EZ, 128), 0)).astype(F32)
-    shown = split_dot(flag, repeat)
-    group = iota((1, 128), 1) // EZ
-    out[32:40, :] = jnp.zeros((8, 128), F32)
-    out[32:33, :] = choose(group, [shown[d : d + 1] for d in range(4)])
-    out[33:34, :] = choose(group, [shown[4:5], shown[5:6]])
-
-
 def local_kernel(
     rhs_in, guess_in, kappa_in, flags_in, rows_in, lines_in, mine, theirs,
-    rhs, guess, kappa, flags, rows_t, lines_t, sems, x, kap, stack, nodes, traces,
+    rhs, guess, kappa, flags, rows_t, lines_t, sems, x, kap, stack, nodes, traces, krep,
 ):
     sec = lax.axis_index("section")
     fetch(
@@ -525,10 +506,12 @@
         r = slice(s * 32, s * 32 + 32)
         image = own * field[r] + along[r] + across[r, :160] - gz * across[r, 160:]
         stack[64 + s * 32 : 96 + s * 32, :] = image
-    stack[128:, :] = field
+    stack[128:192, :] = field
+    stack[192:, :] = kap[...]
     source = stack[...]
     back, back_matrix = split_sections()[1:3]
     nodes[...] = jnp.zeros_like(nodes)
+    krep[...] = jnp.zeros_like(krep)
     for k in range(5):
         parts = split_dot(source, pick_line(k))
         for p, mark in enumerate((True, False)):
@@ -547,9 +530,17 @@
                     r = start + face_place(i, j)
                     traces[r : r + 1, :] = trace[5 * i + j : 5 * i + j + 1]
             traces[start + 11 : start + 16, :] = trace[20:25]
+        krep[25 * k : 25 * k + 25, :] = parts[192:217]
+    repeat = (iota((EZ, 128), 1) % EZ == iota((EZ, 128), 0)).astype(F32)
+    shown = split_dot(flag, repeat)
+    upper = iota((1, 128), 1) < 64
+    for r in range(3):
+        nodes[125 + r : 126 + r, :] = jnp.where(upper, shown[2 * r : 2 * r + 1], shown[2 * r + 1 : 2 * r + 2])
     for p, out in enumerate((mine, theirs)):
         out[:HALF, :] = pack_nodes(nodes[128 * p : 128 * p + 128, :])
-        out[HALF:, :] = pack_nodes(traces[80 * p : 80 * p + 80, :])
+        out[HALF:KAPPA, :] = pack_nodes(traces[80 * p : 80 * p + 80, :])
+    mine[KAPPA:, :] = choose(iota((32, 128), 1) // EZ, [krep[32 * q : 32 * q + 32, :] for q in range(4)])
+    theirs[KAPPA:, :] = jnp.zeros((32, 128), F32)
 
 
 VMEM = pl.BlockSpec(memory_space=pltpu.VMEM)
@@ -558,20 +549,6 @@
 
 def limit(mib):
     return pltpu.CompilerParams(vmem_limit_bytes=mib * 2**20)
-
-
-def coefs_part(kappa, flags):
-    operands = (kappa, flags)
-    return pl.pallas_call(
-        coefs_kernel,
-        out_shape=jax.ShapeDtypeStruct((COEFS, 128), F32),
-        in_specs=[HBM] * 2,
-        out_specs=VMEM,
-        scratch_shapes=[pltpu.VMEM(o.shape, o.dtype) for o in operands]
-        + [pltpu.SemaphoreType.DMA((2,)), pltpu.VMEM((32, 160), F32), pltpu.VMEM((128, 128), F32)],
-        compiler_params=limit(60),
-        name="coefs_part",
-    )(*operands)
 
 
 def local_part(rhs, guess, kappa, flags):
@@ -587,9 +564,10 @@
             pltpu.SemaphoreType.DMA((6,)),
             pltpu.VMEM((64, 160), F32),
             pltpu.VMEM((32, 160), F32),
-            pltpu.VMEM((192, 160), F32),
+            pltpu.VMEM((224, 160), F32),
             pltpu.VMEM((256, 128), F32),
             pltpu.VMEM((160, 128), F32),
+            pltpu.VMEM((128, 128), F32),
         ],
         compiler_params=limit(60),
         cost_estimate=pl.CostEstimate(flops=20_000_000, bytes_accessed=8_000_000, transcendentals=0),
@@ -659,11 +637,28 @@
         return jnp.where(last, pltpu.roll(u, 31, u.ndim - 1), pltpu.roll(u, 127, u.ndim - 1))
 
 
-def assemble_kernel(block0, block1, block2, block3, coefs, field, pieces, edges, traces):
+def load(ref, first, count):
+    return ref[pl.ds(first * 8, count * 8), :].reshape(count, 8, 128)
+
+
+def store(ref, first, value):
+    ref[pl.ds(first * 8, value.shape[0] * 8), :] = value.reshape(value.shape[0] * 8, 128)
+
+
+DIAGS = (0, 250, 304)
+GAINS = (320, 326, 332)
+REGISTERS = 338
+CENTRE = (CHEB_HIGH + CHEB_LOW) / 2.0
+RADIUS = (CHEB_HIGH - CHEB_LOW) / 2.0
+
+
+def assemble_kernel(block0, block1, block2, block3, field, coefs, pieces, edges, kappas, traces, kap):
     blocks = (block0, block1, block2, block3)
     place_pieces(blocks, PIECE, pieces, 0, HALF)
     place_pieces(blocks, PIECE, edges, HALF, TRACE)
+    place_pieces(blocks, PIECE, kappas, KAPPA, 32)
     lanes = Lanes()
+    group, lane = lanes.group, lanes.lane
 
     def widen(source, size, target):
         for r in range(size):
@@ -673,57 +668,34 @@
 
     widen(edges, TRACE, traces)
     widen(pieces, HALF, field)
-    gains = [coefs[tile(GAINS[0] + d), :] for d in range(4)]
-    for k in range(5):
-        def trace(i, j, k=k):
-            return traces[tile(k * 16 + face_place(i, j)), :]
-
-        for m in range(5):
-            for where, term in (
-                (m, gains[0] * lanes.x_before(trace(4, m))),
-                (20 + m, gains[1] * lanes.x_after(trace(0, m))),
-                (5 * m, gains[2] * lanes.y_before(trace(m, 4))),
-                (5 * m + 4, gains[3] * lanes.y_after(trace(m, 0))),
-            ):
-                field[tile(k * 25 + where), :] = field[tile(k * 25 + where), :] + term
-
-
-def load(ref, first, count):
-    start = first * 8 if isinstance(first, int) else pl.multiple_of(first * 8, 8)
-    return ref[pl.ds(start, count * 8), :].reshape(count, 8, 128)
-
-
-def store(ref, first, value):
-    start = first * 8 if isinstance(first, int) else pl.multiple_of(first * 8, 8)
-    ref[pl.ds(start, value.shape[0] * 8), :] = value.reshape(value.shape[0] * 8, 128)
-
-
-DIAGS = (0, 250, 304)
-GAINS = (320, 326, 332)
-REGISTERS = 338
-CENTRE = (CHEB_HIGH + CHEB_LOW) / 2.0
-RADIUS = (CHEB_HIGH - CHEB_LOW) / 2.0
-
-
-def setup_kernel(block0, block1, block2, block3, coefs, pieces, kap):
-    place_pieces((block0, block1, block2, block3), COEFS, pieces, 0, COEFS)
-    lanes = Lanes()
-    group = lanes.group
-
-    def widen(r):
+    flags = []
+    for r in range(3):
+        got = field[tile(125 + r), :]
+        across = pltpu.roll(got, 64, 1)
+        flags += [jnp.where(lane < 64, got, across), jnp.where(lane < 64, across, got)]
+    for r in range(32):
         turned = []
         for h in range(2):
-            got = rows_of(pieces, COEFS, r, h)
+            got = rows_of(kappas, 32, r, h)
             turned.append([pltpu.roll(got, 32 * m, 1) if m else got for m in range(4)])
-        return [choose(group, [turned[g % 2][(g - q) % 4] for g in range(4)]) for q in range(4)]
-
-    for r in range(32):
-        for q, part in enumerate(widen(r)):
-            kap[tile(q * 32 + r), :] = part
-    flags = widen(32) + widen(33)[:2]
+        for q in range(4):
+            kap[tile(q * 32 + r), :] = choose(group, [turned[g % 2][(g - q) % 4] for g in range(4)])
     for p, n in enumerate((5, 3, 2)):
         stride = 4 // (n - 1)
         gains = [face_gains(flags[d], d // 2, d % 2, n) for d in range(6)]
+        if p == 0:
+            for k in range(5):
+                def trace(i, j, k=k):
+                    return traces[tile(k * 16 + face_place(i, j)), :]
+
+                for m in range(5):
+                    for where, term in (
+                        (m, gains[0] * lanes.x_before(trace(4, m))),
+                        (20 + m, gains[1] * lanes.x_after(trace(0, m))),
+                        (5 * m, gains[2] * lanes.y_before(trace(m, 4))),
+                        (5 * m + 4, gains[3] * lanes.y_after(trace(m, 0))),
+                    ):
+                        field[tile(k * 25 + where), :] = field[tile(k * 25 + where), :] + term
         rows = []
         for d in range(3):
             coefs[tile(GAINS[p] + 2 * d), :] = gains[2 * d]
@@ -783,15 +755,16 @@
         gains = level.gains
         source = level.dir if smooth else level.x
         for k in range(n):
-            here = k * n * n
-            v = [load(source, here + i * n, n) for i in range(n)]
-            waiting = []
+            def line_at(i, k=k):
+                return load(source, (k * n + i) * n, n)
+
             for i in range(n):
-                first = here + i * n
-                total = level.diag(first, n) * v[i]
+                first = (k * n + i) * n
+                v = line_at(i)
+                total = level.diag(first, n) * v
                 for m in range(n):
                     if m != i:
-                        total = total + float(kx[i, m]) * v[m]
+                        total = total + float(kx[i, m]) * line_at(m)
                 for m in range(n):
                     if m != k:
                         total = total + float(kz[k, m]) * load(source, (m * n + i) * n, n)
@@ -800,34 +773,30 @@
                     line = None
                     for m in range(n):
                         if m != j:
-                            term = float(ky[j, m]) * v[i][m]
+                            term = float(ky[j, m]) * v[m]
                             line = term if line is None else line + term
                     if j == 0:
-                        line = line - gains[2] * lanes.y_before(v[i][n - 1])
+                        line = line - gains[2] * lanes.y_before(v[n - 1])
                     if j == n - 1:
-                        line = line - gains[3] * lanes.y_after(v[i][0])
+                        line = line - gains[3] * lanes.y_after(v[0])
                     lines.append(line)
                 total = total + jnp.stack(lines)
                 if i == 0:
-                    total = total - gains[0] * lanes.x_before(v[n - 1])
+                    total = total - gains[0] * lanes.x_before(line_at(n - 1))
                 if i == n - 1:
-                    total = total - gains[1] * lanes.x_after(v[0])
+                    total = total - gains[1] * lanes.x_after(line_at(0))
                 if k == 0:
                     total = total - gains[4] * lanes.z_before(load(source, ((n - 1) * n + i) * n, n))
                 if k == n - 1:
                     total = total - gains[5] * lanes.z_after(load(source, i * n, n))
-                image = v[i] + (same * total + swap * pltpu.roll(total, 64, 2))
+                image = v + (same * total + swap * pltpu.roll(total, 64, 2))
                 if smooth:
                     scaled = level.jac(first, n) * (load(level.res, first, n) - image)
-                    waiting.append((level.x, first, load(level.x, first, n) + keep * v[i] + push * scaled))
+                    store(level.x, first, load(level.x, first, n) + keep * v + push * scaled)
                 else:
                     rest = load(level.f, first, n) - image
-                    waiting.append((level.res, first, rest))
-                    waiting.append((level.dir, first, level.jac(first, n) * rest))
-                if i % 2 == 1 or i == n - 1:
-                    for place_out in waiting:
-                        store(*place_out)
-                    waiting = []
+                    store(level.res, first, rest)
+                    store(level.dir, first, level.jac(first, n) * rest)
 
     def combine(weights, parts):
         total = None
@@ -898,58 +867,93 @@
     fields[FIELD + 125 : FIELD + 128, :] = jnp.zeros((3, 128), F32)
 
 
-def finish_kernel(own, other, own_start, other_start, guess, sol, res_out, arnoldi, cols, outs):
+def pair_weights():
+    cross = split_sections()[4]
+    return jnp.where(iota((8, 128), 1) < 64, float(cross[0]), float(cross[1]))
+
+
+def column_factors(p):
     sec = lax.axis_index("section")
-    my_gx, my_gy = lax.axis_index("gx"), lax.axis_index("gy")
-    whole, back, back_matrix, blocks, cross = split_sections()
-    weights = jnp.where(iota((8, 128), 1) < 64, float(cross[0]), float(cross[1]))
-    nothing = jnp.zeros((8, 128), F32)
-
-    lane = iota((32, 128), 1)
-    here = lane // EZ % 2 == my_gx // 2
+    whole = split_sections()[0]
+    lane = iota((25, 128), 1)
+    here = lane // EZ % 2 == lax.axis_index("gx") // 2
     factors = []
     for s in range(2):
-        row = []
-        for p in range(2):
-            parts = []
-            for mine in range(2):
-                t = whole[2 * mine + s]
-                pairs = [jnp.where(lane < 64, float(t[2 * q]), float(t[2 * q + 1])) for q in range(2)]
-                parts.append(pairs[mine] if p == 0 else pairs[1 - mine])
-            row.append(jnp.where(here, jnp.where(sec == 0, parts[0], parts[1]), 0.0)[:25])
-        factors.append(row)
-    column = (my_gx % 2) * 4 + my_gy
+        parts = []
+        for mine in range(2):
+            t = whole[2 * mine + s]
+            q = mine if p == 0 else 1 - mine
+            parts.append(jnp.where(lane < 64, float(t[2 * q]), float(t[2 * q + 1])))
+        factors.append(jnp.where(here, jnp.where(sec == 0, parts[0], parts[1]), 0.0))
+    return factors
+
+
+def column_rows(k):
+    column = (lax.axis_index("gx") % 2) * 4 + lax.axis_index("gy")
+    return pl.ds(k * 200 + column, 25, stride=8)
+
+
+def raw_order(k):
+    return (iota((128, 160), 1) == 5 * (iota((128, 160), 0) % EZ) + k).astype(F32)
+
+
+def early_kernel(own, own_start, other_start, sums, column_out, cols):
+    weights = pair_weights()
     cols[...] = jnp.zeros_like(cols)
     total = jnp.zeros((192, 160), F32)
+    own_factors, other_factors = column_factors(0), column_factors(1)
     for k in range(5):
-        where = pl.ds(k * 200 + column, 25, stride=8)
-        shown = [[ref[FIELD + k * 25 : FIELD + k * 25 + 25, :] for ref in (own, other)]]
-        shown.append([ref[where, :] for ref in (own_start, other_start)])
-        shown.append([b[where, :] - a[where, :] for a, b in ((own, own_start), (other, other_start))])
-        for f, (a, b) in enumerate(shown):
-            for s in range(2):
-                r = f * 64 + s * 32
-                cols[r : r + 25, :] = factors[s][0] * a + factors[s][1] * b
-        hit = (iota((128, 160), 1) == 5 * (iota((128, 160), 0) % EZ) + k).astype(F32)
-        total = total + split_dot(cols[...], hit)
-
-    def product(a, b, c, d):
-        return (a * c + b * d) + weights * (a * d + b * c)
-
+        where = column_rows(k)
+        z = own[FIELD + k * 25 : FIELD + k * 25 + 25, :]
+        start, other = own_start[where, :], other_start[where, :]
+        w = start - own[where, :]
+        for s in range(2):
+            cols[s * 32 : s * 32 + 25, :] = own_factors[s] * z
+            cols[64 + s * 32 : 64 + s * 32 + 25, :] = own_factors[s] * start + other_factors[s] * other
+            cols[128 + s * 32 : 128 + s * 32 + 25, :] = own_factors[s] * w
+        total = total + split_dot(cols[...], raw_order(k))
+    column_out[...] = total
+    nothing = jnp.zeros((8, 128), F32)
     uppers, sizes = [nothing] * 5, [nothing] * 5
     for r in range(125):
-        a, b, c, d = (ref[tile(r), :] for ref in (own, other, own_start, other_start))
-        a, b = c - a, d - b
-        uppers[r % 5] = uppers[r % 5] + product(a, b, c, d)
-        sizes[r % 5] = sizes[r % 5] + product(c, d, c, d)
-    size = jnp.sum(sum(sizes), keepdims=True)
-    upper = jnp.sum(sum(uppers), keepdims=True) / size
+        c, d = own_start[tile(r), :], other_start[tile(r), :]
+        a = c - own[tile(r), :]
+        uppers[r % 5] = uppers[r % 5] + a * (c + weights * d)
+        sizes[r % 5] = sizes[r % 5] + ((c * c + d * d) + 2.0 * (weights * (c * d)))
+    sums[0:8, :] = sum(uppers)
+    sums[8:16, :] = sum(sizes)
+
+
+def finish_kernel(own, other, own_start, other_start, sums, column, guess, sol, res_out, arnoldi, cols, outs):
+    sec = lax.axis_index("section")
+    weights = pair_weights()
+    cols[...] = jnp.zeros_like(cols)
+    total = jnp.zeros((128, 160), F32)
+    factors = column_factors(1)
+    for k in range(5):
+        where = column_rows(k)
+        z = other[FIELD + k * 25 : FIELD + k * 25 + 25, :]
+        w = other_start[where, :] - other[where, :]
+        for s in range(2):
+            cols[s * 32 : s * 32 + 25, :] = factors[s] * z
+            cols[64 + s * 32 : 64 + s * 32 + 25, :] = factors[s] * w
+        total = total + split_dot(cols[...], raw_order(k))
+    nothing = jnp.zeros((8, 128), F32)
+    uppers = [nothing] * 5
+    for r in range(125):
+        c, d = own_start[tile(r), :], other_start[tile(r), :]
+        b = d - other[tile(r), :]
+        uppers[r % 5] = uppers[r % 5] + b * (d + weights * c)
+
+    mine, theirs = sums[0:8, :], sum(uppers)
+    size = jnp.sum(sums[8:16, :], keepdims=True)
+    upper = jnp.sum(mine + theirs, keepdims=True) / size
     rests = [nothing] * 5
     for r in range(125):
-        a, b, c, d = (ref[tile(r), :] for ref in (own, other, own_start, other_start))
-        a, b = c - a, d - b
-        a, b = a - upper * c, b - upper * d
-        rests[r % 5] = rests[r % 5] + product(a, b, a, b)
+        c, d = own_start[tile(r), :], other_start[tile(r), :]
+        a = (c - own[tile(r), :]) - upper * c
+        b = (d - other[tile(r), :]) - upper * d
+        rests[r % 5] = rests[r % 5] + ((a * a + b * b) + 2.0 * (weights * (a * b)))
     rest = jnp.sum(sum(rests), keepdims=True)
     beta = jnp.sqrt(size)
     lower = jnp.sqrt(rest) / beta
@@ -957,8 +961,8 @@
     entries = float(125 * EZ * COLS * 4)
     for place_out, value in enumerate((beta * (1.0 / math.sqrt(entries)), upper, lower)):
         arnoldi[place_out] = value[0, 0]
-    outs[:64, :] = weight * total[:64]
-    outs[64:, :] = total[64:128] - weight * total[128:]
+    outs[:64, :] = weight * (column[:64, :] + total[:64])
+    outs[64:, :] = column[64:128, :] - weight * (column[128:, :] + total[64:])
     for i in range(5):
         for j in range(5):
             r = 5 * i + j
@@ -967,33 +971,25 @@
                 res_out[i, j, s : s + 1, :] = outs[64 + s * 32 + r : 64 + s * 32 + r + 1, :]
 
 
-def setup(blocks):
-    return pl.pallas_call(
-        setup_kernel,
-        out_shape=jax.ShapeDtypeStruct((REGISTERS * 8, 128), F32),
-        in_specs=[VMEM] * 4,
-        out_specs=VMEM,
-        scratch_shapes=[pltpu.VMEM((COLS * COEFS, 128), F32), pltpu.VMEM((128 * 8, 128), F32)],
-        compiler_params=limit(16),
-        cost_estimate=pl.CostEstimate(flops=4_000_000, bytes_accessed=4_000_000, transcendentals=0),
-        name="setup",
-    )(*blocks)
-
-
-def assemble(blocks, coefs):
+def assemble(blocks):
     return pl.pallas_call(
         assemble_kernel,
-        out_shape=jax.ShapeDtypeStruct((128 * 8, 128), F32),
-        in_specs=[VMEM] * 5,
-        out_specs=VMEM,
+        out_shape=[
+            jax.ShapeDtypeStruct((128 * 8, 128), F32),
+            jax.ShapeDtypeStruct((REGISTERS * 8, 128), F32),
+        ],
+        in_specs=[VMEM] * 4,
+        out_specs=[VMEM] * 2,
         scratch_shapes=[
             pltpu.VMEM((COLS * HALF, 128), F32),
             pltpu.VMEM((COLS * TRACE, 128), F32),
+            pltpu.VMEM((COLS * 32, 128), F32),
             pltpu.VMEM((80 * 8, 128), F32),
+            pltpu.VMEM((128 * 8, 128), F32),
         ],
         compiler_params=limit(16),
         name="assemble",
-    )(*blocks, coefs)
+    )(*blocks)
 
 
 def cycle(coefs, assembled):
@@ -1013,7 +1009,20 @@
     )(coefs, assembled)
 
 
-def finish(own, other, own_start, other_start, guess):
+def early(own, own_start, other_start):
+    return pl.pallas_call(
+        early_kernel,
+        out_shape=[jax.ShapeDtypeStruct((16, 128), F32), jax.ShapeDtypeStruct((192, 160), F32)],
+        in_specs=[VMEM] * 3,
+        out_specs=[VMEM] * 2,
+        scratch_shapes=[pltpu.VMEM((192, 128), F32)],
+        compiler_params=limit(16),
+        cost_estimate=pl.CostEstimate(flops=4_000_000, bytes_accessed=4_000_000, transcendentals=0),
+        name="early",
+    )(own, own_start, other_start)
+
+
+def finish(own, other, own_start, other_start, sums, column, guess):
     return pl.pallas_call(
         finish_kernel,
         out_shape=[
@@ -1021,12 +1030,12 @@
             jax.ShapeDtypeStruct(guess.shape, F32),
             jax.ShapeDtypeStruct((3,), F32),
         ],
-        in_specs=[VMEM] * 5,
+        in_specs=[VMEM] * 7,
         out_specs=[VMEM, VMEM, pl.BlockSpec(memory_space=pltpu.SMEM)],
-        scratch_shapes=[pltpu.VMEM((192, 128), F32), pltpu.VMEM((128, 160), F32)],
+        scratch_shapes=[pltpu.VMEM((128, 128), F32), pltpu.VMEM((128, 160), F32)],
         compiler_params=limit(24),
         name="finish",
-    )(own, other, own_start, other_start, guess)
+    )(own, other, own_start, other_start, sums, column, guess)
 
 
 def exchange(x, axis, bits):
@@ -1035,22 +1044,15 @@
 
 def gathered_body(rhs, guess, kappa, bc_flags):
     rhs, guess = (jnp.transpose(v, (1, 2, 0, 3)) for v in (rhs, guess))
-    coefs = coefs_part(kappa, bc_flags)
-    coefs_line = jnp.concatenate([coefs] + [exchange(coefs, "gx", bits) for bits in (1, 2, 3)])
     mine, theirs = local_part(rhs, guess, kappa, bc_flags)
     piece = mine + exchange(theirs, "section", 1)
-    piece, coefs_line = lax.optimization_barrier((piece, coefs_line))
-    parts = [exchange(piece, "gx", bits) for bits in (1, 2, 3)]
-    others = [exchange(coefs_line, "gy", bits) for bits in (1, 2, 3)]
-    parts, others = lax.optimization_barrier((parts, others))
-    coefs_blocks = [coefs_line] + others
-    line = jnp.concatenate([piece] + parts)
+    line = jnp.concatenate([piece] + [exchange(piece, "gx", bits) for bits in (1, 2, 3)])
     blocks = [line] + [exchange(line, "gy", bits) for bits in (1, 2, 3)]
-    all_coefs = setup(coefs_blocks)
-    start = assemble(blocks, all_coefs)
+    start, coefs = assemble(blocks)
     other_start = exchange(start, "section", 1)
-    own, other_start = lax.optimization_barrier((cycle(all_coefs, start), other_start))
-    sol, res, arnoldi = finish(own, exchange(own, "section", 1), start, other_start, guess)
+    own, other_start = lax.optimization_barrier((cycle(coefs, start), other_start))
+    sums, column = early(own, start, other_start)
+    sol, res, arnoldi = finish(own, exchange(own, "section", 1), start, other_start, sums, column, guess)
     sol, res = (jnp.transpose(v, (2, 0, 1, 3)) for v in (sol, res))
     return sol, res, arnoldi
 

time: 48.3 us -> 44 us (0.911)
  starting transfers between devices: 17.9 us -> 10.4 us
  waiting for transfers between devices: 13.7 us -> 19 us
  Pallas kernels: 14.1 us -> 12.8 us
  other arithmetic: 1.56 us -> 0.91 us
    ppermute x15 -> x9, starting transfers between devices: 17.9 us -> 10.4 us  [exchange(): lax.ppermute(x, axis, [(n, n ^ bits) for n in range(lax.axis_size(axis))])]
    ppermute x15 -> x9, waiting for transfers between devices: 13.7 us -> 19 us  [exchange(): lax.ppermute(x, axis, [(n, n ^ bits) for n in range(lax.axis_size(axis))])]
    pallas_call x3 -> x2, Pallas kernels: 2.8 us -> 1.72 us  [the longest x1 0.92 us: assemble(): pl.pallas_call(assemble_kernel, out_shape=[jax.ShapeDtypeStruct((128 * 8,...]
    concatenate x1, other arithmetic: 0.74 us -> 0.02 us  [gathered_body(): jnp.concatenate([piece] + [exchange(piece, 'gx', bits) for bits in (1, 2,...]
  transfers between devices with their start and end apart: 15 -> 9, of which waited for: 10 -> 7; matrix products, arithmetic and copies ran while one was open for 2% -> 0% of each run, Pallas kernels for 21% -> 17%
where the time goes in v7:
time: 44 us; the launch traced here: 43.8 us
  waiting for transfers between devices  19 us (43%)
  Pallas kernels  12.8 us (29%)
  starting transfers between devices  10.4 us (24%)
  other arithmetic  0.91 us (2%)
  between operations  0.7 us (2%)
    ppermute x9, waiting for transfers between devices, exchange(): lax.ppermute(x, axis, [(n, n ^ bits) for n in range(lax.axis_size(axis))])  19 us
    ppermute x9, starting transfers between devices, exchange(): lax.ppermute(x, axis, [(n, n ^ bits) for n in range(lax.axis_size(axis))])  10.4 us
    pallas_call x1, Pallas kernels, cycle(): pl.pallas_call(cycle_kernel, out_shape=jax.ShapeDtypeStruct((FIELD + 128,...  6.69 us
    pallas_call x1, Pallas kernels, local_part(): pl.pallas_call(local_kernel, out_shape=[jax.ShapeDtypeStruct((PIECE, 128)...  2.92 us
    pallas_call x1, Pallas kernels, finish(): pl.pallas_call(finish_kernel, out_shape=[jax.ShapeDtypeStruct(guess.shape...  1.47 us
    pallas_call x1, Pallas kernels, assemble(): pl.pallas_call(assemble_kernel, out_shape=[jax.ShapeDtypeStruct((128 * 8,...  0.92 us
    add x1, other arithmetic, gathered_body(): piece = mine + exchange(theirs, 'section', 1)  0.9 us
  transfers between devices with their start and end apart: 9, of which 7 were waited for; matrix products, arithmetic and copies ran while one was open for 0% of the time, Pallas kernels for 17%

profile of v7, /device:TPU:0, one launch (start us, length us, event | category | flops | bytes accessed | tf_op | source)
XLA Modules:
  0.0 43.8 jit_solution(436755899471242694)
XLA Ops:
  0.6 2.9 %local_part.1 = (f32[136,128]{1,0:T(8,128)}, f32[136,128]{1,0:T(8,128)}) custom-call(f32[5,5,2,160]{3,2,1,0:T(2,128)} %bitcast.6, f32[5,5,2,160]{3,2,1,0:T(2,128)} %bitcast.4, f32[5,5,160]{2,1,0:T(8,128)} %kappa_in.1, s32[6,1,1,32]{3,2,1,0:T(1,128)} %flags_in.1, f32[64,64]{1,0:T(8,128)} %constant.4.clone.rows_in, f32[160,320]{1,0:T(8,128)} %constant.5.clone.lines_in), custom_call_target="tpu_custom_call" | custom-call | flops 20000000 | bytes 8000000 | tf_op jit(solution)/shard_map/local_part/pallas_call | solution.py:557
  3.6 0.5 %collective-permute-start = (f32[136,128]{1,0:T(8,128)}, f32[136,128]{1,0:T(8,128)S(1)}, u32[]{:S(2)}, u32[]{:S(2)}) collective-permute-start(f32[136,128]{1,0:T(8,128)} %get-tuple-element.15), channel_id=1, source_target_pairs={{0,16},{16,0},{1,17},{17,1},{2,18},{18,2},{3,19},{19,3},{4,20},{20... | collective-permute-start | bytes 208904 | tf_op jit(solution)/shard_map/ppermute | solution.py:1042
  4.1 1.1 %collective-permute-done = f32[136,128]{1,0:T(8,128)S(1)} collective-permute-done((f32[136,128]{1,0:T(8,128)}, f32[136,128]{1,0:T(8,128)S(1)}, u32[]{:S(2)}, u32[]{:S(2)}) %collective-permute-start) | collective-permute-done | bytes 69664 | tf_op jit(solution)/shard_map/ppermute | solution.py:1042
  5.2 0.9 %add.3 = f32[136,128]{1,0:T(8,128)S(1)} add(f32[136,128]{1,0:T(8,128)} %get-tuple-element.14, f32[136,128]{1,0:T(8,128)S(1)} %collective-permute-done) | non-fusion elementwise | flops 17408 | bytes 208896 | tf_op jit(solution)/shard_map/add | solution.py:1048
  6.1 5.0 %collective-permute-start.3 = (f32[136,128]{1,0:T(8,128)S(1)}, f32[136,128]{1,0:T(8,128)S(1)}, u32[]{:S(2)}, u32[]{:S(2)}) collective-permute-start(f32[136,128]{1,0:T(8,128)S(1)} %add.3), channel_id=1, source_target_pairs={{0,12},{4,8},{8,4},{12,0},{1,13},{5,9},{9,5},{13,1},{2,14},{6,10},... | collective-permute-start | bytes 208904 | tf_op jit(solution)/shard_map/ppermute | solution.py:1042
  11.1 0.0 collective-permute-start.2
  11.1 0.6 %collective-permute-start.1 = (f32[136,128]{1,0:T(8,128)S(1)}, f32[136,128]{1,0:T(8,128)S(1)}, u32[]{:S(2)}, u32[]{:S(2)}) collective-permute-start(f32[136,128]{1,0:T(8,128)S(1)} %add.3), channel_id=1, source_target_pairs={{0,4},{4,0},{8,12},{12,8},{1,5},{5,1},{9,13},{13,9},{2,6},{6,2},{1... | collective-permute-start | bytes 208904 | tf_op jit(solution)/shard_map/ppermute | solution.py:1042
  11.7 2.2 %collective-permute-done.3 = f32[136,128]{1,0:T(8,128)S(1)} collective-permute-done((f32[136,128]{1,0:T(8,128)S(1)}, f32[136,128]{1,0:T(8,128)S(1)}, u32[]{:S(2)}, u32[]{:S(2)}) %collective-permute-start.3) | collective-permute-done | bytes 69664 | tf_op jit(solution)/shard_map/ppermute | solution.py:1042
  13.9 3.4 %collective-permute-done.2 = f32[136,128]{1,0:T(8,128)S(1)} collective-permute-done((f32[136,128]{1,0:T(8,128)S(1)}, f32[136,128]{1,0:T(8,128)S(1)}, u32[]{:S(2)}, u32[]{:S(2)}) %collective-permute-start.2) | collective-permute-done | bytes 69664 | tf_op jit(solution)/shard_map/ppermute | solution.py:1042
  17.3 0.0 collective-permute-done.1
  17.3 2.5 %collective-permute-start.6 = (f32[544,128]{1,0:T(8,128)S(1)}, f32[544,128]{1,0:T(8,128)S(1)}, u32[]{:S(2)}, u32[]{:S(2)}) collective-permute-start(f32[544,128]{1,0:T(8,128)S(1)} %pad_maximum_fusion.block0), channel_id=1, source_target_pairs={{0,3},{1,2},{2,1},{3,0},{4,7},{5,6},{6,5},{7,4},{8,11},{9,10},{10,... | collective-permute-start | bytes 835592 | tf_op jit(solution)/shard_map/ppermute | solution.py:1042
  19.8 0.5 %collective-permute-start.5 = (f32[544,128]{1,0:T(8,128)S(1)}, f32[544,128]{1,0:T(8,128)S(1)}, u32[]{:S(2)}, u32[]{:S(2)}) collective-permute-start(f32[544,128]{1,0:T(8,128)S(1)} %pad_maximum_fusion.block0), channel_id=1, source_target_pairs={{0,2},{1,3},{2,0},{3,1},{4,6},{5,7},{6,4},{7,5},{8,10},{9,11},{10,... | collective-permute-start | bytes 835592 | tf_op jit(solution)/shard_map/ppermute | solution.py:1042
  20.3 0.5 %collective-permute-start.4 = (f32[544,128]{1,0:T(8,128)S(1)}, f32[544,128]{1,0:T(8,128)S(1)}, u32[]{:S(2)}, u32[]{:S(2)}) collective-permute-start(f32[544,128]{1,0:T(8,128)S(1)} %pad_maximum_fusion.block0), channel_id=1, source_target_pairs={{0,1},{1,0},{2,3},{3,2},{4,5},{5,4},{6,7},{7,6},{8,9},{9,8},{10,11... | collective-permute-start | bytes 835592 | tf_op jit(solution)/shard_map/ppermute | solution.py:1042
  20.9 7.0 %collective-permute-done.6.block3 = f32[544,128]{1,0:T(8,128)S(1)} collective-permute-done((f32[544,128]{1,0:T(8,128)S(1)}, f32[544,128]{1,0:T(8,128)S(1)}, u32[]{:S(2)}, u32[]{:S(2)}) %collective-permute-start.6) | collective-permute-done | bytes 278560 | tf_op jit(solution)/shard_map/ppermute | solution.py:1042
  27.9 4.4 %collective-permute-done.5.block2 = f32[544,128]{1,0:T(8,128)S(1)} collective-permute-done((f32[544,128]{1,0:T(8,128)S(1)}, f32[544,128]{1,0:T(8,128)S(1)}, u32[]{:S(2)}, u32[]{:S(2)}) %collective-permute-start.5) | collective-permute-done | bytes 278560 | tf_op jit(solution)/shard_map/ppermute | solution.py:1042
  32.3 0.1 collective-permute-done.4.block1
  32.4 0.9 %assemble.1 = (f32[1024,128]{1,0:T(8,128)S(1)}, f32[2704,128]{1,0:T(8,128)S(1)}) custom-call(f32[544,128]{1,0:T(8,128)S(1)} %pad_maximum_fusion.block0, f32[544,128]{1,0:T(8,128)S(1)} %collective-permute-done.4.block1, f32[544,128]{1,0:T(8,128)S(1)} %collective-permute-done.5.block2, f32[544,128]{1,0:T(8,128)S(1)} %collective-permute-done.6.block3), custom_call_target="tpu_custom_call" | custom-call | tf_op jit(solution)/shard_map/assemble/pallas_call | solution.py:975
  33.4 0.1 collective-permute-start.7
  33.4 6.7 %cycle.1.own = f32[1128,128]{1,0:T(8,128)S(1)} custom-call(f32[2704,128]{1,0:T(8,128)S(1)} %get-tuple-element.16.coefs, f32[1024,128]{1,0:T(8,128)S(1)} %get-tuple-element.17.assembled.own_start), custom_call_target="tpu_custom_call" | custom-call | flops 40000000 | bytes 30000000 | tf_op jit(solution)/shard_map/cycle/pallas_call | solution.py:1000
  40.1 0.0 copy-start
  40.1 0.0 collective-permute-done.7.other_start
  40.2 0.6 %collective-permute-start.8 = (f32[1128,128]{1,0:T(8,128)S(1)}, f32[1128,128]{1,0:T(8,128)S(1)}, u32[]{:S(2)}, u32[]{:S(2)}) collective-permute-start(f32[1128,128]{1,0:T(8,128)S(1)} %cycle.1.own), channel_id=1, source_target_pairs={{0,16},{16,0},{1,17},{17,1},{2,18},{18,2},{3,19},{19,3},{4,20},{20... | collective-permute-start | bytes 1732616 | tf_op jit(solution)/shard_map/ppermute | solution.py:1042
  40.7 0.8 %early.1 = (f32[16,128]{1,0:T(8,128)S(1)}, f32[192,160]{1,0:T(8,128)S(1)}) custom-call(f32[1128,128]{1,0:T(8,128)S(1)} %cycle.1.own, f32[1024,128]{1,0:T(8,128)S(1)} %get-tuple-element.17.assembled.own_start, f32[1024,128]{1,0:T(8,128)S(1)} %collective-permute-done.7.other_start), custom_call_target="tpu_custom_call" | custom-call | flops 4000000 | bytes 4000000 | tf_op jit(solution)/shard_map/early/pallas_call | solution.py:1013
  41.5 0.8 %collective-permute-done.8.other = f32[1128,128]{1,0:T(8,128)S(1)} collective-permute-done((f32[1128,128]{1,0:T(8,128)S(1)}, f32[1128,128]{1,0:T(8,128)S(1)}, u32[]{:S(2)}, u32[]{:S(2)}) %collective-permute-start.8) | collective-permute-done | bytes 577568 | tf_op jit(solution)/shard_map/ppermute | solution.py:1042
  42.3 0.0 copy-done
  42.3 1.5 %finish.1 = (f32[5,5,2,160]{3,2,1,0:T(2,128)}, f32[5,5,2,160]{3,2,1,0:T(2,128)}, f32[3]{0:T(128)}) custom-call(f32[1128,128]{1,0:T(8,128)S(1)} %cycle.1.own, f32[1128,128]{1,0:T(8,128)S(1)} %collective-permute-done.8.other, f32[1024,128]{1,0:T(8,128)S(1)} %get-tuple-element.17.assembled.own_start, f32[1024,128]{1,0:T(8,128)S(1)} %collective-permute-done.7.other_start, ...), custom_call_target="tpu_custom_call" | custom-call | tf_op jit(solution)/shard_map/finish/pallas_call | solution.py:1026
  (1 shorter events, 0.0 us)
Async XLA Ops:
  3.6 1.6 %collective-permute-start = (f32[136,128]{1,0:T(8,128)}, f32[136,128]{1,0:T(8,128)S(1)}, u32[]{:S(2)}, u32[]{:S(2)}) collective-permute-start(f32[136,128]{1,0:T(8,128)} %get-tuple-element.15), channel_id=1, source_target_pairs={{0,16},{16,0},{1,17},{17,1},{2,18},{18,2},{3,19},{19,3},{4,20},{20... | collective-permute-start | bytes 208904 | tf_op jit(solution)/shard_map/ppermute | solution.py:1042
  6.1 7.8 %collective-permute-start.3 = (f32[136,128]{1,0:T(8,128)S(1)}, f32[136,128]{1,0:T(8,128)S(1)}, u32[]{:S(2)}, u32[]{:S(2)}) collective-permute-start(f32[136,128]{1,0:T(8,128)S(1)} %add.3), channel_id=1, source_target_pairs={{0,12},{4,8},{8,4},{12,0},{1,13},{5,9},{9,5},{13,1},{2,14},{6,10},... | collective-permute-start | bytes 208904 | tf_op jit(solution)/shard_map/ppermute | solution.py:1042
  11.1 6.2 %collective-permute-start.2 = (f32[136,128]{1,0:T(8,128)S(1)}, f32[136,128]{1,0:T(8,128)S(1)}, u32[]{:S(2)}, u32[]{:S(2)}) collective-permute-start(f32[136,128]{1,0:T(8,128)S(1)} %add.3), channel_id=1, source_target_pairs={{0,8},{4,12},{8,0},{12,4},{1,9},{5,13},{9,1},{13,5},{2,10},{6,14},... | collective-permute-start | bytes 208904 | tf_op jit(solution)/shard_map/ppermute | solution.py:1042
  11.1 6.2 %collective-permute-start.1 = (f32[136,128]{1,0:T(8,128)S(1)}, f32[136,128]{1,0:T(8,128)S(1)}, u32[]{:S(2)}, u32[]{:S(2)}) collective-permute-start(f32[136,128]{1,0:T(8,128)S(1)} %add.3), channel_id=1, source_target_pairs={{0,4},{4,0},{8,12},{12,8},{1,5},{5,1},{9,13},{13,9},{2,6},{6,2},{1... | collective-permute-start | bytes 208904 | tf_op jit(solution)/shard_map/ppermute | solution.py:1042
  17.3 10.6 %collective-permute-start.6 = (f32[544,128]{1,0:T(8,128)S(1)}, f32[544,128]{1,0:T(8,128)S(1)}, u32[]{:S(2)}, u32[]{:S(2)}) collective-permute-start(f32[544,128]{1,0:T(8,128)S(1)} %pad_maximum_fusion.block0), channel_id=1, source_target_pairs={{0,3},{1,2},{2,1},{3,0},{4,7},{5,6},{6,5},{7,4},{8,11},{9,10},{10,... | collective-permute-start | bytes 835592 | tf_op jit(solution)/shard_map/ppermute | solution.py:1042
  19.8 12.5 %collective-permute-start.5 = (f32[544,128]{1,0:T(8,128)S(1)}, f32[544,128]{1,0:T(8,128)S(1)}, u32[]{:S(2)}, u32[]{:S(2)}) collective-permute-start(f32[544,128]{1,0:T(8,128)S(1)} %pad_maximum_fusion.block0), channel_id=1, source_target_pairs={{0,2},{1,3},{2,0},{3,1},{4,6},{5,7},{6,4},{7,5},{8,10},{9,11},{10,... | collective-permute-start | bytes 835592 | tf_op jit(solution)/shard_map/ppermute | solution.py:1042
  20.3 12.1 %collective-permute-start.4 = (f32[544,128]{1,0:T(8,128)S(1)}, f32[544,128]{1,0:T(8,128)S(1)}, u32[]{:S(2)}, u32[]{:S(2)}) collective-permute-start(f32[544,128]{1,0:T(8,128)S(1)} %pad_maximum_fusion.block0), channel_id=1, source_target_pairs={{0,1},{1,0},{2,3},{3,2},{4,5},{5,4},{6,7},{7,6},{8,9},{9,8},{10,11... | collective-permute-start | bytes 835592 | tf_op jit(solution)/shard_map/ppermute | solution.py:1042
  33.4 6.8 %collective-permute-start.7 = (f32[1024,128]{1,0:T(8,128)S(1)}, f32[1024,128]{1,0:T(8,128)S(1)}, u32[]{:S(2)}, u32[]{:S(2)}) collective-permute-start(f32[1024,128]{1,0:T(8,128)S(1)} %get-tuple-element.17.assembled.own_start), channel_id=1, source_target_pairs={{0,16},{16,0},{1,17},{17,1},{2,18},{18,2},{3,19},{19,3},{4,20},{20... | collective-permute-start | bytes 1572872 | tf_op jit(solution)/shard_map/ppermute | solution.py:1042
  40.1 2.2 %copy-start = (f32[2,5,5,160]{3,0,2,1:T(2,128)S(1)}, f32[2,5,5,160]{3,0,2,1:T(2,128)}, u32[]{:S(2)}) copy-start(f32[2,5,5,160]{3,0,2,1:T(2,128)} %param.7) | copy-start | bytes 96004
  40.2 2.2 %collective-permute-start.8 = (f32[1128,128]{1,0:T(8,128)S(1)}, f32[1128,128]{1,0:T(8,128)S(1)}, u32[]{:S(2)}, u32[]{:S(2)}) collective-permute-start(f32[1128,128]{1,0:T(8,128)S(1)} %cycle.1.own), channel_id=1, source_target_pairs={{0,16},{16,0},{1,17},{17,1},{2,18},{18,2},{3,19},{19,3},{4,20},{20... | collective-permute-start | bytes 1732616 | tf_op jit(solution)/shard_map/ppermute | solution.py:1042

commit v8 on v7

--- a/solution.py
+++ b/solution.py
@@ -352,8 +352,7 @@
 COLS = 16
 HALF = 64
 TRACE = 40
-KAPPA = HALF + TRACE
-PIECE = KAPPA + 32
+PIECE = HALF + TRACE
 FIELD = 1000
 F32 = jnp.float32
 
@@ -413,8 +412,8 @@
     return (nu - c * (1.0 - flag) / 2.0) * (1.0 / float(weights[-1]))
 
 
-def column_tables():
-    kx, ky, kz = (element_matrix(5, d) for d in range(3))
+def row_table():
+    kx, ky = (element_matrix(5, d) for d in range(2))
     rows = np.zeros((64, 64))
     for s in range(2):
         for i in range(5):
@@ -423,12 +422,7 @@
                 for m in range(5):
                     rows[r, s * 32 + m * 5 + j] += kx[i, m]
                     rows[r, s * 32 + i * 5 + m] += ky[j, m]
-    lines = np.zeros((160, 320))
-    for e in range(EZ):
-        lines[e * 5 : e * 5 + 5, e * 5 : e * 5 + 5] = kz.T
-        lines[(e - 1) % EZ * 5 + 4, 160 + e * 5] = 1.0
-        lines[(e + 1) % EZ * 5, 160 + e * 5 + 4] = 1.0
-    return rows.astype(np.float32), lines.astype(np.float32)
+    return rows.astype(np.float32)
 
 
 def pick_line(k):
@@ -468,60 +462,64 @@
 
 
 def local_kernel(
-    rhs_in, guess_in, kappa_in, flags_in, rows_in, lines_in, mine, theirs,
-    rhs, guess, kappa, flags, rows_t, lines_t, sems, x, kap, stack, nodes, traces, krep,
+    rhs_in, guess_in, kappa_in, flags_in, rows_in, mine, theirs,
+    rhs, guess, kappa, flags, rows_t, sems, stack, lines, nodes, traces,
 ):
     sec = lax.axis_index("section")
-    fetch(
-        [(rhs_in, rhs), (guess_in, guess), (kappa_in, kappa), (flags_in, flags), (rows_in, rows_t), (lines_in, lines_t)],
-        sems,
-    )
-    x[...] = jnp.zeros_like(x)
-    kap[...] = jnp.zeros_like(kap)
+    fetch([(rhs_in, rhs), (guess_in, guess), (kappa_in, kappa), (flags_in, flags), (rows_in, rows_t)], sems)
     stack[...] = jnp.zeros_like(stack)
     for i in range(5):
-        kap[5 * i : 5 * i + 5, :] = kappa[i]
+        stack[192 + 5 * i : 197 + 5 * i, :] = kappa[i]
         for j in range(5):
             r = 5 * i + j
             value = guess[i, j]
             left = rhs[i, j] - value
             for s in range(2):
-                x[s * 32 + r : s * 32 + r + 1, :] = value[s : s + 1]
                 stack[s * 32 + r : s * 32 + r + 1, :] = left[s : s + 1]
-    flag = flags[:, 0, 0, :].astype(F32)
-    spread = (iota((EZ, 160), 1) // 5 == iota((EZ, 160), 0)).astype(F32)
-    wide = split_dot(flag, spread)
-    gains = [face_gains(wide[d : d + 1, :], d // 2, d % 2, 5) for d in range(6)]
-    row = iota((32, 160), 0)
-    lane = iota((32, 160), 1) % 5
-    none = jnp.zeros((32, 160), F32)
-    gx = jnp.where(row < 5, gains[0], jnp.where((row >= 20) & (row < 25), gains[1], none))
-    gy = jnp.where(row % 5 == 0, gains[2], jnp.where(row % 5 == 4, gains[3], none))
-    gz = jnp.where(lane == 0, gains[4], jnp.where(lane == 4, gains[5], none))
-    field = x[...]
-    along = exact_dot(rows_t[...], field)
-    across = exact_dot(field, lines_t[...])
-    own = kap[...] + gx + gy + gz
-    for s in range(2):
-        r = slice(s * 32, s * 32 + 32)
-        image = own * field[r] + along[r] + across[r, :160] - gz * across[r, 160:]
-        stack[64 + s * 32 : 96 + s * 32, :] = image
-    stack[128:192, :] = field
-    stack[192:, :] = kap[...]
+                stack[128 + s * 32 + r : 128 + s * 32 + r + 1, :] = value[s : s + 1]
+    stack[64:128, :] = exact_dot(rows_t[...], stack[128:192, :])
     source = stack[...]
+    for k in range(5):
+        lines[224 * k : 224 * k + 224, :] = split_dot(source, pick_line(k))
+
+    def part(k, first):
+        return lines[224 * k + first : 224 * k + first + 32, :]
+
+    repeat = (iota((EZ, 128), 1) % EZ == iota((EZ, 128), 0)).astype(F32)
+    shown = split_dot(flags[:, 0, 0, :].astype(F32), repeat)
+    gains = [face_gains(shown[d : d + 1, :], d // 2, d % 2, 5) for d in range(6)]
+    row = iota((32, 128), 0)
+    none = jnp.zeros((32, 128), F32)
+    own = jnp.where(row < 5, gains[0], jnp.where((row >= 20) & (row < 25), gains[1], none))
+    own = own + jnp.where(row % 5 == 0, gains[2], jnp.where(row % 5 == 4, gains[3], none))
+    kz = element_matrix(5, 2)
     back, back_matrix = split_sections()[1:3]
     nodes[...] = jnp.zeros_like(nodes)
-    krep[...] = jnp.zeros_like(krep)
     for k in range(5):
-        parts = split_dot(source, pick_line(k))
+        diagonal = part(k, 192) + own
+        if k == 0:
+            diagonal = diagonal + gains[4]
+        if k == 4:
+            diagonal = diagonal + gains[5]
+        images = []
+        for s in range(2):
+            first = 128 + 32 * s
+            image = diagonal * part(k, first) + part(k, 64 + 32 * s)
+            for m in range(5):
+                image = image + float(kz[k, m]) * part(m, first)
+            if k == 0:
+                image = image - gains[4] * pltpu.roll(part(4, first), 1, 1)
+            if k == 4:
+                image = image - gains[5] * pltpu.roll(part(0, first), 127, 1)
+            images.append(image)
         for p, mark in enumerate((True, False)):
             total = jnp.zeros((32, 128), F32)
             trace = jnp.zeros((32, 128), F32)
             for s in range(2):
-                total = total + pair_factors(sec, back, mark, s) * parts[s * 32 : s * 32 + 32]
+                total = total + pair_factors(sec, back, mark, s) * part(k, 32 * s)
                 factor = pair_factors(sec, STEP_SIZE * back_matrix, mark, s)
-                total = total - factor * parts[64 + s * 32 : 96 + s * 32]
-                trace = trace + factor * parts[128 + s * 32 : 160 + s * 32]
+                total = total - factor * images[s]
+                trace = trace + factor * part(k, 128 + 32 * s)
             nodes[128 * p + 25 * k : 128 * p + 25 * k + 25, :] = total[:25]
             start = 80 * p + 16 * k
             traces[start : start + 5, :] = trace[:5]
@@ -530,17 +528,20 @@
                     r = start + face_place(i, j)
                     traces[r : r + 1, :] = trace[5 * i + j : 5 * i + j + 1]
             traces[start + 11 : start + 16, :] = trace[20:25]
-        krep[25 * k : 25 * k + 25, :] = parts[192:217]
-    repeat = (iota((EZ, 128), 1) % EZ == iota((EZ, 128), 0)).astype(F32)
-    shown = split_dot(flag, repeat)
     upper = iota((1, 128), 1) < 64
     for r in range(3):
         nodes[125 + r : 126 + r, :] = jnp.where(upper, shown[2 * r : 2 * r + 1], shown[2 * r + 1 : 2 * r + 2])
     for p, out in enumerate((mine, theirs)):
         out[:HALF, :] = pack_nodes(nodes[128 * p : 128 * p + 128, :])
-        out[HALF:KAPPA, :] = pack_nodes(traces[80 * p : 80 * p + 80, :])
-    mine[KAPPA:, :] = choose(iota((32, 128), 1) // EZ, [krep[32 * q : 32 * q + 32, :] for q in range(4)])
-    theirs[KAPPA:, :] = jnp.zeros((32, 128), F32)
+        out[HALF:PIECE, :] = pack_nodes(traces[80 * p : 80 * p + 80, :])
+    for k in range(5):
+        nodes[25 * k : 25 * k + 25, :] = part(k, 192)[:25]
+    mine[PIECE:, :] = choose(iota((32, 128), 1) // EZ, [nodes[32 * q : 32 * q + 32, :] for q in range(4)])
+
+
+def part_kernel(source, piece, kappa):
+    piece[...] = source[:PIECE, :]
+    kappa[...] = source[PIECE:, :]
 
 
 VMEM = pl.BlockSpec(memory_space=pltpu.VMEM)
@@ -552,27 +553,35 @@
 
 
 def local_part(rhs, guess, kappa, flags):
-    rows_t, lines_t = column_tables()
-    operands = (rhs, guess, kappa, flags, jnp.asarray(rows_t), jnp.asarray(lines_t))
+    operands = (rhs, guess, kappa, flags, jnp.asarray(row_table()))
     return pl.pallas_call(
         local_kernel,
-        out_shape=[jax.ShapeDtypeStruct((PIECE, 128), F32)] * 2,
-        in_specs=[HBM] * 6,
+        out_shape=[jax.ShapeDtypeStruct((rows, 128), F32) for rows in (PIECE + 32, PIECE)],
+        in_specs=[HBM] * 5,
         out_specs=[VMEM] * 2,
         scratch_shapes=[pltpu.VMEM(o.shape, o.dtype) for o in operands]
         + [
-            pltpu.SemaphoreType.DMA((6,)),
-            pltpu.VMEM((64, 160), F32),
-            pltpu.VMEM((32, 160), F32),
+            pltpu.SemaphoreType.DMA((5,)),
             pltpu.VMEM((224, 160), F32),
+            pltpu.VMEM((5 * 224, 128), F32),
             pltpu.VMEM((256, 128), F32),
             pltpu.VMEM((160, 128), F32),
-            pltpu.VMEM((128, 128), F32),
         ],
         compiler_params=limit(60),
         cost_estimate=pl.CostEstimate(flops=20_000_000, bytes_accessed=8_000_000, transcendentals=0),
         name="local_part",
     )(*operands)
+
+
+def part(x):
+    return pl.pallas_call(
+        part_kernel,
+        out_shape=[jax.ShapeDtypeStruct((rows, 128), F32) for rows in (PIECE, 32)],
+        in_specs=[VMEM],
+        out_specs=[VMEM] * 2,
+        compiler_params=limit(16),
+        name="part",
+    )(x)
 
 
 class Level:
@@ -591,11 +600,11 @@
     return pieces[pl.ds(8 * h * size + r, 8, stride=size), :]
 
 
-def place_pieces(blocks, stride, pieces, first, size):
+def place_pieces(blocks, stride, pieces, first, size, outer="gy"):
     my_gx, my_gy = lax.axis_index("gx"), lax.axis_index("gy")
     for b, block in enumerate(blocks):
         for a in range(4):
-            column = (my_gx ^ a) * 4 + (my_gy ^ b)
+            column = (my_gx ^ a) * 4 + (my_gy ^ b) if outer == "gy" else (my_gx ^ b) * 4 + (my_gy ^ a)
             start = pl.multiple_of(column * size, 8)
             pieces[pl.ds(start, size), :] = block[a * stride + first : a * stride + first + size, :]
 
@@ -652,11 +661,11 @@
 RADIUS = (CHEB_HIGH - CHEB_LOW) / 2.0
 
 
-def assemble_kernel(block0, block1, block2, block3, field, coefs, pieces, edges, kappas, traces, kap):
+def assemble_kernel(block0, block1, block2, block3, kappa0, kappa1, kappa2, kappa3, field, coefs, pieces, edges, kappas, traces, kap):
     blocks = (block0, block1, block2, block3)
     place_pieces(blocks, PIECE, pieces, 0, HALF)
     place_pieces(blocks, PIECE, edges, HALF, TRACE)
-    place_pieces(blocks, PIECE, kappas, KAPPA, 32)
+    place_pieces((kappa0, kappa1, kappa2, kappa3), 32, kappas, 0, 32, outer="gx")
     lanes = Lanes()
     group, lane = lanes.group, lanes.lane
 
@@ -971,14 +980,14 @@
                 res_out[i, j, s : s + 1, :] = outs[64 + s * 32 + r : 64 + s * 32 + r + 1, :]
 
 
-def assemble(blocks):
+def assemble(blocks, kappas):
     return pl.pallas_call(
         assemble_kernel,
         out_shape=[
             jax.ShapeDtypeStruct((128 * 8, 128), F32),
             jax.ShapeDtypeStruct((REGISTERS * 8, 128), F32),
         ],
-        in_specs=[VMEM] * 4,
+        in_specs=[VMEM] * 8,
         out_specs=[VMEM] * 2,
         scratch_shapes=[
             pltpu.VMEM((COLS * HALF, 128), F32),
@@ -989,7 +998,7 @@
         ],
         compiler_params=limit(16),
         name="assemble",
-    )(*blocks)
+    )(*blocks, *kappas)
 
 
 def cycle(coefs, assembled):
@@ -1045,10 +1054,17 @@
 def gathered_body(rhs, guess, kappa, bc_flags):
     rhs, guess = (jnp.transpose(v, (1, 2, 0, 3)) for v in (rhs, guess))
     mine, theirs = local_part(rhs, guess, kappa, bc_flags)
-    piece = mine + exchange(theirs, "section", 1)
-    line = jnp.concatenate([piece] + [exchange(piece, "gx", bits) for bits in (1, 2, 3)])
+    got, mine, kappa_piece = lax.optimization_barrier((exchange(theirs, "section", 1), *part(mine)))
+    piece = mine + got
+    parts = [exchange(piece, "gx", bits) for bits in (1, 2, 3)]
+    parts[0], kappa_piece = lax.optimization_barrier((parts[0], kappa_piece))
+    others = [exchange(kappa_piece, "gy", bits) for bits in (1, 2, 3)]
+    parts, others = lax.optimization_barrier((parts, others))
+    line = jnp.concatenate([piece] + parts)
+    across = jnp.concatenate([kappa_piece] + others)
     blocks = [line] + [exchange(line, "gy", bits) for bits in (1, 2, 3)]
-    start, coefs = assemble(blocks)
+    kappas = [across] + [exchange(across, "gx", bits) for bits in (1, 2, 3)]
+    start, coefs = assemble(blocks, kappas)
     other_start = exchange(start, "section", 1)
     own, other_start = lax.optimization_barrier((cycle(coefs, start), other_start))
     sums, column = early(own, start, other_start)

time: 44 us -> 42.8 us (0.973)
  waiting for transfers between devices: 19 us -> 10.6 us
  starting transfers between devices: 10.4 us -> 17.9 us
  other arithmetic: 0.91 us -> 0.02 us
  local copies, waits for them, and re-layouts: 0.01 us -> 0.9 us
    ppermute x9 -> x15, waiting for transfers between devices: 19 us -> 10.6 us  [exchange(): lax.ppermute(x, axis, [(n, n ^ bits) for n in range(lax.axis_size(axis))])]
    ppermute x9 -> x15, starting transfers between devices: 10.4 us -> 17.9 us  [exchange(): lax.ppermute(x, axis, [(n, n ^ bits) for n in range(lax.axis_size(axis))])]
    unnamed x2 -> x7, local copies, waits for them, and re-layouts: 0.01 us -> 0.89 us
    add x1, other arithmetic: 0.9 us -> 0.01 us  [gathered_body(): piece = mine + got]
    pallas_call x1 -> x2, Pallas kernels: 2.92 us -> 2.52 us  [the longest x1 2.52 us: local_part(): pl.pallas_call(local_kernel, out_shape=[jax.ShapeDtypeStruct((rows, 128),...]
  transfers between devices with their start and end apart: 9 -> 15, of which waited for: 7 -> 9; matrix products, arithmetic and copies ran while one was open for 0% -> 0% of each run, Pallas kernels for 17% -> 18%
where the time goes in v8:
time: 42.8 us; the launch traced here: 42.6 us
  starting transfers between devices  17.9 us (42%)
  Pallas kernels  12.4 us (29%)
  waiting for transfers between devices  10.6 us (25%)
  local copies, waits for them, and re-layouts  0.9 us (2%)
  between operations  0.71 us (2%)
    ppermute x15, starting transfers between devices, exchange(): lax.ppermute(x, axis, [(n, n ^ bits) for n in range(lax.axis_size(axis))])  17.9 us
    ppermute x15, waiting for transfers between devices, exchange(): lax.ppermute(x, axis, [(n, n ^ bits) for n in range(lax.axis_size(axis))])  10.6 us
    pallas_call x1, Pallas kernels, cycle(): pl.pallas_call(cycle_kernel, out_shape=jax.ShapeDtypeStruct((FIELD + 128,...  6.69 us
    pallas_call x1, Pallas kernels, local_part(): pl.pallas_call(local_kernel, out_shape=[jax.ShapeDtypeStruct((rows, 128),...  2.52 us
    pallas_call x1, Pallas kernels, finish(): pl.pallas_call(finish_kernel, out_shape=[jax.ShapeDtypeStruct(guess.shape...  1.47 us
    pallas_call x1, Pallas kernels, assemble(): pl.pallas_call(assemble_kernel, out_shape=[jax.ShapeDtypeStruct((128 * 8,...  0.92 us
    unnamed x7, local copies, waits for them, and re-layouts  0.89 us
  transfers between devices with their start and end apart: 15, of which 9 were waited for; matrix products, arithmetic and copies ran while one was open for 0% of the time, Pallas kernels for 18%

profile of v8, /device:TPU:0, one launch (start us, length us, event | category | flops | bytes accessed | tf_op | source)
XLA Modules:
  0.0 42.6 jit_solution(3005006156034066120)
XLA Ops:
  0.6 2.5 %local_part.1 = (f32[136,128]{1,0:T(8,128)}, f32[104,128]{1,0:T(8,128)}) custom-call(f32[5,5,2,160]{3,2,1,0:T(2,128)} %bitcast.6, f32[5,5,2,160]{3,2,1,0:T(2,128)} %bitcast.4, f32[5,5,160]{2,1,0:T(8,128)} %kappa_in.1, s32[6,1,1,32]{3,2,1,0:T(1,128)} %flags_in.1, f32[64,64]{1,0:T(8,128)} %constant.2.clone.rows_in), custom_call_target="tpu_custom_call" | custom-call | flops 20000000 | bytes 8000000 | tf_op jit(solution)/shard_map/local_part/pallas_call | solution.py:557
  3.2 0.5 %collective-permute-start = (f32[104,128]{1,0:T(8,128)}, f32[104,128]{1,0:T(8,128)S(1)}, u32[]{:S(2)}, u32[]{:S(2)}) collective-permute-start(f32[104,128]{1,0:T(8,128)} %get-tuple-element.27), channel_id=1, source_target_pairs={{0,16},{16,0},{1,17},{17,1},{2,18},{18,2},{3,19},{19,3},{4,20},{20... | collective-permute-start | bytes 159752 | tf_op jit(solution)/shard_map/ppermute | solution.py:1051
  3.7 0.9 %copy-done.1 = f32[136,128]{1,0:T(8,128)S(1)} copy-done((f32[136,128]{1,0:T(8,128)S(1)}, f32[136,128]{1,0:T(8,128)}, u32[]{:S(2)}) %copy-start.1) | copy-done | bytes 69656
  4.6 0.2 collective-permute-done
  4.8 3.0 %collective-permute-start.1 = (f32[104,128]{1,0:T(8,128)S(1)}, f32[104,128]{1,0:T(8,128)S(1)}, u32[]{:S(2)}, u32[]{:S(2)}) collective-permute-start(f32[104,128]{1,0:T(8,128)S(1)} %add.3), channel_id=1, source_target_pairs={{0,4},{4,0},{8,12},{12,8},{1,5},{5,1},{9,13},{13,9},{2,6},{6,2},{1... | collective-permute-start | bytes 159752 | tf_op jit(solution)/shard_map/ppermute | solution.py:1051
  7.8 2.5 %collective-permute-start.3 = (f32[104,128]{1,0:T(8,128)S(1)}, f32[104,128]{1,0:T(8,128)S(1)}, u32[]{:S(2)}, u32[]{:S(2)}) collective-permute-start(f32[104,128]{1,0:T(8,128)S(1)} %add.3), channel_id=1, source_target_pairs={{0,12},{4,8},{8,4},{12,0},{1,13},{5,9},{9,5},{13,1},{2,14},{6,10},... | collective-permute-start | bytes 159752 | tf_op jit(solution)/shard_map/ppermute | solution.py:1051
  10.2 0.1 collective-permute-start.2
  10.4 0.0 collective-permute-done.1
  10.4 2.4 %collective-permute-start.6 = (f32[32,128]{1,0:T(8,128)S(1)}, f32[32,128]{1,0:T(8,128)S(1)}, u32[]{:S(2)}, u32[]{:S(2)}) collective-permute-start(f32[32,128]{1,0:T(8,128)S(1)} %get-tuple-element.35), channel_id=1, source_target_pairs={{0,3},{1,2},{2,1},{3,0},{4,7},{5,6},{6,5},{7,4},{8,11},{9,10},{10,... | collective-permute-start | bytes 49160 | tf_op jit(solution)/shard_map/ppermute | solution.py:1051
  12.8 0.5 %collective-permute-start.5 = (f32[32,128]{1,0:T(8,128)S(1)}, f32[32,128]{1,0:T(8,128)S(1)}, u32[]{:S(2)}, u32[]{:S(2)}) collective-permute-start(f32[32,128]{1,0:T(8,128)S(1)} %get-tuple-element.35), channel_id=1, source_target_pairs={{0,2},{1,3},{2,0},{3,1},{4,6},{5,7},{6,4},{7,5},{8,10},{9,11},{10,... | collective-permute-start | bytes 49160 | tf_op jit(solution)/shard_map/ppermute | solution.py:1051
  13.3 0.5 %collective-permute-start.4 = (f32[32,128]{1,0:T(8,128)S(1)}, f32[32,128]{1,0:T(8,128)S(1)}, u32[]{:S(2)}, u32[]{:S(2)}) collective-permute-start(f32[32,128]{1,0:T(8,128)S(1)} %get-tuple-element.35), channel_id=1, source_target_pairs={{0,1},{1,0},{2,3},{3,2},{4,5},{5,4},{6,7},{7,6},{8,9},{9,8},{10,11... | collective-permute-start | bytes 49160 | tf_op jit(solution)/shard_map/ppermute | solution.py:1051
  13.9 0.1 collective-permute-done.3
  14.0 2.0 %collective-permute-done.2 = f32[104,128]{1,0:T(8,128)S(1)} collective-permute-done((f32[104,128]{1,0:T(8,128)S(1)}, f32[104,128]{1,0:T(8,128)S(1)}, u32[]{:S(2)}, u32[]{:S(2)}) %collective-permute-start.2) | collective-permute-done | bytes 53280 | tf_op jit(solution)/shard_map/ppermute | solution.py:1051
  16.0 0.0 collective-permute-done.6
  16.0 0.6 %collective-permute-done.5 = f32[32,128]{1,0:T(8,128)S(1)} collective-permute-done((f32[32,128]{1,0:T(8,128)S(1)}, f32[32,128]{1,0:T(8,128)S(1)}, u32[]{:S(2)}, u32[]{:S(2)}) %collective-permute-start.5) | collective-permute-done | bytes 16416 | tf_op jit(solution)/shard_map/ppermute | solution.py:1051
  16.6 0.5 %collective-permute-done.4 = f32[32,128]{1,0:T(8,128)S(1)} collective-permute-done((f32[32,128]{1,0:T(8,128)S(1)}, f32[32,128]{1,0:T(8,128)S(1)}, u32[]{:S(2)}, u32[]{:S(2)}) %collective-permute-start.4) | collective-permute-done | bytes 16416 | tf_op jit(solution)/shard_map/ppermute | solution.py:1051
  17.1 1.6 %collective-permute-start.9 = (f32[416,128]{1,0:T(8,128)S(1)}, f32[416,128]{1,0:T(8,128)S(1)}, u32[]{:S(2)}, u32[]{:S(2)}) collective-permute-start(f32[416,128]{1,0:T(8,128)S(1)} %pad_maximum_fusion.block0), channel_id=1, source_target_pairs={{0,3},{1,2},{2,1},{3,0},{4,7},{5,6},{6,5},{7,4},{8,11},{9,10},{10,... | collective-permute-start | bytes 638984 | tf_op jit(solution)/shard_map/ppermute | solution.py:1051
  18.6 0.5 %collective-permute-start.8 = (f32[416,128]{1,0:T(8,128)S(1)}, f32[416,128]{1,0:T(8,128)S(1)}, u32[]{:S(2)}, u32[]{:S(2)}) collective-permute-start(f32[416,128]{1,0:T(8,128)S(1)} %pad_maximum_fusion.block0), channel_id=1, source_target_pairs={{0,2},{1,3},{2,0},{3,1},{4,6},{5,7},{6,4},{7,5},{8,10},{9,11},{10,... | collective-permute-start | bytes 638984 | tf_op jit(solution)/shard_map/ppermute | solution.py:1051
  19.1 1.5 %collective-permute-start.7 = (f32[416,128]{1,0:T(8,128)S(1)}, f32[416,128]{1,0:T(8,128)S(1)}, u32[]{:S(2)}, u32[]{:S(2)}) collective-permute-start(f32[416,128]{1,0:T(8,128)S(1)} %pad_maximum_fusion.block0), channel_id=1, source_target_pairs={{0,1},{1,0},{2,3},{3,2},{4,5},{5,4},{6,7},{7,6},{8,9},{9,8},{10,11... | collective-permute-start | bytes 638984 | tf_op jit(solution)/shard_map/ppermute | solution.py:1051
  20.6 3.6 %collective-permute-start.12 = (f32[128,128]{1,0:T(8,128)S(1)}, f32[128,128]{1,0:T(8,128)S(1)}, u32[]{:S(2)}, u32[]{:S(2)}) collective-permute-start(f32[128,128]{1,0:T(8,128)S(1)} %constant_dynamic-update-slice_fusion.kappa0), channel_id=1, source_target_pairs={{0,12},{4,8},{8,4},{12,0},{1,13},{5,9},{9,5},{13,1},{2,14},{6,10},... | collective-permute-start | bytes 196616 | tf_op jit(solution)/shard_map/ppermute | solution.py:1051
  24.3 2.7 %collective-permute-done.12.kappa3 = f32[128,128]{1,0:T(8,128)S(1)} collective-permute-done((f32[128,128]{1,0:T(8,128)S(1)}, f32[128,128]{1,0:T(8,128)S(1)}, u32[]{:S(2)}, u32[]{:S(2)}) %collective-permute-start.12) | collective-permute-done | bytes 65568 | tf_op jit(solution)/shard_map/ppermute | solution.py:1051
  26.9 0.5 %collective-permute-start.10 = (f32[128,128]{1,0:T(8,128)S(1)}, f32[128,128]{1,0:T(8,128)S(1)}, u32[]{:S(2)}, u32[]{:S(2)}) collective-permute-start(f32[128,128]{1,0:T(8,128)S(1)} %constant_dynamic-update-slice_fusion.kappa0), channel_id=1, source_target_pairs={{0,4},{4,0},{8,12},{12,8},{1,5},{5,1},{9,13},{13,9},{2,6},{6,2},{1... | collective-permute-start | bytes 196616 | tf_op jit(solution)/shard_map/ppermute | solution.py:1051
  27.5 2.0 %collective-permute-done.11.kappa2 = f32[128,128]{1,0:T(8,128)S(1)} collective-permute-done((f32[128,128]{1,0:T(8,128)S(1)}, f32[128,128]{1,0:T(8,128)S(1)}, u32[]{:S(2)}, u32[]{:S(2)}) %collective-permute-start.11) | collective-permute-done | bytes 65568 | tf_op jit(solution)/shard_map/ppermute | solution.py:1051
  29.5 1.7 %collective-permute-done.10.kappa1 = f32[128,128]{1,0:T(8,128)S(1)} collective-permute-done((f32[128,128]{1,0:T(8,128)S(1)}, f32[128,128]{1,0:T(8,128)S(1)}, u32[]{:S(2)}, u32[]{:S(2)}) %collective-permute-start.10) | collective-permute-done | bytes 65568 | tf_op jit(solution)/shard_map/ppermute | solution.py:1051
  31.2 0.9 %assemble.1 = (f32[1024,128]{1,0:T(8,128)S(1)}, f32[2704,128]{1,0:T(8,128)S(1)}) custom-call(f32[416,128]{1,0:T(8,128)S(1)} %pad_maximum_fusion.block0, f32[416,128]{1,0:T(8,128)S(1)} %collective-permute-done.7.block1, f32[416,128]{1,0:T(8,128)S(1)} %collective-permute-done.8.block2, f32[416,128]{1,0:T(8,128)S(1)} %collective-permute-done.9.block3, ...), custom_call_target="tpu_custom_call" | custom-call | tf_op jit(solution)/shard_map/assemble/pallas_call | solution.py:984
  32.1 0.1 collective-permute-start.13
  32.2 6.7 %cycle.1.own = f32[1128,128]{1,0:T(8,128)S(1)} custom-call(f32[2704,128]{1,0:T(8,128)S(1)} %get-tuple-element.42.coefs, f32[1024,128]{1,0:T(8,128)S(1)} %get-tuple-element.43.assembled.own_start), custom_call_target="tpu_custom_call" | custom-call | flops 40000000 | bytes 30000000 | tf_op jit(solution)/shard_map/cycle/pallas_call | solution.py:1009
  38.9 0.0 copy-start
  38.9 0.6 %collective-permute-start.14 = (f32[1128,128]{1,0:T(8,128)S(1)}, f32[1128,128]{1,0:T(8,128)S(1)}, u32[]{:S(2)}, u32[]{:S(2)}) collective-permute-start(f32[1128,128]{1,0:T(8,128)S(1)} %cycle.1.own), channel_id=1, source_target_pairs={{0,16},{16,0},{1,17},{17,1},{2,18},{18,2},{3,19},{19,3},{4,20},{20... | collective-permute-start | bytes 1732616 | tf_op jit(solution)/shard_map/ppermute | solution.py:1051
  39.5 0.8 %early.1 = (f32[16,128]{1,0:T(8,128)S(1)}, f32[192,160]{1,0:T(8,128)S(1)}) custom-call(f32[1128,128]{1,0:T(8,128)S(1)} %cycle.1.own, f32[1024,128]{1,0:T(8,128)S(1)} %get-tuple-element.43.assembled.own_start, f32[1024,128]{1,0:T(8,128)S(1)} %collective-permute-done.13.other_start), custom_call_target="tpu_custom_call" | custom-call | flops 4000000 | bytes 4000000 | tf_op jit(solution)/shard_map/early/pallas_call | solution.py:1022
  40.3 0.8 %collective-permute-done.14.other = f32[1128,128]{1,0:T(8,128)S(1)} collective-permute-done((f32[1128,128]{1,0:T(8,128)S(1)}, f32[1128,128]{1,0:T(8,128)S(1)}, u32[]{:S(2)}, u32[]{:S(2)}) %collective-permute-start.14) | collective-permute-done | bytes 577568 | tf_op jit(solution)/shard_map/ppermute | solution.py:1051
  41.1 1.5 %finish.1 = (f32[5,5,2,160]{3,2,1,0:T(2,128)}, f32[5,5,2,160]{3,2,1,0:T(2,128)}, f32[3]{0:T(128)}) custom-call(f32[1128,128]{1,0:T(8,128)S(1)} %cycle.1.own, f32[1128,128]{1,0:T(8,128)S(1)} %collective-permute-done.14.other, f32[1024,128]{1,0:T(8,128)S(1)} %get-tuple-element.43.assembled.own_start, f32[1024,128]{1,0:T(8,128)S(1)} %collective-permute-done.13.other_start, ...), custom_call_target="tpu_custom_call" | custom-call | tf_op jit(solution)/shard_map/finish/pallas_call | solution.py:1035
  (14 shorter events, 0.1 us)
Async XLA Ops:
  3.2 1.6 %collective-permute-start = (f32[104,128]{1,0:T(8,128)}, f32[104,128]{1,0:T(8,128)S(1)}, u32[]{:S(2)}, u32[]{:S(2)}) collective-permute-start(f32[104,128]{1,0:T(8,128)} %get-tuple-element.27), channel_id=1, source_target_pairs={{0,16},{16,0},{1,17},{17,1},{2,18},{18,2},{3,19},{19,3},{4,20},{20... | collective-permute-start | bytes 159752 | tf_op jit(solution)/shard_map/ppermute | solution.py:1051
  3.7 0.9 %copy-start.1 = (f32[136,128]{1,0:T(8,128)S(1)}, f32[136,128]{1,0:T(8,128)}, u32[]{:S(2)}) copy-start(f32[136,128]{1,0:T(8,128)} %get-tuple-element.28.source) | copy-start | bytes 208900
  4.8 5.6 %collective-permute-start.1 = (f32[104,128]{1,0:T(8,128)S(1)}, f32[104,128]{1,0:T(8,128)S(1)}, u32[]{:S(2)}, u32[]{:S(2)}) collective-permute-start(f32[104,128]{1,0:T(8,128)S(1)} %add.3), channel_id=1, source_target_pairs={{0,4},{4,0},{8,12},{12,8},{1,5},{5,1},{9,13},{13,9},{2,6},{6,2},{1... | collective-permute-start | bytes 159752 | tf_op jit(solution)/shard_map/ppermute | solution.py:1051
  7.8 6.2 %collective-permute-start.3 = (f32[104,128]{1,0:T(8,128)S(1)}, f32[104,128]{1,0:T(8,128)S(1)}, u32[]{:S(2)}, u32[]{:S(2)}) collective-permute-start(f32[104,128]{1,0:T(8,128)S(1)} %add.3), channel_id=1, source_target_pairs={{0,12},{4,8},{8,4},{12,0},{1,13},{5,9},{9,5},{13,1},{2,14},{6,10},... | collective-permute-start | bytes 159752 | tf_op jit(solution)/shard_map/ppermute | solution.py:1051
  10.2 5.7 %collective-permute-start.2 = (f32[104,128]{1,0:T(8,128)S(1)}, f32[104,128]{1,0:T(8,128)S(1)}, u32[]{:S(2)}, u32[]{:S(2)}) collective-permute-start(f32[104,128]{1,0:T(8,128)S(1)} %add.3), channel_id=1, source_target_pairs={{0,8},{4,12},{8,0},{12,4},{1,9},{5,13},{9,1},{13,5},{2,10},{6,14},... | collective-permute-start | bytes 159752 | tf_op jit(solution)/shard_map/ppermute | solution.py:1051
  10.4 5.6 %collective-permute-start.6 = (f32[32,128]{1,0:T(8,128)S(1)}, f32[32,128]{1,0:T(8,128)S(1)}, u32[]{:S(2)}, u32[]{:S(2)}) collective-permute-start(f32[32,128]{1,0:T(8,128)S(1)} %get-tuple-element.35), channel_id=1, source_target_pairs={{0,3},{1,2},{2,1},{3,0},{4,7},{5,6},{6,5},{7,4},{8,11},{9,10},{10,... | collective-permute-start | bytes 49160 | tf_op jit(solution)/shard_map/ppermute | solution.py:1051
  12.8 3.7 %collective-permute-start.5 = (f32[32,128]{1,0:T(8,128)S(1)}, f32[32,128]{1,0:T(8,128)S(1)}, u32[]{:S(2)}, u32[]{:S(2)}) collective-permute-start(f32[32,128]{1,0:T(8,128)S(1)} %get-tuple-element.35), channel_id=1, source_target_pairs={{0,2},{1,3},{2,0},{3,1},{4,6},{5,7},{6,4},{7,5},{8,10},{9,11},{10,... | collective-permute-start | bytes 49160 | tf_op jit(solution)/shard_map/ppermute | solution.py:1051
  13.3 3.7 %collective-permute-start.4 = (f32[32,128]{1,0:T(8,128)S(1)}, f32[32,128]{1,0:T(8,128)S(1)}, u32[]{:S(2)}, u32[]{:S(2)}) collective-permute-start(f32[32,128]{1,0:T(8,128)S(1)} %get-tuple-element.35), channel_id=1, source_target_pairs={{0,1},{1,0},{2,3},{3,2},{4,5},{5,4},{6,7},{7,6},{8,9},{9,8},{10,11... | collective-permute-start | bytes 49160 | tf_op jit(solution)/shard_map/ppermute | solution.py:1051
  17.1 14.1 %collective-permute-start.9 = (f32[416,128]{1,0:T(8,128)S(1)}, f32[416,128]{1,0:T(8,128)S(1)}, u32[]{:S(2)}, u32[]{:S(2)}) collective-permute-start(f32[416,128]{1,0:T(8,128)S(1)} %pad_maximum_fusion.block0), channel_id=1, source_target_pairs={{0,3},{1,2},{2,1},{3,0},{4,7},{5,6},{6,5},{7,4},{8,11},{9,10},{10,... | collective-permute-start | bytes 638984 | tf_op jit(solution)/shard_map/ppermute | solution.py:1051
  18.6 12.6 %collective-permute-start.8 = (f32[416,128]{1,0:T(8,128)S(1)}, f32[416,128]{1,0:T(8,128)S(1)}, u32[]{:S(2)}, u32[]{:S(2)}) collective-permute-start(f32[416,128]{1,0:T(8,128)S(1)} %pad_maximum_fusion.block0), channel_id=1, source_target_pairs={{0,2},{1,3},{2,0},{3,1},{4,6},{5,7},{6,4},{7,5},{8,10},{9,11},{10,... | collective-permute-start | bytes 638984 | tf_op jit(solution)/shard_map/ppermute | solution.py:1051
  19.1 12.1 %collective-permute-start.7 = (f32[416,128]{1,0:T(8,128)S(1)}, f32[416,128]{1,0:T(8,128)S(1)}, u32[]{:S(2)}, u32[]{:S(2)}) collective-permute-start(f32[416,128]{1,0:T(8,128)S(1)} %pad_maximum_fusion.block0), channel_id=1, source_target_pairs={{0,1},{1,0},{2,3},{3,2},{4,5},{5,4},{6,7},{7,6},{8,9},{9,8},{10,11... | collective-permute-start | bytes 638984 | tf_op jit(solution)/shard_map/ppermute | solution.py:1051
  20.6 6.3 %collective-permute-start.12 = (f32[128,128]{1,0:T(8,128)S(1)}, f32[128,128]{1,0:T(8,128)S(1)}, u32[]{:S(2)}, u32[]{:S(2)}) collective-permute-start(f32[128,128]{1,0:T(8,128)S(1)} %constant_dynamic-update-slice_fusion.kappa0), channel_id=1, source_target_pairs={{0,12},{4,8},{8,4},{12,0},{1,13},{5,9},{9,5},{13,1},{2,14},{6,10},... | collective-permute-start | bytes 196616 | tf_op jit(solution)/shard_map/ppermute | solution.py:1051
  24.3 5.2 %collective-permute-start.11 = (f32[128,128]{1,0:T(8,128)S(1)}, f32[128,128]{1,0:T(8,128)S(1)}, u32[]{:S(2)}, u32[]{:S(2)}) collective-permute-start(f32[128,128]{1,0:T(8,128)S(1)} %constant_dynamic-update-slice_fusion.kappa0), channel_id=1, source_target_pairs={{0,8},{4,12},{8,0},{12,4},{1,9},{5,13},{9,1},{13,5},{2,10},{6,14},... | collective-permute-start | bytes 196616 | tf_op jit(solution)/shard_map/ppermute | solution.py:1051
  26.9 4.3 %collective-permute-start.10 = (f32[128,128]{1,0:T(8,128)S(1)}, f32[128,128]{1,0:T(8,128)S(1)}, u32[]{:S(2)}, u32[]{:S(2)}) collective-permute-start(f32[128,128]{1,0:T(8,128)S(1)} %constant_dynamic-update-slice_fusion.kappa0), channel_id=1, source_target_pairs={{0,4},{4,0},{8,12},{12,8},{1,5},{5,1},{9,13},{13,9},{2,6},{6,2},{1... | collective-permute-start | bytes 196616 | tf_op jit(solution)/shard_map/ppermute | solution.py:1051
  32.1 6.8 %collective-permute-start.13 = (f32[1024,128]{1,0:T(8,128)S(1)}, f32[1024,128]{1,0:T(8,128)S(1)}, u32[]{:S(2)}, u32[]{:S(2)}) collective-permute-start(f32[1024,128]{1,0:T(8,128)S(1)} %get-tuple-element.43.assembled.own_start), channel_id=1, source_target_pairs={{0,16},{16,0},{1,17},{17,1},{2,18},{18,2},{3,19},{19,3},{4,20},{20... | collective-permute-start | bytes 1572872 | tf_op jit(solution)/shard_map/ppermute | solution.py:1051
  38.9 2.2 %copy-start = (f32[2,5,5,160]{3,0,2,1:T(2,128)S(1)}, f32[2,5,5,160]{3,0,2,1:T(2,128)}, u32[]{:S(2)}) copy-start(f32[2,5,5,160]{3,0,2,1:T(2,128)} %param.6) | copy-start | bytes 96004
  38.9 2.2 %collective-permute-start.14 = (f32[1128,128]{1,0:T(8,128)S(1)}, f32[1128,128]{1,0:T(8,128)S(1)}, u32[]{:S(2)}, u32[]{:S(2)}) collective-permute-start(f32[1128,128]{1,0:T(8,128)S(1)} %cycle.1.own), channel_id=1, source_target_pairs={{0,16},{16,0},{1,17},{17,1},{2,18},{18,2},{3,19},{19,3},{4,20},{20... | collective-permute-start | bytes 1732616 | tf_op jit(solution)/shard_map/ppermute | solution.py:1051

commit v9 on v8

--- a/solution.py
+++ b/solution.py
@@ -352,7 +352,8 @@
 COLS = 16
 HALF = 64
 TRACE = 40
-PIECE = HALF + TRACE
+KAPPA = HALF + TRACE
+PIECE = KAPPA + 32
 FIELD = 1000
 F32 = jnp.float32
 
@@ -533,15 +534,15 @@
         nodes[125 + r : 126 + r, :] = jnp.where(upper, shown[2 * r : 2 * r + 1], shown[2 * r + 1 : 2 * r + 2])
     for p, out in enumerate((mine, theirs)):
         out[:HALF, :] = pack_nodes(nodes[128 * p : 128 * p + 128, :])
-        out[HALF:PIECE, :] = pack_nodes(traces[80 * p : 80 * p + 80, :])
+        out[HALF:KAPPA, :] = pack_nodes(traces[80 * p : 80 * p + 80, :])
     for k in range(5):
         nodes[25 * k : 25 * k + 25, :] = part(k, 192)[:25]
-    mine[PIECE:, :] = choose(iota((32, 128), 1) // EZ, [nodes[32 * q : 32 * q + 32, :] for q in range(4)])
+    mine[KAPPA:, :] = choose(iota((32, 128), 1) // EZ, [nodes[32 * q : 32 * q + 32, :] for q in range(4)])
 
 
 def part_kernel(source, piece, kappa):
-    piece[...] = source[:PIECE, :]
-    kappa[...] = source[PIECE:, :]
+    piece[...] = source[:KAPPA, :]
+    kappa[...] = source[KAPPA:, :]
 
 
 VMEM = pl.BlockSpec(memory_space=pltpu.VMEM)
@@ -556,7 +557,7 @@
     operands = (rhs, guess, kappa, flags, jnp.asarray(row_table()))
     return pl.pallas_call(
         local_kernel,
-        out_shape=[jax.ShapeDtypeStruct((rows, 128), F32) for rows in (PIECE + 32, PIECE)],
+        out_shape=[jax.ShapeDtypeStruct((rows, 128), F32) for rows in (PIECE, KAPPA)],
         in_specs=[HBM] * 5,
         out_specs=[VMEM] * 2,
         scratch_shapes=[pltpu.VMEM(o.shape, o.dtype) for o in operands]
@@ -576,7 +577,7 @@
 def part(x):
     return pl.pallas_call(
         part_kernel,
-        out_shape=[jax.ShapeDtypeStruct((rows, 128), F32) for rows in (PIECE, 32)],
+        out_shape=[jax.ShapeDtypeStruct((rows, 128), F32) for rows in (KAPPA, 32)],
         in_specs=[VMEM],
         out_specs=[VMEM] * 2,
         compiler_params=limit(16),
@@ -600,11 +601,11 @@
     return pieces[pl.ds(8 * h * size + r, 8, stride=size), :]
 
 
-def place_pieces(blocks, stride, pieces, first, size, outer="gy"):
+def place_pieces(blocks, stride, pieces, first, size):
     my_gx, my_gy = lax.axis_index("gx"), lax.axis_index("gy")
     for b, block in enumerate(blocks):
         for a in range(4):
-            column = (my_gx ^ a) * 4 + (my_gy ^ b) if outer == "gy" else (my_gx ^ b) * 4 + (my_gy ^ a)
+            column = (my_gx ^ a) * 4 + (my_gy ^ b)
             start = pl.multiple_of(column * size, 8)
             pieces[pl.ds(start, size), :] = block[a * stride + first : a * stride + first + size, :]
 
@@ -661,11 +662,11 @@
 RADIUS = (CHEB_HIGH - CHEB_LOW) / 2.0
 
 
-def assemble_kernel(block0, block1, block2, block3, kappa0, kappa1, kappa2, kappa3, field, coefs, pieces, edges, kappas, traces, kap):
+def assemble_kernel(block0, block1, block2, block3, field, coefs, pieces, edges, kappas, traces, kap):
     blocks = (block0, block1, block2, block3)
     place_pieces(blocks, PIECE, pieces, 0, HALF)
     place_pieces(blocks, PIECE, edges, HALF, TRACE)
-    place_pieces((kappa0, kappa1, kappa2, kappa3), 32, kappas, 0, 32, outer="gx")
+    place_pieces(blocks, PIECE, kappas, KAPPA, 32)
     lanes = Lanes()
     group, lane = lanes.group, lanes.lane
 
@@ -758,13 +759,13 @@
             store(level.res, first, f)
             store(level.x, first, jnp.zeros_like(f))
 
-    def apply(level, smooth):
+    def apply(level, smooth, always):
         n = level.count
         kx, ky, kz = level.tables
         gains = level.gains
         source = level.dir if smooth else level.x
-        for k in range(n):
-            def line_at(i, k=k):
+        def plane(k):
+            def line_at(i):
                 return load(source, (k * n + i) * n, n)
 
             for i in range(n):
@@ -807,6 +808,11 @@
                     store(level.res, first, rest)
                     store(level.dir, first, level.jac(first, n) * rest)
 
+        for k in range(n):
+            @pl.when(always)
+            def _(k=k):
+                plane(k)
+
     def combine(weights, parts):
         total = None
         for weight, part in zip(weights, parts):
@@ -838,28 +844,28 @@
     def up(m, n):
         return lagrange_table(lobatto(m)[0], lobatto(n)[0])
 
-    def solve(p):
+    def solve(p, always=None):
         level = levels[p]
         if p == 2:
-            apply(level, True)
+            apply(level, True, always)
             return
         below = levels[p + 1]
 
         def step(t, carry):
             @pl.when(t != 1)
             def _():
-                apply(level, True)
+                apply(level, True, t >= 0)
 
             @pl.when((t != 2) | (p == 0))
             def _():
-                apply(level, False)
+                apply(level, False, t >= 0)
 
             @pl.when(t == 0)
             def _():
                 n, m = level.count, below.count
                 change(down(n, m), level.res, below.f, False)
                 begin(below, below.f)
-                solve(p + 1)
+                solve(p + 1, t >= 0)
                 change(up(m, n), below.x, level.x, True)
             return carry
         lax.fori_loop(0, 3, step, 0)
@@ -980,14 +986,14 @@
                 res_out[i, j, s : s + 1, :] = outs[64 + s * 32 + r : 64 + s * 32 + r + 1, :]
 
 
-def assemble(blocks, kappas):
+def assemble(blocks):
     return pl.pallas_call(
         assemble_kernel,
         out_shape=[
             jax.ShapeDtypeStruct((128 * 8, 128), F32),
             jax.ShapeDtypeStruct((REGISTERS * 8, 128), F32),
         ],
-        in_specs=[VMEM] * 8,
+        in_specs=[VMEM] * 4,
         out_specs=[VMEM] * 2,
         scratch_shapes=[
             pltpu.VMEM((COLS * HALF, 128), F32),
@@ -998,7 +1004,7 @@
         ],
         compiler_params=limit(16),
         name="assemble",
-    )(*blocks, *kappas)
+    )(*blocks)
 
 
 def cycle(coefs, assembled):
@@ -1055,16 +1061,10 @@
     rhs, guess = (jnp.transpose(v, (1, 2, 0, 3)) for v in (rhs, guess))
     mine, theirs = local_part(rhs, guess, kappa, bc_flags)
     got, mine, kappa_piece = lax.optimization_barrier((exchange(theirs, "section", 1), *part(mine)))
-    piece = mine + got
-    parts = [exchange(piece, "gx", bits) for bits in (1, 2, 3)]
-    parts[0], kappa_piece = lax.optimization_barrier((parts[0], kappa_piece))
-    others = [exchange(kappa_piece, "gy", bits) for bits in (1, 2, 3)]
-    parts, others = lax.optimization_barrier((parts, others))
-    line = jnp.concatenate([piece] + parts)
-    across = jnp.concatenate([kappa_piece] + others)
+    piece = jnp.concatenate([mine + got, kappa_piece])
+    line = jnp.concatenate([piece] + [exchange(piece, "gx", bits) for bits in (1, 2, 3)])
     blocks = [line] + [exchange(line, "gy", bits) for bits in (1, 2, 3)]
-    kappas = [across] + [exchange(across, "gx", bits) for bits in (1, 2, 3)]
-    start, coefs = assemble(blocks, kappas)
+    start, coefs = assemble(blocks)
     other_start = exchange(start, "section", 1)
     own, other_start = lax.optimization_barrier((cycle(coefs, start), other_start))
     sums, column = early(own, start, other_start)

time: 42.8 us -> 42.8 us (level)
  waiting for transfers between devices: 10.6 us -> 18.1 us
  starting transfers between devices: 17.9 us -> 10.4 us
    ppermute x15 -> x9, starting transfers between devices: 17.9 us -> 10.4 us  [exchange(): lax.ppermute(x, axis, [(n, n ^ bits) for n in range(lax.axis_size(axis))])]
    ppermute x15 -> x9, waiting for transfers between devices: 10.6 us -> 18.1 us  [exchange(): lax.ppermute(x, axis, [(n, n ^ bits) for n in range(lax.axis_size(axis))])]
  transfers between devices with their start and end apart: 15 -> 9, of which waited for: 9 -> 7; matrix products, arithmetic and copies ran while one was open for 0% -> 0% of each run, Pallas kernels for 18% -> 18%
where the time goes in v9:
time: 42.8 us; the launch traced here: 42.6 us
  waiting for transfers between devices  18.1 us (42%)
  Pallas kernels  12.4 us (29%)
  starting transfers between devices  10.4 us (24%)
  local copies, waits for them, and re-layouts  0.91 us (2%)
  between operations  0.72 us (2%)
    ppermute x9, waiting for transfers between devices, exchange(): lax.ppermute(x, axis, [(n, n ^ bits) for n in range(lax.axis_size(axis))])  18.1 us
    ppermute x9, starting transfers between devices, exchange(): lax.ppermute(x, axis, [(n, n ^ bits) for n in range(lax.axis_size(axis))])  10.4 us
    pallas_call x1, Pallas kernels, cycle(): pl.pallas_call(cycle_kernel, out_shape=jax.ShapeDtypeStruct((FIELD + 128,...  6.72 us
    pallas_call x1, Pallas kernels, local_part(): pl.pallas_call(local_kernel, out_shape=[jax.ShapeDtypeStruct((rows, 128),...  2.52 us
    pallas_call x1, Pallas kernels, finish(): pl.pallas_call(finish_kernel, out_shape=[jax.ShapeDtypeStruct(guess.shape...  1.47 us
    pallas_call x1, Pallas kernels, assemble(): pl.pallas_call(assemble_kernel, out_shape=[jax.ShapeDtypeStruct((128 * 8,...  0.92 us
    unnamed x7, local copies, waits for them, and re-layouts  0.9 us
  transfers between devices with their start and end apart: 9, of which 7 were waited for; matrix products, arithmetic and copies ran while one was open for 0% of the time, Pallas kernels for 18%

profile of v9, /device:TPU:0, one launch (start us, length us, event | category | flops | bytes accessed | tf_op | source)
XLA Modules:
  0.0 42.6 jit_solution(6072292779953267494)
XLA Ops:
  0.6 2.5 %local_part.1 = (f32[136,128]{1,0:T(8,128)}, f32[104,128]{1,0:T(8,128)}) custom-call(f32[5,5,2,160]{3,2,1,0:T(2,128)} %bitcast.6, f32[5,5,2,160]{3,2,1,0:T(2,128)} %bitcast.4, f32[5,5,160]{2,1,0:T(8,128)} %kappa_in.1, s32[6,1,1,32]{3,2,1,0:T(1,128)} %flags_in.1, f32[64,64]{1,0:T(8,128)} %constant.2.clone.rows_in), custom_call_target="tpu_custom_call" | custom-call | flops 20000000 | bytes 8000000 | tf_op jit(solution)/shard_map/local_part/pallas_call | solution.py:558
  3.2 0.5 %collective-permute-start = (f32[104,128]{1,0:T(8,128)}, f32[104,128]{1,0:T(8,128)S(1)}, u32[]{:S(2)}, u32[]{:S(2)}) collective-permute-start(f32[104,128]{1,0:T(8,128)} %get-tuple-element.19), channel_id=1, source_target_pairs={{0,16},{16,0},{1,17},{17,1},{2,18},{18,2},{3,19},{19,3},{4,20},{20... | collective-permute-start | bytes 159752 | tf_op jit(solution)/shard_map/ppermute | solution.py:1057
  3.7 0.0 copy-start.1
  3.7 0.9 %copy-done.1 = f32[136,128]{1,0:T(8,128)S(1)} copy-done((f32[136,128]{1,0:T(8,128)S(1)}, f32[136,128]{1,0:T(8,128)}, u32[]{:S(2)}) %copy-start.1) | copy-done | bytes 69656
  4.6 0.2 collective-permute-done
  4.8 5.0 %collective-permute-start.3 = (f32[136,128]{1,0:T(8,128)S(1)}, f32[136,128]{1,0:T(8,128)S(1)}, u32[]{:S(2)}, u32[]{:S(2)}) collective-permute-start(f32[136,128]{1,0:T(8,128)S(1)} %pad_maximum_fusion), channel_id=1, source_target_pairs={{0,12},{4,8},{8,4},{12,0},{1,13},{5,9},{9,5},{13,1},{2,14},{6,10},... | collective-permute-start | bytes 208904 | tf_op jit(solution)/shard_map/ppermute | solution.py:1057
  9.8 0.0 collective-permute-start.2
  9.8 0.6 %collective-permute-start.1 = (f32[136,128]{1,0:T(8,128)S(1)}, f32[136,128]{1,0:T(8,128)S(1)}, u32[]{:S(2)}, u32[]{:S(2)}) collective-permute-start(f32[136,128]{1,0:T(8,128)S(1)} %pad_maximum_fusion), channel_id=1, source_target_pairs={{0,4},{4,0},{8,12},{12,8},{1,5},{5,1},{9,13},{13,9},{2,6},{6,2},{1... | collective-permute-start | bytes 208904 | tf_op jit(solution)/shard_map/ppermute | solution.py:1057
  10.5 4.1 %collective-permute-done.1 = f32[136,128]{1,0:T(8,128)S(1)} collective-permute-done((f32[136,128]{1,0:T(8,128)S(1)}, f32[136,128]{1,0:T(8,128)S(1)}, u32[]{:S(2)}, u32[]{:S(2)}) %collective-permute-start.1) | collective-permute-done | bytes 69664 | tf_op jit(solution)/shard_map/ppermute | solution.py:1057
  14.6 1.4 %collective-permute-done.2 = f32[136,128]{1,0:T(8,128)S(1)} collective-permute-done((f32[136,128]{1,0:T(8,128)S(1)}, f32[136,128]{1,0:T(8,128)S(1)}, u32[]{:S(2)}, u32[]{:S(2)}) %collective-permute-start.2) | collective-permute-done | bytes 69664 | tf_op jit(solution)/shard_map/ppermute | solution.py:1057
  16.0 0.0 collective-permute-done.3
  16.0 2.5 %collective-permute-start.6 = (f32[544,128]{1,0:T(8,128)S(1)}, f32[544,128]{1,0:T(8,128)S(1)}, u32[]{:S(2)}, u32[]{:S(2)}) collective-permute-start(f32[544,128]{1,0:T(8,128)S(1)} %constant_dynamic-update-slice_fusion.block0), channel_id=1, source_target_pairs={{0,3},{1,2},{2,1},{3,0},{4,7},{5,6},{6,5},{7,4},{8,11},{9,10},{10,... | collective-permute-start | bytes 835592 | tf_op jit(solution)/shard_map/ppermute | solution.py:1057
  18.6 0.5 %collective-permute-start.5 = (f32[544,128]{1,0:T(8,128)S(1)}, f32[544,128]{1,0:T(8,128)S(1)}, u32[]{:S(2)}, u32[]{:S(2)}) collective-permute-start(f32[544,128]{1,0:T(8,128)S(1)} %constant_dynamic-update-slice_fusion.block0), channel_id=1, source_target_pairs={{0,2},{1,3},{2,0},{3,1},{4,6},{5,7},{6,4},{7,5},{8,10},{9,11},{10,... | collective-permute-start | bytes 835592 | tf_op jit(solution)/shard_map/ppermute | solution.py:1057
  19.1 0.5 %collective-permute-start.4 = (f32[544,128]{1,0:T(8,128)S(1)}, f32[544,128]{1,0:T(8,128)S(1)}, u32[]{:S(2)}, u32[]{:S(2)}) collective-permute-start(f32[544,128]{1,0:T(8,128)S(1)} %constant_dynamic-update-slice_fusion.block0), channel_id=1, source_target_pairs={{0,1},{1,0},{2,3},{3,2},{4,5},{5,4},{6,7},{7,6},{8,9},{9,8},{10,11... | collective-permute-start | bytes 835592 | tf_op jit(solution)/shard_map/ppermute | solution.py:1057
  19.6 7.0 %collective-permute-done.6.block3 = f32[544,128]{1,0:T(8,128)S(1)} collective-permute-done((f32[544,128]{1,0:T(8,128)S(1)}, f32[544,128]{1,0:T(8,128)S(1)}, u32[]{:S(2)}, u32[]{:S(2)}) %collective-permute-start.6) | collective-permute-done | bytes 278560 | tf_op jit(solution)/shard_map/ppermute | solution.py:1057
  26.6 4.4 %collective-permute-done.5.block2 = f32[544,128]{1,0:T(8,128)S(1)} collective-permute-done((f32[544,128]{1,0:T(8,128)S(1)}, f32[544,128]{1,0:T(8,128)S(1)}, u32[]{:S(2)}, u32[]{:S(2)}) %collective-permute-start.5) | collective-permute-done | bytes 278560 | tf_op jit(solution)/shard_map/ppermute | solution.py:1057
  31.1 0.1 collective-permute-done.4.block1
  31.2 0.9 %assemble.1 = (f32[1024,128]{1,0:T(8,128)S(1)}, f32[2704,128]{1,0:T(8,128)S(1)}) custom-call(f32[544,128]{1,0:T(8,128)S(1)} %constant_dynamic-update-slice_fusion.block0, f32[544,128]{1,0:T(8,128)S(1)} %collective-permute-done.4.block1, f32[544,128]{1,0:T(8,128)S(1)} %collective-permute-done.5.block2, f32[544,128]{1,0:T(8,128)S(1)} %collective-permute-done.6.block3), custom_call_target="tpu_custom_call" | custom-call | tf_op jit(solution)/shard_map/assemble/pallas_call | solution.py:990
  32.1 0.1 collective-permute-start.7
  32.2 6.7 %cycle.1.own = f32[1128,128]{1,0:T(8,128)S(1)} custom-call(f32[2704,128]{1,0:T(8,128)S(1)} %get-tuple-element.26.coefs, f32[1024,128]{1,0:T(8,128)S(1)} %get-tuple-element.27.assembled.own_start), custom_call_target="tpu_custom_call" | custom-call | flops 40000000 | bytes 30000000 | tf_op jit(solution)/shard_map/cycle/pallas_call | solution.py:1015
  38.9 0.0 copy-start
  38.9 0.0 collective-permute-done.7.other_start
  38.9 0.6 %collective-permute-start.8 = (f32[1128,128]{1,0:T(8,128)S(1)}, f32[1128,128]{1,0:T(8,128)S(1)}, u32[]{:S(2)}, u32[]{:S(2)}) collective-permute-start(f32[1128,128]{1,0:T(8,128)S(1)} %cycle.1.own), channel_id=1, source_target_pairs={{0,16},{16,0},{1,17},{17,1},{2,18},{18,2},{3,19},{19,3},{4,20},{20... | collective-permute-start | bytes 1732616 | tf_op jit(solution)/shard_map/ppermute | solution.py:1057
  39.5 0.8 %early.1 = (f32[16,128]{1,0:T(8,128)S(1)}, f32[192,160]{1,0:T(8,128)S(1)}) custom-call(f32[1128,128]{1,0:T(8,128)S(1)} %cycle.1.own, f32[1024,128]{1,0:T(8,128)S(1)} %get-tuple-element.27.assembled.own_start, f32[1024,128]{1,0:T(8,128)S(1)} %collective-permute-done.7.other_start), custom_call_target="tpu_custom_call" | custom-call | flops 4000000 | bytes 4000000 | tf_op jit(solution)/shard_map/early/pallas_call | solution.py:1028
  40.3 0.8 %collective-permute-done.8.other = f32[1128,128]{1,0:T(8,128)S(1)} collective-permute-done((f32[1128,128]{1,0:T(8,128)S(1)}, f32[1128,128]{1,0:T(8,128)S(1)}, u32[]{:S(2)}, u32[]{:S(2)}) %collective-permute-start.8) | collective-permute-done | bytes 577568 | tf_op jit(solution)/shard_map/ppermute | solution.py:1057
  41.1 0.0 copy-done
  41.1 1.5 %finish.1 = (f32[5,5,2,160]{3,2,1,0:T(2,128)}, f32[5,5,2,160]{3,2,1,0:T(2,128)}, f32[3]{0:T(128)}) custom-call(f32[1128,128]{1,0:T(8,128)S(1)} %cycle.1.own, f32[1128,128]{1,0:T(8,128)S(1)} %collective-permute-done.8.other, f32[1024,128]{1,0:T(8,128)S(1)} %get-tuple-element.27.assembled.own_start, f32[1024,128]{1,0:T(8,128)S(1)} %collective-permute-done.7.other_start, ...), custom_call_target="tpu_custom_call" | custom-call | tf_op jit(solution)/shard_map/finish/pallas_call | solution.py:1041
  (7 shorter events, 0.0 us)
Async XLA Ops:
  3.2 1.6 %collective-permute-start = (f32[104,128]{1,0:T(8,128)}, f32[104,128]{1,0:T(8,128)S(1)}, u32[]{:S(2)}, u32[]{:S(2)}) collective-permute-start(f32[104,128]{1,0:T(8,128)} %get-tuple-element.19), channel_id=1, source_target_pairs={{0,16},{16,0},{1,17},{17,1},{2,18},{18,2},{3,19},{19,3},{4,20},{20... | collective-permute-start | bytes 159752 | tf_op jit(solution)/shard_map/ppermute | solution.py:1057
  3.7 0.9 %copy-start.1 = (f32[136,128]{1,0:T(8,128)S(1)}, f32[136,128]{1,0:T(8,128)}, u32[]{:S(2)}) copy-start(f32[136,128]{1,0:T(8,128)} %get-tuple-element.20.source) | copy-start | bytes 208900
  4.8 11.2 %collective-permute-start.3 = (f32[136,128]{1,0:T(8,128)S(1)}, f32[136,128]{1,0:T(8,128)S(1)}, u32[]{:S(2)}, u32[]{:S(2)}) collective-permute-start(f32[136,128]{1,0:T(8,128)S(1)} %pad_maximum_fusion), channel_id=1, source_target_pairs={{0,12},{4,8},{8,4},{12,0},{1,13},{5,9},{9,5},{13,1},{2,14},{6,10},... | collective-permute-start | bytes 208904 | tf_op jit(solution)/shard_map/ppermute | solution.py:1057
  9.8 6.2 %collective-permute-start.2 = (f32[136,128]{1,0:T(8,128)S(1)}, f32[136,128]{1,0:T(8,128)S(1)}, u32[]{:S(2)}, u32[]{:S(2)}) collective-permute-start(f32[136,128]{1,0:T(8,128)S(1)} %pad_maximum_fusion), channel_id=1, source_target_pairs={{0,8},{4,12},{8,0},{12,4},{1,9},{5,13},{9,1},{13,5},{2,10},{6,14},... | collective-permute-start | bytes 208904 | tf_op jit(solution)/shard_map/ppermute | solution.py:1057
  9.8 4.8 %collective-permute-start.1 = (f32[136,128]{1,0:T(8,128)S(1)}, f32[136,128]{1,0:T(8,128)S(1)}, u32[]{:S(2)}, u32[]{:S(2)}) collective-permute-start(f32[136,128]{1,0:T(8,128)S(1)} %pad_maximum_fusion), channel_id=1, source_target_pairs={{0,4},{4,0},{8,12},{12,8},{1,5},{5,1},{9,13},{13,9},{2,6},{6,2},{1... | collective-permute-start | bytes 208904 | tf_op jit(solution)/shard_map/ppermute | solution.py:1057
  16.0 10.6 %collective-permute-start.6 = (f32[544,128]{1,0:T(8,128)S(1)}, f32[544,128]{1,0:T(8,128)S(1)}, u32[]{:S(2)}, u32[]{:S(2)}) collective-permute-start(f32[544,128]{1,0:T(8,128)S(1)} %constant_dynamic-update-slice_fusion.block0), channel_id=1, source_target_pairs={{0,3},{1,2},{2,1},{3,0},{4,7},{5,6},{6,5},{7,4},{8,11},{9,10},{10,... | collective-permute-start | bytes 835592 | tf_op jit(solution)/shard_map/ppermute | solution.py:1057
  18.6 12.5 %collective-permute-start.5 = (f32[544,128]{1,0:T(8,128)S(1)}, f32[544,128]{1,0:T(8,128)S(1)}, u32[]{:S(2)}, u32[]{:S(2)}) collective-permute-start(f32[544,128]{1,0:T(8,128)S(1)} %constant_dynamic-update-slice_fusion.block0), channel_id=1, source_target_pairs={{0,2},{1,3},{2,0},{3,1},{4,6},{5,7},{6,4},{7,5},{8,10},{9,11},{10,... | collective-permute-start | bytes 835592 | tf_op jit(solution)/shard_map/ppermute | solution.py:1057
  19.1 12.1 %collective-permute-start.4 = (f32[544,128]{1,0:T(8,128)S(1)}, f32[544,128]{1,0:T(8,128)S(1)}, u32[]{:S(2)}, u32[]{:S(2)}) collective-permute-start(f32[544,128]{1,0:T(8,128)S(1)} %constant_dynamic-update-slice_fusion.block0), channel_id=1, source_target_pairs={{0,1},{1,0},{2,3},{3,2},{4,5},{5,4},{6,7},{7,6},{8,9},{9,8},{10,11... | collective-permute-start | bytes 835592 | tf_op jit(solution)/shard_map/ppermute | solution.py:1057
  32.1 6.8 %collective-permute-start.7 = (f32[1024,128]{1,0:T(8,128)S(1)}, f32[1024,128]{1,0:T(8,128)S(1)}, u32[]{:S(2)}, u32[]{:S(2)}) collective-permute-start(f32[1024,128]{1,0:T(8,128)S(1)} %get-tuple-element.27.assembled.own_start), channel_id=1, source_target_pairs={{0,16},{16,0},{1,17},{17,1},{2,18},{18,2},{3,19},{19,3},{4,20},{20... | collective-permute-start | bytes 1572872 | tf_op jit(solution)/shard_map/ppermute | solution.py:1057
  38.9 2.2 %copy-start = (f32[2,5,5,160]{3,0,2,1:T(2,128)S(1)}, f32[2,5,5,160]{3,0,2,1:T(2,128)}, u32[]{:S(2)}) copy-start(f32[2,5,5,160]{3,0,2,1:T(2,128)} %param.6) | copy-start | bytes 96004
  38.9 2.2 %collective-permute-start.8 = (f32[1128,128]{1,0:T(8,128)S(1)}, f32[1128,128]{1,0:T(8,128)S(1)}, u32[]{:S(2)}, u32[]{:S(2)}) collective-permute-start(f32[1128,128]{1,0:T(8,128)S(1)} %cycle.1.own), channel_id=1, source_target_pairs={{0,16},{16,0},{1,17},{17,1},{2,18},{18,2},{3,19},{19,3},{4,20},{20... | collective-permute-start | bytes 1732616 | tf_op jit(solution)/shard_map/ppermute | solution.py:1057

commit v10 on v9

--- a/solution.py
+++ b/solution.py
@@ -351,9 +351,12 @@
 EZ = 32
 COLS = 16
 HALF = 64
-TRACE = 40
-KAPPA = HALF + TRACE
-PIECE = KAPPA + 32
+FACE_X = HALF + 25
+KAPPA = FACE_X + 15
+PIECE = KAPPA + 16
+LINE_KAPPA = 4 * HALF
+LINE_Y = LINE_KAPPA + 4 * 16
+LINE = LINE_Y + 104
 FIELD = 1000
 F32 = jnp.float32
 
@@ -446,14 +449,6 @@
     return jnp.where(odd, nodes[half:, :], nodes[:half, :])
 
 
-def face_place(i, j):
-    if i == 0:
-        return j
-    if i == 4:
-        return 11 + j
-    return 3 + 2 * i + (0 if j == 0 else 1)
-
-
 def fetch(pairs, sems):
     copies = [pltpu.make_async_copy(src, dst, sems.at[n]) for n, (src, dst) in enumerate(pairs)]
     for copy in copies:
@@ -464,7 +459,7 @@
 
 def local_kernel(
     rhs_in, guess_in, kappa_in, flags_in, rows_in, mine, theirs,
-    rhs, guess, kappa, flags, rows_t, sems, stack, lines, nodes, traces,
+    rhs, guess, kappa, flags, rows_t, sems, stack, lines, nodes, y_faces, x_faces,
 ):
     sec = lax.axis_index("section")
     fetch([(rhs_in, rhs), (guess_in, guess), (kappa_in, kappa), (flags_in, flags), (rows_in, rows_t)], sems)
@@ -495,7 +490,8 @@
     own = own + jnp.where(row % 5 == 0, gains[2], jnp.where(row % 5 == 4, gains[3], none))
     kz = element_matrix(5, 2)
     back, back_matrix = split_sections()[1:3]
-    nodes[...] = jnp.zeros_like(nodes)
+    for ref in (nodes, y_faces, x_faces):
+        ref[...] = jnp.zeros_like(ref)
     for k in range(5):
         diagonal = part(k, 192) + own
         if k == 0:
@@ -522,22 +518,24 @@
                 total = total - factor * images[s]
                 trace = trace + factor * part(k, 128 + 32 * s)
             nodes[128 * p + 25 * k : 128 * p + 25 * k + 25, :] = total[:25]
-            start = 80 * p + 16 * k
-            traces[start : start + 5, :] = trace[:5]
-            for i in range(1, 4):
-                for j in (0, 4):
-                    r = start + face_place(i, j)
-                    traces[r : r + 1, :] = trace[5 * i + j : 5 * i + j + 1]
-            traces[start + 11 : start + 16, :] = trace[20:25]
+            for i in range(5):
+                for f in range(2):
+                    r = 64 * p + 32 * f + 5 * k + i
+                    y_faces[r : r + 1, :] = trace[5 * i + 4 * f : 5 * i + 4 * f + 1]
+            for f in range(2):
+                r = 32 * p + 16 * f + 3 * k
+                x_faces[r : r + 3, :] = trace[20 * f + 1 : 20 * f + 4]
     upper = iota((1, 128), 1) < 64
     for r in range(3):
         nodes[125 + r : 126 + r, :] = jnp.where(upper, shown[2 * r : 2 * r + 1], shown[2 * r + 1 : 2 * r + 2])
     for p, out in enumerate((mine, theirs)):
         out[:HALF, :] = pack_nodes(nodes[128 * p : 128 * p + 128, :])
-        out[HALF:KAPPA, :] = pack_nodes(traces[80 * p : 80 * p + 80, :])
+        out[HALF:FACE_X, :] = pack_nodes(y_faces[64 * p : 64 * p + 64, :])[:25]
+        out[FACE_X:KAPPA, :] = pack_nodes(x_faces[32 * p : 32 * p + 32, :])[:15]
     for k in range(5):
         nodes[25 * k : 25 * k + 25, :] = part(k, 192)[:25]
-    mine[KAPPA:, :] = choose(iota((32, 128), 1) // EZ, [nodes[32 * q : 32 * q + 32, :] for q in range(4)])
+    kappas = choose(iota((32, 128), 1) // EZ, [nodes[32 * q : 32 * q + 32, :] for q in range(4)])
+    mine[KAPPA:, :] = jnp.where(sec == 0, kappas[:16], kappas[16:])
 
 
 def part_kernel(source, piece, kappa):
@@ -566,7 +564,8 @@
             pltpu.VMEM((224, 160), F32),
             pltpu.VMEM((5 * 224, 128), F32),
             pltpu.VMEM((256, 128), F32),
-            pltpu.VMEM((160, 128), F32),
+            pltpu.VMEM((128, 128), F32),
+            pltpu.VMEM((64, 128), F32),
         ],
         compiler_params=limit(60),
         cost_estimate=pl.CostEstimate(flops=20_000_000, bytes_accessed=8_000_000, transcendentals=0),
@@ -577,7 +576,7 @@
 def part(x):
     return pl.pallas_call(
         part_kernel,
-        out_shape=[jax.ShapeDtypeStruct((rows, 128), F32) for rows in (KAPPA, 32)],
+        out_shape=[jax.ShapeDtypeStruct((rows, 128), F32) for rows in (KAPPA, 16)],
         in_specs=[VMEM],
         out_specs=[VMEM] * 2,
         compiler_params=limit(16),
@@ -601,13 +600,13 @@
     return pieces[pl.ds(8 * h * size + r, 8, stride=size), :]
 
 
-def place_pieces(blocks, stride, pieces, first, size):
+def place_pieces(blocks, pieces, first, size, room):
     my_gx, my_gy = lax.axis_index("gx"), lax.axis_index("gy")
     for b, block in enumerate(blocks):
         for a in range(4):
             column = (my_gx ^ a) * 4 + (my_gy ^ b)
-            start = pl.multiple_of(column * size, 8)
-            pieces[pl.ds(start, size), :] = block[a * stride + first : a * stride + first + size, :]
+            start = pl.multiple_of(column * room, 8)
+            pieces[pl.ds(start, size), :] = block[first + a * size : first + a * size + size, :]
 
 
 class Lanes:
@@ -662,50 +661,106 @@
 RADIUS = (CHEB_HIGH - CHEB_LOW) / 2.0
 
 
-def assemble_kernel(block0, block1, block2, block3, field, coefs, pieces, edges, kappas, traces, kap):
+def flag_lanes(row, slot):
+    turned = [row] + [pltpu.roll(row, 32 * m, 1) for m in range(1, 4)]
+    return choose(iota(row.shape, 1) // EZ, [turned[(g - 2 * slot - 1) % 4] for g in range(4)])
+
+
+def line_kernel(piece0, piece1, piece2, piece3, line, faces):
+    pieces = (piece0, piece1, piece2, piece3)
+    even = lax.axis_index("gx") % 2 == 0
+    odd = iota((8, 128), 1) // EZ % 2 == 1
+    faces[...] = jnp.zeros_like(faces)
+
+    def both(rows, f):
+        side = odd[:1] if f else jnp.logical_not(odd[:1])
+        return jnp.where(side, rows, pltpu.roll(rows, 96 if f else 32, 1))
+
+    for a, piece in enumerate(pieces):
+        for f in range(2):
+            base = 64 * a + 32 * f
+            inner = both(piece[FACE_X:KAPPA, :], f)
+            ends = [both(piece[HALF:FACE_X, :], g) for g in range(2)]
+            for k in range(5):
+                r = base + 5 * k
+                node = 5 * k + 4 * f
+                faces[r : r + 1, :] = ends[0][node : node + 1]
+                faces[r + 1 : r + 4, :] = inner[3 * k : 3 * k + 3]
+                faces[r + 4 : r + 5, :] = ends[1][node : node + 1]
+    for a, piece in enumerate(pieces):
+        line[HALF * a : HALF * a + HALF, :] = piece[:HALF, :]
+        line[LINE_KAPPA + 16 * a : LINE_KAPPA + 16 * a + 16, :] = piece[KAPPA:, :]
+        line[LINE_Y + 25 * a : LINE_Y + 25 * a + 25, :] = piece[HALF:FACE_X, :]
+        flags = [flag_lanes(piece[61:62, :], slot) for slot in range(2)]
+        gains = [face_gains(flags[d], 0, d, 5) for d in range(2)]
+        next_first = even if a % 2 == 0 else jnp.logical_not(even)
+        for f in range(2):
+            one = faces[64 * (a ^ 1) + 32 * (1 - f) : 64 * (a ^ 1) + 32 * (1 - f) + 32, :]
+            three = faces[64 * (a ^ 3) + 32 * (1 - f) : 64 * (a ^ 3) + 32 * (1 - f) + 32, :]
+            near = jnp.where(next_first, one, three) if f else jnp.where(next_first, three, one)
+            term = gains[f] * near
+            for k in range(5):
+                node = 25 * k + 20 * f
+                side = odd[:5] if node >= HALF else jnp.logical_not(odd[:5])
+                r = HALF * a + node % HALF
+                line[r : r + 5, :] = line[r : r + 5, :] + jnp.where(side, term[5 * k : 5 * k + 5], 0.0)
+    line[LINE_Y + 100 :, :] = jnp.zeros((4, 128), F32)
+
+
+def halves_kernel(block0, block1, block2, block3, out):
+    place_pieces((block0, block1, block2, block3), out, LINE_KAPPA, 16, 16)
+
+
+def widen(low, high, odd):
+    return jnp.where(odd, pltpu.roll(high, 32, 1), low), jnp.where(odd, high, pltpu.roll(low, 96, 1))
+
+
+def assemble_kernel(block0, block1, block2, block3, field, pieces, edges, traces):
     blocks = (block0, block1, block2, block3)
-    place_pieces(blocks, PIECE, pieces, 0, HALF)
-    place_pieces(blocks, PIECE, edges, HALF, TRACE)
-    place_pieces(blocks, PIECE, kappas, KAPPA, 32)
+    place_pieces(blocks, pieces, 0, HALF, HALF)
+    place_pieces(blocks, edges, LINE_Y, 25, 32)
+    lanes = Lanes()
+    for source, size, rows, target, apart in ((edges, 32, 25, traces, 25), (pieces, HALF, HALF, field, HALF)):
+        for r in range(rows):
+            first, second = widen(rows_of(source, size, r, 0), rows_of(source, size, r, 1), lanes.odd)
+            target[tile(r), :] = first
+            target[tile(apart + r), :] = second
+    got = field[tile(126), :]
+    across = pltpu.roll(got, 64, 1)
+    gains = [
+        face_gains(jnp.where(lanes.lane < 64, got, across), 1, 0, 5),
+        face_gains(jnp.where(lanes.lane < 64, across, got), 1, 1, 5),
+    ]
+    for k in range(5):
+        for i in range(5):
+            lower, upper = traces[tile(5 * k + i), :], traces[tile(25 + 5 * k + i), :]
+            node = 25 * k + 5 * i
+            field[tile(node), :] = field[tile(node), :] + gains[0] * lanes.y_before(upper)
+            field[tile(node + 4), :] = field[tile(node + 4), :] + gains[1] * lanes.y_after(lower)
+
+
+def setup_kernel(field, own_halves, other_halves, coefs, kap):
+    sec = lax.axis_index("section")
     lanes = Lanes()
     group, lane = lanes.group, lanes.lane
-
-    def widen(source, size, target):
-        for r in range(size):
-            low, high = rows_of(source, size, r, 0), rows_of(source, size, r, 1)
-            target[tile(r), :] = jnp.where(lanes.odd, pltpu.roll(high, 32, 1), low)
-            target[tile(size + r), :] = jnp.where(lanes.odd, high, pltpu.roll(low, 96, 1))
-
-    widen(edges, TRACE, traces)
-    widen(pieces, HALF, field)
     flags = []
     for r in range(3):
         got = field[tile(125 + r), :]
         across = pltpu.roll(got, 64, 1)
         flags += [jnp.where(lane < 64, got, across), jnp.where(lane < 64, across, got)]
-    for r in range(32):
-        turned = []
-        for h in range(2):
-            got = rows_of(kappas, 32, r, h)
-            turned.append([pltpu.roll(got, 32 * m, 1) if m else got for m in range(4)])
-        for q in range(4):
-            kap[tile(q * 32 + r), :] = choose(group, [turned[g % 2][(g - q) % 4] for g in range(4)])
+    for r in range(16):
+        pairs = [[rows_of(ref, 16, r, h) for h in range(2)] for ref in (own_halves, other_halves)]
+        for half in range(2):
+            turned = []
+            for h in range(2):
+                got = jnp.where(sec == half, pairs[0][h], pairs[1][h])
+                turned.append([pltpu.roll(got, 32 * m, 1) if m else got for m in range(4)])
+            for q in range(4):
+                value = choose(group, [turned[g % 2][(g - q) % 4] for g in range(4)])
+                kap[tile(q * 32 + half * 16 + r), :] = value
     for p, n in enumerate((5, 3, 2)):
         stride = 4 // (n - 1)
         gains = [face_gains(flags[d], d // 2, d % 2, n) for d in range(6)]
-        if p == 0:
-            for k in range(5):
-                def trace(i, j, k=k):
-                    return traces[tile(k * 16 + face_place(i, j)), :]
-
-                for m in range(5):
-                    for where, term in (
-                        (m, gains[0] * lanes.x_before(trace(4, m))),
-                        (20 + m, gains[1] * lanes.x_after(trace(0, m))),
-                        (5 * m, gains[2] * lanes.y_before(trace(m, 4))),
-                        (5 * m + 4, gains[3] * lanes.y_after(trace(m, 0))),
-                    ):
-                        field[tile(k * 25 + where), :] = field[tile(k * 25 + where), :] + term
         rows = []
         for d in range(3):
             coefs[tile(GAINS[p] + 2 * d), :] = gains[2 * d]
@@ -986,25 +1041,17 @@
                 res_out[i, j, s : s + 1, :] = outs[64 + s * 32 + r : 64 + s * 32 + r + 1, :]
 
 
-def assemble(blocks):
+def plain_call(kernel, name, rows, scratch, operands, cost=1_000_000):
     return pl.pallas_call(
-        assemble_kernel,
-        out_shape=[
-            jax.ShapeDtypeStruct((128 * 8, 128), F32),
-            jax.ShapeDtypeStruct((REGISTERS * 8, 128), F32),
-        ],
-        in_specs=[VMEM] * 4,
-        out_specs=[VMEM] * 2,
-        scratch_shapes=[
-            pltpu.VMEM((COLS * HALF, 128), F32),
-            pltpu.VMEM((COLS * TRACE, 128), F32),
-            pltpu.VMEM((COLS * 32, 128), F32),
-            pltpu.VMEM((80 * 8, 128), F32),
-            pltpu.VMEM((128 * 8, 128), F32),
-        ],
+        kernel,
+        out_shape=jax.ShapeDtypeStruct((rows, 128), F32),
+        in_specs=[VMEM] * len(operands),
+        out_specs=VMEM,
+        scratch_shapes=[pltpu.VMEM((r, 128), F32) for r in scratch],
         compiler_params=limit(16),
-        name="assemble",
-    )(*blocks)
+        cost_estimate=pl.CostEstimate(flops=cost, bytes_accessed=cost, transcendentals=0),
+        name=name,
+    )(*operands)
 
 
 def cycle(coefs, assembled):
@@ -1062,9 +1109,14 @@
     mine, theirs = local_part(rhs, guess, kappa, bc_flags)
     got, mine, kappa_piece = lax.optimization_barrier((exchange(theirs, "section", 1), *part(mine)))
     piece = jnp.concatenate([mine + got, kappa_piece])
-    line = jnp.concatenate([piece] + [exchange(piece, "gx", bits) for bits in (1, 2, 3)])
+    pieces = [piece] + [exchange(piece, "gx", bits) for bits in (1, 2, 3)]
+    line = plain_call(line_kernel, "line", LINE, [4 * 64], pieces)
     blocks = [line] + [exchange(line, "gy", bits) for bits in (1, 2, 3)]
-    start, coefs = assemble(blocks)
+    halves = plain_call(halves_kernel, "halves", COLS * 16, [], blocks)
+    other_halves = exchange(halves, "section", 1)
+    start = plain_call(assemble_kernel, "assemble", 128 * 8, [COLS * HALF, COLS * 32, 50 * 8], blocks, 4_000_000)
+    start, other_halves = lax.optimization_barrier((start, other_halves))
+    coefs = plain_call(setup_kernel, "setup", REGISTERS * 8, [128 * 8], (start, halves, other_halves))
     other_start = exchange(start, "section", 1)
     own, other_start = lax.optimization_barrier((cycle(coefs, start), other_start))
     sums, column = early(own, start, other_start)

time: 42.8 us -> 40.8 us (0.953)
  waiting for transfers between devices: 18.1 us -> 16.1 us
    ppermute x9 -> x10, waiting for transfers between devices: 18.1 us -> 16.1 us  [exchange(): lax.ppermute(x, axis, [(n, n ^ bits) for n in range(lax.axis_size(axis))])]
    pallas_call x1 -> x4, Pallas kernels: 0.92 us -> 1.08 us  [plain_call(): pl.pallas_call(kernel, out_shape=jax.ShapeDtypeStruct((rows, 128), F32),...]
    unnamed x7 -> x4, local copies, waits for them, and re-layouts: 0.9 us -> 0.83 us
    ppermute x9 -> x10, starting transfers between devices: 10.4 us -> 10.3 us  [exchange(): lax.ppermute(x, axis, [(n, n ^ bits) for n in range(lax.axis_size(axis))])]
  transfers between devices with their start and end apart: 9 -> 10, of which waited for: 7 -> 7; matrix products, arithmetic and copies ran while one was open for 0% -> 0% of each run, Pallas kernels for 18% -> 21%
where the time goes in v10:
time: 40.8 us; the launch traced here: 40.6 us
  waiting for transfers between devices  16.1 us (39%)
  Pallas kernels  12.6 us (31%)
  starting transfers between devices  10.3 us (25%)
  local copies, waits for them, and re-layouts  0.83 us (2%)
  between operations  0.71 us (2%)
    ppermute x10, waiting for transfers between devices, exchange(): lax.ppermute(x, axis, [(n, n ^ bits) for n in range(lax.axis_size(axis))])  16.1 us
    ppermute x10, starting transfers between devices, exchange(): lax.ppermute(x, axis, [(n, n ^ bits) for n in range(lax.axis_size(axis))])  10.3 us
    pallas_call x1, Pallas kernels, cycle(): pl.pallas_call(cycle_kernel, out_shape=jax.ShapeDtypeStruct((FIELD + 128,...  6.7 us
    pallas_call x1, Pallas kernels, local_part(): pl.pallas_call(local_kernel, out_shape=[jax.ShapeDtypeStruct((rows, 128),...  2.52 us
    pallas_call x1, Pallas kernels, finish(): pl.pallas_call(finish_kernel, out_shape=[jax.ShapeDtypeStruct(guess.shape...  1.49 us
    pallas_call x4, Pallas kernels, plain_call(): pl.pallas_call(kernel, out_shape=jax.ShapeDtypeStruct((rows, 128), F32),...  1.08 us
    unnamed x4, local copies, waits for them, and re-layouts  0.83 us
    pallas_call x1, Pallas kernels, early(): pl.pallas_call(early_kernel, out_shape=[jax.ShapeDtypeStruct((16, 128), F...  0.82 us
  transfers between devices with their start and end apart: 10, of which 7 were waited for; matrix products, arithmetic and copies ran while one was open for 0% of the time, Pallas kernels for 21%

profile of v10, /device:TPU:0, one launch (start us, length us, event | category | flops | bytes accessed | tf_op | source)
XLA Modules:
  0.0 40.6 jit_solution(12250527634933491528)
XLA Ops:
  0.6 2.5 %local_part.1 = (f32[120,128]{1,0:T(8,128)}, f32[104,128]{1,0:T(8,128)}) custom-call(f32[5,5,2,160]{3,2,1,0:T(2,128)} %bitcast.6, f32[5,5,2,160]{3,2,1,0:T(2,128)} %bitcast.4, f32[5,5,160]{2,1,0:T(8,128)} %kappa_in.1, s32[6,1,1,32]{3,2,1,0:T(1,128)} %flags_in.1, f32[64,64]{1,0:T(8,128)} %constant.2.clone.rows_in), custom_call_target="tpu_custom_call" | custom-call | flops 20000000 | bytes 8000000 | tf_op jit(solution)/shard_map/local_part/pallas_call | solution.py:556
  3.2 0.5 %collective-permute-start = (f32[104,128]{1,0:T(8,128)}, f32[104,128]{1,0:T(8,128)S(1)}, u32[]{:S(2)}, u32[]{:S(2)}) collective-permute-start(f32[104,128]{1,0:T(8,128)} %get-tuple-element.19), channel_id=1, source_target_pairs={{0,16},{16,0},{1,17},{17,1},{2,18},{18,2},{3,19},{19,3},{4,20},{20... | collective-permute-start | bytes 159752 | tf_op jit(solution)/shard_map/ppermute | solution.py:1104
  3.7 0.0 copy-start.1
  3.7 0.8 %copy-done.1 = f32[120,128]{1,0:T(8,128)S(1)} copy-done((f32[120,128]{1,0:T(8,128)S(1)}, f32[120,128]{1,0:T(8,128)}, u32[]{:S(2)}) %copy-start.1) | copy-done | bytes 61464
  4.5 0.3 collective-permute-done
  4.8 3.0 %collective-permute-start.1 = (f32[120,128]{1,0:T(8,128)S(1)}, f32[120,128]{1,0:T(8,128)S(1)}, u32[]{:S(2)}, u32[]{:S(2)}) collective-permute-start(f32[120,128]{1,0:T(8,128)S(1)} %pad_maximum_fusion.piece0), channel_id=1, source_target_pairs={{0,4},{4,0},{8,12},{12,8},{1,5},{5,1},{9,13},{13,9},{2,6},{6,2},{1... | collective-permute-start | bytes 184328 | tf_op jit(solution)/shard_map/ppermute | solution.py:1104
  7.8 2.6 %collective-permute-start.2 = (f32[120,128]{1,0:T(8,128)S(1)}, f32[120,128]{1,0:T(8,128)S(1)}, u32[]{:S(2)}, u32[]{:S(2)}) collective-permute-start(f32[120,128]{1,0:T(8,128)S(1)} %pad_maximum_fusion.piece0), channel_id=1, source_target_pairs={{0,8},{4,12},{8,0},{12,4},{1,9},{5,13},{9,1},{13,5},{2,10},{6,14},... | collective-permute-start | bytes 184328 | tf_op jit(solution)/shard_map/ppermute | solution.py:1104
  10.4 0.0 collective-permute-start.3
  10.4 0.0 collective-permute-done.1.piece1
  10.4 4.0 %collective-permute-done.2.piece2 = f32[120,128]{1,0:T(8,128)S(1)} collective-permute-done((f32[120,128]{1,0:T(8,128)S(1)}, f32[120,128]{1,0:T(8,128)S(1)}, u32[]{:S(2)}, u32[]{:S(2)}) %collective-permute-start.2) | collective-permute-done | bytes 61472 | tf_op jit(solution)/shard_map/ppermute | solution.py:1104
  14.4 2.1 %collective-permute-done.3.piece3 = f32[120,128]{1,0:T(8,128)S(1)} collective-permute-done((f32[120,128]{1,0:T(8,128)S(1)}, f32[120,128]{1,0:T(8,128)S(1)}, u32[]{:S(2)}, u32[]{:S(2)}) %collective-permute-start.3) | collective-permute-done | bytes 61472 | tf_op jit(solution)/shard_map/ppermute | solution.py:1104
  16.5 0.2 line.1.block0
  16.7 1.6 %collective-permute-start.4 = (f32[424,128]{1,0:T(8,128)S(1)}, f32[424,128]{1,0:T(8,128)S(1)}, u32[]{:S(2)}, u32[]{:S(2)}) collective-permute-start(f32[424,128]{1,0:T(8,128)S(1)} %line.1.block0), channel_id=1, source_target_pairs={{0,1},{1,0},{2,3},{3,2},{4,5},{5,4},{6,7},{7,6},{8,9},{9,8},{10,11... | collective-permute-start | bytes 651272 | tf_op jit(solution)/shard_map/ppermute | solution.py:1104
  18.2 1.5 %collective-permute-start.5 = (f32[424,128]{1,0:T(8,128)S(1)}, f32[424,128]{1,0:T(8,128)S(1)}, u32[]{:S(2)}, u32[]{:S(2)}) collective-permute-start(f32[424,128]{1,0:T(8,128)S(1)} %line.1.block0), channel_id=1, source_target_pairs={{0,2},{1,3},{2,0},{3,1},{4,6},{5,7},{6,4},{7,5},{8,10},{9,11},{10,... | collective-permute-start | bytes 651272 | tf_op jit(solution)/shard_map/ppermute | solution.py:1104
  19.7 0.5 %collective-permute-start.6 = (f32[424,128]{1,0:T(8,128)S(1)}, f32[424,128]{1,0:T(8,128)S(1)}, u32[]{:S(2)}, u32[]{:S(2)}) collective-permute-start(f32[424,128]{1,0:T(8,128)S(1)} %line.1.block0), channel_id=1, source_target_pairs={{0,3},{1,2},{2,1},{3,0},{4,7},{5,6},{6,5},{7,4},{8,11},{9,10},{10,... | collective-permute-start | bytes 651272 | tf_op jit(solution)/shard_map/ppermute | solution.py:1104
  20.2 4.6 %collective-permute-done.4.block1 = f32[424,128]{1,0:T(8,128)S(1)} collective-permute-done((f32[424,128]{1,0:T(8,128)S(1)}, f32[424,128]{1,0:T(8,128)S(1)}, u32[]{:S(2)}, u32[]{:S(2)}) %collective-permute-start.4) | collective-permute-done | bytes 217120 | tf_op jit(solution)/shard_map/ppermute | solution.py:1104
  24.8 3.5 %collective-permute-done.5.block2 = f32[424,128]{1,0:T(8,128)S(1)} collective-permute-done((f32[424,128]{1,0:T(8,128)S(1)}, f32[424,128]{1,0:T(8,128)S(1)}, u32[]{:S(2)}, u32[]{:S(2)}) %collective-permute-start.5) | collective-permute-done | bytes 217120 | tf_op jit(solution)/shard_map/ppermute | solution.py:1104
  28.4 0.0 collective-permute-done.6.block3
  28.4 0.1 collective-permute-start.7
  28.5 0.6 %assemble.1.field.assembled.own_start = f32[1024,128]{1,0:T(8,128)S(1)} custom-call(f32[424,128]{1,0:T(8,128)S(1)} %line.1.block0, f32[424,128]{1,0:T(8,128)S(1)} %collective-permute-done.4.block1, f32[424,128]{1,0:T(8,128)S(1)} %collective-permute-done.5.block2, f32[424,128]{1,0:T(8,128)S(1)} %collective-permute-done.6.block3), custom_call_target="tpu_custom_call" | custom-call | flops 4000000 | bytes 4000000 | tf_op jit(solution)/shard_map/assemble/pallas_call | solution.py:1045
  29.1 0.8 %collective-permute-done.7.other_halves = f32[256,128]{1,0:T(8,128)S(1)} collective-permute-done((f32[256,128]{1,0:T(8,128)S(1)}, f32[256,128]{1,0:T(8,128)S(1)}, u32[]{:S(2)}, u32[]{:S(2)}) %collective-permute-start.7) | collective-permute-done | bytes 131104 | tf_op jit(solution)/shard_map/ppermute | solution.py:1104
  29.8 0.1 collective-permute-start.8
  30.0 0.3 setup.1.coefs
  30.3 6.7 %cycle.1.own = f32[1128,128]{1,0:T(8,128)S(1)} custom-call(f32[2704,128]{1,0:T(8,128)S(1)} %setup.1.coefs, f32[1024,128]{1,0:T(8,128)S(1)} %assemble.1.field.assembled.own_start), custom_call_target="tpu_custom_call" | custom-call | flops 40000000 | bytes 30000000 | tf_op jit(solution)/shard_map/cycle/pallas_call | solution.py:1062
  37.0 0.0 copy-start
  37.0 0.0 collective-permute-done.8.other_start
  37.0 0.4 %collective-permute-start.9 = (f32[1128,128]{1,0:T(8,128)S(1)}, f32[1128,128]{1,0:T(8,128)S(1)}, u32[]{:S(2)}, u32[]{:S(2)}) collective-permute-start(f32[1128,128]{1,0:T(8,128)S(1)} %cycle.1.own), channel_id=1, source_target_pairs={{0,16},{16,0},{1,17},{17,1},{2,18},{18,2},{3,19},{19,3},{4,20},{20... | collective-permute-start | bytes 1732616 | tf_op jit(solution)/shard_map/ppermute | solution.py:1104
  37.5 0.8 %early.1 = (f32[16,128]{1,0:T(8,128)S(1)}, f32[192,160]{1,0:T(8,128)S(1)}) custom-call(f32[1128,128]{1,0:T(8,128)S(1)} %cycle.1.own, f32[1024,128]{1,0:T(8,128)S(1)} %assemble.1.field.assembled.own_start, f32[1024,128]{1,0:T(8,128)S(1)} %collective-permute-done.8.other_start), custom_call_target="tpu_custom_call" | custom-call | flops 4000000 | bytes 4000000 | tf_op jit(solution)/shard_map/early/pallas_call | solution.py:1075
  38.3 0.8 %collective-permute-done.9.other = f32[1128,128]{1,0:T(8,128)S(1)} collective-permute-done((f32[1128,128]{1,0:T(8,128)S(1)}, f32[1128,128]{1,0:T(8,128)S(1)}, u32[]{:S(2)}, u32[]{:S(2)}) %collective-permute-start.9) | collective-permute-done | bytes 577568 | tf_op jit(solution)/shard_map/ppermute | solution.py:1104
  39.1 0.0 copy-done
  39.1 1.5 %finish.1 = (f32[5,5,2,160]{3,2,1,0:T(2,128)}, f32[5,5,2,160]{3,2,1,0:T(2,128)}, f32[3]{0:T(128)}) custom-call(f32[1128,128]{1,0:T(8,128)S(1)} %cycle.1.own, f32[1128,128]{1,0:T(8,128)S(1)} %collective-permute-done.9.other, f32[1024,128]{1,0:T(8,128)S(1)} %assemble.1.field.assembled.own_start, f32[1024,128]{1,0:T(8,128)S(1)} %collective-permute-done.8.other_start, ...), custom_call_target="tpu_custom_call" | custom-call | tf_op jit(solution)/shard_map/finish/pallas_call | solution.py:1088
  (4 shorter events, 0.0 us)
Async XLA Ops:
  3.2 1.6 %collective-permute-start = (f32[104,128]{1,0:T(8,128)}, f32[104,128]{1,0:T(8,128)S(1)}, u32[]{:S(2)}, u32[]{:S(2)}) collective-permute-start(f32[104,128]{1,0:T(8,128)} %get-tuple-element.19), channel_id=1, source_target_pairs={{0,16},{16,0},{1,17},{17,1},{2,18},{18,2},{3,19},{19,3},{4,20},{20... | collective-permute-start | bytes 159752 | tf_op jit(solution)/shard_map/ppermute | solution.py:1104
  3.7 0.8 %copy-start.1 = (f32[120,128]{1,0:T(8,128)S(1)}, f32[120,128]{1,0:T(8,128)}, u32[]{:S(2)}) copy-start(f32[120,128]{1,0:T(8,128)} %get-tuple-element.20.source) | copy-start | bytes 184324
  4.8 5.6 %collective-permute-start.1 = (f32[120,128]{1,0:T(8,128)S(1)}, f32[120,128]{1,0:T(8,128)S(1)}, u32[]{:S(2)}, u32[]{:S(2)}) collective-permute-start(f32[120,128]{1,0:T(8,128)S(1)} %pad_maximum_fusion.piece0), channel_id=1, source_target_pairs={{0,4},{4,0},{8,12},{12,8},{1,5},{5,1},{9,13},{13,9},{2,6},{6,2},{1... | collective-permute-start | bytes 184328 | tf_op jit(solution)/shard_map/ppermute | solution.py:1104
  7.8 6.6 %collective-permute-start.2 = (f32[120,128]{1,0:T(8,128)S(1)}, f32[120,128]{1,0:T(8,128)S(1)}, u32[]{:S(2)}, u32[]{:S(2)}) collective-permute-start(f32[120,128]{1,0:T(8,128)S(1)} %pad_maximum_fusion.piece0), channel_id=1, source_target_pairs={{0,8},{4,12},{8,0},{12,4},{1,9},{5,13},{9,1},{13,5},{2,10},{6,14},... | collective-permute-start | bytes 184328 | tf_op jit(solution)/shard_map/ppermute | solution.py:1104
  10.4 6.1 %collective-permute-start.3 = (f32[120,128]{1,0:T(8,128)S(1)}, f32[120,128]{1,0:T(8,128)S(1)}, u32[]{:S(2)}, u32[]{:S(2)}) collective-permute-start(f32[120,128]{1,0:T(8,128)S(1)} %pad_maximum_fusion.piece0), channel_id=1, source_target_pairs={{0,12},{4,8},{8,4},{12,0},{1,13},{5,9},{9,5},{13,1},{2,14},{6,10},... | collective-permute-start | bytes 184328 | tf_op jit(solution)/shard_map/ppermute | solution.py:1104
  16.7 8.2 %collective-permute-start.4 = (f32[424,128]{1,0:T(8,128)S(1)}, f32[424,128]{1,0:T(8,128)S(1)}, u32[]{:S(2)}, u32[]{:S(2)}) collective-permute-start(f32[424,128]{1,0:T(8,128)S(1)} %line.1.block0), channel_id=1, source_target_pairs={{0,1},{1,0},{2,3},{3,2},{4,5},{5,4},{6,7},{7,6},{8,9},{9,8},{10,11... | collective-permute-start | bytes 651272 | tf_op jit(solution)/shard_map/ppermute | solution.py:1104
  18.2 10.2 %collective-permute-start.5 = (f32[424,128]{1,0:T(8,128)S(1)}, f32[424,128]{1,0:T(8,128)S(1)}, u32[]{:S(2)}, u32[]{:S(2)}) collective-permute-start(f32[424,128]{1,0:T(8,128)S(1)} %line.1.block0), channel_id=1, source_target_pairs={{0,2},{1,3},{2,0},{3,1},{4,6},{5,7},{6,4},{7,5},{8,10},{9,11},{10,... | collective-permute-start | bytes 651272 | tf_op jit(solution)/shard_map/ppermute | solution.py:1104
  19.7 8.6 %collective-permute-start.6 = (f32[424,128]{1,0:T(8,128)S(1)}, f32[424,128]{1,0:T(8,128)S(1)}, u32[]{:S(2)}, u32[]{:S(2)}) collective-permute-start(f32[424,128]{1,0:T(8,128)S(1)} %line.1.block0), channel_id=1, source_target_pairs={{0,3},{1,2},{2,1},{3,0},{4,7},{5,6},{6,5},{7,4},{8,11},{9,10},{10,... | collective-permute-start | bytes 651272 | tf_op jit(solution)/shard_map/ppermute | solution.py:1104
  28.4 1.4 %collective-permute-start.7 = (f32[256,128]{1,0:T(8,128)S(1)}, f32[256,128]{1,0:T(8,128)S(1)}, u32[]{:S(2)}, u32[]{:S(2)}) collective-permute-start(f32[256,128]{1,0:T(8,128)S(1)} %halves.1.own_halves), channel_id=1, source_target_pairs={{0,16},{16,0},{1,17},{17,1},{2,18},{18,2},{3,19},{19,3},{4,20},{20... | collective-permute-start | bytes 393224 | tf_op jit(solution)/shard_map/ppermute | solution.py:1104
  29.8 7.2 %collective-permute-start.8 = (f32[1024,128]{1,0:T(8,128)S(1)}, f32[1024,128]{1,0:T(8,128)S(1)}, u32[]{:S(2)}, u32[]{:S(2)}) collective-permute-start(f32[1024,128]{1,0:T(8,128)S(1)} %assemble.1.field.assembled.own_start), channel_id=1, source_target_pairs={{0,16},{16,0},{1,17},{17,1},{2,18},{18,2},{3,19},{19,3},{4,20},{20... | collective-permute-start | bytes 1572872 | tf_op jit(solution)/shard_map/ppermute | solution.py:1104
  37.0 2.1 %copy-start = (f32[2,5,5,160]{3,0,2,1:T(2,128)S(1)}, f32[2,5,5,160]{3,0,2,1:T(2,128)}, u32[]{:S(2)}) copy-start(f32[2,5,5,160]{3,0,2,1:T(2,128)} %param.6) | copy-start | bytes 96004
  37.0 2.1 %collective-permute-start.9 = (f32[1128,128]{1,0:T(8,128)S(1)}, f32[1128,128]{1,0:T(8,128)S(1)}, u32[]{:S(2)}, u32[]{:S(2)}) collective-permute-start(f32[1128,128]{1,0:T(8,128)S(1)} %cycle.1.own), channel_id=1, source_target_pairs={{0,16},{16,0},{1,17},{17,1},{2,18},{18,2},{3,19},{19,3},{4,20},{20... | collective-permute-start | bytes 1732616 | tf_op jit(solution)/shard_map/ppermute | solution.py:1104

commit v11 on v10

--- a/solution.py
+++ b/solution.py
@@ -429,8 +429,9 @@
     return rows.astype(np.float32)
 
 
-def pick_line(k):
-    return (iota((160, 128), 0) == 5 * (iota((160, 128), 1) % EZ) + k).astype(F32)
+def pick_lines(k):
+    lane = iota((160, 256), 1)
+    return (iota((160, 256), 0) == 5 * (lane % EZ) + k + lane // 128).astype(F32)
 
 
 def pair_factors(sec, table, own, s):
@@ -475,8 +476,11 @@
                 stack[128 + s * 32 + r : 128 + s * 32 + r + 1, :] = value[s : s + 1]
     stack[64:128, :] = exact_dot(rows_t[...], stack[128:192, :])
     source = stack[...]
-    for k in range(5):
-        lines[224 * k : 224 * k + 224, :] = split_dot(source, pick_line(k))
+    for k in (0, 2, 4):
+        shown = split_dot(source, pick_lines(k))
+        lines[224 * k : 224 * k + 224, :] = shown[:, :128]
+        if k < 4:
+            lines[224 * k + 224 : 224 * k + 448, :] = shown[:, 128:]
 
     def part(k, first):
         return lines[224 * k + first : 224 * k + first + 32, :]
@@ -666,7 +670,7 @@
     return choose(iota(row.shape, 1) // EZ, [turned[(g - 2 * slot - 1) % 4] for g in range(4)])
 
 
-def line_kernel(piece0, piece1, piece2, piece3, line, faces):
+def line_kernel(piece3, piece2, piece1, piece0, line, faces):
     pieces = (piece0, piece1, piece2, piece3)
     even = lax.axis_index("gx") % 2 == 0
     odd = iota((8, 128), 1) // EZ % 2 == 1
@@ -964,7 +968,8 @@
 
 
 def raw_order(k):
-    return (iota((128, 160), 1) == 5 * (iota((128, 160), 0) % EZ) + k).astype(F32)
+    lane = iota((256, 160), 0)
+    return (iota((256, 160), 1) == 5 * (lane % EZ) + k + lane // 128).astype(F32)
 
 
 def early_kernel(own, own_start, other_start, sums, column_out, cols):
@@ -977,11 +982,15 @@
         z = own[FIELD + k * 25 : FIELD + k * 25 + 25, :]
         start, other = own_start[where, :], other_start[where, :]
         w = start - own[where, :]
+        side = slice(0, 128) if k % 2 == 0 else slice(128, 256)
         for s in range(2):
-            cols[s * 32 : s * 32 + 25, :] = own_factors[s] * z
-            cols[64 + s * 32 : 64 + s * 32 + 25, :] = own_factors[s] * start + other_factors[s] * other
-            cols[128 + s * 32 : 128 + s * 32 + 25, :] = own_factors[s] * w
-        total = total + split_dot(cols[...], raw_order(k))
+            cols[s * 32 : s * 32 + 25, side] = own_factors[s] * z
+            cols[64 + s * 32 : 64 + s * 32 + 25, side] = own_factors[s] * start + other_factors[s] * other
+            cols[128 + s * 32 : 128 + s * 32 + 25, side] = own_factors[s] * w
+        if k % 2 == 1:
+            total = total + split_dot(cols[...], raw_order(k - 1))
+    cols[:, 128:] = jnp.zeros((192, 128), F32)
+    total = total + split_dot(cols[...], raw_order(4))
     column_out[...] = total
     nothing = jnp.zeros((8, 128), F32)
     uppers, sizes = [nothing] * 5, [nothing] * 5
@@ -1004,10 +1013,14 @@
         where = column_rows(k)
         z = other[FIELD + k * 25 : FIELD + k * 25 + 25, :]
         w = other_start[where, :] - other[where, :]
+        side = slice(0, 128) if k % 2 == 0 else slice(128, 256)
         for s in range(2):
-            cols[s * 32 : s * 32 + 25, :] = factors[s] * z
-            cols[64 + s * 32 : 64 + s * 32 + 25, :] = factors[s] * w
-        total = total + split_dot(cols[...], raw_order(k))
+            cols[s * 32 : s * 32 + 25, side] = factors[s] * z
+            cols[64 + s * 32 : 64 + s * 32 + 25, side] = factors[s] * w
+        if k % 2 == 1:
+            total = total + split_dot(cols[...], raw_order(k - 1))
+    cols[:, 128:] = jnp.zeros((128, 128), F32)
+    total = total + split_dot(cols[...], raw_order(4))
     nothing = jnp.zeros((8, 128), F32)
     uppers = [nothing] * 5
     for r in range(125):
@@ -1077,7 +1090,7 @@
         out_shape=[jax.ShapeDtypeStruct((16, 128), F32), jax.ShapeDtypeStruct((192, 160), F32)],
         in_specs=[VMEM] * 3,
         out_specs=[VMEM] * 2,
-        scratch_shapes=[pltpu.VMEM((192, 128), F32)],
+        scratch_shapes=[pltpu.VMEM((192, 256), F32)],
         compiler_params=limit(16),
         cost_estimate=pl.CostEstimate(flops=4_000_000, bytes_accessed=4_000_000, transcendentals=0),
         name="early",
@@ -1094,7 +1107,7 @@
         ],
         in_specs=[VMEM] * 7,
         out_specs=[VMEM, VMEM, pl.BlockSpec(memory_space=pltpu.SMEM)],
-        scratch_shapes=[pltpu.VMEM((128, 128), F32), pltpu.VMEM((128, 160), F32)],
+        scratch_shapes=[pltpu.VMEM((128, 256), F32), pltpu.VMEM((128, 160), F32)],
         compiler_params=limit(24),
         name="finish",
     )(own, other, own_start, other_start, sums, column, guess)
@@ -1110,7 +1123,7 @@
     got, mine, kappa_piece = lax.optimization_barrier((exchange(theirs, "section", 1), *part(mine)))
     piece = jnp.concatenate([mine + got, kappa_piece])
     pieces = [piece] + [exchange(piece, "gx", bits) for bits in (1, 2, 3)]
-    line = plain_call(line_kernel, "line", LINE, [4 * 64], pieces)
+    line = plain_call(line_kernel, "line", LINE, [4 * 64], pieces[::-1])
     blocks = [line] + [exchange(line, "gy", bits) for bits in (1, 2, 3)]
     halves = plain_call(halves_kernel, "halves", COLS * 16, [], blocks)
     other_halves = exchange(halves, "section", 1)

time: 40.8 us -> 40.9 us (level)
  transfers between devices with their start and end apart: 10 -> 10, of which waited for: 7 -> 7; matrix products, arithmetic and copies ran while one was open for 0% -> 0% of each run, Pallas kernels for 21% -> 20%
where the time goes in v11:
time: 40.9 us; the launch traced here: 40.7 us
  waiting for transfers between devices  16.4 us (40%)
  Pallas kernels  12.4 us (30%)
  starting transfers between devices  10.4 us (25%)
  local copies, waits for them, and re-layouts  0.83 us (2%)
  between operations  0.71 us (2%)
    ppermute x10, waiting for transfers between devices, exchange(): lax.ppermute(x, axis, [(n, n ^ bits) for n in range(lax.axis_size(axis))])  16.4 us
    ppermute x10, starting transfers between devices, exchange(): lax.ppermute(x, axis, [(n, n ^ bits) for n in range(lax.axis_size(axis))])  10.4 us
    pallas_call x1, Pallas kernels, cycle(): pl.pallas_call(cycle_kernel, out_shape=jax.ShapeDtypeStruct((FIELD + 128,...  6.7 us
    pallas_call x1, Pallas kernels, local_part(): pl.pallas_call(local_kernel, out_shape=[jax.ShapeDtypeStruct((rows, 128),...  2.34 us
    pallas_call x1, Pallas kernels, finish(): pl.pallas_call(finish_kernel, out_shape=[jax.ShapeDtypeStruct(guess.shape...  1.47 us
    pallas_call x4, Pallas kernels, plain_call(): pl.pallas_call(kernel, out_shape=jax.ShapeDtypeStruct((rows, 128), F32),...  1.08 us
    unnamed x4, local copies, waits for them, and re-layouts  0.83 us
  transfers between devices with their start and end apart: 10, of which 7 were waited for; matrix products, arithmetic and copies ran while one was open for 0% of the time, Pallas kernels for 20%

profile of v11, /device:TPU:0, one launch (start us, length us, event | category | flops | bytes accessed | tf_op | source)
XLA Modules:
  0.0 40.7 jit_solution(7312948614341586715)
XLA Ops:
  0.6 2.3 %local_part.1 = (f32[120,128]{1,0:T(8,128)}, f32[104,128]{1,0:T(8,128)}) custom-call(f32[5,5,2,160]{3,2,1,0:T(2,128)} %bitcast.6, f32[5,5,2,160]{3,2,1,0:T(2,128)} %bitcast.4, f32[5,5,160]{2,1,0:T(8,128)} %kappa_in.1, s32[6,1,1,32]{3,2,1,0:T(1,128)} %flags_in.1, f32[64,64]{1,0:T(8,128)} %constant.2.clone.rows_in), custom_call_target="tpu_custom_call" | custom-call | flops 20000000 | bytes 8000000 | tf_op jit(solution)/shard_map/local_part/pallas_call | solution.py:560
  3.0 0.5 %collective-permute-start = (f32[104,128]{1,0:T(8,128)}, f32[104,128]{1,0:T(8,128)S(1)}, u32[]{:S(2)}, u32[]{:S(2)}) collective-permute-start(f32[104,128]{1,0:T(8,128)} %get-tuple-element.19), channel_id=1, source_target_pairs={{0,16},{16,0},{1,17},{17,1},{2,18},{18,2},{3,19},{19,3},{4,20},{20... | collective-permute-start | bytes 159752 | tf_op jit(solution)/shard_map/ppermute | solution.py:1117
  3.5 0.0 copy-start.1
  3.5 0.8 %copy-done.1 = f32[120,128]{1,0:T(8,128)S(1)} copy-done((f32[120,128]{1,0:T(8,128)S(1)}, f32[120,128]{1,0:T(8,128)}, u32[]{:S(2)}) %copy-start.1) | copy-done | bytes 61464
  4.3 0.3 collective-permute-done
  4.6 5.0 %collective-permute-start.1 = (f32[120,128]{1,0:T(8,128)S(1)}, f32[120,128]{1,0:T(8,128)S(1)}, u32[]{:S(2)}, u32[]{:S(2)}) collective-permute-start(f32[120,128]{1,0:T(8,128)S(1)} %pad_maximum_fusion.piece0), channel_id=1, source_target_pairs={{0,12},{4,8},{8,4},{12,0},{1,13},{5,9},{9,5},{13,1},{2,14},{6,10},... | collective-permute-start | bytes 184328 | tf_op jit(solution)/shard_map/ppermute | solution.py:1117
  9.6 0.0 collective-permute-start.2
  9.6 0.6 %collective-permute-start.3 = (f32[120,128]{1,0:T(8,128)S(1)}, f32[120,128]{1,0:T(8,128)S(1)}, u32[]{:S(2)}, u32[]{:S(2)}) collective-permute-start(f32[120,128]{1,0:T(8,128)S(1)} %pad_maximum_fusion.piece0), channel_id=1, source_target_pairs={{0,4},{4,0},{8,12},{12,8},{1,5},{5,1},{9,13},{13,9},{2,6},{6,2},{1... | collective-permute-start | bytes 184328 | tf_op jit(solution)/shard_map/ppermute | solution.py:1117
  10.3 1.8 %collective-permute-done.1.piece3 = f32[120,128]{1,0:T(8,128)S(1)} collective-permute-done((f32[120,128]{1,0:T(8,128)S(1)}, f32[120,128]{1,0:T(8,128)S(1)}, u32[]{:S(2)}, u32[]{:S(2)}) %collective-permute-start.1) | collective-permute-done | bytes 61472 | tf_op jit(solution)/shard_map/ppermute | solution.py:1117
  12.1 3.1 %collective-permute-done.2.piece2 = f32[120,128]{1,0:T(8,128)S(1)} collective-permute-done((f32[120,128]{1,0:T(8,128)S(1)}, f32[120,128]{1,0:T(8,128)S(1)}, u32[]{:S(2)}, u32[]{:S(2)}) %collective-permute-start.2) | collective-permute-done | bytes 61472 | tf_op jit(solution)/shard_map/ppermute | solution.py:1117
  15.2 0.0 collective-permute-done.3.piece1
  15.2 0.2 line.1.block0
  15.4 1.6 %collective-permute-start.4 = (f32[424,128]{1,0:T(8,128)S(1)}, f32[424,128]{1,0:T(8,128)S(1)}, u32[]{:S(2)}, u32[]{:S(2)}) collective-permute-start(f32[424,128]{1,0:T(8,128)S(1)} %line.1.block0), channel_id=1, source_target_pairs={{0,1},{1,0},{2,3},{3,2},{4,5},{5,4},{6,7},{7,6},{8,9},{9,8},{10,11... | collective-permute-start | bytes 651272 | tf_op jit(solution)/shard_map/ppermute | solution.py:1117
  17.0 1.5 %collective-permute-start.5 = (f32[424,128]{1,0:T(8,128)S(1)}, f32[424,128]{1,0:T(8,128)S(1)}, u32[]{:S(2)}, u32[]{:S(2)}) collective-permute-start(f32[424,128]{1,0:T(8,128)S(1)} %line.1.block0), channel_id=1, source_target_pairs={{0,2},{1,3},{2,0},{3,1},{4,6},{5,7},{6,4},{7,5},{8,10},{9,11},{10,... | collective-permute-start | bytes 651272 | tf_op jit(solution)/shard_map/ppermute | solution.py:1117
  18.5 0.5 %collective-permute-start.6 = (f32[424,128]{1,0:T(8,128)S(1)}, f32[424,128]{1,0:T(8,128)S(1)}, u32[]{:S(2)}, u32[]{:S(2)}) collective-permute-start(f32[424,128]{1,0:T(8,128)S(1)} %line.1.block0), channel_id=1, source_target_pairs={{0,3},{1,2},{2,1},{3,0},{4,7},{5,6},{6,5},{7,4},{8,11},{9,10},{10,... | collective-permute-start | bytes 651272 | tf_op jit(solution)/shard_map/ppermute | solution.py:1117
  19.0 4.7 %collective-permute-done.4.block1 = f32[424,128]{1,0:T(8,128)S(1)} collective-permute-done((f32[424,128]{1,0:T(8,128)S(1)}, f32[424,128]{1,0:T(8,128)S(1)}, u32[]{:S(2)}, u32[]{:S(2)}) %collective-permute-start.4) | collective-permute-done | bytes 217120 | tf_op jit(solution)/shard_map/ppermute | solution.py:1117
  23.7 4.8 %collective-permute-done.5.block2 = f32[424,128]{1,0:T(8,128)S(1)} collective-permute-done((f32[424,128]{1,0:T(8,128)S(1)}, f32[424,128]{1,0:T(8,128)S(1)}, u32[]{:S(2)}, u32[]{:S(2)}) %collective-permute-start.5) | collective-permute-done | bytes 217120 | tf_op jit(solution)/shard_map/ppermute | solution.py:1117
  28.5 0.0 collective-permute-done.6.block3
  28.5 0.1 collective-permute-start.7
  28.6 0.6 %assemble.1.field.assembled.own_start = f32[1024,128]{1,0:T(8,128)S(1)} custom-call(f32[424,128]{1,0:T(8,128)S(1)} %line.1.block0, f32[424,128]{1,0:T(8,128)S(1)} %collective-permute-done.4.block1, f32[424,128]{1,0:T(8,128)S(1)} %collective-permute-done.5.block2, f32[424,128]{1,0:T(8,128)S(1)} %collective-permute-done.6.block3), custom_call_target="tpu_custom_call" | custom-call | flops 4000000 | bytes 4000000 | tf_op jit(solution)/shard_map/assemble/pallas_call | solution.py:1058
  29.2 0.8 %collective-permute-done.7.other_halves = f32[256,128]{1,0:T(8,128)S(1)} collective-permute-done((f32[256,128]{1,0:T(8,128)S(1)}, f32[256,128]{1,0:T(8,128)S(1)}, u32[]{:S(2)}, u32[]{:S(2)}) %collective-permute-start.7) | collective-permute-done | bytes 131104 | tf_op jit(solution)/shard_map/ppermute | solution.py:1117
  29.9 0.1 collective-permute-start.8
  30.1 0.3 setup.1.coefs
  30.4 6.7 %cycle.1.own = f32[1128,128]{1,0:T(8,128)S(1)} custom-call(f32[2704,128]{1,0:T(8,128)S(1)} %setup.1.coefs, f32[1024,128]{1,0:T(8,128)S(1)} %assemble.1.field.assembled.own_start), custom_call_target="tpu_custom_call" | custom-call | flops 40000000 | bytes 30000000 | tf_op jit(solution)/shard_map/cycle/pallas_call | solution.py:1075
  37.1 0.0 copy-start
  37.1 0.0 collective-permute-done.8.other_start
  37.1 0.4 %collective-permute-start.9 = (f32[1128,128]{1,0:T(8,128)S(1)}, f32[1128,128]{1,0:T(8,128)S(1)}, u32[]{:S(2)}, u32[]{:S(2)}) collective-permute-start(f32[1128,128]{1,0:T(8,128)S(1)} %cycle.1.own), channel_id=1, source_target_pairs={{0,16},{16,0},{1,17},{17,1},{2,18},{18,2},{3,19},{19,3},{4,20},{20... | collective-permute-start | bytes 1732616 | tf_op jit(solution)/shard_map/ppermute | solution.py:1117
  37.6 0.8 %early.1 = (f32[16,128]{1,0:T(8,128)S(1)}, f32[192,160]{1,0:T(8,128)S(1)}) custom-call(f32[1128,128]{1,0:T(8,128)S(1)} %cycle.1.own, f32[1024,128]{1,0:T(8,128)S(1)} %assemble.1.field.assembled.own_start, f32[1024,128]{1,0:T(8,128)S(1)} %collective-permute-done.8.other_start), custom_call_target="tpu_custom_call" | custom-call | flops 4000000 | bytes 4000000 | tf_op jit(solution)/shard_map/early/pallas_call | solution.py:1088
  38.3 0.9 %collective-permute-done.9.other = f32[1128,128]{1,0:T(8,128)S(1)} collective-permute-done((f32[1128,128]{1,0:T(8,128)S(1)}, f32[1128,128]{1,0:T(8,128)S(1)}, u32[]{:S(2)}, u32[]{:S(2)}) %collective-permute-start.9) | collective-permute-done | bytes 577568 | tf_op jit(solution)/shard_map/ppermute | solution.py:1117
  39.2 0.0 copy-done
  39.2 1.5 %finish.1 = (f32[5,5,2,160]{3,2,1,0:T(2,128)}, f32[5,5,2,160]{3,2,1,0:T(2,128)}, f32[3]{0:T(128)}) custom-call(f32[1128,128]{1,0:T(8,128)S(1)} %cycle.1.own, f32[1128,128]{1,0:T(8,128)S(1)} %collective-permute-done.9.other, f32[1024,128]{1,0:T(8,128)S(1)} %assemble.1.field.assembled.own_start, f32[1024,128]{1,0:T(8,128)S(1)} %collective-permute-done.8.other_start, ...), custom_call_target="tpu_custom_call" | custom-call | tf_op jit(solution)/shard_map/finish/pallas_call | solution.py:1101
  (4 shorter events, 0.0 us)
Async XLA Ops:
  3.0 1.6 %collective-permute-start = (f32[104,128]{1,0:T(8,128)}, f32[104,128]{1,0:T(8,128)S(1)}, u32[]{:S(2)}, u32[]{:S(2)}) collective-permute-start(f32[104,128]{1,0:T(8,128)} %get-tuple-element.19), channel_id=1, source_target_pairs={{0,16},{16,0},{1,17},{17,1},{2,18},{18,2},{3,19},{19,3},{4,20},{20... | collective-permute-start | bytes 159752 | tf_op jit(solution)/shard_map/ppermute | solution.py:1117
  3.5 0.8 %copy-start.1 = (f32[120,128]{1,0:T(8,128)S(1)}, f32[120,128]{1,0:T(8,128)}, u32[]{:S(2)}) copy-start(f32[120,128]{1,0:T(8,128)} %get-tuple-element.20.source) | copy-start | bytes 184324
  4.6 7.5 %collective-permute-start.1 = (f32[120,128]{1,0:T(8,128)S(1)}, f32[120,128]{1,0:T(8,128)S(1)}, u32[]{:S(2)}, u32[]{:S(2)}) collective-permute-start(f32[120,128]{1,0:T(8,128)S(1)} %pad_maximum_fusion.piece0), channel_id=1, source_target_pairs={{0,12},{4,8},{8,4},{12,0},{1,13},{5,9},{9,5},{13,1},{2,14},{6,10},... | collective-permute-start | bytes 184328 | tf_op jit(solution)/shard_map/ppermute | solution.py:1117
  9.6 5.6 %collective-permute-start.2 = (f32[120,128]{1,0:T(8,128)S(1)}, f32[120,128]{1,0:T(8,128)S(1)}, u32[]{:S(2)}, u32[]{:S(2)}) collective-permute-start(f32[120,128]{1,0:T(8,128)S(1)} %pad_maximum_fusion.piece0), channel_id=1, source_target_pairs={{0,8},{4,12},{8,0},{12,4},{1,9},{5,13},{9,1},{13,5},{2,10},{6,14},... | collective-permute-start | bytes 184328 | tf_op jit(solution)/shard_map/ppermute | solution.py:1117
  9.6 5.6 %collective-permute-start.3 = (f32[120,128]{1,0:T(8,128)S(1)}, f32[120,128]{1,0:T(8,128)S(1)}, u32[]{:S(2)}, u32[]{:S(2)}) collective-permute-start(f32[120,128]{1,0:T(8,128)S(1)} %pad_maximum_fusion.piece0), channel_id=1, source_target_pairs={{0,4},{4,0},{8,12},{12,8},{1,5},{5,1},{9,13},{13,9},{2,6},{6,2},{1... | collective-permute-start | bytes 184328 | tf_op jit(solution)/shard_map/ppermute | solution.py:1117
  15.4 8.3 %collective-permute-start.4 = (f32[424,128]{1,0:T(8,128)S(1)}, f32[424,128]{1,0:T(8,128)S(1)}, u32[]{:S(2)}, u32[]{:S(2)}) collective-permute-start(f32[424,128]{1,0:T(8,128)S(1)} %line.1.block0), channel_id=1, source_target_pairs={{0,1},{1,0},{2,3},{3,2},{4,5},{5,4},{6,7},{7,6},{8,9},{9,8},{10,11... | collective-permute-start | bytes 651272 | tf_op jit(solution)/shard_map/ppermute | solution.py:1117
  17.0 11.5 %collective-permute-start.5 = (f32[424,128]{1,0:T(8,128)S(1)}, f32[424,128]{1,0:T(8,128)S(1)}, u32[]{:S(2)}, u32[]{:S(2)}) collective-permute-start(f32[424,128]{1,0:T(8,128)S(1)} %line.1.block0), channel_id=1, source_target_pairs={{0,2},{1,3},{2,0},{3,1},{4,6},{5,7},{6,4},{7,5},{8,10},{9,11},{10,... | collective-permute-start | bytes 651272 | tf_op jit(solution)/shard_map/ppermute | solution.py:1117
  18.5 10.0 %collective-permute-start.6 = (f32[424,128]{1,0:T(8,128)S(1)}, f32[424,128]{1,0:T(8,128)S(1)}, u32[]{:S(2)}, u32[]{:S(2)}) collective-permute-start(f32[424,128]{1,0:T(8,128)S(1)} %line.1.block0), channel_id=1, source_target_pairs={{0,3},{1,2},{2,1},{3,0},{4,7},{5,6},{6,5},{7,4},{8,11},{9,10},{10,... | collective-permute-start | bytes 651272 | tf_op jit(solution)/shard_map/ppermute | solution.py:1117
  28.5 1.4 %collective-permute-start.7 = (f32[256,128]{1,0:T(8,128)S(1)}, f32[256,128]{1,0:T(8,128)S(1)}, u32[]{:S(2)}, u32[]{:S(2)}) collective-permute-start(f32[256,128]{1,0:T(8,128)S(1)} %halves.1.own_halves), channel_id=1, source_target_pairs={{0,16},{16,0},{1,17},{17,1},{2,18},{18,2},{3,19},{19,3},{4,20},{20... | collective-permute-start | bytes 393224 | tf_op jit(solution)/shard_map/ppermute | solution.py:1117
  29.9 7.2 %collective-permute-start.8 = (f32[1024,128]{1,0:T(8,128)S(1)}, f32[1024,128]{1,0:T(8,128)S(1)}, u32[]{:S(2)}, u32[]{:S(2)}) collective-permute-start(f32[1024,128]{1,0:T(8,128)S(1)} %assemble.1.field.assembled.own_start), channel_id=1, source_target_pairs={{0,16},{16,0},{1,17},{17,1},{2,18},{18,2},{3,19},{19,3},{4,20},{20... | collective-permute-start | bytes 1572872 | tf_op jit(solution)/shard_map/ppermute | solution.py:1117
  37.1 2.1 %copy-start = (f32[2,5,5,160]{3,0,2,1:T(2,128)S(1)}, f32[2,5,5,160]{3,0,2,1:T(2,128)}, u32[]{:S(2)}) copy-start(f32[2,5,5,160]{3,0,2,1:T(2,128)} %param.6) | copy-start | bytes 96004
  37.1 2.1 %collective-permute-start.9 = (f32[1128,128]{1,0:T(8,128)S(1)}, f32[1128,128]{1,0:T(8,128)S(1)}, u32[]{:S(2)}, u32[]{:S(2)}) collective-permute-start(f32[1128,128]{1,0:T(8,128)S(1)} %cycle.1.own), channel_id=1, source_target_pairs={{0,16},{16,0},{1,17},{17,1},{2,18},{18,2},{3,19},{19,3},{4,20},{20... | collective-permute-start | bytes 1732616 | tf_op jit(solution)/shard_map/ppermute | solution.py:1117

commit v12 on v11

--- a/solution.py
+++ b/solution.py
@@ -806,7 +806,7 @@
     push = 2.0 * second_rho / RADIUS * CENTRE
     for p, level in enumerate(levels):
         size = level.count**3
-        level.gains = [coefs[tile(GAINS[p] + d), :] for d in range(6)]
+        level.gains = [-coefs[tile(GAINS[p] + d), :] for d in range(6)]
         level.diag = lambda first, count, p=p: load(coefs, DIAGS[p] + first, count)
         level.jac = lambda first, count, p=p, size=size: load(coefs, DIAGS[p] + size + first, count)
 
@@ -823,45 +823,48 @@
         kx, ky, kz = level.tables
         gains = level.gains
         source = level.dir if smooth else level.x
+        def tree(terms):
+            while len(terms) > 1:
+                pairs = [a + b for a, b in zip(terms[::2], terms[1::2])]
+                terms = pairs + terms[len(terms) // 2 * 2 :]
+            return terms[0]
+
         def plane(k):
             def line_at(i):
                 return load(source, (k * n + i) * n, n)
 
+            lines, totals = [], []
             for i in range(n):
                 first = (k * n + i) * n
                 v = line_at(i)
-                total = level.diag(first, n) * v
-                for m in range(n):
-                    if m != i:
-                        total = total + float(kx[i, m]) * line_at(m)
-                for m in range(n):
-                    if m != k:
-                        total = total + float(kz[k, m]) * load(source, (m * n + i) * n, n)
-                lines = []
+                along_x = [float(kx[i, m]) * line_at(m) for m in range(n) if m != i]
+                if i == 0:
+                    along_x.append(gains[0] * lanes.x_before(line_at(n - 1)))
+                if i == n - 1:
+                    along_x.append(gains[1] * lanes.x_after(line_at(0)))
+                along_z = [float(kz[k, m]) * load(source, (m * n + i) * n, n) for m in range(n) if m != k]
+                if k == 0:
+                    along_z.append(gains[4] * lanes.z_before(load(source, ((n - 1) * n + i) * n, n)))
+                if k == n - 1:
+                    along_z.append(gains[5] * lanes.z_after(load(source, i * n, n)))
+                along_y = []
                 for j in range(n):
-                    line = None
-                    for m in range(n):
-                        if m != j:
-                            term = float(ky[j, m]) * v[m]
-                            line = term if line is None else line + term
+                    terms = [float(ky[j, m]) * v[m] for m in range(n) if m != j]
                     if j == 0:
-                        line = line - gains[2] * lanes.y_before(v[n - 1])
+                        terms.append(gains[2] * lanes.y_before(v[n - 1]))
                     if j == n - 1:
-                        line = line - gains[3] * lanes.y_after(v[0])
-                    lines.append(line)
-                total = total + jnp.stack(lines)
-                if i == 0:
-                    total = total - gains[0] * lanes.x_before(line_at(n - 1))
-                if i == n - 1:
-                    total = total - gains[1] * lanes.x_after(line_at(0))
-                if k == 0:
-                    total = total - gains[4] * lanes.z_before(load(source, ((n - 1) * n + i) * n, n))
-                if k == n - 1:
-                    total = total - gains[5] * lanes.z_after(load(source, i * n, n))
-                image = v + (same * total + swap * pltpu.roll(total, 64, 2))
+                        terms.append(gains[3] * lanes.y_after(v[0]))
+                    along_y.append(tree(terms))
+                lines.append(v)
+                totals.append(tree([level.diag(first, n) * v, tree(along_x), tree(along_z), jnp.stack(along_y)]))
+            moved = [pltpu.roll(total, 64, 2) for total in totals]
+            for i in range(n):
+                first = (k * n + i) * n
+                v = lines[i]
+                image = v + (same * totals[i] + swap * moved[i])
                 if smooth:
                     scaled = level.jac(first, n) * (load(level.res, first, n) - image)
-                    store(level.x, first, load(level.x, first, n) + keep * v + push * scaled)
+                    store(level.x, first, (load(level.x, first, n) + keep * v) + push * scaled)
                 else:
                     rest = load(level.f, first, n) - image
                     store(level.res, first, rest)

time: 40.9 us -> 39.7 us (0.971)
  Pallas kernels: 12.4 us -> 11.2 us
    pallas_call x1, Pallas kernels: 6.7 us -> 5.51 us  [cycle(): pl.pallas_call(cycle_kernel, out_shape=jax.ShapeDtypeStruct((FIELD + 128,...]
  transfers between devices with their start and end apart: 10 -> 10, of which waited for: 7 -> 7; matrix products, arithmetic and copies ran while one was open for 0% -> 0% of each run, Pallas kernels for 20% -> 18%
where the time goes in v12:
time: 39.7 us; the launch traced here: 39.5 us
  waiting for transfers between devices  16.4 us (41%)
  Pallas kernels  11.2 us (28%)
  starting transfers between devices  10.4 us (26%)
  local copies, waits for them, and re-layouts  0.83 us (2%)
  between operations  0.71 us (2%)
    ppermute x10, waiting for transfers between devices, exchange(): lax.ppermute(x, axis, [(n, n ^ bits) for n in range(lax.axis_size(axis))])  16.4 us
    ppermute x10, starting transfers between devices, exchange(): lax.ppermute(x, axis, [(n, n ^ bits) for n in range(lax.axis_size(axis))])  10.4 us
    pallas_call x1, Pallas kernels, cycle(): pl.pallas_call(cycle_kernel, out_shape=jax.ShapeDtypeStruct((FIELD + 128,...  5.51 us
    pallas_call x1, Pallas kernels, local_part(): pl.pallas_call(local_kernel, out_shape=[jax.ShapeDtypeStruct((rows, 128),...  2.34 us
    pallas_call x1, Pallas kernels, finish(): pl.pallas_call(finish_kernel, out_shape=[jax.ShapeDtypeStruct(guess.shape...  1.47 us
    pallas_call x4, Pallas kernels, plain_call(): pl.pallas_call(kernel, out_shape=jax.ShapeDtypeStruct((rows, 128), F32),...  1.08 us
    unnamed x4, local copies, waits for them, and re-layouts  0.83 us
  transfers between devices with their start and end apart: 10, of which 7 were waited for; matrix products, arithmetic and copies ran while one was open for 0% of the time, Pallas kernels for 18%

profile of v12, /device:TPU:0, one launch (start us, length us, event | category | flops | bytes accessed | tf_op | source)
XLA Modules:
  0.0 39.5 jit_solution(183583799967677007)
XLA Ops:
  0.6 2.3 %local_part.1 = (f32[120,128]{1,0:T(8,128)}, f32[104,128]{1,0:T(8,128)}) custom-call(f32[5,5,2,160]{3,2,1,0:T(2,128)} %bitcast.6, f32[5,5,2,160]{3,2,1,0:T(2,128)} %bitcast.4, f32[5,5,160]{2,1,0:T(8,128)} %kappa_in.1, s32[6,1,1,32]{3,2,1,0:T(1,128)} %flags_in.1, f32[64,64]{1,0:T(8,128)} %constant.2.clone.rows_in), custom_call_target="tpu_custom_call" | custom-call | flops 20000000 | bytes 8000000 | tf_op jit(solution)/shard_map/local_part/pallas_call | solution.py:560
  3.0 0.5 %collective-permute-start = (f32[104,128]{1,0:T(8,128)}, f32[104,128]{1,0:T(8,128)S(1)}, u32[]{:S(2)}, u32[]{:S(2)}) collective-permute-start(f32[104,128]{1,0:T(8,128)} %get-tuple-element.19), channel_id=1, source_target_pairs={{0,16},{16,0},{1,17},{17,1},{2,18},{18,2},{3,19},{19,3},{4,20},{20... | collective-permute-start | bytes 159752 | tf_op jit(solution)/shard_map/ppermute | solution.py:1120
  3.5 0.0 copy-start.1
  3.5 0.8 %copy-done.1 = f32[120,128]{1,0:T(8,128)S(1)} copy-done((f32[120,128]{1,0:T(8,128)S(1)}, f32[120,128]{1,0:T(8,128)}, u32[]{:S(2)}) %copy-start.1) | copy-done | bytes 61464
  4.3 0.3 collective-permute-done
  4.6 5.0 %collective-permute-start.1 = (f32[120,128]{1,0:T(8,128)S(1)}, f32[120,128]{1,0:T(8,128)S(1)}, u32[]{:S(2)}, u32[]{:S(2)}) collective-permute-start(f32[120,128]{1,0:T(8,128)S(1)} %pad_maximum_fusion.piece0), channel_id=1, source_target_pairs={{0,12},{4,8},{8,4},{12,0},{1,13},{5,9},{9,5},{13,1},{2,14},{6,10},... | collective-permute-start | bytes 184328 | tf_op jit(solution)/shard_map/ppermute | solution.py:1120
  9.6 0.0 collective-permute-start.2
  9.6 0.6 %collective-permute-start.3 = (f32[120,128]{1,0:T(8,128)S(1)}, f32[120,128]{1,0:T(8,128)S(1)}, u32[]{:S(2)}, u32[]{:S(2)}) collective-permute-start(f32[120,128]{1,0:T(8,128)S(1)} %pad_maximum_fusion.piece0), channel_id=1, source_target_pairs={{0,4},{4,0},{8,12},{12,8},{1,5},{5,1},{9,13},{13,9},{2,6},{6,2},{1... | collective-permute-start | bytes 184328 | tf_op jit(solution)/shard_map/ppermute | solution.py:1120
  10.3 1.8 %collective-permute-done.1.piece3 = f32[120,128]{1,0:T(8,128)S(1)} collective-permute-done((f32[120,128]{1,0:T(8,128)S(1)}, f32[120,128]{1,0:T(8,128)S(1)}, u32[]{:S(2)}, u32[]{:S(2)}) %collective-permute-start.1) | collective-permute-done | bytes 61472 | tf_op jit(solution)/shard_map/ppermute | solution.py:1120
  12.1 3.1 %collective-permute-done.2.piece2 = f32[120,128]{1,0:T(8,128)S(1)} collective-permute-done((f32[120,128]{1,0:T(8,128)S(1)}, f32[120,128]{1,0:T(8,128)S(1)}, u32[]{:S(2)}, u32[]{:S(2)}) %collective-permute-start.2) | collective-permute-done | bytes 61472 | tf_op jit(solution)/shard_map/ppermute | solution.py:1120
  15.2 0.0 collective-permute-done.3.piece1
  15.2 0.2 line.1.block0
  15.4 1.6 %collective-permute-start.4 = (f32[424,128]{1,0:T(8,128)S(1)}, f32[424,128]{1,0:T(8,128)S(1)}, u32[]{:S(2)}, u32[]{:S(2)}) collective-permute-start(f32[424,128]{1,0:T(8,128)S(1)} %line.1.block0), channel_id=1, source_target_pairs={{0,1},{1,0},{2,3},{3,2},{4,5},{5,4},{6,7},{7,6},{8,9},{9,8},{10,11... | collective-permute-start | bytes 651272 | tf_op jit(solution)/shard_map/ppermute | solution.py:1120
  17.0 1.5 %collective-permute-start.5 = (f32[424,128]{1,0:T(8,128)S(1)}, f32[424,128]{1,0:T(8,128)S(1)}, u32[]{:S(2)}, u32[]{:S(2)}) collective-permute-start(f32[424,128]{1,0:T(8,128)S(1)} %line.1.block0), channel_id=1, source_target_pairs={{0,2},{1,3},{2,0},{3,1},{4,6},{5,7},{6,4},{7,5},{8,10},{9,11},{10,... | collective-permute-start | bytes 651272 | tf_op jit(solution)/shard_map/ppermute | solution.py:1120
  18.5 0.5 %collective-permute-start.6 = (f32[424,128]{1,0:T(8,128)S(1)}, f32[424,128]{1,0:T(8,128)S(1)}, u32[]{:S(2)}, u32[]{:S(2)}) collective-permute-start(f32[424,128]{1,0:T(8,128)S(1)} %line.1.block0), channel_id=1, source_target_pairs={{0,3},{1,2},{2,1},{3,0},{4,7},{5,6},{6,5},{7,4},{8,11},{9,10},{10,... | collective-permute-start | bytes 651272 | tf_op jit(solution)/shard_map/ppermute | solution.py:1120
  19.0 4.7 %collective-permute-done.4.block1 = f32[424,128]{1,0:T(8,128)S(1)} collective-permute-done((f32[424,128]{1,0:T(8,128)S(1)}, f32[424,128]{1,0:T(8,128)S(1)}, u32[]{:S(2)}, u32[]{:S(2)}) %collective-permute-start.4) | collective-permute-done | bytes 217120 | tf_op jit(solution)/shard_map/ppermute | solution.py:1120
  23.7 4.8 %collective-permute-done.5.block2 = f32[424,128]{1,0:T(8,128)S(1)} collective-permute-done((f32[424,128]{1,0:T(8,128)S(1)}, f32[424,128]{1,0:T(8,128)S(1)}, u32[]{:S(2)}, u32[]{:S(2)}) %collective-permute-start.5) | collective-permute-done | bytes 217120 | tf_op jit(solution)/shard_map/ppermute | solution.py:1120
  28.5 0.0 collective-permute-done.6.block3
  28.5 0.1 collective-permute-start.7
  28.6 0.6 %assemble.1.field.assembled.own_start = f32[1024,128]{1,0:T(8,128)S(1)} custom-call(f32[424,128]{1,0:T(8,128)S(1)} %line.1.block0, f32[424,128]{1,0:T(8,128)S(1)} %collective-permute-done.4.block1, f32[424,128]{1,0:T(8,128)S(1)} %collective-permute-done.5.block2, f32[424,128]{1,0:T(8,128)S(1)} %collective-permute-done.6.block3), custom_call_target="tpu_custom_call" | custom-call | flops 4000000 | bytes 4000000 | tf_op jit(solution)/shard_map/assemble/pallas_call | solution.py:1061
  29.2 0.8 %collective-permute-done.7.other_halves = f32[256,128]{1,0:T(8,128)S(1)} collective-permute-done((f32[256,128]{1,0:T(8,128)S(1)}, f32[256,128]{1,0:T(8,128)S(1)}, u32[]{:S(2)}, u32[]{:S(2)}) %collective-permute-start.7) | collective-permute-done | bytes 131104 | tf_op jit(solution)/shard_map/ppermute | solution.py:1120
  29.9 0.1 collective-permute-start.8
  30.1 0.3 setup.1.coefs
  30.4 5.5 %cycle.1.own = f32[1128,128]{1,0:T(8,128)S(1)} custom-call(f32[2704,128]{1,0:T(8,128)S(1)} %setup.1.coefs, f32[1024,128]{1,0:T(8,128)S(1)} %assemble.1.field.assembled.own_start), custom_call_target="tpu_custom_call" | custom-call | flops 40000000 | bytes 30000000 | tf_op jit(solution)/shard_map/cycle/pallas_call | solution.py:1078
  35.9 0.0 copy-start
  35.9 0.0 collective-permute-done.8.other_start
  36.0 0.4 %collective-permute-start.9 = (f32[1128,128]{1,0:T(8,128)S(1)}, f32[1128,128]{1,0:T(8,128)S(1)}, u32[]{:S(2)}, u32[]{:S(2)}) collective-permute-start(f32[1128,128]{1,0:T(8,128)S(1)} %cycle.1.own), channel_id=1, source_target_pairs={{0,16},{16,0},{1,17},{17,1},{2,18},{18,2},{3,19},{19,3},{4,20},{20... | collective-permute-start | bytes 1732616 | tf_op jit(solution)/shard_map/ppermute | solution.py:1120
  36.4 0.8 %early.1 = (f32[16,128]{1,0:T(8,128)S(1)}, f32[192,160]{1,0:T(8,128)S(1)}) custom-call(f32[1128,128]{1,0:T(8,128)S(1)} %cycle.1.own, f32[1024,128]{1,0:T(8,128)S(1)} %assemble.1.field.assembled.own_start, f32[1024,128]{1,0:T(8,128)S(1)} %collective-permute-done.8.other_start), custom_call_target="tpu_custom_call" | custom-call | flops 4000000 | bytes 4000000 | tf_op jit(solution)/shard_map/early/pallas_call | solution.py:1091
  37.1 0.9 %collective-permute-done.9.other = f32[1128,128]{1,0:T(8,128)S(1)} collective-permute-done((f32[1128,128]{1,0:T(8,128)S(1)}, f32[1128,128]{1,0:T(8,128)S(1)}, u32[]{:S(2)}, u32[]{:S(2)}) %collective-permute-start.9) | collective-permute-done | bytes 577568 | tf_op jit(solution)/shard_map/ppermute | solution.py:1120
  38.0 0.0 copy-done
  38.0 1.5 %finish.1 = (f32[5,5,2,160]{3,2,1,0:T(2,128)}, f32[5,5,2,160]{3,2,1,0:T(2,128)}, f32[3]{0:T(128)}) custom-call(f32[1128,128]{1,0:T(8,128)S(1)} %cycle.1.own, f32[1128,128]{1,0:T(8,128)S(1)} %collective-permute-done.9.other, f32[1024,128]{1,0:T(8,128)S(1)} %assemble.1.field.assembled.own_start, f32[1024,128]{1,0:T(8,128)S(1)} %collective-permute-done.8.other_start, ...), custom_call_target="tpu_custom_call" | custom-call | tf_op jit(solution)/shard_map/finish/pallas_call | solution.py:1104
  (4 shorter events, 0.0 us)
Async XLA Ops:
  3.0 1.6 %collective-permute-start = (f32[104,128]{1,0:T(8,128)}, f32[104,128]{1,0:T(8,128)S(1)}, u32[]{:S(2)}, u32[]{:S(2)}) collective-permute-start(f32[104,128]{1,0:T(8,128)} %get-tuple-element.19), channel_id=1, source_target_pairs={{0,16},{16,0},{1,17},{17,1},{2,18},{18,2},{3,19},{19,3},{4,20},{20... | collective-permute-start | bytes 159752 | tf_op jit(solution)/shard_map/ppermute | solution.py:1120
  3.5 0.8 %copy-start.1 = (f32[120,128]{1,0:T(8,128)S(1)}, f32[120,128]{1,0:T(8,128)}, u32[]{:S(2)}) copy-start(f32[120,128]{1,0:T(8,128)} %get-tuple-element.20.source) | copy-start | bytes 184324
  4.6 7.5 %collective-permute-start.1 = (f32[120,128]{1,0:T(8,128)S(1)}, f32[120,128]{1,0:T(8,128)S(1)}, u32[]{:S(2)}, u32[]{:S(2)}) collective-permute-start(f32[120,128]{1,0:T(8,128)S(1)} %pad_maximum_fusion.piece0), channel_id=1, source_target_pairs={{0,12},{4,8},{8,4},{12,0},{1,13},{5,9},{9,5},{13,1},{2,14},{6,10},... | collective-permute-start | bytes 184328 | tf_op jit(solution)/shard_map/ppermute | solution.py:1120
  9.6 5.6 %collective-permute-start.2 = (f32[120,128]{1,0:T(8,128)S(1)}, f32[120,128]{1,0:T(8,128)S(1)}, u32[]{:S(2)}, u32[]{:S(2)}) collective-permute-start(f32[120,128]{1,0:T(8,128)S(1)} %pad_maximum_fusion.piece0), channel_id=1, source_target_pairs={{0,8},{4,12},{8,0},{12,4},{1,9},{5,13},{9,1},{13,5},{2,10},{6,14},... | collective-permute-start | bytes 184328 | tf_op jit(solution)/shard_map/ppermute | solution.py:1120
  9.6 5.6 %collective-permute-start.3 = (f32[120,128]{1,0:T(8,128)S(1)}, f32[120,128]{1,0:T(8,128)S(1)}, u32[]{:S(2)}, u32[]{:S(2)}) collective-permute-start(f32[120,128]{1,0:T(8,128)S(1)} %pad_maximum_fusion.piece0), channel_id=1, source_target_pairs={{0,4},{4,0},{8,12},{12,8},{1,5},{5,1},{9,13},{13,9},{2,6},{6,2},{1... | collective-permute-start | bytes 184328 | tf_op jit(solution)/shard_map/ppermute | solution.py:1120
  15.4 8.3 %collective-permute-start.4 = (f32[424,128]{1,0:T(8,128)S(1)}, f32[424,128]{1,0:T(8,128)S(1)}, u32[]{:S(2)}, u32[]{:S(2)}) collective-permute-start(f32[424,128]{1,0:T(8,128)S(1)} %line.1.block0), channel_id=1, source_target_pairs={{0,1},{1,0},{2,3},{3,2},{4,5},{5,4},{6,7},{7,6},{8,9},{9,8},{10,11... | collective-permute-start | bytes 651272 | tf_op jit(solution)/shard_map/ppermute | solution.py:1120
  17.0 11.5 %collective-permute-start.5 = (f32[424,128]{1,0:T(8,128)S(1)}, f32[424,128]{1,0:T(8,128)S(1)}, u32[]{:S(2)}, u32[]{:S(2)}) collective-permute-start(f32[424,128]{1,0:T(8,128)S(1)} %line.1.block0), channel_id=1, source_target_pairs={{0,2},{1,3},{2,0},{3,1},{4,6},{5,7},{6,4},{7,5},{8,10},{9,11},{10,... | collective-permute-start | bytes 651272 | tf_op jit(solution)/shard_map/ppermute | solution.py:1120
  18.5 10.0 %collective-permute-start.6 = (f32[424,128]{1,0:T(8,128)S(1)}, f32[424,128]{1,0:T(8,128)S(1)}, u32[]{:S(2)}, u32[]{:S(2)}) collective-permute-start(f32[424,128]{1,0:T(8,128)S(1)} %line.1.block0), channel_id=1, source_target_pairs={{0,3},{1,2},{2,1},{3,0},{4,7},{5,6},{6,5},{7,4},{8,11},{9,10},{10,... | collective-permute-start | bytes 651272 | tf_op jit(solution)/shard_map/ppermute | solution.py:1120
  28.5 1.4 %collective-permute-start.7 = (f32[256,128]{1,0:T(8,128)S(1)}, f32[256,128]{1,0:T(8,128)S(1)}, u32[]{:S(2)}, u32[]{:S(2)}) collective-permute-start(f32[256,128]{1,0:T(8,128)S(1)} %halves.1.own_halves), channel_id=1, source_target_pairs={{0,16},{16,0},{1,17},{17,1},{2,18},{18,2},{3,19},{19,3},{4,20},{20... | collective-permute-start | bytes 393224 | tf_op jit(solution)/shard_map/ppermute | solution.py:1120
  29.9 6.0 %collective-permute-start.8 = (f32[1024,128]{1,0:T(8,128)S(1)}, f32[1024,128]{1,0:T(8,128)S(1)}, u32[]{:S(2)}, u32[]{:S(2)}) collective-permute-start(f32[1024,128]{1,0:T(8,128)S(1)} %assemble.1.field.assembled.own_start), channel_id=1, source_target_pairs={{0,16},{16,0},{1,17},{17,1},{2,18},{18,2},{3,19},{19,3},{4,20},{20... | collective-permute-start | bytes 1572872 | tf_op jit(solution)/shard_map/ppermute | solution.py:1120
  35.9 2.1 %copy-start = (f32[2,5,5,160]{3,0,2,1:T(2,128)S(1)}, f32[2,5,5,160]{3,0,2,1:T(2,128)}, u32[]{:S(2)}) copy-start(f32[2,5,5,160]{3,0,2,1:T(2,128)} %param.6) | copy-start | bytes 96004
  36.0 2.1 %collective-permute-start.9 = (f32[1128,128]{1,0:T(8,128)S(1)}, f32[1128,128]{1,0:T(8,128)S(1)}, u32[]{:S(2)}, u32[]{:S(2)}) collective-permute-start(f32[1128,128]{1,0:T(8,128)S(1)} %cycle.1.own), channel_id=1, source_target_pairs={{0,16},{16,0},{1,17},{17,1},{2,18},{18,2},{3,19},{19,3},{4,20},{20... | collective-permute-start | bytes 1732616 | tf_op jit(solution)/shard_map/ppermute | solution.py:1120

commit v13 on v12

--- a/solution.py
+++ b/solution.py
@@ -818,7 +818,7 @@
             store(level.res, first, f)
             store(level.x, first, jnp.zeros_like(f))
 
-    def apply(level, smooth, always):
+    def apply(level, smooth):
         n = level.count
         kx, ky, kz = level.tables
         gains = level.gains
@@ -829,11 +829,11 @@
                 terms = pairs + terms[len(terms) // 2 * 2 :]
             return terms[0]
 
-        def plane(k):
+        def sums(k):
             def line_at(i):
                 return load(source, (k * n + i) * n, n)
 
-            lines, totals = [], []
+            totals = []
             for i in range(n):
                 first = (k * n + i) * n
                 v = line_at(i)
@@ -855,12 +855,14 @@
                     if j == n - 1:
                         terms.append(gains[3] * lanes.y_after(v[0]))
                     along_y.append(tree(terms))
-                lines.append(v)
                 totals.append(tree([level.diag(first, n) * v, tree(along_x), tree(along_z), jnp.stack(along_y)]))
+            return totals
+
+        def update(k, totals):
             moved = [pltpu.roll(total, 64, 2) for total in totals]
             for i in range(n):
                 first = (k * n + i) * n
-                v = lines[i]
+                v = load(source, first, n)
                 image = v + (same * totals[i] + swap * moved[i])
                 if smooth:
                     scaled = level.jac(first, n) * (load(level.res, first, n) - image)
@@ -870,10 +872,12 @@
                     store(level.res, first, rest)
                     store(level.dir, first, level.jac(first, n) * rest)
 
-        for k in range(n):
-            @pl.when(always)
-            def _(k=k):
-                plane(k)
+        if n == 5:
+            for k in range(n):
+                update(k, sums(k))
+        else:
+            for k, totals in enumerate([sums(k) for k in range(n)]):
+                update(k, totals)
 
     def combine(weights, parts):
         total = None
@@ -906,28 +910,28 @@
     def up(m, n):
         return lagrange_table(lobatto(m)[0], lobatto(n)[0])
 
-    def solve(p, always=None):
+    def solve(p):
         level = levels[p]
         if p == 2:
-            apply(level, True, always)
+            apply(level, True)
             return
         below = levels[p + 1]
 
         def step(t, carry):
             @pl.when(t != 1)
             def _():
-                apply(level, True, t >= 0)
+                apply(level, True)
 
             @pl.when((t != 2) | (p == 0))
             def _():
-                apply(level, False, t >= 0)
+                apply(level, False)
 
             @pl.when(t == 0)
             def _():
                 n, m = level.count, below.count
                 change(down(n, m), level.res, below.f, False)
                 begin(below, below.f)
-                solve(p + 1, t >= 0)
+                solve(p + 1)
                 change(up(m, n), below.x, level.x, True)
             return carry
         lax.fori_loop(0, 3, step, 0)

time: 39.7 us -> 39.6 us (level)
  no operation moved by 1% of the time
where the time goes in v13:
time: 39.6 us; the launch traced here: 39.4 us
  waiting for transfers between devices  16.4 us (41%)
  Pallas kernels  11.1 us (28%)
  starting transfers between devices  10.4 us (26%)
  local copies, waits for them, and re-layouts  0.83 us (2%)
  between operations  0.71 us (2%)
    ppermute x10, waiting for transfers between devices, exchange(): lax.ppermute(x, axis, [(n, n ^ bits) for n in range(lax.axis_size(axis))])  16.4 us
    ppermute x10, starting transfers between devices, exchange(): lax.ppermute(x, axis, [(n, n ^ bits) for n in range(lax.axis_size(axis))])  10.4 us
    pallas_call x1, Pallas kernels, cycle(): pl.pallas_call(cycle_kernel, out_shape=jax.ShapeDtypeStruct((FIELD + 128,...  5.45 us
    pallas_call x1, Pallas kernels, local_part(): pl.pallas_call(local_kernel, out_shape=[jax.ShapeDtypeStruct((rows, 128),...  2.34 us
    pallas_call x1, Pallas kernels, finish(): pl.pallas_call(finish_kernel, out_shape=[jax.ShapeDtypeStruct(guess.shape...  1.47 us
    pallas_call x4, Pallas kernels, plain_call(): pl.pallas_call(kernel, out_shape=jax.ShapeDtypeStruct((rows, 128), F32),...  1.08 us
    unnamed x4, local copies, waits for them, and re-layouts  0.83 us
  transfers between devices with their start and end apart: 10, of which 7 were waited for; matrix products, arithmetic and copies ran while one was open for 0% of the time, Pallas kernels for 18%

profile of v13, /device:TPU:0, one launch (start us, length us, event | category | flops | bytes accessed | tf_op | source)
XLA Modules:
  0.0 39.4 jit_solution(13464918232478875260)
XLA Ops:
  0.6 2.3 %local_part.1 = (f32[120,128]{1,0:T(8,128)}, f32[104,128]{1,0:T(8,128)}) custom-call(f32[5,5,2,160]{3,2,1,0:T(2,128)} %bitcast.6, f32[5,5,2,160]{3,2,1,0:T(2,128)} %bitcast.4, f32[5,5,160]{2,1,0:T(8,128)} %kappa_in.1, s32[6,1,1,32]{3,2,1,0:T(1,128)} %flags_in.1, f32[64,64]{1,0:T(8,128)} %constant.2.clone.rows_in), custom_call_target="tpu_custom_call" | custom-call | flops 20000000 | bytes 8000000 | tf_op jit(solution)/shard_map/local_part/pallas_call | solution.py:560
  3.0 0.5 %collective-permute-start = (f32[104,128]{1,0:T(8,128)}, f32[104,128]{1,0:T(8,128)S(1)}, u32[]{:S(2)}, u32[]{:S(2)}) collective-permute-start(f32[104,128]{1,0:T(8,128)} %get-tuple-element.19), channel_id=1, source_target_pairs={{0,16},{16,0},{1,17},{17,1},{2,18},{18,2},{3,19},{19,3},{4,20},{20... | collective-permute-start | bytes 159752 | tf_op jit(solution)/shard_map/ppermute | solution.py:1124
  3.5 0.0 copy-start.1
  3.5 0.8 %copy-done.1 = f32[120,128]{1,0:T(8,128)S(1)} copy-done((f32[120,128]{1,0:T(8,128)S(1)}, f32[120,128]{1,0:T(8,128)}, u32[]{:S(2)}) %copy-start.1) | copy-done | bytes 61464
  4.3 0.3 collective-permute-done
  4.6 5.0 %collective-permute-start.1 = (f32[120,128]{1,0:T(8,128)S(1)}, f32[120,128]{1,0:T(8,128)S(1)}, u32[]{:S(2)}, u32[]{:S(2)}) collective-permute-start(f32[120,128]{1,0:T(8,128)S(1)} %pad_maximum_fusion.piece0), channel_id=1, source_target_pairs={{0,12},{4,8},{8,4},{12,0},{1,13},{5,9},{9,5},{13,1},{2,14},{6,10},... | collective-permute-start | bytes 184328 | tf_op jit(solution)/shard_map/ppermute | solution.py:1124
  9.6 0.0 collective-permute-start.2
  9.6 0.6 %collective-permute-start.3 = (f32[120,128]{1,0:T(8,128)S(1)}, f32[120,128]{1,0:T(8,128)S(1)}, u32[]{:S(2)}, u32[]{:S(2)}) collective-permute-start(f32[120,128]{1,0:T(8,128)S(1)} %pad_maximum_fusion.piece0), channel_id=1, source_target_pairs={{0,4},{4,0},{8,12},{12,8},{1,5},{5,1},{9,13},{13,9},{2,6},{6,2},{1... | collective-permute-start | bytes 184328 | tf_op jit(solution)/shard_map/ppermute | solution.py:1124
  10.3 1.8 %collective-permute-done.1.piece3 = f32[120,128]{1,0:T(8,128)S(1)} collective-permute-done((f32[120,128]{1,0:T(8,128)S(1)}, f32[120,128]{1,0:T(8,128)S(1)}, u32[]{:S(2)}, u32[]{:S(2)}) %collective-permute-start.1) | collective-permute-done | bytes 61472 | tf_op jit(solution)/shard_map/ppermute | solution.py:1124
  12.1 3.1 %collective-permute-done.2.piece2 = f32[120,128]{1,0:T(8,128)S(1)} collective-permute-done((f32[120,128]{1,0:T(8,128)S(1)}, f32[120,128]{1,0:T(8,128)S(1)}, u32[]{:S(2)}, u32[]{:S(2)}) %collective-permute-start.2) | collective-permute-done | bytes 61472 | tf_op jit(solution)/shard_map/ppermute | solution.py:1124
  15.2 0.0 collective-permute-done.3.piece1
  15.2 0.2 line.1.block0
  15.4 1.6 %collective-permute-start.4 = (f32[424,128]{1,0:T(8,128)S(1)}, f32[424,128]{1,0:T(8,128)S(1)}, u32[]{:S(2)}, u32[]{:S(2)}) collective-permute-start(f32[424,128]{1,0:T(8,128)S(1)} %line.1.block0), channel_id=1, source_target_pairs={{0,1},{1,0},{2,3},{3,2},{4,5},{5,4},{6,7},{7,6},{8,9},{9,8},{10,11... | collective-permute-start | bytes 651272 | tf_op jit(solution)/shard_map/ppermute | solution.py:1124
  17.0 1.5 %collective-permute-start.5 = (f32[424,128]{1,0:T(8,128)S(1)}, f32[424,128]{1,0:T(8,128)S(1)}, u32[]{:S(2)}, u32[]{:S(2)}) collective-permute-start(f32[424,128]{1,0:T(8,128)S(1)} %line.1.block0), channel_id=1, source_target_pairs={{0,2},{1,3},{2,0},{3,1},{4,6},{5,7},{6,4},{7,5},{8,10},{9,11},{10,... | collective-permute-start | bytes 651272 | tf_op jit(solution)/shard_map/ppermute | solution.py:1124
  18.5 0.5 %collective-permute-start.6 = (f32[424,128]{1,0:T(8,128)S(1)}, f32[424,128]{1,0:T(8,128)S(1)}, u32[]{:S(2)}, u32[]{:S(2)}) collective-permute-start(f32[424,128]{1,0:T(8,128)S(1)} %line.1.block0), channel_id=1, source_target_pairs={{0,3},{1,2},{2,1},{3,0},{4,7},{5,6},{6,5},{7,4},{8,11},{9,10},{10,... | collective-permute-start | bytes 651272 | tf_op jit(solution)/shard_map/ppermute | solution.py:1124
  19.0 4.7 %collective-permute-done.4.block1 = f32[424,128]{1,0:T(8,128)S(1)} collective-permute-done((f32[424,128]{1,0:T(8,128)S(1)}, f32[424,128]{1,0:T(8,128)S(1)}, u32[]{:S(2)}, u32[]{:S(2)}) %collective-permute-start.4) | collective-permute-done | bytes 217120 | tf_op jit(solution)/shard_map/ppermute | solution.py:1124
  23.7 4.8 %collective-permute-done.5.block2 = f32[424,128]{1,0:T(8,128)S(1)} collective-permute-done((f32[424,128]{1,0:T(8,128)S(1)}, f32[424,128]{1,0:T(8,128)S(1)}, u32[]{:S(2)}, u32[]{:S(2)}) %collective-permute-start.5) | collective-permute-done | bytes 217120 | tf_op jit(solution)/shard_map/ppermute | solution.py:1124
  28.5 0.0 collective-permute-done.6.block3
  28.5 0.1 collective-permute-start.7
  28.6 0.6 %assemble.1.field.assembled.own_start = f32[1024,128]{1,0:T(8,128)S(1)} custom-call(f32[424,128]{1,0:T(8,128)S(1)} %line.1.block0, f32[424,128]{1,0:T(8,128)S(1)} %collective-permute-done.4.block1, f32[424,128]{1,0:T(8,128)S(1)} %collective-permute-done.5.block2, f32[424,128]{1,0:T(8,128)S(1)} %collective-permute-done.6.block3), custom_call_target="tpu_custom_call" | custom-call | flops 4000000 | bytes 4000000 | tf_op jit(solution)/shard_map/assemble/pallas_call | solution.py:1065
  29.2 0.8 %collective-permute-done.7.other_halves = f32[256,128]{1,0:T(8,128)S(1)} collective-permute-done((f32[256,128]{1,0:T(8,128)S(1)}, f32[256,128]{1,0:T(8,128)S(1)}, u32[]{:S(2)}, u32[]{:S(2)}) %collective-permute-start.7) | collective-permute-done | bytes 131104 | tf_op jit(solution)/shard_map/ppermute | solution.py:1124
  29.9 0.1 collective-permute-start.8
  30.1 0.3 setup.1.coefs
  30.4 5.5 %cycle.1.own = f32[1128,128]{1,0:T(8,128)S(1)} custom-call(f32[2704,128]{1,0:T(8,128)S(1)} %setup.1.coefs, f32[1024,128]{1,0:T(8,128)S(1)} %assemble.1.field.assembled.own_start), custom_call_target="tpu_custom_call" | custom-call | flops 40000000 | bytes 30000000 | tf_op jit(solution)/shard_map/cycle/pallas_call | solution.py:1082
  35.9 0.0 copy-start
  35.9 0.0 collective-permute-done.8.other_start
  35.9 0.4 %collective-permute-start.9 = (f32[1128,128]{1,0:T(8,128)S(1)}, f32[1128,128]{1,0:T(8,128)S(1)}, u32[]{:S(2)}, u32[]{:S(2)}) collective-permute-start(f32[1128,128]{1,0:T(8,128)S(1)} %cycle.1.own), channel_id=1, source_target_pairs={{0,16},{16,0},{1,17},{17,1},{2,18},{18,2},{3,19},{19,3},{4,20},{20... | collective-permute-start | bytes 1732616 | tf_op jit(solution)/shard_map/ppermute | solution.py:1124
  36.3 0.8 %early.1 = (f32[16,128]{1,0:T(8,128)S(1)}, f32[192,160]{1,0:T(8,128)S(1)}) custom-call(f32[1128,128]{1,0:T(8,128)S(1)} %cycle.1.own, f32[1024,128]{1,0:T(8,128)S(1)} %assemble.1.field.assembled.own_start, f32[1024,128]{1,0:T(8,128)S(1)} %collective-permute-done.8.other_start), custom_call_target="tpu_custom_call" | custom-call | flops 4000000 | bytes 4000000 | tf_op jit(solution)/shard_map/early/pallas_call | solution.py:1095
  37.1 0.9 %collective-permute-done.9.other = f32[1128,128]{1,0:T(8,128)S(1)} collective-permute-done((f32[1128,128]{1,0:T(8,128)S(1)}, f32[1128,128]{1,0:T(8,128)S(1)}, u32[]{:S(2)}, u32[]{:S(2)}) %collective-permute-start.9) | collective-permute-done | bytes 577568 | tf_op jit(solution)/shard_map/ppermute | solution.py:1124
  37.9 0.0 copy-done
  37.9 1.5 %finish.1 = (f32[5,5,2,160]{3,2,1,0:T(2,128)}, f32[5,5,2,160]{3,2,1,0:T(2,128)}, f32[3]{0:T(128)}) custom-call(f32[1128,128]{1,0:T(8,128)S(1)} %cycle.1.own, f32[1128,128]{1,0:T(8,128)S(1)} %collective-permute-done.9.other, f32[1024,128]{1,0:T(8,128)S(1)} %assemble.1.field.assembled.own_start, f32[1024,128]{1,0:T(8,128)S(1)} %collective-permute-done.8.other_start, ...), custom_call_target="tpu_custom_call" | custom-call | tf_op jit(solution)/shard_map/finish/pallas_call | solution.py:1108
  (4 shorter events, 0.0 us)
Async XLA Ops:
  3.0 1.6 %collective-permute-start = (f32[104,128]{1,0:T(8,128)}, f32[104,128]{1,0:T(8,128)S(1)}, u32[]{:S(2)}, u32[]{:S(2)}) collective-permute-start(f32[104,128]{1,0:T(8,128)} %get-tuple-element.19), channel_id=1, source_target_pairs={{0,16},{16,0},{1,17},{17,1},{2,18},{18,2},{3,19},{19,3},{4,20},{20... | collective-permute-start | bytes 159752 | tf_op jit(solution)/shard_map/ppermute | solution.py:1124
  3.5 0.8 %copy-start.1 = (f32[120,128]{1,0:T(8,128)S(1)}, f32[120,128]{1,0:T(8,128)}, u32[]{:S(2)}) copy-start(f32[120,128]{1,0:T(8,128)} %get-tuple-element.20.source) | copy-start | bytes 184324
  4.6 7.5 %collective-permute-start.1 = (f32[120,128]{1,0:T(8,128)S(1)}, f32[120,128]{1,0:T(8,128)S(1)}, u32[]{:S(2)}, u32[]{:S(2)}) collective-permute-start(f32[120,128]{1,0:T(8,128)S(1)} %pad_maximum_fusion.piece0), channel_id=1, source_target_pairs={{0,12},{4,8},{8,4},{12,0},{1,13},{5,9},{9,5},{13,1},{2,14},{6,10},... | collective-permute-start | bytes 184328 | tf_op jit(solution)/shard_map/ppermute | solution.py:1124
  9.6 5.6 %collective-permute-start.2 = (f32[120,128]{1,0:T(8,128)S(1)}, f32[120,128]{1,0:T(8,128)S(1)}, u32[]{:S(2)}, u32[]{:S(2)}) collective-permute-start(f32[120,128]{1,0:T(8,128)S(1)} %pad_maximum_fusion.piece0), channel_id=1, source_target_pairs={{0,8},{4,12},{8,0},{12,4},{1,9},{5,13},{9,1},{13,5},{2,10},{6,14},... | collective-permute-start | bytes 184328 | tf_op jit(solution)/shard_map/ppermute | solution.py:1124
  9.6 5.6 %collective-permute-start.3 = (f32[120,128]{1,0:T(8,128)S(1)}, f32[120,128]{1,0:T(8,128)S(1)}, u32[]{:S(2)}, u32[]{:S(2)}) collective-permute-start(f32[120,128]{1,0:T(8,128)S(1)} %pad_maximum_fusion.piece0), channel_id=1, source_target_pairs={{0,4},{4,0},{8,12},{12,8},{1,5},{5,1},{9,13},{13,9},{2,6},{6,2},{1... | collective-permute-start | bytes 184328 | tf_op jit(solution)/shard_map/ppermute | solution.py:1124
  15.4 8.3 %collective-permute-start.4 = (f32[424,128]{1,0:T(8,128)S(1)}, f32[424,128]{1,0:T(8,128)S(1)}, u32[]{:S(2)}, u32[]{:S(2)}) collective-permute-start(f32[424,128]{1,0:T(8,128)S(1)} %line.1.block0), channel_id=1, source_target_pairs={{0,1},{1,0},{2,3},{3,2},{4,5},{5,4},{6,7},{7,6},{8,9},{9,8},{10,11... | collective-permute-start | bytes 651272 | tf_op jit(solution)/shard_map/ppermute | solution.py:1124
  17.0 11.5 %collective-permute-start.5 = (f32[424,128]{1,0:T(8,128)S(1)}, f32[424,128]{1,0:T(8,128)S(1)}, u32[]{:S(2)}, u32[]{:S(2)}) collective-permute-start(f32[424,128]{1,0:T(8,128)S(1)} %line.1.block0), channel_id=1, source_target_pairs={{0,2},{1,3},{2,0},{3,1},{4,6},{5,7},{6,4},{7,5},{8,10},{9,11},{10,... | collective-permute-start | bytes 651272 | tf_op jit(solution)/shard_map/ppermute | solution.py:1124
  18.5 10.0 %collective-permute-start.6 = (f32[424,128]{1,0:T(8,128)S(1)}, f32[424,128]{1,0:T(8,128)S(1)}, u32[]{:S(2)}, u32[]{:S(2)}) collective-permute-start(f32[424,128]{1,0:T(8,128)S(1)} %line.1.block0), channel_id=1, source_target_pairs={{0,3},{1,2},{2,1},{3,0},{4,7},{5,6},{6,5},{7,4},{8,11},{9,10},{10,... | collective-permute-start | bytes 651272 | tf_op jit(solution)/shard_map/ppermute | solution.py:1124
  28.5 1.4 %collective-permute-start.7 = (f32[256,128]{1,0:T(8,128)S(1)}, f32[256,128]{1,0:T(8,128)S(1)}, u32[]{:S(2)}, u32[]{:S(2)}) collective-permute-start(f32[256,128]{1,0:T(8,128)S(1)} %halves.1.own_halves), channel_id=1, source_target_pairs={{0,16},{16,0},{1,17},{17,1},{2,18},{18,2},{3,19},{19,3},{4,20},{20... | collective-permute-start | bytes 393224 | tf_op jit(solution)/shard_map/ppermute | solution.py:1124
  29.9 5.9 %collective-permute-start.8 = (f32[1024,128]{1,0:T(8,128)S(1)}, f32[1024,128]{1,0:T(8,128)S(1)}, u32[]{:S(2)}, u32[]{:S(2)}) collective-permute-start(f32[1024,128]{1,0:T(8,128)S(1)} %assemble.1.field.assembled.own_start), channel_id=1, source_target_pairs={{0,16},{16,0},{1,17},{17,1},{2,18},{18,2},{3,19},{19,3},{4,20},{20... | collective-permute-start | bytes 1572872 | tf_op jit(solution)/shard_map/ppermute | solution.py:1124
  35.9 2.1 %copy-start = (f32[2,5,5,160]{3,0,2,1:T(2,128)S(1)}, f32[2,5,5,160]{3,0,2,1:T(2,128)}, u32[]{:S(2)}) copy-start(f32[2,5,5,160]{3,0,2,1:T(2,128)} %param.6) | copy-start | bytes 96004
  35.9 2.1 %collective-permute-start.9 = (f32[1128,128]{1,0:T(8,128)S(1)}, f32[1128,128]{1,0:T(8,128)S(1)}, u32[]{:S(2)}, u32[]{:S(2)}) collective-permute-start(f32[1128,128]{1,0:T(8,128)S(1)} %cycle.1.own), channel_id=1, source_target_pairs={{0,16},{16,0},{1,17},{17,1},{2,18},{18,2},{3,19},{19,3},{4,20},{20... | collective-permute-start | bytes 1732616 | tf_op jit(solution)/shard_map/ppermute | solution.py:1124

commit v14 on v13

--- a/solution.py
+++ b/solution.py
@@ -604,11 +604,20 @@
     return pieces[pl.ds(8 * h * size + r, 8, stride=size), :]
 
 
+ORDER_X = ((3, 2), (2, 3), (1, 1))
+ORDER_Y = ((1, 2), (2, 1), (3, 3))
+
+
+def partner(bits):
+    return jnp.where(lax.axis_index("section") == 0, bits[0], bits[1])
+
+
 def place_pieces(blocks, pieces, first, size, room):
     my_gx, my_gy = lax.axis_index("gx"), lax.axis_index("gy")
     for b, block in enumerate(blocks):
+        gy = my_gy ^ partner(ORDER_Y[b - 1]) if b else my_gy
         for a in range(4):
-            column = (my_gx ^ a) * 4 + (my_gy ^ b)
+            column = (my_gx ^ a) * 4 + gy
             start = pl.multiple_of(column * room, 8)
             pieces[pl.ds(start, size), :] = block[first + a * size : first + a * size + size, :]
 
@@ -670,8 +679,11 @@
     return choose(iota(row.shape, 1) // EZ, [turned[(g - 2 * slot - 1) % 4] for g in range(4)])
 
 
-def line_kernel(piece3, piece2, piece1, piece0, line, faces):
-    pieces = (piece0, piece1, piece2, piece3)
+def line_kernel(first, second, third, own, line, faces, sorted_pieces):
+    sorted_pieces[:PIECE, :] = own[...]
+    for bits, piece in zip(ORDER_X, (first, second, third)):
+        sorted_pieces[pl.ds(pl.multiple_of(partner(bits) * PIECE, 8), PIECE), :] = piece[...]
+    pieces = [sorted_pieces.at[PIECE * a : PIECE * a + PIECE, :] for a in range(4)]
     even = lax.axis_index("gx") % 2 == 0
     odd = iota((8, 128), 1) // EZ % 2 == 1
     faces[...] = jnp.zeros_like(faces)
@@ -1124,14 +1136,20 @@
     return lax.ppermute(x, axis, [(n, n ^ bits) for n in range(lax.axis_size(axis))])
 
 
+def exchange_by_core(x, axis, bits):
+    count = lax.axis_size(axis)
+    pairs = [(s * count + n, s * count + (n ^ bits[s])) for s in range(2) for n in range(count)]
+    return lax.ppermute(x, ("section", axis), pairs)
+
+
 def gathered_body(rhs, guess, kappa, bc_flags):
     rhs, guess = (jnp.transpose(v, (1, 2, 0, 3)) for v in (rhs, guess))
     mine, theirs = local_part(rhs, guess, kappa, bc_flags)
     got, mine, kappa_piece = lax.optimization_barrier((exchange(theirs, "section", 1), *part(mine)))
     piece = jnp.concatenate([mine + got, kappa_piece])
-    pieces = [piece] + [exchange(piece, "gx", bits) for bits in (1, 2, 3)]
-    line = plain_call(line_kernel, "line", LINE, [4 * 64], pieces[::-1])
-    blocks = [line] + [exchange(line, "gy", bits) for bits in (1, 2, 3)]
+    pieces = [exchange_by_core(piece, "gx", bits) for bits in ORDER_X] + [piece]
+    line = plain_call(line_kernel, "line", LINE, [4 * 64, 4 * PIECE], pieces)
+    blocks = [line] + [exchange_by_core(line, "gy", bits) for bits in ORDER_Y]
     halves = plain_call(halves_kernel, "halves", COLS * 16, [], blocks)
     other_halves = exchange(halves, "section", 1)
     start = plain_call(assemble_kernel, "assemble", 128 * 8, [COLS * HALF, COLS * 32, 50 * 8], blocks, 4_000_000)

time: 39.6 us -> 38.6 us (0.975)
  waiting for transfers between devices: 16.4 us -> 15.4 us
    ppermute x10 -> x4, waiting for transfers between devices: 16.4 us -> 1.89 us  [exchange(): lax.ppermute(x, axis, [(n, n ^ bits) for n in range(lax.axis_size(axis))])]
    ppermute x0 -> x6, waiting for transfers between devices: none -> 13.5 us  [exchange_by_core(): return lax.ppermute(x, ('section', axis), pairs)]
    ppermute x10 -> x4, starting transfers between devices: 10.4 us -> 1.17 us  [exchange(): lax.ppermute(x, axis, [(n, n ^ bits) for n in range(lax.axis_size(axis))])]
    ppermute x0 -> x6, starting transfers between devices: none -> 9.21 us  [exchange_by_core(): return lax.ppermute(x, ('section', axis), pairs)]
where the time goes in v14:
time: 38.6 us; the launch traced here: 38.4 us
  waiting for transfers between devices  15.4 us (40%)
  Pallas kernels  11.1 us (29%)
  starting transfers between devices  10.4 us (27%)
  local copies, waits for them, and re-layouts  0.83 us (2%)
  between operations  0.71 us (2%)
    ppermute x6, waiting for transfers between devices, exchange_by_core(): return lax.ppermute(x, ('section', axis), pairs)  13.5 us
    ppermute x6, starting transfers between devices, exchange_by_core(): return lax.ppermute(x, ('section', axis), pairs)  9.21 us
    pallas_call x1, Pallas kernels, cycle(): pl.pallas_call(cycle_kernel, out_shape=jax.ShapeDtypeStruct((FIELD + 128,...  5.45 us
    pallas_call x1, Pallas kernels, local_part(): pl.pallas_call(local_kernel, out_shape=[jax.ShapeDtypeStruct((rows, 128),...  2.34 us
    ppermute x4, waiting for transfers between devices, exchange(): lax.ppermute(x, axis, [(n, n ^ bits) for n in range(lax.axis_size(axis))])  1.89 us
    pallas_call x1, Pallas kernels, finish(): pl.pallas_call(finish_kernel, out_shape=[jax.ShapeDtypeStruct(guess.shape...  1.47 us
    ppermute x4, starting transfers between devices, exchange(): lax.ppermute(x, axis, [(n, n ^ bits) for n in range(lax.axis_size(axis))])  1.17 us
    pallas_call x4, Pallas kernels, plain_call(): pl.pallas_call(kernel, out_shape=jax.ShapeDtypeStruct((rows, 128), F32),...  1.08 us
  transfers between devices with their start and end apart: 10, of which 7 were waited for; matrix products, arithmetic and copies ran while one was open for 0% of the time, Pallas kernels for 18%

profile of v14, /device:TPU:0, one launch (start us, length us, event | category | flops | bytes accessed | tf_op | source)
XLA Modules:
  0.0 38.4 jit_solution(17991671467588262990)
XLA Ops:
  0.6 2.3 %local_part.1 = (f32[120,128]{1,0:T(8,128)}, f32[104,128]{1,0:T(8,128)}) custom-call(f32[5,5,2,160]{3,2,1,0:T(2,128)} %bitcast.6, f32[5,5,2,160]{3,2,1,0:T(2,128)} %bitcast.4, f32[5,5,160]{2,1,0:T(8,128)} %kappa_in.1, s32[6,1,1,32]{3,2,1,0:T(1,128)} %flags_in.1, f32[64,64]{1,0:T(8,128)} %constant.2.clone.rows_in), custom_call_target="tpu_custom_call" | custom-call | flops 20000000 | bytes 8000000 | tf_op jit(solution)/shard_map/local_part/pallas_call | solution.py:560
  3.0 0.5 %collective-permute-start = (f32[104,128]{1,0:T(8,128)}, f32[104,128]{1,0:T(8,128)S(1)}, u32[]{:S(2)}, u32[]{:S(2)}) collective-permute-start(f32[104,128]{1,0:T(8,128)} %get-tuple-element.19), channel_id=1, source_target_pairs={{0,16},{16,0},{1,17},{17,1},{2,18},{18,2},{3,19},{19,3},{4,20},{20... | collective-permute-start | bytes 159752 | tf_op jit(solution)/shard_map/ppermute | solution.py:1136
  3.5 0.0 copy-start.1
  3.5 0.8 %copy-done.1 = f32[120,128]{1,0:T(8,128)S(1)} copy-done((f32[120,128]{1,0:T(8,128)S(1)}, f32[120,128]{1,0:T(8,128)}, u32[]{:S(2)}) %copy-start.1) | copy-done | bytes 61464
  4.3 0.3 collective-permute-done
  4.6 5.0 %collective-permute-start.1 = (f32[120,128]{1,0:T(8,128)S(1)}, f32[120,128]{1,0:T(8,128)S(1)}, u32[]{:S(2)}, u32[]{:S(2)}) collective-permute-start(f32[120,128]{1,0:T(8,128)S(1)} %pad_maximum_fusion.own), channel_id=1, source_target_pairs={{0,12},{4,8},{8,4},{12,0},{16,24},{20,28},{24,16},{28,20},{1,13},{... | collective-permute-start | bytes 184328 | tf_op jit(solution)/shard_map/ppermute | solution.py:1142
  9.6 0.0 collective-permute-start.2
  9.6 0.6 %collective-permute-start.3 = (f32[120,128]{1,0:T(8,128)S(1)}, f32[120,128]{1,0:T(8,128)S(1)}, u32[]{:S(2)}, u32[]{:S(2)}) collective-permute-start(f32[120,128]{1,0:T(8,128)S(1)} %pad_maximum_fusion.own), channel_id=1, source_target_pairs={{0,4},{4,0},{8,12},{12,8},{16,20},{20,16},{24,28},{28,24},{1,5},{5... | collective-permute-start | bytes 184328 | tf_op jit(solution)/shard_map/ppermute | solution.py:1142
  10.3 1.8 %collective-permute-done.1.first = f32[120,128]{1,0:T(8,128)S(1)} collective-permute-done((f32[120,128]{1,0:T(8,128)S(1)}, f32[120,128]{1,0:T(8,128)S(1)}, u32[]{:S(2)}, u32[]{:S(2)}) %collective-permute-start.1) | collective-permute-done | bytes 61472 | tf_op jit(solution)/shard_map/ppermute | solution.py:1142
  12.1 3.1 %collective-permute-done.2.second = f32[120,128]{1,0:T(8,128)S(1)} collective-permute-done((f32[120,128]{1,0:T(8,128)S(1)}, f32[120,128]{1,0:T(8,128)S(1)}, u32[]{:S(2)}, u32[]{:S(2)}) %collective-permute-start.2) | collective-permute-done | bytes 61472 | tf_op jit(solution)/shard_map/ppermute | solution.py:1142
  15.2 0.0 collective-permute-done.3.third
  15.2 0.2 line.1.block0
  15.4 1.6 %collective-permute-start.4 = (f32[424,128]{1,0:T(8,128)S(1)}, f32[424,128]{1,0:T(8,128)S(1)}, u32[]{:S(2)}, u32[]{:S(2)}) collective-permute-start(f32[424,128]{1,0:T(8,128)S(1)} %line.1.block0), channel_id=1, source_target_pairs={{0,1},{1,0},{2,3},{3,2},{16,18},{17,19},{18,16},{19,17},{4,5},{5,4... | collective-permute-start | bytes 651272 | tf_op jit(solution)/shard_map/ppermute | solution.py:1142
  17.0 1.5 %collective-permute-start.5 = (f32[424,128]{1,0:T(8,128)S(1)}, f32[424,128]{1,0:T(8,128)S(1)}, u32[]{:S(2)}, u32[]{:S(2)}) collective-permute-start(f32[424,128]{1,0:T(8,128)S(1)} %line.1.block0), channel_id=1, source_target_pairs={{0,2},{1,3},{2,0},{3,1},{16,17},{17,16},{18,19},{19,18},{4,6},{5,7... | collective-permute-start | bytes 651272 | tf_op jit(solution)/shard_map/ppermute | solution.py:1142
  18.5 0.5 %collective-permute-start.6 = (f32[424,128]{1,0:T(8,128)S(1)}, f32[424,128]{1,0:T(8,128)S(1)}, u32[]{:S(2)}, u32[]{:S(2)}) collective-permute-start(f32[424,128]{1,0:T(8,128)S(1)} %line.1.block0), channel_id=1, source_target_pairs={{0,3},{1,2},{2,1},{3,0},{16,19},{17,18},{18,17},{19,16},{4,7},{5,6... | collective-permute-start | bytes 651272 | tf_op jit(solution)/shard_map/ppermute | solution.py:1142
  19.0 4.7 %collective-permute-done.4.block1 = f32[424,128]{1,0:T(8,128)S(1)} collective-permute-done((f32[424,128]{1,0:T(8,128)S(1)}, f32[424,128]{1,0:T(8,128)S(1)}, u32[]{:S(2)}, u32[]{:S(2)}) %collective-permute-start.4) | collective-permute-done | bytes 217120 | tf_op jit(solution)/shard_map/ppermute | solution.py:1142
  23.7 3.8 %collective-permute-done.5.block2 = f32[424,128]{1,0:T(8,128)S(1)} collective-permute-done((f32[424,128]{1,0:T(8,128)S(1)}, f32[424,128]{1,0:T(8,128)S(1)}, u32[]{:S(2)}, u32[]{:S(2)}) %collective-permute-start.5) | collective-permute-done | bytes 217120 | tf_op jit(solution)/shard_map/ppermute | solution.py:1142
  27.5 0.0 collective-permute-done.6.block3
  27.5 0.1 collective-permute-start.7
  27.6 0.6 %assemble.1.field.assembled.own_start = f32[1024,128]{1,0:T(8,128)S(1)} custom-call(f32[424,128]{1,0:T(8,128)S(1)} %line.1.block0, f32[424,128]{1,0:T(8,128)S(1)} %collective-permute-done.4.block1, f32[424,128]{1,0:T(8,128)S(1)} %collective-permute-done.5.block2, f32[424,128]{1,0:T(8,128)S(1)} %collective-permute-done.6.block3), custom_call_target="tpu_custom_call" | custom-call | flops 4000000 | bytes 4000000 | tf_op jit(solution)/shard_map/assemble/pallas_call | solution.py:1077
  28.2 0.8 %collective-permute-done.7.other_halves = f32[256,128]{1,0:T(8,128)S(1)} collective-permute-done((f32[256,128]{1,0:T(8,128)S(1)}, f32[256,128]{1,0:T(8,128)S(1)}, u32[]{:S(2)}, u32[]{:S(2)}) %collective-permute-start.7) | collective-permute-done | bytes 131104 | tf_op jit(solution)/shard_map/ppermute | solution.py:1136
  28.9 0.1 collective-permute-start.8
  29.1 0.3 setup.1.coefs
  29.4 5.5 %cycle.1.own = f32[1128,128]{1,0:T(8,128)S(1)} custom-call(f32[2704,128]{1,0:T(8,128)S(1)} %setup.1.coefs, f32[1024,128]{1,0:T(8,128)S(1)} %assemble.1.field.assembled.own_start), custom_call_target="tpu_custom_call" | custom-call | flops 40000000 | bytes 30000000 | tf_op jit(solution)/shard_map/cycle/pallas_call | solution.py:1094
  34.9 0.0 copy-start
  34.9 0.0 collective-permute-done.8.other_start
  34.9 0.4 %collective-permute-start.9 = (f32[1128,128]{1,0:T(8,128)S(1)}, f32[1128,128]{1,0:T(8,128)S(1)}, u32[]{:S(2)}, u32[]{:S(2)}) collective-permute-start(f32[1128,128]{1,0:T(8,128)S(1)} %cycle.1.own), channel_id=1, source_target_pairs={{0,16},{16,0},{1,17},{17,1},{2,18},{18,2},{3,19},{19,3},{4,20},{20... | collective-permute-start | bytes 1732616 | tf_op jit(solution)/shard_map/ppermute | solution.py:1136
  35.3 0.8 %early.1 = (f32[16,128]{1,0:T(8,128)S(1)}, f32[192,160]{1,0:T(8,128)S(1)}) custom-call(f32[1128,128]{1,0:T(8,128)S(1)} %cycle.1.own, f32[1024,128]{1,0:T(8,128)S(1)} %assemble.1.field.assembled.own_start, f32[1024,128]{1,0:T(8,128)S(1)} %collective-permute-done.8.other_start), custom_call_target="tpu_custom_call" | custom-call | flops 4000000 | bytes 4000000 | tf_op jit(solution)/shard_map/early/pallas_call | solution.py:1107
  36.1 0.9 %collective-permute-done.9.other = f32[1128,128]{1,0:T(8,128)S(1)} collective-permute-done((f32[1128,128]{1,0:T(8,128)S(1)}, f32[1128,128]{1,0:T(8,128)S(1)}, u32[]{:S(2)}, u32[]{:S(2)}) %collective-permute-start.9) | collective-permute-done | bytes 577568 | tf_op jit(solution)/shard_map/ppermute | solution.py:1136
  36.9 0.0 copy-done
  36.9 1.5 %finish.1 = (f32[5,5,2,160]{3,2,1,0:T(2,128)}, f32[5,5,2,160]{3,2,1,0:T(2,128)}, f32[3]{0:T(128)}) custom-call(f32[1128,128]{1,0:T(8,128)S(1)} %cycle.1.own, f32[1128,128]{1,0:T(8,128)S(1)} %collective-permute-done.9.other, f32[1024,128]{1,0:T(8,128)S(1)} %assemble.1.field.assembled.own_start, f32[1024,128]{1,0:T(8,128)S(1)} %collective-permute-done.8.other_start, ...), custom_call_target="tpu_custom_call" | custom-call | tf_op jit(solution)/shard_map/finish/pallas_call | solution.py:1120
  (4 shorter events, 0.0 us)
Async XLA Ops:
  3.0 1.6 %collective-permute-start = (f32[104,128]{1,0:T(8,128)}, f32[104,128]{1,0:T(8,128)S(1)}, u32[]{:S(2)}, u32[]{:S(2)}) collective-permute-start(f32[104,128]{1,0:T(8,128)} %get-tuple-element.19), channel_id=1, source_target_pairs={{0,16},{16,0},{1,17},{17,1},{2,18},{18,2},{3,19},{19,3},{4,20},{20... | collective-permute-start | bytes 159752 | tf_op jit(solution)/shard_map/ppermute | solution.py:1136
  3.5 0.8 %copy-start.1 = (f32[120,128]{1,0:T(8,128)S(1)}, f32[120,128]{1,0:T(8,128)}, u32[]{:S(2)}) copy-start(f32[120,128]{1,0:T(8,128)} %get-tuple-element.20.source) | copy-start | bytes 184324
  4.6 7.5 %collective-permute-start.1 = (f32[120,128]{1,0:T(8,128)S(1)}, f32[120,128]{1,0:T(8,128)S(1)}, u32[]{:S(2)}, u32[]{:S(2)}) collective-permute-start(f32[120,128]{1,0:T(8,128)S(1)} %pad_maximum_fusion.own), channel_id=1, source_target_pairs={{0,12},{4,8},{8,4},{12,0},{16,24},{20,28},{24,16},{28,20},{1,13},{... | collective-permute-start | bytes 184328 | tf_op jit(solution)/shard_map/ppermute | solution.py:1142
  9.6 5.6 %collective-permute-start.2 = (f32[120,128]{1,0:T(8,128)S(1)}, f32[120,128]{1,0:T(8,128)S(1)}, u32[]{:S(2)}, u32[]{:S(2)}) collective-permute-start(f32[120,128]{1,0:T(8,128)S(1)} %pad_maximum_fusion.own), channel_id=1, source_target_pairs={{0,8},{4,12},{8,0},{12,4},{16,28},{20,24},{24,20},{28,16},{1,9},{5... | collective-permute-start | bytes 184328 | tf_op jit(solution)/shard_map/ppermute | solution.py:1142
  9.6 5.6 %collective-permute-start.3 = (f32[120,128]{1,0:T(8,128)S(1)}, f32[120,128]{1,0:T(8,128)S(1)}, u32[]{:S(2)}, u32[]{:S(2)}) collective-permute-start(f32[120,128]{1,0:T(8,128)S(1)} %pad_maximum_fusion.own), channel_id=1, source_target_pairs={{0,4},{4,0},{8,12},{12,8},{16,20},{20,16},{24,28},{28,24},{1,5},{5... | collective-permute-start | bytes 184328 | tf_op jit(solution)/shard_map/ppermute | solution.py:1142
  15.4 8.3 %collective-permute-start.4 = (f32[424,128]{1,0:T(8,128)S(1)}, f32[424,128]{1,0:T(8,128)S(1)}, u32[]{:S(2)}, u32[]{:S(2)}) collective-permute-start(f32[424,128]{1,0:T(8,128)S(1)} %line.1.block0), channel_id=1, source_target_pairs={{0,1},{1,0},{2,3},{3,2},{16,18},{17,19},{18,16},{19,17},{4,5},{5,4... | collective-permute-start | bytes 651272 | tf_op jit(solution)/shard_map/ppermute | solution.py:1142
  17.0 10.5 %collective-permute-start.5 = (f32[424,128]{1,0:T(8,128)S(1)}, f32[424,128]{1,0:T(8,128)S(1)}, u32[]{:S(2)}, u32[]{:S(2)}) collective-permute-start(f32[424,128]{1,0:T(8,128)S(1)} %line.1.block0), channel_id=1, source_target_pairs={{0,2},{1,3},{2,0},{3,1},{16,17},{17,16},{18,19},{19,18},{4,6},{5,7... | collective-permute-start | bytes 651272 | tf_op jit(solution)/shard_map/ppermute | solution.py:1142
  18.5 9.0 %collective-permute-start.6 = (f32[424,128]{1,0:T(8,128)S(1)}, f32[424,128]{1,0:T(8,128)S(1)}, u32[]{:S(2)}, u32[]{:S(2)}) collective-permute-start(f32[424,128]{1,0:T(8,128)S(1)} %line.1.block0), channel_id=1, source_target_pairs={{0,3},{1,2},{2,1},{3,0},{16,19},{17,18},{18,17},{19,16},{4,7},{5,6... | collective-permute-start | bytes 651272 | tf_op jit(solution)/shard_map/ppermute | solution.py:1142
  27.5 1.4 %collective-permute-start.7 = (f32[256,128]{1,0:T(8,128)S(1)}, f32[256,128]{1,0:T(8,128)S(1)}, u32[]{:S(2)}, u32[]{:S(2)}) collective-permute-start(f32[256,128]{1,0:T(8,128)S(1)} %halves.1.own_halves), channel_id=1, source_target_pairs={{0,16},{16,0},{1,17},{17,1},{2,18},{18,2},{3,19},{19,3},{4,20},{20... | collective-permute-start | bytes 393224 | tf_op jit(solution)/shard_map/ppermute | solution.py:1136
  28.9 5.9 %collective-permute-start.8 = (f32[1024,128]{1,0:T(8,128)S(1)}, f32[1024,128]{1,0:T(8,128)S(1)}, u32[]{:S(2)}, u32[]{:S(2)}) collective-permute-start(f32[1024,128]{1,0:T(8,128)S(1)} %assemble.1.field.assembled.own_start), channel_id=1, source_target_pairs={{0,16},{16,0},{1,17},{17,1},{2,18},{18,2},{3,19},{19,3},{4,20},{20... | collective-permute-start | bytes 1572872 | tf_op jit(solution)/shard_map/ppermute | solution.py:1136
  34.9 2.1 %copy-start = (f32[2,5,5,160]{3,0,2,1:T(2,128)S(1)}, f32[2,5,5,160]{3,0,2,1:T(2,128)}, u32[]{:S(2)}) copy-start(f32[2,5,5,160]{3,0,2,1:T(2,128)} %param.6) | copy-start | bytes 96004
  34.9 2.1 %collective-permute-start.9 = (f32[1128,128]{1,0:T(8,128)S(1)}, f32[1128,128]{1,0:T(8,128)S(1)}, u32[]{:S(2)}, u32[]{:S(2)}) collective-permute-start(f32[1128,128]{1,0:T(8,128)S(1)} %cycle.1.own), channel_id=1, source_target_pairs={{0,16},{16,0},{1,17},{17,1},{2,18},{18,2},{3,19},{19,3},{4,20},{20... | collective-permute-start | bytes 1732616 | tf_op jit(solution)/shard_map/ppermute | solution.py:1136

commit v15 on v14

--- a/solution.py
+++ b/solution.py
@@ -1149,7 +1149,9 @@
     piece = jnp.concatenate([mine + got, kappa_piece])
     pieces = [exchange_by_core(piece, "gx", bits) for bits in ORDER_X] + [piece]
     line = plain_call(line_kernel, "line", LINE, [4 * 64, 4 * PIECE], pieces)
-    blocks = [line] + [exchange_by_core(line, "gy", bits) for bits in ORDER_Y]
+    first = exchange_by_core(line, "gy", ORDER_Y[0])
+    second = exchange_by_core(line, "gy", ORDER_Y[1])
+    blocks = [line, first, second, exchange_by_core(first, "gy", ORDER_Y[1])]
     halves = plain_call(halves_kernel, "halves", COLS * 16, [], blocks)
     other_halves = exchange(halves, "section", 1)
     start = plain_call(assemble_kernel, "assemble", 128 * 8, [COLS * HALF, COLS * 32, 50 * 8], blocks, 4_000_000)

time: 38.6 us -> 40.5 us (1.049)
  waiting for transfers between devices: 15.4 us -> 17.7 us
  starting transfers between devices: 10.4 us -> 9.9 us
    ppermute x6, waiting for transfers between devices: 13.5 us -> 15.8 us  [exchange_by_core(): return lax.ppermute(x, ('section', axis), pairs)]
    ppermute x6, starting transfers between devices: 9.21 us -> 8.74 us  [exchange_by_core(): return lax.ppermute(x, ('section', axis), pairs)]
where the time goes in v15:
time: 40.5 us; the launch traced here: 40.3 us
  waiting for transfers between devices  17.7 us (44%)
  Pallas kernels  11.1 us (27%)
  starting transfers between devices  9.9 us (24%)
  local copies, waits for them, and re-layouts  0.83 us (2%)
  between operations  0.71 us (2%)
    ppermute x6, waiting for transfers between devices, exchange_by_core(): return lax.ppermute(x, ('section', axis), pairs)  15.8 us
    ppermute x6, starting transfers between devices, exchange_by_core(): return lax.ppermute(x, ('section', axis), pairs)  8.74 us
    pallas_call x1, Pallas kernels, cycle(): pl.pallas_call(cycle_kernel, out_shape=jax.ShapeDtypeStruct((FIELD + 128,...  5.45 us
    pallas_call x1, Pallas kernels, local_part(): pl.pallas_call(local_kernel, out_shape=[jax.ShapeDtypeStruct((rows, 128),...  2.34 us
    ppermute x4, waiting for transfers between devices, exchange(): lax.ppermute(x, axis, [(n, n ^ bits) for n in range(lax.axis_size(axis))])  1.89 us
    pallas_call x1, Pallas kernels, finish(): pl.pallas_call(finish_kernel, out_shape=[jax.ShapeDtypeStruct(guess.shape...  1.47 us
    ppermute x4, starting transfers between devices, exchange(): lax.ppermute(x, axis, [(n, n ^ bits) for n in range(lax.axis_size(axis))])  1.17 us
    pallas_call x4, Pallas kernels, plain_call(): pl.pallas_call(kernel, out_shape=jax.ShapeDtypeStruct((rows, 128), F32),...  1.08 us
  transfers between devices with their start and end apart: 10, of which 7 were waited for; matrix products, arithmetic and copies ran while one was open for 0% of the time, Pallas kernels for 18%

profile of v15, /device:TPU:0, one launch (start us, length us, event | category | flops | bytes accessed | tf_op | source)
XLA Modules:
  0.0 40.3 jit_solution(14873286878483470635)
XLA Ops:
  0.6 2.3 %local_part.1 = (f32[120,128]{1,0:T(8,128)}, f32[104,128]{1,0:T(8,128)}) custom-call(f32[5,5,2,160]{3,2,1,0:T(2,128)} %bitcast.6, f32[5,5,2,160]{3,2,1,0:T(2,128)} %bitcast.4, f32[5,5,160]{2,1,0:T(8,128)} %kappa_in.1, s32[6,1,1,32]{3,2,1,0:T(1,128)} %flags_in.1, f32[64,64]{1,0:T(8,128)} %constant.2.clone.rows_in), custom_call_target="tpu_custom_call" | custom-call | flops 20000000 | bytes 8000000 | tf_op jit(solution)/shard_map/local_part/pallas_call | solution.py:560
  3.0 0.5 %collective-permute-start = (f32[104,128]{1,0:T(8,128)}, f32[104,128]{1,0:T(8,128)S(1)}, u32[]{:S(2)}, u32[]{:S(2)}) collective-permute-start(f32[104,128]{1,0:T(8,128)} %get-tuple-element.19), channel_id=1, source_target_pairs={{0,16},{16,0},{1,17},{17,1},{2,18},{18,2},{3,19},{19,3},{4,20},{20... | collective-permute-start | bytes 159752 | tf_op jit(solution)/shard_map/ppermute | solution.py:1136
  3.5 0.0 copy-start.1
  3.5 0.8 %copy-done.1 = f32[120,128]{1,0:T(8,128)S(1)} copy-done((f32[120,128]{1,0:T(8,128)S(1)}, f32[120,128]{1,0:T(8,128)}, u32[]{:S(2)}) %copy-start.1) | copy-done | bytes 61464
  4.3 0.3 collective-permute-done
  4.6 5.0 %collective-permute-start.1 = (f32[120,128]{1,0:T(8,128)S(1)}, f32[120,128]{1,0:T(8,128)S(1)}, u32[]{:S(2)}, u32[]{:S(2)}) collective-permute-start(f32[120,128]{1,0:T(8,128)S(1)} %pad_maximum_fusion.own), channel_id=1, source_target_pairs={{0,12},{4,8},{8,4},{12,0},{16,24},{20,28},{24,16},{28,20},{1,13},{... | collective-permute-start | bytes 184328 | tf_op jit(solution)/shard_map/ppermute | solution.py:1142
  9.6 0.0 collective-permute-start.2
  9.6 0.6 %collective-permute-start.3 = (f32[120,128]{1,0:T(8,128)S(1)}, f32[120,128]{1,0:T(8,128)S(1)}, u32[]{:S(2)}, u32[]{:S(2)}) collective-permute-start(f32[120,128]{1,0:T(8,128)S(1)} %pad_maximum_fusion.own), channel_id=1, source_target_pairs={{0,4},{4,0},{8,12},{12,8},{16,20},{20,16},{24,28},{28,24},{1,5},{5... | collective-permute-start | bytes 184328 | tf_op jit(solution)/shard_map/ppermute | solution.py:1142
  10.3 1.8 %collective-permute-done.1.first = f32[120,128]{1,0:T(8,128)S(1)} collective-permute-done((f32[120,128]{1,0:T(8,128)S(1)}, f32[120,128]{1,0:T(8,128)S(1)}, u32[]{:S(2)}, u32[]{:S(2)}) %collective-permute-start.1) | collective-permute-done | bytes 61472 | tf_op jit(solution)/shard_map/ppermute | solution.py:1142
  12.1 3.1 %collective-permute-done.2.second = f32[120,128]{1,0:T(8,128)S(1)} collective-permute-done((f32[120,128]{1,0:T(8,128)S(1)}, f32[120,128]{1,0:T(8,128)S(1)}, u32[]{:S(2)}, u32[]{:S(2)}) %collective-permute-start.2) | collective-permute-done | bytes 61472 | tf_op jit(solution)/shard_map/ppermute | solution.py:1142
  15.2 0.0 collective-permute-done.3.third
  15.2 0.2 line.1.block0
  15.4 1.6 %collective-permute-start.4 = (f32[424,128]{1,0:T(8,128)S(1)}, f32[424,128]{1,0:T(8,128)S(1)}, u32[]{:S(2)}, u32[]{:S(2)}) collective-permute-start(f32[424,128]{1,0:T(8,128)S(1)} %line.1.block0), channel_id=1, source_target_pairs={{0,1},{1,0},{2,3},{3,2},{16,18},{17,19},{18,16},{19,17},{4,5},{5,4... | collective-permute-start | bytes 651272 | tf_op jit(solution)/shard_map/ppermute | solution.py:1142
  17.0 1.5 %collective-permute-start.5 = (f32[424,128]{1,0:T(8,128)S(1)}, f32[424,128]{1,0:T(8,128)S(1)}, u32[]{:S(2)}, u32[]{:S(2)}) collective-permute-start(f32[424,128]{1,0:T(8,128)S(1)} %line.1.block0), channel_id=1, source_target_pairs={{0,2},{1,3},{2,0},{3,1},{16,17},{17,16},{18,19},{19,18},{4,6},{5,7... | collective-permute-start | bytes 651272 | tf_op jit(solution)/shard_map/ppermute | solution.py:1142
  18.5 5.0 %collective-permute-done.4.block1 = f32[424,128]{1,0:T(8,128)S(1)} collective-permute-done((f32[424,128]{1,0:T(8,128)S(1)}, f32[424,128]{1,0:T(8,128)S(1)}, u32[]{:S(2)}, u32[]{:S(2)}) %collective-permute-start.4) | collective-permute-done | bytes 217120 | tf_op jit(solution)/shard_map/ppermute | solution.py:1142
  23.5 0.0 collective-permute-start.6
  23.5 0.0 collective-permute-done.5.block2
  23.5 5.9 %collective-permute-done.6.block3 = f32[424,128]{1,0:T(8,128)S(1)} collective-permute-done((f32[424,128]{1,0:T(8,128)S(1)}, f32[424,128]{1,0:T(8,128)S(1)}, u32[]{:S(2)}, u32[]{:S(2)}) %collective-permute-start.6) | collective-permute-done | bytes 217120 | tf_op jit(solution)/shard_map/ppermute | solution.py:1142
  29.4 0.1 collective-permute-start.7
  29.5 0.6 %assemble.1.field.assembled.own_start = f32[1024,128]{1,0:T(8,128)S(1)} custom-call(f32[424,128]{1,0:T(8,128)S(1)} %line.1.block0, f32[424,128]{1,0:T(8,128)S(1)} %collective-permute-done.4.block1, f32[424,128]{1,0:T(8,128)S(1)} %collective-permute-done.5.block2, f32[424,128]{1,0:T(8,128)S(1)} %collective-permute-done.6.block3), custom_call_target="tpu_custom_call" | custom-call | flops 4000000 | bytes 4000000 | tf_op jit(solution)/shard_map/assemble/pallas_call | solution.py:1077
  30.0 0.8 %collective-permute-done.7.other_halves = f32[256,128]{1,0:T(8,128)S(1)} collective-permute-done((f32[256,128]{1,0:T(8,128)S(1)}, f32[256,128]{1,0:T(8,128)S(1)}, u32[]{:S(2)}, u32[]{:S(2)}) %collective-permute-start.7) | collective-permute-done | bytes 131104 | tf_op jit(solution)/shard_map/ppermute | solution.py:1136
  30.8 0.1 collective-permute-start.8
  30.9 0.3 setup.1.coefs
  31.3 5.5 %cycle.1.own = f32[1128,128]{1,0:T(8,128)S(1)} custom-call(f32[2704,128]{1,0:T(8,128)S(1)} %setup.1.coefs, f32[1024,128]{1,0:T(8,128)S(1)} %assemble.1.field.assembled.own_start), custom_call_target="tpu_custom_call" | custom-call | flops 40000000 | bytes 30000000 | tf_op jit(solution)/shard_map/cycle/pallas_call | solution.py:1094
  36.7 0.0 copy-start
  36.7 0.0 collective-permute-done.8.other_start
  36.7 0.4 %collective-permute-start.9 = (f32[1128,128]{1,0:T(8,128)S(1)}, f32[1128,128]{1,0:T(8,128)S(1)}, u32[]{:S(2)}, u32[]{:S(2)}) collective-permute-start(f32[1128,128]{1,0:T(8,128)S(1)} %cycle.1.own), channel_id=1, source_target_pairs={{0,16},{16,0},{1,17},{17,1},{2,18},{18,2},{3,19},{19,3},{4,20},{20... | collective-permute-start | bytes 1732616 | tf_op jit(solution)/shard_map/ppermute | solution.py:1136
  37.2 0.8 %early.1 = (f32[16,128]{1,0:T(8,128)S(1)}, f32[192,160]{1,0:T(8,128)S(1)}) custom-call(f32[1128,128]{1,0:T(8,128)S(1)} %cycle.1.own, f32[1024,128]{1,0:T(8,128)S(1)} %assemble.1.field.assembled.own_start, f32[1024,128]{1,0:T(8,128)S(1)} %collective-permute-done.8.other_start), custom_call_target="tpu_custom_call" | custom-call | flops 4000000 | bytes 4000000 | tf_op jit(solution)/shard_map/early/pallas_call | solution.py:1107
  37.9 0.9 %collective-permute-done.9.other = f32[1128,128]{1,0:T(8,128)S(1)} collective-permute-done((f32[1128,128]{1,0:T(8,128)S(1)}, f32[1128,128]{1,0:T(8,128)S(1)}, u32[]{:S(2)}, u32[]{:S(2)}) %collective-permute-start.9) | collective-permute-done | bytes 577568 | tf_op jit(solution)/shard_map/ppermute | solution.py:1136
  38.8 0.0 copy-done
  38.8 1.5 %finish.1 = (f32[5,5,2,160]{3,2,1,0:T(2,128)}, f32[5,5,2,160]{3,2,1,0:T(2,128)}, f32[3]{0:T(128)}) custom-call(f32[1128,128]{1,0:T(8,128)S(1)} %cycle.1.own, f32[1128,128]{1,0:T(8,128)S(1)} %collective-permute-done.9.other, f32[1024,128]{1,0:T(8,128)S(1)} %assemble.1.field.assembled.own_start, f32[1024,128]{1,0:T(8,128)S(1)} %collective-permute-done.8.other_start, ...), custom_call_target="tpu_custom_call" | custom-call | tf_op jit(solution)/shard_map/finish/pallas_call | solution.py:1120
  (4 shorter events, 0.0 us)
Async XLA Ops:
  3.0 1.6 %collective-permute-start = (f32[104,128]{1,0:T(8,128)}, f32[104,128]{1,0:T(8,128)S(1)}, u32[]{:S(2)}, u32[]{:S(2)}) collective-permute-start(f32[104,128]{1,0:T(8,128)} %get-tuple-element.19), channel_id=1, source_target_pairs={{0,16},{16,0},{1,17},{17,1},{2,18},{18,2},{3,19},{19,3},{4,20},{20... | collective-permute-start | bytes 159752 | tf_op jit(solution)/shard_map/ppermute | solution.py:1136
  3.5 0.8 %copy-start.1 = (f32[120,128]{1,0:T(8,128)S(1)}, f32[120,128]{1,0:T(8,128)}, u32[]{:S(2)}) copy-start(f32[120,128]{1,0:T(8,128)} %get-tuple-element.20.source) | copy-start | bytes 184324
  4.6 7.5 %collective-permute-start.1 = (f32[120,128]{1,0:T(8,128)S(1)}, f32[120,128]{1,0:T(8,128)S(1)}, u32[]{:S(2)}, u32[]{:S(2)}) collective-permute-start(f32[120,128]{1,0:T(8,128)S(1)} %pad_maximum_fusion.own), channel_id=1, source_target_pairs={{0,12},{4,8},{8,4},{12,0},{16,24},{20,28},{24,16},{28,20},{1,13},{... | collective-permute-start | bytes 184328 | tf_op jit(solution)/shard_map/ppermute | solution.py:1142
  9.6 5.6 %collective-permute-start.2 = (f32[120,128]{1,0:T(8,128)S(1)}, f32[120,128]{1,0:T(8,128)S(1)}, u32[]{:S(2)}, u32[]{:S(2)}) collective-permute-start(f32[120,128]{1,0:T(8,128)S(1)} %pad_maximum_fusion.own), channel_id=1, source_target_pairs={{0,8},{4,12},{8,0},{12,4},{16,28},{20,24},{24,20},{28,16},{1,9},{5... | collective-permute-start | bytes 184328 | tf_op jit(solution)/shard_map/ppermute | solution.py:1142
  9.6 5.6 %collective-permute-start.3 = (f32[120,128]{1,0:T(8,128)S(1)}, f32[120,128]{1,0:T(8,128)S(1)}, u32[]{:S(2)}, u32[]{:S(2)}) collective-permute-start(f32[120,128]{1,0:T(8,128)S(1)} %pad_maximum_fusion.own), channel_id=1, source_target_pairs={{0,4},{4,0},{8,12},{12,8},{16,20},{20,16},{24,28},{28,24},{1,5},{5... | collective-permute-start | bytes 184328 | tf_op jit(solution)/shard_map/ppermute | solution.py:1142
  15.4 8.0 %collective-permute-start.4 = (f32[424,128]{1,0:T(8,128)S(1)}, f32[424,128]{1,0:T(8,128)S(1)}, u32[]{:S(2)}, u32[]{:S(2)}) collective-permute-start(f32[424,128]{1,0:T(8,128)S(1)} %line.1.block0), channel_id=1, source_target_pairs={{0,1},{1,0},{2,3},{3,2},{16,18},{17,19},{18,16},{19,17},{4,5},{5,4... | collective-permute-start | bytes 651272 | tf_op jit(solution)/shard_map/ppermute | solution.py:1142
  17.0 6.5 %collective-permute-start.5 = (f32[424,128]{1,0:T(8,128)S(1)}, f32[424,128]{1,0:T(8,128)S(1)}, u32[]{:S(2)}, u32[]{:S(2)}) collective-permute-start(f32[424,128]{1,0:T(8,128)S(1)} %line.1.block0), channel_id=1, source_target_pairs={{0,2},{1,3},{2,0},{3,1},{16,17},{17,16},{18,19},{19,18},{4,6},{5,7... | collective-permute-start | bytes 651272 | tf_op jit(solution)/shard_map/ppermute | solution.py:1142
  23.5 5.9 %collective-permute-start.6 = (f32[424,128]{1,0:T(8,128)S(1)}, f32[424,128]{1,0:T(8,128)S(1)}, u32[]{:S(2)}, u32[]{:S(2)}) collective-permute-start(f32[424,128]{1,0:T(8,128)S(1)} %collective-permute-done.4.block1), channel_id=1, source_target_pairs={{0,2},{1,3},{2,0},{3,1},{16,17},{17,16},{18,19},{19,18},{4,6},{5,7... | collective-permute-start | bytes 651272 | tf_op jit(solution)/shard_map/ppermute | solution.py:1142
  29.4 1.4 %collective-permute-start.7 = (f32[256,128]{1,0:T(8,128)S(1)}, f32[256,128]{1,0:T(8,128)S(1)}, u32[]{:S(2)}, u32[]{:S(2)}) collective-permute-start(f32[256,128]{1,0:T(8,128)S(1)} %halves.1.own_halves), channel_id=1, source_target_pairs={{0,16},{16,0},{1,17},{17,1},{2,18},{18,2},{3,19},{19,3},{4,20},{20... | collective-permute-start | bytes 393224 | tf_op jit(solution)/shard_map/ppermute | solution.py:1136
  30.8 5.9 %collective-permute-start.8 = (f32[1024,128]{1,0:T(8,128)S(1)}, f32[1024,128]{1,0:T(8,128)S(1)}, u32[]{:S(2)}, u32[]{:S(2)}) collective-permute-start(f32[1024,128]{1,0:T(8,128)S(1)} %assemble.1.field.assembled.own_start), channel_id=1, source_target_pairs={{0,16},{16,0},{1,17},{17,1},{2,18},{18,2},{3,19},{19,3},{4,20},{20... | collective-permute-start | bytes 1572872 | tf_op jit(solution)/shard_map/ppermute | solution.py:1136
  36.7 2.1 %copy-start = (f32[2,5,5,160]{3,0,2,1:T(2,128)S(1)}, f32[2,5,5,160]{3,0,2,1:T(2,128)}, u32[]{:S(2)}) copy-start(f32[2,5,5,160]{3,0,2,1:T(2,128)} %param.6) | copy-start | bytes 96004
  36.7 2.1 %collective-permute-start.9 = (f32[1128,128]{1,0:T(8,128)S(1)}, f32[1128,128]{1,0:T(8,128)S(1)}, u32[]{:S(2)}, u32[]{:S(2)}) collective-permute-start(f32[1128,128]{1,0:T(8,128)S(1)} %cycle.1.own), channel_id=1, source_target_pairs={{0,16},{16,0},{1,17},{17,1},{2,18},{18,2},{3,19},{19,3},{4,20},{20... | collective-permute-start | bytes 1732616 | tf_op jit(solution)/shard_map/ppermute | solution.py:1136

commit v16 on v14

--- a/solution.py
+++ b/solution.py
@@ -845,28 +845,39 @@
             def line_at(i):
                 return load(source, (k * n + i) * n, n)
 
+            x_left = gains[0] * lanes.x_before(line_at(n - 1))
+            x_right = gains[1] * lanes.x_after(line_at(0))
+            z_low, z_high, y_low, y_high = [], [], [], []
+            for i in range(n):
+                if k == 0:
+                    z_low.append(gains[4] * lanes.z_before(load(source, ((n - 1) * n + i) * n, n)))
+                if k == n - 1:
+                    z_high.append(gains[5] * lanes.z_after(load(source, i * n, n)))
+                v = line_at(i)
+                y_low.append(gains[2] * lanes.y_before(v[n - 1]))
+                y_high.append(gains[3] * lanes.y_after(v[0]))
             totals = []
             for i in range(n):
                 first = (k * n + i) * n
                 v = line_at(i)
                 along_x = [float(kx[i, m]) * line_at(m) for m in range(n) if m != i]
-                if i == 0:
-                    along_x.append(gains[0] * lanes.x_before(line_at(n - 1)))
-                if i == n - 1:
-                    along_x.append(gains[1] * lanes.x_after(line_at(0)))
                 along_z = [float(kz[k, m]) * load(source, (m * n + i) * n, n) for m in range(n) if m != k]
-                if k == 0:
-                    along_z.append(gains[4] * lanes.z_before(load(source, ((n - 1) * n + i) * n, n)))
-                if k == n - 1:
-                    along_z.append(gains[5] * lanes.z_after(load(source, i * n, n)))
                 along_y = []
                 for j in range(n):
                     terms = [float(ky[j, m]) * v[m] for m in range(n) if m != j]
                     if j == 0:
-                        terms.append(gains[2] * lanes.y_before(v[n - 1]))
+                        terms.append(y_low[i])
                     if j == n - 1:
-                        terms.append(gains[3] * lanes.y_after(v[0]))
+                        terms.append(y_high[i])
                     along_y.append(tree(terms))
+                if i == 0:
+                    along_x.append(x_left)
+                if i == n - 1:
+                    along_x.append(x_right)
+                if k == 0:
+                    along_z.append(z_low[i])
+                if k == n - 1:
+                    along_z.append(z_high[i])
                 totals.append(tree([level.diag(first, n) * v, tree(along_x), tree(along_z), jnp.stack(along_y)]))
             return totals
 
@@ -885,8 +896,11 @@
                     store(level.dir, first, level.jac(first, n) * rest)
 
         if n == 5:
+            ready = sums(0)
             for k in range(n):
-                update(k, sums(k))
+                following = sums(k + 1) if k + 1 < n else None
+                update(k, ready)
+                ready = following
         else:
             for k, totals in enumerate([sums(k) for k in range(n)]):
                 update(k, totals)
@@ -1019,12 +1033,21 @@
         uppers[r % 5] = uppers[r % 5] + a * (c + weights * d)
         sizes[r % 5] = sizes[r % 5] + ((c * c + d * d) + 2.0 * (weights * (c * d)))
     sums[0:8, :] = sum(uppers)
-    sums[8:16, :] = sum(sizes)
+    sums[8:16, :] = jnp.broadcast_to(jnp.sum(sum(sizes), keepdims=True), (8, 128))
 
 
 def finish_kernel(own, other, own_start, other_start, sums, column, guess, sol, res_out, arnoldi, cols, outs):
-    sec = lax.axis_index("section")
     weights = pair_weights()
+    nothing = jnp.zeros((8, 128), F32)
+    uppers = [nothing] * 5
+    for r in range(125):
+        c, d = own_start[tile(r), :], other_start[tile(r), :]
+        b = d - other[tile(r), :]
+        uppers[r % 5] = uppers[r % 5] + b * (d + weights * c)
+
+    mine, theirs = sums[0:8, :], sum(uppers)
+    size = sums[8:9, 0:1]
+    upper = jnp.sum(mine + theirs, keepdims=True) / size
     cols[...] = jnp.zeros_like(cols)
     total = jnp.zeros((128, 160), F32)
     factors = column_factors(1)
@@ -1040,16 +1063,6 @@
             total = total + split_dot(cols[...], raw_order(k - 1))
     cols[:, 128:] = jnp.zeros((128, 128), F32)
     total = total + split_dot(cols[...], raw_order(4))
-    nothing = jnp.zeros((8, 128), F32)
-    uppers = [nothing] * 5
-    for r in range(125):
-        c, d = own_start[tile(r), :], other_start[tile(r), :]
-        b = d - other[tile(r), :]
-        uppers[r % 5] = uppers[r % 5] + b * (d + weights * c)
-
-    mine, theirs = sums[0:8, :], sum(uppers)
-    size = jnp.sum(sums[8:16, :], keepdims=True)
-    upper = jnp.sum(mine + theirs, keepdims=True) / size
     rests = [nothing] * 5
     for r in range(125):
         c, d = own_start[tile(r), :], other_start[tile(r), :]

time: 38.6 us -> 38.4 us (level)
  Pallas kernels: 11.1 us -> 10.7 us
  transfers between devices with their start and end apart: 10 -> 10, of which waited for: 7 -> 7; matrix products, arithmetic and copies ran while one was open for 0% -> 0% of each run, Pallas kernels for 18% -> 17%
where the time goes in v16:
time: 38.4 us; the launch traced here: 38.1 us
  waiting for transfers between devices  15.5 us (40%)
  Pallas kernels  10.7 us (28%)
  starting transfers between devices  10.4 us (27%)
  local copies, waits for them, and re-layouts  0.83 us (2%)
  between operations  0.71 us (2%)
    ppermute x6, waiting for transfers between devices, exchange_by_core(): return lax.ppermute(x, ('section', axis), pairs)  13.5 us
    ppermute x6, starting transfers between devices, exchange_by_core(): return lax.ppermute(x, ('section', axis), pairs)  9.21 us
    pallas_call x1, Pallas kernels, cycle(): pl.pallas_call(cycle_kernel, out_shape=jax.ShapeDtypeStruct((FIELD + 128,...  5.08 us
    pallas_call x1, Pallas kernels, local_part(): pl.pallas_call(local_kernel, out_shape=[jax.ShapeDtypeStruct((rows, 128),...  2.34 us
    ppermute x4, waiting for transfers between devices, exchange(): lax.ppermute(x, axis, [(n, n ^ bits) for n in range(lax.axis_size(axis))])  2 us
    pallas_call x1, Pallas kernels, finish(): pl.pallas_call(finish_kernel, out_shape=[jax.ShapeDtypeStruct(guess.shape...  1.55 us
    ppermute x4, starting transfers between devices, exchange(): lax.ppermute(x, axis, [(n, n ^ bits) for n in range(lax.axis_size(axis))])  1.17 us
    pallas_call x4, Pallas kernels, plain_call(): pl.pallas_call(kernel, out_shape=jax.ShapeDtypeStruct((rows, 128), F32),...  1.08 us
  transfers between devices with their start and end apart: 10, of which 7 were waited for; matrix products, arithmetic and copies ran while one was open for 0% of the time, Pallas kernels for 17%

profile of v16, /device:TPU:0, one launch (start us, length us, event | category | flops | bytes accessed | tf_op | source)
XLA Modules:
  0.0 38.1 jit_solution(15155041101521721750)
XLA Ops:
  0.6 2.3 %local_part.1 = (f32[120,128]{1,0:T(8,128)}, f32[104,128]{1,0:T(8,128)}) custom-call(f32[5,5,2,160]{3,2,1,0:T(2,128)} %bitcast.6, f32[5,5,2,160]{3,2,1,0:T(2,128)} %bitcast.4, f32[5,5,160]{2,1,0:T(8,128)} %kappa_in.1, s32[6,1,1,32]{3,2,1,0:T(1,128)} %flags_in.1, f32[64,64]{1,0:T(8,128)} %constant.2.clone.rows_in), custom_call_target="tpu_custom_call" | custom-call | flops 20000000 | bytes 8000000 | tf_op jit(solution)/shard_map/local_part/pallas_call | solution.py:560
  3.0 0.5 %collective-permute-start = (f32[104,128]{1,0:T(8,128)}, f32[104,128]{1,0:T(8,128)S(1)}, u32[]{:S(2)}, u32[]{:S(2)}) collective-permute-start(f32[104,128]{1,0:T(8,128)} %get-tuple-element.19), channel_id=1, source_target_pairs={{0,16},{16,0},{1,17},{17,1},{2,18},{18,2},{3,19},{19,3},{4,20},{20... | collective-permute-start | bytes 159752 | tf_op jit(solution)/shard_map/ppermute | solution.py:1149
  3.5 0.0 copy-start.1
  3.5 0.8 %copy-done.1 = f32[120,128]{1,0:T(8,128)S(1)} copy-done((f32[120,128]{1,0:T(8,128)S(1)}, f32[120,128]{1,0:T(8,128)}, u32[]{:S(2)}) %copy-start.1) | copy-done | bytes 61464
  4.3 0.3 collective-permute-done
  4.6 5.0 %collective-permute-start.1 = (f32[120,128]{1,0:T(8,128)S(1)}, f32[120,128]{1,0:T(8,128)S(1)}, u32[]{:S(2)}, u32[]{:S(2)}) collective-permute-start(f32[120,128]{1,0:T(8,128)S(1)} %pad_maximum_fusion.own), channel_id=1, source_target_pairs={{0,12},{4,8},{8,4},{12,0},{16,24},{20,28},{24,16},{28,20},{1,13},{... | collective-permute-start | bytes 184328 | tf_op jit(solution)/shard_map/ppermute | solution.py:1155
  9.6 0.0 collective-permute-start.2
  9.6 0.6 %collective-permute-start.3 = (f32[120,128]{1,0:T(8,128)S(1)}, f32[120,128]{1,0:T(8,128)S(1)}, u32[]{:S(2)}, u32[]{:S(2)}) collective-permute-start(f32[120,128]{1,0:T(8,128)S(1)} %pad_maximum_fusion.own), channel_id=1, source_target_pairs={{0,4},{4,0},{8,12},{12,8},{16,20},{20,16},{24,28},{28,24},{1,5},{5... | collective-permute-start | bytes 184328 | tf_op jit(solution)/shard_map/ppermute | solution.py:1155
  10.3 1.8 %collective-permute-done.1.first = f32[120,128]{1,0:T(8,128)S(1)} collective-permute-done((f32[120,128]{1,0:T(8,128)S(1)}, f32[120,128]{1,0:T(8,128)S(1)}, u32[]{:S(2)}, u32[]{:S(2)}) %collective-permute-start.1) | collective-permute-done | bytes 61472 | tf_op jit(solution)/shard_map/ppermute | solution.py:1155
  12.1 3.1 %collective-permute-done.2.second = f32[120,128]{1,0:T(8,128)S(1)} collective-permute-done((f32[120,128]{1,0:T(8,128)S(1)}, f32[120,128]{1,0:T(8,128)S(1)}, u32[]{:S(2)}, u32[]{:S(2)}) %collective-permute-start.2) | collective-permute-done | bytes 61472 | tf_op jit(solution)/shard_map/ppermute | solution.py:1155
  15.2 0.0 collective-permute-done.3.third
  15.2 0.2 line.1.block0
  15.4 1.6 %collective-permute-start.4 = (f32[424,128]{1,0:T(8,128)S(1)}, f32[424,128]{1,0:T(8,128)S(1)}, u32[]{:S(2)}, u32[]{:S(2)}) collective-permute-start(f32[424,128]{1,0:T(8,128)S(1)} %line.1.block0), channel_id=1, source_target_pairs={{0,1},{1,0},{2,3},{3,2},{16,18},{17,19},{18,16},{19,17},{4,5},{5,4... | collective-permute-start | bytes 651272 | tf_op jit(solution)/shard_map/ppermute | solution.py:1155
  17.0 1.5 %collective-permute-start.5 = (f32[424,128]{1,0:T(8,128)S(1)}, f32[424,128]{1,0:T(8,128)S(1)}, u32[]{:S(2)}, u32[]{:S(2)}) collective-permute-start(f32[424,128]{1,0:T(8,128)S(1)} %line.1.block0), channel_id=1, source_target_pairs={{0,2},{1,3},{2,0},{3,1},{16,17},{17,16},{18,19},{19,18},{4,6},{5,7... | collective-permute-start | bytes 651272 | tf_op jit(solution)/shard_map/ppermute | solution.py:1155
  18.5 0.5 %collective-permute-start.6 = (f32[424,128]{1,0:T(8,128)S(1)}, f32[424,128]{1,0:T(8,128)S(1)}, u32[]{:S(2)}, u32[]{:S(2)}) collective-permute-start(f32[424,128]{1,0:T(8,128)S(1)} %line.1.block0), channel_id=1, source_target_pairs={{0,3},{1,2},{2,1},{3,0},{16,19},{17,18},{18,17},{19,16},{4,7},{5,6... | collective-permute-start | bytes 651272 | tf_op jit(solution)/shard_map/ppermute | solution.py:1155
  19.0 4.7 %collective-permute-done.4.block1 = f32[424,128]{1,0:T(8,128)S(1)} collective-permute-done((f32[424,128]{1,0:T(8,128)S(1)}, f32[424,128]{1,0:T(8,128)S(1)}, u32[]{:S(2)}, u32[]{:S(2)}) %collective-permute-start.4) | collective-permute-done | bytes 217120 | tf_op jit(solution)/shard_map/ppermute | solution.py:1155
  23.7 3.8 %collective-permute-done.5.block2 = f32[424,128]{1,0:T(8,128)S(1)} collective-permute-done((f32[424,128]{1,0:T(8,128)S(1)}, f32[424,128]{1,0:T(8,128)S(1)}, u32[]{:S(2)}, u32[]{:S(2)}) %collective-permute-start.5) | collective-permute-done | bytes 217120 | tf_op jit(solution)/shard_map/ppermute | solution.py:1155
  27.5 0.0 collective-permute-done.6.block3
  27.5 0.1 collective-permute-start.7
  27.6 0.6 %assemble.1.field.assembled.own_start = f32[1024,128]{1,0:T(8,128)S(1)} custom-call(f32[424,128]{1,0:T(8,128)S(1)} %line.1.block0, f32[424,128]{1,0:T(8,128)S(1)} %collective-permute-done.4.block1, f32[424,128]{1,0:T(8,128)S(1)} %collective-permute-done.5.block2, f32[424,128]{1,0:T(8,128)S(1)} %collective-permute-done.6.block3), custom_call_target="tpu_custom_call" | custom-call | flops 4000000 | bytes 4000000 | tf_op jit(solution)/shard_map/assemble/pallas_call | solution.py:1090
  28.2 0.8 %collective-permute-done.7.other_halves = f32[256,128]{1,0:T(8,128)S(1)} collective-permute-done((f32[256,128]{1,0:T(8,128)S(1)}, f32[256,128]{1,0:T(8,128)S(1)}, u32[]{:S(2)}, u32[]{:S(2)}) %collective-permute-start.7) | collective-permute-done | bytes 131104 | tf_op jit(solution)/shard_map/ppermute | solution.py:1149
  28.9 0.1 collective-permute-start.8
  29.1 0.3 setup.1.coefs
  29.4 5.1 %cycle.1.own = f32[1128,128]{1,0:T(8,128)S(1)} custom-call(f32[2704,128]{1,0:T(8,128)S(1)} %setup.1.coefs, f32[1024,128]{1,0:T(8,128)S(1)} %assemble.1.field.assembled.own_start), custom_call_target="tpu_custom_call" | custom-call | flops 40000000 | bytes 30000000 | tf_op jit(solution)/shard_map/cycle/pallas_call | solution.py:1107
  34.5 0.0 copy-start
  34.5 0.0 collective-permute-done.8.other_start
  34.5 0.4 %collective-permute-start.9 = (f32[1128,128]{1,0:T(8,128)S(1)}, f32[1128,128]{1,0:T(8,128)S(1)}, u32[]{:S(2)}, u32[]{:S(2)}) collective-permute-start(f32[1128,128]{1,0:T(8,128)S(1)} %cycle.1.own), channel_id=1, source_target_pairs={{0,16},{16,0},{1,17},{17,1},{2,18},{18,2},{3,19},{19,3},{4,20},{20... | collective-permute-start | bytes 1732616 | tf_op jit(solution)/shard_map/ppermute | solution.py:1149
  35.0 0.6 %early.1 = (f32[16,128]{1,0:T(8,128)S(1)}, f32[192,160]{1,0:T(8,128)S(1)}) custom-call(f32[1128,128]{1,0:T(8,128)S(1)} %cycle.1.own, f32[1024,128]{1,0:T(8,128)S(1)} %assemble.1.field.assembled.own_start, f32[1024,128]{1,0:T(8,128)S(1)} %collective-permute-done.8.other_start), custom_call_target="tpu_custom_call" | custom-call | flops 4000000 | bytes 4000000 | tf_op jit(solution)/shard_map/early/pallas_call | solution.py:1120
  35.6 1.0 %collective-permute-done.9.other = f32[1128,128]{1,0:T(8,128)S(1)} collective-permute-done((f32[1128,128]{1,0:T(8,128)S(1)}, f32[1128,128]{1,0:T(8,128)S(1)}, u32[]{:S(2)}, u32[]{:S(2)}) %collective-permute-start.9) | collective-permute-done | bytes 577568 | tf_op jit(solution)/shard_map/ppermute | solution.py:1149
  36.6 0.0 copy-done
  36.6 1.6 %finish.1 = (f32[5,5,2,160]{3,2,1,0:T(2,128)}, f32[5,5,2,160]{3,2,1,0:T(2,128)}, f32[3]{0:T(128)}) custom-call(f32[1128,128]{1,0:T(8,128)S(1)} %cycle.1.own, f32[1128,128]{1,0:T(8,128)S(1)} %collective-permute-done.9.other, f32[1024,128]{1,0:T(8,128)S(1)} %assemble.1.field.assembled.own_start, f32[1024,128]{1,0:T(8,128)S(1)} %collective-permute-done.8.other_start, ...), custom_call_target="tpu_custom_call" | custom-call | tf_op jit(solution)/shard_map/finish/pallas_call | solution.py:1133
  (4 shorter events, 0.0 us)
Async XLA Ops:
  3.0 1.6 %collective-permute-start = (f32[104,128]{1,0:T(8,128)}, f32[104,128]{1,0:T(8,128)S(1)}, u32[]{:S(2)}, u32[]{:S(2)}) collective-permute-start(f32[104,128]{1,0:T(8,128)} %get-tuple-element.19), channel_id=1, source_target_pairs={{0,16},{16,0},{1,17},{17,1},{2,18},{18,2},{3,19},{19,3},{4,20},{20... | collective-permute-start | bytes 159752 | tf_op jit(solution)/shard_map/ppermute | solution.py:1149
  3.5 0.8 %copy-start.1 = (f32[120,128]{1,0:T(8,128)S(1)}, f32[120,128]{1,0:T(8,128)}, u32[]{:S(2)}) copy-start(f32[120,128]{1,0:T(8,128)} %get-tuple-element.20.source) | copy-start | bytes 184324
  4.6 7.5 %collective-permute-start.1 = (f32[120,128]{1,0:T(8,128)S(1)}, f32[120,128]{1,0:T(8,128)S(1)}, u32[]{:S(2)}, u32[]{:S(2)}) collective-permute-start(f32[120,128]{1,0:T(8,128)S(1)} %pad_maximum_fusion.own), channel_id=1, source_target_pairs={{0,12},{4,8},{8,4},{12,0},{16,24},{20,28},{24,16},{28,20},{1,13},{... | collective-permute-start | bytes 184328 | tf_op jit(solution)/shard_map/ppermute | solution.py:1155
  9.6 5.6 %collective-permute-start.2 = (f32[120,128]{1,0:T(8,128)S(1)}, f32[120,128]{1,0:T(8,128)S(1)}, u32[]{:S(2)}, u32[]{:S(2)}) collective-permute-start(f32[120,128]{1,0:T(8,128)S(1)} %pad_maximum_fusion.own), channel_id=1, source_target_pairs={{0,8},{4,12},{8,0},{12,4},{16,28},{20,24},{24,20},{28,16},{1,9},{5... | collective-permute-start | bytes 184328 | tf_op jit(solution)/shard_map/ppermute | solution.py:1155
  9.6 5.6 %collective-permute-start.3 = (f32[120,128]{1,0:T(8,128)S(1)}, f32[120,128]{1,0:T(8,128)S(1)}, u32[]{:S(2)}, u32[]{:S(2)}) collective-permute-start(f32[120,128]{1,0:T(8,128)S(1)} %pad_maximum_fusion.own), channel_id=1, source_target_pairs={{0,4},{4,0},{8,12},{12,8},{16,20},{20,16},{24,28},{28,24},{1,5},{5... | collective-permute-start | bytes 184328 | tf_op jit(solution)/shard_map/ppermute | solution.py:1155
  15.4 8.3 %collective-permute-start.4 = (f32[424,128]{1,0:T(8,128)S(1)}, f32[424,128]{1,0:T(8,128)S(1)}, u32[]{:S(2)}, u32[]{:S(2)}) collective-permute-start(f32[424,128]{1,0:T(8,128)S(1)} %line.1.block0), channel_id=1, source_target_pairs={{0,1},{1,0},{2,3},{3,2},{16,18},{17,19},{18,16},{19,17},{4,5},{5,4... | collective-permute-start | bytes 651272 | tf_op jit(solution)/shard_map/ppermute | solution.py:1155
  17.0 10.5 %collective-permute-start.5 = (f32[424,128]{1,0:T(8,128)S(1)}, f32[424,128]{1,0:T(8,128)S(1)}, u32[]{:S(2)}, u32[]{:S(2)}) collective-permute-start(f32[424,128]{1,0:T(8,128)S(1)} %line.1.block0), channel_id=1, source_target_pairs={{0,2},{1,3},{2,0},{3,1},{16,17},{17,16},{18,19},{19,18},{4,6},{5,7... | collective-permute-start | bytes 651272 | tf_op jit(solution)/shard_map/ppermute | solution.py:1155
  18.5 9.0 %collective-permute-start.6 = (f32[424,128]{1,0:T(8,128)S(1)}, f32[424,128]{1,0:T(8,128)S(1)}, u32[]{:S(2)}, u32[]{:S(2)}) collective-permute-start(f32[424,128]{1,0:T(8,128)S(1)} %line.1.block0), channel_id=1, source_target_pairs={{0,3},{1,2},{2,1},{3,0},{16,19},{17,18},{18,17},{19,16},{4,7},{5,6... | collective-permute-start | bytes 651272 | tf_op jit(solution)/shard_map/ppermute | solution.py:1155
  27.5 1.4 %collective-permute-start.7 = (f32[256,128]{1,0:T(8,128)S(1)}, f32[256,128]{1,0:T(8,128)S(1)}, u32[]{:S(2)}, u32[]{:S(2)}) collective-permute-start(f32[256,128]{1,0:T(8,128)S(1)} %halves.1.own_halves), channel_id=1, source_target_pairs={{0,16},{16,0},{1,17},{17,1},{2,18},{18,2},{3,19},{19,3},{4,20},{20... | collective-permute-start | bytes 393224 | tf_op jit(solution)/shard_map/ppermute | solution.py:1149
  28.9 5.6 %collective-permute-start.8 = (f32[1024,128]{1,0:T(8,128)S(1)}, f32[1024,128]{1,0:T(8,128)S(1)}, u32[]{:S(2)}, u32[]{:S(2)}) collective-permute-start(f32[1024,128]{1,0:T(8,128)S(1)} %assemble.1.field.assembled.own_start), channel_id=1, source_target_pairs={{0,16},{16,0},{1,17},{17,1},{2,18},{18,2},{3,19},{19,3},{4,20},{20... | collective-permute-start | bytes 1572872 | tf_op jit(solution)/shard_map/ppermute | solution.py:1149
  34.5 2.1 %copy-start = (f32[2,5,5,160]{3,0,2,1:T(2,128)S(1)}, f32[2,5,5,160]{3,0,2,1:T(2,128)}, u32[]{:S(2)}) copy-start(f32[2,5,5,160]{3,0,2,1:T(2,128)} %param.6) | copy-start | bytes 96004
  34.5 2.1 %collective-permute-start.9 = (f32[1128,128]{1,0:T(8,128)S(1)}, f32[1128,128]{1,0:T(8,128)S(1)}, u32[]{:S(2)}, u32[]{:S(2)}) collective-permute-start(f32[1128,128]{1,0:T(8,128)S(1)} %cycle.1.own), channel_id=1, source_target_pairs={{0,16},{16,0},{1,17},{17,1},{2,18},{18,2},{3,19},{19,3},{4,20},{20... | collective-permute-start | bytes 1732616 | tf_op jit(solution)/shard_map/ppermute | solution.py:1149

commit v17 on v16

--- a/solution.py
+++ b/solution.py
@@ -422,10 +422,10 @@
     for s in range(2):
         for i in range(5):
             for j in range(5):
-                r = s * 32 + i * 5 + j
+                r = 2 * (i * 5 + j) + s
                 for m in range(5):
-                    rows[r, s * 32 + m * 5 + j] += kx[i, m]
-                    rows[r, s * 32 + i * 5 + m] += ky[j, m]
+                    rows[r, 2 * (m * 5 + j) + s] += kx[i, m]
+                    rows[r, 2 * (i * 5 + m) + s] += ky[j, m]
     return rows.astype(np.float32)
 
 
@@ -450,30 +450,26 @@
     return jnp.where(odd, nodes[half:, :], nodes[:half, :])
 
 
-def fetch(pairs, sems):
-    copies = [pltpu.make_async_copy(src, dst, sems.at[n]) for n, (src, dst) in enumerate(pairs)]
-    for copy in copies:
-        copy.start()
-    for copy in copies:
-        copy.wait()
-
-
 def local_kernel(
     rhs_in, guess_in, kappa_in, flags_in, rows_in, mine, theirs,
     rhs, guess, kappa, flags, rows_t, sems, stack, lines, nodes, y_faces, x_faces,
 ):
     sec = lax.axis_index("section")
-    fetch([(rhs_in, rhs), (guess_in, guess), (kappa_in, kappa), (flags_in, flags), (rows_in, rows_t)], sems)
-    stack[...] = jnp.zeros_like(stack)
+    pairs = [(guess_in, guess), (rhs_in, rhs), (rows_in, rows_t), (kappa_in, kappa), (flags_in, flags)]
+    copies = [pltpu.make_async_copy(source, target, sems.at[n]) for n, (source, target) in enumerate(pairs)]
+    for copy in copies:
+        copy.start()
+    for ref in (stack, nodes, y_faces, x_faces):
+        ref[...] = jnp.zeros_like(ref)
+    for copy in copies:
+        copy.wait()
     for i in range(5):
         stack[192 + 5 * i : 197 + 5 * i, :] = kappa[i]
         for j in range(5):
-            r = 5 * i + j
+            r = 2 * (5 * i + j)
             value = guess[i, j]
-            left = rhs[i, j] - value
-            for s in range(2):
-                stack[s * 32 + r : s * 32 + r + 1, :] = left[s : s + 1]
-                stack[128 + s * 32 + r : 128 + s * 32 + r + 1, :] = value[s : s + 1]
+            stack[128 + r : 130 + r, :] = value
+            stack[r : r + 2, :] = rhs[i, j] - value
     stack[64:128, :] = exact_dot(rows_t[...], stack[128:192, :])
     source = stack[...]
     for k in (0, 2, 4):
@@ -482,8 +478,11 @@
         if k < 4:
             lines[224 * k + 224 : 224 * k + 448, :] = shown[:, 128:]
 
-    def part(k, first):
-        return lines[224 * k + first : 224 * k + first + 32, :]
+    def part(k, first, s):
+        return lines[pl.ds(224 * k + first + s, 32, stride=2), :]
+
+    def kappa_part(k):
+        return lines[224 * k + 192 : 224 * k + 224, :]
 
     repeat = (iota((EZ, 128), 1) % EZ == iota((EZ, 128), 0)).astype(F32)
     shown = split_dot(flags[:, 0, 0, :].astype(F32), repeat)
@@ -494,33 +493,31 @@
     own = own + jnp.where(row % 5 == 0, gains[2], jnp.where(row % 5 == 4, gains[3], none))
     kz = element_matrix(5, 2)
     back, back_matrix = split_sections()[1:3]
-    for ref in (nodes, y_faces, x_faces):
-        ref[...] = jnp.zeros_like(ref)
+    fields = [[part(k, 128, s) for k in range(5)] for s in range(2)]
     for k in range(5):
-        diagonal = part(k, 192) + own
+        diagonal = kappa_part(k) + own
         if k == 0:
             diagonal = diagonal + gains[4]
         if k == 4:
             diagonal = diagonal + gains[5]
         images = []
         for s in range(2):
-            first = 128 + 32 * s
-            image = diagonal * part(k, first) + part(k, 64 + 32 * s)
+            image = diagonal * fields[s][k] + part(k, 64, s)
             for m in range(5):
-                image = image + float(kz[k, m]) * part(m, first)
+                image = image + float(kz[k, m]) * fields[s][m]
             if k == 0:
-                image = image - gains[4] * pltpu.roll(part(4, first), 1, 1)
+                image = image - gains[4] * pltpu.roll(fields[s][4], 1, 1)
             if k == 4:
-                image = image - gains[5] * pltpu.roll(part(0, first), 127, 1)
+                image = image - gains[5] * pltpu.roll(fields[s][0], 127, 1)
             images.append(image)
         for p, mark in enumerate((True, False)):
             total = jnp.zeros((32, 128), F32)
             trace = jnp.zeros((32, 128), F32)
             for s in range(2):
-                total = total + pair_factors(sec, back, mark, s) * part(k, 32 * s)
+                total = total + pair_factors(sec, back, mark, s) * part(k, 0, s)
                 factor = pair_factors(sec, STEP_SIZE * back_matrix, mark, s)
                 total = total - factor * images[s]
-                trace = trace + factor * part(k, 128 + 32 * s)
+                trace = trace + factor * fields[s][k]
             nodes[128 * p + 25 * k : 128 * p + 25 * k + 25, :] = total[:25]
             for i in range(5):
                 for f in range(2):
@@ -537,7 +534,7 @@
         out[HALF:FACE_X, :] = pack_nodes(y_faces[64 * p : 64 * p + 64, :])[:25]
         out[FACE_X:KAPPA, :] = pack_nodes(x_faces[32 * p : 32 * p + 32, :])[:15]
     for k in range(5):
-        nodes[25 * k : 25 * k + 25, :] = part(k, 192)[:25]
+        nodes[25 * k : 25 * k + 25, :] = kappa_part(k)[:25]
     kappas = choose(iota((32, 128), 1) // EZ, [nodes[32 * q : 32 * q + 32, :] for q in range(4)])
     mine[KAPPA:, :] = jnp.where(sec == 0, kappas[:16], kappas[16:])
 
@@ -1005,6 +1002,11 @@
     return (iota((256, 160), 1) == 5 * (lane % EZ) + k + lane // 128).astype(F32)
 
 
+def side_by_side(cols):
+    half = cols.shape[0] // 2
+    return jnp.concatenate([cols[:half, :], cols[half:, :]], axis=1)
+
+
 def early_kernel(own, own_start, other_start, sums, column_out, cols):
     weights = pair_weights()
     cols[...] = jnp.zeros_like(cols)
@@ -1015,15 +1017,15 @@
         z = own[FIELD + k * 25 : FIELD + k * 25 + 25, :]
         start, other = own_start[where, :], other_start[where, :]
         w = start - own[where, :]
-        side = slice(0, 128) if k % 2 == 0 else slice(128, 256)
+        side = 192 * (k % 2)
         for s in range(2):
-            cols[s * 32 : s * 32 + 25, side] = own_factors[s] * z
-            cols[64 + s * 32 : 64 + s * 32 + 25, side] = own_factors[s] * start + other_factors[s] * other
-            cols[128 + s * 32 : 128 + s * 32 + 25, side] = own_factors[s] * w
+            cols[pl.ds(side + s, 25, stride=2), :] = own_factors[s] * z
+            cols[pl.ds(side + 64 + s, 25, stride=2), :] = own_factors[s] * start + other_factors[s] * other
+            cols[pl.ds(side + 128 + s, 25, stride=2), :] = own_factors[s] * w
         if k % 2 == 1:
-            total = total + split_dot(cols[...], raw_order(k - 1))
-    cols[:, 128:] = jnp.zeros((192, 128), F32)
-    total = total + split_dot(cols[...], raw_order(4))
+            total = total + split_dot(side_by_side(cols), raw_order(k - 1))
+    cols[192:, :] = jnp.zeros((192, 128), F32)
+    total = total + split_dot(side_by_side(cols), raw_order(4))
     column_out[...] = total
     nothing = jnp.zeros((8, 128), F32)
     uppers, sizes = [nothing] * 5, [nothing] * 5
@@ -1037,6 +1039,21 @@
 
 
 def finish_kernel(own, other, own_start, other_start, sums, column, guess, sol, res_out, arnoldi, cols, outs):
+    cols[...] = jnp.zeros_like(cols)
+    total = jnp.zeros((128, 160), F32)
+    factors = column_factors(1)
+    for k in range(5):
+        where = column_rows(k)
+        z = other[FIELD + k * 25 : FIELD + k * 25 + 25, :]
+        w = other_start[where, :] - other[where, :]
+        side = 128 * (k % 2)
+        for s in range(2):
+            cols[pl.ds(side + s, 25, stride=2), :] = factors[s] * z
+            cols[pl.ds(side + 64 + s, 25, stride=2), :] = factors[s] * w
+        if k % 2 == 1:
+            total = total + split_dot(side_by_side(cols), raw_order(k - 1))
+    cols[128:, :] = jnp.zeros((128, 128), F32)
+    total = total + split_dot(side_by_side(cols), raw_order(4))
     weights = pair_weights()
     nothing = jnp.zeros((8, 128), F32)
     uppers = [nothing] * 5
@@ -1048,21 +1065,6 @@
     mine, theirs = sums[0:8, :], sum(uppers)
     size = sums[8:9, 0:1]
     upper = jnp.sum(mine + theirs, keepdims=True) / size
-    cols[...] = jnp.zeros_like(cols)
-    total = jnp.zeros((128, 160), F32)
-    factors = column_factors(1)
-    for k in range(5):
-        where = column_rows(k)
-        z = other[FIELD + k * 25 : FIELD + k * 25 + 25, :]
-        w = other_start[where, :] - other[where, :]
-        side = slice(0, 128) if k % 2 == 0 else slice(128, 256)
-        for s in range(2):
-            cols[s * 32 : s * 32 + 25, side] = factors[s] * z
-            cols[64 + s * 32 : 64 + s * 32 + 25, side] = factors[s] * w
-        if k % 2 == 1:
-            total = total + split_dot(cols[...], raw_order(k - 1))
-    cols[:, 128:] = jnp.zeros((128, 128), F32)
-    total = total + split_dot(cols[...], raw_order(4))
     rests = [nothing] * 5
     for r in range(125):
         c, d = own_start[tile(r), :], other_start[tile(r), :]
@@ -1080,10 +1082,9 @@
     outs[64:, :] = column[64:128, :] - weight * (column[128:, :] + total[64:])
     for i in range(5):
         for j in range(5):
-            r = 5 * i + j
-            for s in range(2):
-                sol[i, j, s : s + 1, :] = guess[i, j, s : s + 1, :] + outs[s * 32 + r : s * 32 + r + 1, :]
-                res_out[i, j, s : s + 1, :] = outs[64 + s * 32 + r : 64 + s * 32 + r + 1, :]
+            r = 2 * (5 * i + j)
+            sol[i, j] = guess[i, j] + outs[r : r + 2, :]
+            res_out[i, j] = outs[64 + r : 66 + r, :]
 
 
 def plain_call(kernel, name, rows, scratch, operands, cost=1_000_000):
@@ -1122,7 +1123,7 @@
         out_shape=[jax.ShapeDtypeStruct((16, 128), F32), jax.ShapeDtypeStruct((192, 160), F32)],
         in_specs=[VMEM] * 3,
         out_specs=[VMEM] * 2,
-        scratch_shapes=[pltpu.VMEM((192, 256), F32)],
+        scratch_shapes=[pltpu.VMEM((384, 128), F32)],
         compiler_params=limit(16),
         cost_estimate=pl.CostEstimate(flops=4_000_000, bytes_accessed=4_000_000, transcendentals=0),
         name="early",
@@ -1139,7 +1140,7 @@
         ],
         in_specs=[VMEM] * 7,
         out_specs=[VMEM, VMEM, pl.BlockSpec(memory_space=pltpu.SMEM)],
-        scratch_shapes=[pltpu.VMEM((128, 256), F32), pltpu.VMEM((128, 160), F32)],
+        scratch_shapes=[pltpu.VMEM((256, 128), F32), pltpu.VMEM((128, 160), F32)],
         compiler_params=limit(24),
         name="finish",
     )(own, other, own_start, other_start, sums, column, guess)

time: 38.4 us -> 38.3 us (level)
  no operation moved by 1% of the time
where the time goes in v17:
time: 38.3 us; the launch traced here: 38.1 us
  waiting for transfers between devices  15.5 us (40%)
  Pallas kernels  10.7 us (28%)
  starting transfers between devices  10.4 us (27%)
  local copies, waits for them, and re-layouts  0.83 us (2%)
  between operations  0.71 us (2%)
    ppermute x6, waiting for transfers between devices, exchange_by_core(): return lax.ppermute(x, ('section', axis), pairs)  13.5 us
    ppermute x6, starting transfers between devices, exchange_by_core(): return lax.ppermute(x, ('section', axis), pairs)  9.22 us
    pallas_call x1, Pallas kernels, cycle(): pl.pallas_call(cycle_kernel, out_shape=jax.ShapeDtypeStruct((FIELD + 128,...  5.08 us
    pallas_call x1, Pallas kernels, local_part(): pl.pallas_call(local_kernel, out_shape=[jax.ShapeDtypeStruct((rows, 128),...  2.35 us
    ppermute x4, waiting for transfers between devices, exchange(): lax.ppermute(x, axis, [(n, n ^ bits) for n in range(lax.axis_size(axis))])  1.98 us
    pallas_call x1, Pallas kernels, finish(): pl.pallas_call(finish_kernel, out_shape=[jax.ShapeDtypeStruct(guess.shape...  1.52 us
    ppermute x4, starting transfers between devices, exchange(): lax.ppermute(x, axis, [(n, n ^ bits) for n in range(lax.axis_size(axis))])  1.17 us
    pallas_call x4, Pallas kernels, plain_call(): pl.pallas_call(kernel, out_shape=jax.ShapeDtypeStruct((rows, 128), F32),...  1.08 us
  transfers between devices with their start and end apart: 10, of which 7 were waited for; matrix products, arithmetic and copies ran while one was open for 0% of the time, Pallas kernels for 17%

profile of v17, /device:TPU:0, one launch (start us, length us, event | category | flops | bytes accessed | tf_op | source)
XLA Modules:
  0.0 38.1 jit_solution(14282334680303313001)
XLA Ops:
  0.6 2.3 %local_part.1 = (f32[120,128]{1,0:T(8,128)}, f32[104,128]{1,0:T(8,128)}) custom-call(f32[5,5,2,160]{3,2,1,0:T(2,128)} %bitcast.6, f32[5,5,2,160]{3,2,1,0:T(2,128)} %bitcast.4, f32[5,5,160]{2,1,0:T(8,128)} %kappa_in.1, s32[6,1,1,32]{3,2,1,0:T(1,128)} %flags_in.1, f32[64,64]{1,0:T(8,128)} %constant.2.clone.rows_in), custom_call_target="tpu_custom_call" | custom-call | flops 20000000 | bytes 8000000 | tf_op jit(solution)/shard_map/local_part/pallas_call | solution.py:557
  3.0 0.5 %collective-permute-start = (f32[104,128]{1,0:T(8,128)}, f32[104,128]{1,0:T(8,128)S(1)}, u32[]{:S(2)}, u32[]{:S(2)}) collective-permute-start(f32[104,128]{1,0:T(8,128)} %get-tuple-element.19), channel_id=1, source_target_pairs={{0,16},{16,0},{1,17},{17,1},{2,18},{18,2},{3,19},{19,3},{4,20},{20... | collective-permute-start | bytes 159752 | tf_op jit(solution)/shard_map/ppermute | solution.py:1150
  3.5 0.0 copy-start.1
  3.5 0.8 %copy-done.1 = f32[120,128]{1,0:T(8,128)S(1)} copy-done((f32[120,128]{1,0:T(8,128)S(1)}, f32[120,128]{1,0:T(8,128)}, u32[]{:S(2)}) %copy-start.1) | copy-done | bytes 61464
  4.3 0.3 collective-permute-done
  4.6 5.0 %collective-permute-start.1 = (f32[120,128]{1,0:T(8,128)S(1)}, f32[120,128]{1,0:T(8,128)S(1)}, u32[]{:S(2)}, u32[]{:S(2)}) collective-permute-start(f32[120,128]{1,0:T(8,128)S(1)} %pad_maximum_fusion.own), channel_id=1, source_target_pairs={{0,12},{4,8},{8,4},{12,0},{16,24},{20,28},{24,16},{28,20},{1,13},{... | collective-permute-start | bytes 184328 | tf_op jit(solution)/shard_map/ppermute | solution.py:1156
  9.6 0.0 collective-permute-start.2
  9.6 0.6 %collective-permute-start.3 = (f32[120,128]{1,0:T(8,128)S(1)}, f32[120,128]{1,0:T(8,128)S(1)}, u32[]{:S(2)}, u32[]{:S(2)}) collective-permute-start(f32[120,128]{1,0:T(8,128)S(1)} %pad_maximum_fusion.own), channel_id=1, source_target_pairs={{0,4},{4,0},{8,12},{12,8},{16,20},{20,16},{24,28},{28,24},{1,5},{5... | collective-permute-start | bytes 184328 | tf_op jit(solution)/shard_map/ppermute | solution.py:1156
  10.3 1.8 %collective-permute-done.1.first = f32[120,128]{1,0:T(8,128)S(1)} collective-permute-done((f32[120,128]{1,0:T(8,128)S(1)}, f32[120,128]{1,0:T(8,128)S(1)}, u32[]{:S(2)}, u32[]{:S(2)}) %collective-permute-start.1) | collective-permute-done | bytes 61472 | tf_op jit(solution)/shard_map/ppermute | solution.py:1156
  12.1 3.1 %collective-permute-done.2.second = f32[120,128]{1,0:T(8,128)S(1)} collective-permute-done((f32[120,128]{1,0:T(8,128)S(1)}, f32[120,128]{1,0:T(8,128)S(1)}, u32[]{:S(2)}, u32[]{:S(2)}) %collective-permute-start.2) | collective-permute-done | bytes 61472 | tf_op jit(solution)/shard_map/ppermute | solution.py:1156
  15.2 0.0 collective-permute-done.3.third
  15.2 0.2 line.1.block0
  15.4 1.6 %collective-permute-start.4 = (f32[424,128]{1,0:T(8,128)S(1)}, f32[424,128]{1,0:T(8,128)S(1)}, u32[]{:S(2)}, u32[]{:S(2)}) collective-permute-start(f32[424,128]{1,0:T(8,128)S(1)} %line.1.block0), channel_id=1, source_target_pairs={{0,1},{1,0},{2,3},{3,2},{16,18},{17,19},{18,16},{19,17},{4,5},{5,4... | collective-permute-start | bytes 651272 | tf_op jit(solution)/shard_map/ppermute | solution.py:1156
  17.0 1.5 %collective-permute-start.5 = (f32[424,128]{1,0:T(8,128)S(1)}, f32[424,128]{1,0:T(8,128)S(1)}, u32[]{:S(2)}, u32[]{:S(2)}) collective-permute-start(f32[424,128]{1,0:T(8,128)S(1)} %line.1.block0), channel_id=1, source_target_pairs={{0,2},{1,3},{2,0},{3,1},{16,17},{17,16},{18,19},{19,18},{4,6},{5,7... | collective-permute-start | bytes 651272 | tf_op jit(solution)/shard_map/ppermute | solution.py:1156
  18.5 0.5 %collective-permute-start.6 = (f32[424,128]{1,0:T(8,128)S(1)}, f32[424,128]{1,0:T(8,128)S(1)}, u32[]{:S(2)}, u32[]{:S(2)}) collective-permute-start(f32[424,128]{1,0:T(8,128)S(1)} %line.1.block0), channel_id=1, source_target_pairs={{0,3},{1,2},{2,1},{3,0},{16,19},{17,18},{18,17},{19,16},{4,7},{5,6... | collective-permute-start | bytes 651272 | tf_op jit(solution)/shard_map/ppermute | solution.py:1156
  19.0 4.7 %collective-permute-done.4.block1 = f32[424,128]{1,0:T(8,128)S(1)} collective-permute-done((f32[424,128]{1,0:T(8,128)S(1)}, f32[424,128]{1,0:T(8,128)S(1)}, u32[]{:S(2)}, u32[]{:S(2)}) %collective-permute-start.4) | collective-permute-done | bytes 217120 | tf_op jit(solution)/shard_map/ppermute | solution.py:1156
  23.7 3.8 %collective-permute-done.5.block2 = f32[424,128]{1,0:T(8,128)S(1)} collective-permute-done((f32[424,128]{1,0:T(8,128)S(1)}, f32[424,128]{1,0:T(8,128)S(1)}, u32[]{:S(2)}, u32[]{:S(2)}) %collective-permute-start.5) | collective-permute-done | bytes 217120 | tf_op jit(solution)/shard_map/ppermute | solution.py:1156
  27.5 0.0 collective-permute-done.6.block3
  27.5 0.1 collective-permute-start.7
  27.6 0.6 %assemble.1.field.assembled.own_start = f32[1024,128]{1,0:T(8,128)S(1)} custom-call(f32[424,128]{1,0:T(8,128)S(1)} %line.1.block0, f32[424,128]{1,0:T(8,128)S(1)} %collective-permute-done.4.block1, f32[424,128]{1,0:T(8,128)S(1)} %collective-permute-done.5.block2, f32[424,128]{1,0:T(8,128)S(1)} %collective-permute-done.6.block3), custom_call_target="tpu_custom_call" | custom-call | flops 4000000 | bytes 4000000 | tf_op jit(solution)/shard_map/assemble/pallas_call | solution.py:1091
  28.2 0.8 %collective-permute-done.7.other_halves = f32[256,128]{1,0:T(8,128)S(1)} collective-permute-done((f32[256,128]{1,0:T(8,128)S(1)}, f32[256,128]{1,0:T(8,128)S(1)}, u32[]{:S(2)}, u32[]{:S(2)}) %collective-permute-start.7) | collective-permute-done | bytes 131104 | tf_op jit(solution)/shard_map/ppermute | solution.py:1150
  28.9 0.1 collective-permute-start.8
  29.1 0.3 setup.1.coefs
  29.4 5.1 %cycle.1.own = f32[1128,128]{1,0:T(8,128)S(1)} custom-call(f32[2704,128]{1,0:T(8,128)S(1)} %setup.1.coefs, f32[1024,128]{1,0:T(8,128)S(1)} %assemble.1.field.assembled.own_start), custom_call_target="tpu_custom_call" | custom-call | flops 40000000 | bytes 30000000 | tf_op jit(solution)/shard_map/cycle/pallas_call | solution.py:1108
  34.5 0.0 copy-start
  34.5 0.0 collective-permute-done.8.other_start
  34.5 0.4 %collective-permute-start.9 = (f32[1128,128]{1,0:T(8,128)S(1)}, f32[1128,128]{1,0:T(8,128)S(1)}, u32[]{:S(2)}, u32[]{:S(2)}) collective-permute-start(f32[1128,128]{1,0:T(8,128)S(1)} %cycle.1.own), channel_id=1, source_target_pairs={{0,16},{16,0},{1,17},{17,1},{2,18},{18,2},{3,19},{19,3},{4,20},{20... | collective-permute-start | bytes 1732616 | tf_op jit(solution)/shard_map/ppermute | solution.py:1150
  35.0 0.7 %early.1 = (f32[16,128]{1,0:T(8,128)S(1)}, f32[192,160]{1,0:T(8,128)S(1)}) custom-call(f32[1128,128]{1,0:T(8,128)S(1)} %cycle.1.own, f32[1024,128]{1,0:T(8,128)S(1)} %assemble.1.field.assembled.own_start, f32[1024,128]{1,0:T(8,128)S(1)} %collective-permute-done.8.other_start), custom_call_target="tpu_custom_call" | custom-call | flops 4000000 | bytes 4000000 | tf_op jit(solution)/shard_map/early/pallas_call | solution.py:1121
  35.6 1.0 %collective-permute-done.9.other = f32[1128,128]{1,0:T(8,128)S(1)} collective-permute-done((f32[1128,128]{1,0:T(8,128)S(1)}, f32[1128,128]{1,0:T(8,128)S(1)}, u32[]{:S(2)}, u32[]{:S(2)}) %collective-permute-start.9) | collective-permute-done | bytes 577568 | tf_op jit(solution)/shard_map/ppermute | solution.py:1150
  36.6 0.0 copy-done
  36.6 1.5 %finish.1 = (f32[5,5,2,160]{3,2,1,0:T(2,128)}, f32[5,5,2,160]{3,2,1,0:T(2,128)}, f32[3]{0:T(128)}) custom-call(f32[1128,128]{1,0:T(8,128)S(1)} %cycle.1.own, f32[1128,128]{1,0:T(8,128)S(1)} %collective-permute-done.9.other, f32[1024,128]{1,0:T(8,128)S(1)} %assemble.1.field.assembled.own_start, f32[1024,128]{1,0:T(8,128)S(1)} %collective-permute-done.8.other_start, ...), custom_call_target="tpu_custom_call" | custom-call | tf_op jit(solution)/shard_map/finish/pallas_call | solution.py:1134
  (4 shorter events, 0.0 us)
Async XLA Ops:
  3.0 1.6 %collective-permute-start = (f32[104,128]{1,0:T(8,128)}, f32[104,128]{1,0:T(8,128)S(1)}, u32[]{:S(2)}, u32[]{:S(2)}) collective-permute-start(f32[104,128]{1,0:T(8,128)} %get-tuple-element.19), channel_id=1, source_target_pairs={{0,16},{16,0},{1,17},{17,1},{2,18},{18,2},{3,19},{19,3},{4,20},{20... | collective-permute-start | bytes 159752 | tf_op jit(solution)/shard_map/ppermute | solution.py:1150
  3.5 0.8 %copy-start.1 = (f32[120,128]{1,0:T(8,128)S(1)}, f32[120,128]{1,0:T(8,128)}, u32[]{:S(2)}) copy-start(f32[120,128]{1,0:T(8,128)} %get-tuple-element.20.source) | copy-start | bytes 184324
  4.6 7.5 %collective-permute-start.1 = (f32[120,128]{1,0:T(8,128)S(1)}, f32[120,128]{1,0:T(8,128)S(1)}, u32[]{:S(2)}, u32[]{:S(2)}) collective-permute-start(f32[120,128]{1,0:T(8,128)S(1)} %pad_maximum_fusion.own), channel_id=1, source_target_pairs={{0,12},{4,8},{8,4},{12,0},{16,24},{20,28},{24,16},{28,20},{1,13},{... | collective-permute-start | bytes 184328 | tf_op jit(solution)/shard_map/ppermute | solution.py:1156
  9.6 5.6 %collective-permute-start.2 = (f32[120,128]{1,0:T(8,128)S(1)}, f32[120,128]{1,0:T(8,128)S(1)}, u32[]{:S(2)}, u32[]{:S(2)}) collective-permute-start(f32[120,128]{1,0:T(8,128)S(1)} %pad_maximum_fusion.own), channel_id=1, source_target_pairs={{0,8},{4,12},{8,0},{12,4},{16,28},{20,24},{24,20},{28,16},{1,9},{5... | collective-permute-start | bytes 184328 | tf_op jit(solution)/shard_map/ppermute | solution.py:1156
  9.6 5.6 %collective-permute-start.3 = (f32[120,128]{1,0:T(8,128)S(1)}, f32[120,128]{1,0:T(8,128)S(1)}, u32[]{:S(2)}, u32[]{:S(2)}) collective-permute-start(f32[120,128]{1,0:T(8,128)S(1)} %pad_maximum_fusion.own), channel_id=1, source_target_pairs={{0,4},{4,0},{8,12},{12,8},{16,20},{20,16},{24,28},{28,24},{1,5},{5... | collective-permute-start | bytes 184328 | tf_op jit(solution)/shard_map/ppermute | solution.py:1156
  15.4 8.3 %collective-permute-start.4 = (f32[424,128]{1,0:T(8,128)S(1)}, f32[424,128]{1,0:T(8,128)S(1)}, u32[]{:S(2)}, u32[]{:S(2)}) collective-permute-start(f32[424,128]{1,0:T(8,128)S(1)} %line.1.block0), channel_id=1, source_target_pairs={{0,1},{1,0},{2,3},{3,2},{16,18},{17,19},{18,16},{19,17},{4,5},{5,4... | collective-permute-start | bytes 651272 | tf_op jit(solution)/shard_map/ppermute | solution.py:1156
  17.0 10.5 %collective-permute-start.5 = (f32[424,128]{1,0:T(8,128)S(1)}, f32[424,128]{1,0:T(8,128)S(1)}, u32[]{:S(2)}, u32[]{:S(2)}) collective-permute-start(f32[424,128]{1,0:T(8,128)S(1)} %line.1.block0), channel_id=1, source_target_pairs={{0,2},{1,3},{2,0},{3,1},{16,17},{17,16},{18,19},{19,18},{4,6},{5,7... | collective-permute-start | bytes 651272 | tf_op jit(solution)/shard_map/ppermute | solution.py:1156
  18.5 9.0 %collective-permute-start.6 = (f32[424,128]{1,0:T(8,128)S(1)}, f32[424,128]{1,0:T(8,128)S(1)}, u32[]{:S(2)}, u32[]{:S(2)}) collective-permute-start(f32[424,128]{1,0:T(8,128)S(1)} %line.1.block0), channel_id=1, source_target_pairs={{0,3},{1,2},{2,1},{3,0},{16,19},{17,18},{18,17},{19,16},{4,7},{5,6... | collective-permute-start | bytes 651272 | tf_op jit(solution)/shard_map/ppermute | solution.py:1156
  27.5 1.4 %collective-permute-start.7 = (f32[256,128]{1,0:T(8,128)S(1)}, f32[256,128]{1,0:T(8,128)S(1)}, u32[]{:S(2)}, u32[]{:S(2)}) collective-permute-start(f32[256,128]{1,0:T(8,128)S(1)} %halves.1.own_halves), channel_id=1, source_target_pairs={{0,16},{16,0},{1,17},{17,1},{2,18},{18,2},{3,19},{19,3},{4,20},{20... | collective-permute-start | bytes 393224 | tf_op jit(solution)/shard_map/ppermute | solution.py:1150
  28.9 5.6 %collective-permute-start.8 = (f32[1024,128]{1,0:T(8,128)S(1)}, f32[1024,128]{1,0:T(8,128)S(1)}, u32[]{:S(2)}, u32[]{:S(2)}) collective-permute-start(f32[1024,128]{1,0:T(8,128)S(1)} %assemble.1.field.assembled.own_start), channel_id=1, source_target_pairs={{0,16},{16,0},{1,17},{17,1},{2,18},{18,2},{3,19},{19,3},{4,20},{20... | collective-permute-start | bytes 1572872 | tf_op jit(solution)/shard_map/ppermute | solution.py:1150
  34.5 2.1 %copy-start = (f32[2,5,5,160]{3,0,2,1:T(2,128)S(1)}, f32[2,5,5,160]{3,0,2,1:T(2,128)}, u32[]{:S(2)}) copy-start(f32[2,5,5,160]{3,0,2,1:T(2,128)} %param.6) | copy-start | bytes 96004
  34.5 2.1 %collective-permute-start.9 = (f32[1128,128]{1,0:T(8,128)S(1)}, f32[1128,128]{1,0:T(8,128)S(1)}, u32[]{:S(2)}, u32[]{:S(2)}) collective-permute-start(f32[1128,128]{1,0:T(8,128)S(1)} %cycle.1.own), channel_id=1, source_target_pairs={{0,16},{16,0},{1,17},{17,1},{2,18},{18,2},{3,19},{19,3},{4,20},{20... | collective-permute-start | bytes 1732616 | tf_op jit(solution)/shard_map/ppermute | solution.py:1150

commit v18 on v17

--- a/solution.py
+++ b/solution.py
@@ -794,7 +794,7 @@
                 store(coefs, DIAGS[p] + n**3 + (k * n + i) * n, scale * (1.0 / CENTRE))
 
 
-def cycle_kernel(coefs, assembled, fields, *scratch):
+def cycle_kernel(coefs, assembled, fields, more, *scratch):
     sec = lax.axis_index("section")
     my_gx, my_gy = lax.axis_index("gx"), lax.axis_index("gy")
     levels = [Level(n, scratch[4 * p : 4 * p + 4]) for p, n in enumerate((5, 3, 2))]
@@ -940,22 +940,31 @@
             return
         below = levels[p + 1]
 
+        def correct():
+            n, m = level.count, below.count
+            change(down(n, m), level.res, below.f, False)
+            begin(below, below.f)
+            solve(p + 1)
+            change(up(m, n), below.x, level.x, True)
+
+        if p == 1:
+            apply(level, True)
+            apply(level, False)
+            correct()
+            apply(level, False)
+            apply(level, True)
+            return
+
         def step(t, carry):
             @pl.when(t != 1)
             def _():
                 apply(level, True)
 
-            @pl.when((t != 2) | (p == 0))
-            def _():
-                apply(level, False)
+            apply(level, False)
 
             @pl.when(t == 0)
             def _():
-                n, m = level.count, below.count
-                change(down(n, m), level.res, below.f, False)
-                begin(below, below.f)
-                solve(p + 1)
-                change(up(m, n), below.x, level.x, True)
+                correct()
             return carry
         lax.fori_loop(0, 3, step, 0)
 
@@ -965,10 +974,28 @@
     solve(0)
 
     for first in range(0, 125, 5):
-        store(fields, first, load(fine.res, first, 5))
+        part, place = (fields, first) if first < SPLIT else (more, first - SPLIT)
+        store(part, place, load(fine.res, first, 5))
     column = (my_gx % 2) * 4 + my_gy
-    fields[FIELD : FIELD + 125, :] = fine.x[pl.ds(column, 125, stride=8), :]
-    fields[FIELD + 125 : FIELD + 128, :] = jnp.zeros((3, 128), F32)
+    more[AFTER : AFTER + 125, :] = fine.x[pl.ds(column, 125, stride=8), :]
+    more[AFTER + 125 :, :] = jnp.zeros((3, 128), F32)
+
+
+SPLIT = 75
+AFTER = 8 * (125 - SPLIT)
+
+
+def register(parts, r):
+    return parts[0][tile(r), :] if r < SPLIT else parts[1][tile(r - SPLIT), :]
+
+
+def column_of(parts, k):
+    first = 3 * (k // 3)
+    return parts[k // 3][column_rows(k - first), :]
+
+
+def column_z(parts, k):
+    return parts[1][AFTER + 25 * k : AFTER + 25 * k + 25, :]
 
 
 def pair_weights():
@@ -1007,16 +1034,17 @@
     return jnp.concatenate([cols[:half, :], cols[half:, :]], axis=1)
 
 
-def early_kernel(own, own_start, other_start, sums, column_out, cols):
+def early_kernel(own0, own1, own_start, other_start, sums, column_out, cols):
+    own = (own0, own1)
     weights = pair_weights()
     cols[...] = jnp.zeros_like(cols)
     total = jnp.zeros((192, 160), F32)
     own_factors, other_factors = column_factors(0), column_factors(1)
     for k in range(5):
         where = column_rows(k)
-        z = own[FIELD + k * 25 : FIELD + k * 25 + 25, :]
+        z = column_z(own, k)
         start, other = own_start[where, :], other_start[where, :]
-        w = start - own[where, :]
+        w = start - column_of(own, k)
         side = 192 * (k % 2)
         for s in range(2):
             cols[pl.ds(side + s, 25, stride=2), :] = own_factors[s] * z
@@ -1031,21 +1059,22 @@
     uppers, sizes = [nothing] * 5, [nothing] * 5
     for r in range(125):
         c, d = own_start[tile(r), :], other_start[tile(r), :]
-        a = c - own[tile(r), :]
+        a = c - register(own, r)
         uppers[r % 5] = uppers[r % 5] + a * (c + weights * d)
         sizes[r % 5] = sizes[r % 5] + ((c * c + d * d) + 2.0 * (weights * (c * d)))
     sums[0:8, :] = sum(uppers)
     sums[8:16, :] = jnp.broadcast_to(jnp.sum(sum(sizes), keepdims=True), (8, 128))
 
 
-def finish_kernel(own, other, own_start, other_start, sums, column, guess, sol, res_out, arnoldi, cols, outs):
+def finish_kernel(own0, own1, other0, other1, own_start, other_start, sums, column, guess, sol, res_out, arnoldi, cols, outs):
+    own, other = (own0, own1), (other0, other1)
     cols[...] = jnp.zeros_like(cols)
     total = jnp.zeros((128, 160), F32)
     factors = column_factors(1)
     for k in range(5):
         where = column_rows(k)
-        z = other[FIELD + k * 25 : FIELD + k * 25 + 25, :]
-        w = other_start[where, :] - other[where, :]
+        z = column_z(other, k)
+        w = other_start[where, :] - column_of(other, k)
         side = 128 * (k % 2)
         for s in range(2):
             cols[pl.ds(side + s, 25, stride=2), :] = factors[s] * z
@@ -1059,7 +1088,7 @@
     uppers = [nothing] * 5
     for r in range(125):
         c, d = own_start[tile(r), :], other_start[tile(r), :]
-        b = d - other[tile(r), :]
+        b = d - register(other, r)
         uppers[r % 5] = uppers[r % 5] + b * (d + weights * c)
 
     mine, theirs = sums[0:8, :], sum(uppers)
@@ -1068,8 +1097,8 @@
     rests = [nothing] * 5
     for r in range(125):
         c, d = own_start[tile(r), :], other_start[tile(r), :]
-        a = (c - own[tile(r), :]) - upper * c
-        b = (d - other[tile(r), :]) - upper * d
+        a = (c - register(own, r)) - upper * c
+        b = (d - register(other, r)) - upper * d
         rests[r % 5] = rests[r % 5] + ((a * a + b * b) + 2.0 * (weights * (a * b)))
     rest = jnp.sum(sum(rests), keepdims=True)
     beta = jnp.sqrt(size)
@@ -1107,9 +1136,9 @@
     scratch += [pltpu.VMEM((FIELD, 128), F32)]
     return pl.pallas_call(
         cycle_kernel,
-        out_shape=jax.ShapeDtypeStruct((FIELD + 128, 128), F32),
+        out_shape=[jax.ShapeDtypeStruct((rows, 128), F32) for rows in (SPLIT * 8, AFTER + 128)],
         in_specs=[VMEM] * 2,
-        out_specs=VMEM,
+        out_specs=[VMEM] * 2,
         scratch_shapes=scratch,
         compiler_params=limit(24),
         cost_estimate=pl.CostEstimate(flops=40_000_000, bytes_accessed=30_000_000, transcendentals=0),
@@ -1121,13 +1150,13 @@
     return pl.pallas_call(
         early_kernel,
         out_shape=[jax.ShapeDtypeStruct((16, 128), F32), jax.ShapeDtypeStruct((192, 160), F32)],
-        in_specs=[VMEM] * 3,
+        in_specs=[VMEM] * 4,
         out_specs=[VMEM] * 2,
         scratch_shapes=[pltpu.VMEM((384, 128), F32)],
         compiler_params=limit(16),
         cost_estimate=pl.CostEstimate(flops=4_000_000, bytes_accessed=4_000_000, transcendentals=0),
         name="early",
-    )(own, own_start, other_start)
+    )(*own, own_start, other_start)
 
 
 def finish(own, other, own_start, other_start, sums, column, guess):
@@ -1138,12 +1167,12 @@
             jax.ShapeDtypeStruct(guess.shape, F32),
             jax.ShapeDtypeStruct((3,), F32),
         ],
-        in_specs=[VMEM] * 7,
+        in_specs=[VMEM] * 9,
         out_specs=[VMEM, VMEM, pl.BlockSpec(memory_space=pltpu.SMEM)],
         scratch_shapes=[pltpu.VMEM((256, 128), F32), pltpu.VMEM((128, 160), F32)],
         compiler_params=limit(24),
         name="finish",
-    )(own, other, own_start, other_start, sums, column, guess)
+    )(*own, *other, own_start, other_start, sums, column, guess)
 
 
 def exchange(x, axis, bits):
@@ -1171,8 +1200,9 @@
     coefs = plain_call(setup_kernel, "setup", REGISTERS * 8, [128 * 8], (start, halves, other_halves))
     other_start = exchange(start, "section", 1)
     own, other_start = lax.optimization_barrier((cycle(coefs, start), other_start))
+    other = [exchange(part, "section", 1) for part in own]
     sums, column = early(own, start, other_start)
-    sol, res, arnoldi = finish(own, exchange(own, "section", 1), start, other_start, sums, column, guess)
+    sol, res, arnoldi = finish(own, other, start, other_start, sums, column, guess)
     sol, res = (jnp.transpose(v, (2, 0, 1, 3)) for v in (sol, res))
     return sol, res, arnoldi
 

time: 38.3 us -> 38.1 us (level)
    ppermute x4 -> x5, starting transfers between devices: 1.17 us -> 1.31 us  [exchange(): lax.ppermute(x, axis, [(n, n ^ bits) for n in range(lax.axis_size(axis))])]
    ppermute x4 -> x5, waiting for transfers between devices: 1.98 us -> 1.84 us  [exchange(): lax.ppermute(x, axis, [(n, n ^ bits) for n in range(lax.axis_size(axis))])]
  transfers between devices with their start and end apart: 10 -> 11, of which waited for: 7 -> 7; matrix products, arithmetic and copies ran while one was open for 0% -> 0% of each run, Pallas kernels for 17% -> 17%
where the time goes in v18:
time: 38.1 us; the launch traced here: 37.9 us
  waiting for transfers between devices  15.3 us (40%)
  Pallas kernels  10.5 us (28%)
  starting transfers between devices  10.5 us (28%)
  local copies, waits for them, and re-layouts  0.83 us (2%)
  between operations  0.71 us (2%)
    ppermute x6, waiting for transfers between devices, exchange_by_core(): return lax.ppermute(x, ('section', axis), pairs)  13.5 us
    ppermute x6, starting transfers between devices, exchange_by_core(): return lax.ppermute(x, ('section', axis), pairs)  9.22 us
    pallas_call x1, Pallas kernels, cycle(): pl.pallas_call(cycle_kernel, out_shape=[jax.ShapeDtypeStruct((rows, 128),...  4.9 us
    pallas_call x1, Pallas kernels, local_part(): pl.pallas_call(local_kernel, out_shape=[jax.ShapeDtypeStruct((rows, 128),...  2.35 us
    ppermute x5, waiting for transfers between devices, exchange(): lax.ppermute(x, axis, [(n, n ^ bits) for n in range(lax.axis_size(axis))])  1.84 us
    pallas_call x1, Pallas kernels, finish(): pl.pallas_call(finish_kernel, out_shape=[jax.ShapeDtypeStruct(guess.shape...  1.51 us
    ppermute x5, starting transfers between devices, exchange(): lax.ppermute(x, axis, [(n, n ^ bits) for n in range(lax.axis_size(axis))])  1.31 us
    pallas_call x4, Pallas kernels, plain_call(): pl.pallas_call(kernel, out_shape=jax.ShapeDtypeStruct((rows, 128), F32),...  1.08 us
  transfers between devices with their start and end apart: 11, of which 7 were waited for; matrix products, arithmetic and copies ran while one was open for 0% of the time, Pallas kernels for 17%

profile of v18, /device:TPU:0, one launch (start us, length us, event | category | flops | bytes accessed | tf_op | source)
XLA Modules:
  0.0 37.9 jit_solution(629418900016140323)
XLA Ops:
  0.6 2.3 %local_part.1 = (f32[120,128]{1,0:T(8,128)}, f32[104,128]{1,0:T(8,128)}) custom-call(f32[5,5,2,160]{3,2,1,0:T(2,128)} %bitcast.6, f32[5,5,2,160]{3,2,1,0:T(2,128)} %bitcast.4, f32[5,5,160]{2,1,0:T(8,128)} %kappa_in.1, s32[6,1,1,32]{3,2,1,0:T(1,128)} %flags_in.1, f32[64,64]{1,0:T(8,128)} %constant.2.clone.rows_in), custom_call_target="tpu_custom_call" | custom-call | flops 20000000 | bytes 8000000 | tf_op jit(solution)/shard_map/local_part/pallas_call | solution.py:557
  3.0 0.5 %collective-permute-start = (f32[104,128]{1,0:T(8,128)}, f32[104,128]{1,0:T(8,128)S(1)}, u32[]{:S(2)}, u32[]{:S(2)}) collective-permute-start(f32[104,128]{1,0:T(8,128)} %get-tuple-element.22), channel_id=1, source_target_pairs={{0,16},{16,0},{1,17},{17,1},{2,18},{18,2},{3,19},{19,3},{4,20},{20... | collective-permute-start | bytes 159752 | tf_op jit(solution)/shard_map/ppermute | solution.py:1179
  3.5 0.8 %copy-done.1 = f32[120,128]{1,0:T(8,128)S(1)} copy-done((f32[120,128]{1,0:T(8,128)S(1)}, f32[120,128]{1,0:T(8,128)}, u32[]{:S(2)}) %copy-start.1) | copy-done | bytes 61464
  4.3 0.3 collective-permute-done
  4.6 5.0 %collective-permute-start.1 = (f32[120,128]{1,0:T(8,128)S(1)}, f32[120,128]{1,0:T(8,128)S(1)}, u32[]{:S(2)}, u32[]{:S(2)}) collective-permute-start(f32[120,128]{1,0:T(8,128)S(1)} %pad_maximum_fusion.own), channel_id=1, source_target_pairs={{0,12},{4,8},{8,4},{12,0},{16,24},{20,28},{24,16},{28,20},{1,13},{... | collective-permute-start | bytes 184328 | tf_op jit(solution)/shard_map/ppermute | solution.py:1185
  9.6 0.0 collective-permute-start.2
  9.6 0.6 %collective-permute-start.3 = (f32[120,128]{1,0:T(8,128)S(1)}, f32[120,128]{1,0:T(8,128)S(1)}, u32[]{:S(2)}, u32[]{:S(2)}) collective-permute-start(f32[120,128]{1,0:T(8,128)S(1)} %pad_maximum_fusion.own), channel_id=1, source_target_pairs={{0,4},{4,0},{8,12},{12,8},{16,20},{20,16},{24,28},{28,24},{1,5},{5... | collective-permute-start | bytes 184328 | tf_op jit(solution)/shard_map/ppermute | solution.py:1185
  10.3 1.8 %collective-permute-done.1.first = f32[120,128]{1,0:T(8,128)S(1)} collective-permute-done((f32[120,128]{1,0:T(8,128)S(1)}, f32[120,128]{1,0:T(8,128)S(1)}, u32[]{:S(2)}, u32[]{:S(2)}) %collective-permute-start.1) | collective-permute-done | bytes 61472 | tf_op jit(solution)/shard_map/ppermute | solution.py:1185
  12.1 3.1 %collective-permute-done.2.second = f32[120,128]{1,0:T(8,128)S(1)} collective-permute-done((f32[120,128]{1,0:T(8,128)S(1)}, f32[120,128]{1,0:T(8,128)S(1)}, u32[]{:S(2)}, u32[]{:S(2)}) %collective-permute-start.2) | collective-permute-done | bytes 61472 | tf_op jit(solution)/shard_map/ppermute | solution.py:1185
  15.2 0.0 collective-permute-done.3.third
  15.2 0.2 line.1.block0
  15.4 1.6 %collective-permute-start.4 = (f32[424,128]{1,0:T(8,128)S(1)}, f32[424,128]{1,0:T(8,128)S(1)}, u32[]{:S(2)}, u32[]{:S(2)}) collective-permute-start(f32[424,128]{1,0:T(8,128)S(1)} %line.1.block0), channel_id=1, source_target_pairs={{0,1},{1,0},{2,3},{3,2},{16,18},{17,19},{18,16},{19,17},{4,5},{5,4... | collective-permute-start | bytes 651272 | tf_op jit(solution)/shard_map/ppermute | solution.py:1185
  17.0 1.5 %collective-permute-start.5 = (f32[424,128]{1,0:T(8,128)S(1)}, f32[424,128]{1,0:T(8,128)S(1)}, u32[]{:S(2)}, u32[]{:S(2)}) collective-permute-start(f32[424,128]{1,0:T(8,128)S(1)} %line.1.block0), channel_id=1, source_target_pairs={{0,2},{1,3},{2,0},{3,1},{16,17},{17,16},{18,19},{19,18},{4,6},{5,7... | collective-permute-start | bytes 651272 | tf_op jit(solution)/shard_map/ppermute | solution.py:1185
  18.5 0.5 %collective-permute-start.6 = (f32[424,128]{1,0:T(8,128)S(1)}, f32[424,128]{1,0:T(8,128)S(1)}, u32[]{:S(2)}, u32[]{:S(2)}) collective-permute-start(f32[424,128]{1,0:T(8,128)S(1)} %line.1.block0), channel_id=1, source_target_pairs={{0,3},{1,2},{2,1},{3,0},{16,19},{17,18},{18,17},{19,16},{4,7},{5,6... | collective-permute-start | bytes 651272 | tf_op jit(solution)/shard_map/ppermute | solution.py:1185
  19.0 4.7 %collective-permute-done.4.block1 = f32[424,128]{1,0:T(8,128)S(1)} collective-permute-done((f32[424,128]{1,0:T(8,128)S(1)}, f32[424,128]{1,0:T(8,128)S(1)}, u32[]{:S(2)}, u32[]{:S(2)}) %collective-permute-start.4) | collective-permute-done | bytes 217120 | tf_op jit(solution)/shard_map/ppermute | solution.py:1185
  23.7 3.8 %collective-permute-done.5.block2 = f32[424,128]{1,0:T(8,128)S(1)} collective-permute-done((f32[424,128]{1,0:T(8,128)S(1)}, f32[424,128]{1,0:T(8,128)S(1)}, u32[]{:S(2)}, u32[]{:S(2)}) %collective-permute-start.5) | collective-permute-done | bytes 217120 | tf_op jit(solution)/shard_map/ppermute | solution.py:1185
  27.5 0.0 collective-permute-done.6.block3
  27.5 0.1 collective-permute-start.7
  27.6 0.6 %assemble.1.field.assembled.own_start = f32[1024,128]{1,0:T(8,128)S(1)} custom-call(f32[424,128]{1,0:T(8,128)S(1)} %line.1.block0, f32[424,128]{1,0:T(8,128)S(1)} %collective-permute-done.4.block1, f32[424,128]{1,0:T(8,128)S(1)} %collective-permute-done.5.block2, f32[424,128]{1,0:T(8,128)S(1)} %collective-permute-done.6.block3), custom_call_target="tpu_custom_call" | custom-call | flops 4000000 | bytes 4000000 | tf_op jit(solution)/shard_map/assemble/pallas_call | solution.py:1120
  28.2 0.8 %collective-permute-done.7.other_halves = f32[256,128]{1,0:T(8,128)S(1)} collective-permute-done((f32[256,128]{1,0:T(8,128)S(1)}, f32[256,128]{1,0:T(8,128)S(1)}, u32[]{:S(2)}, u32[]{:S(2)}) %collective-permute-start.7) | collective-permute-done | bytes 131104 | tf_op jit(solution)/shard_map/ppermute | solution.py:1179
  29.0 0.1 collective-permute-start.8
  29.1 0.3 setup.1.coefs
  29.4 0.0 copy-start
  29.4 4.9 %cycle.1 = (f32[600,128]{1,0:T(8,128)S(1)}, f32[528,128]{1,0:T(8,128)S(1)}) custom-call(f32[2704,128]{1,0:T(8,128)S(1)} %setup.1.coefs, f32[1024,128]{1,0:T(8,128)S(1)} %assemble.1.field.assembled.own_start), custom_call_target="tpu_custom_call" | custom-call | flops 40000000 | bytes 30000000 | tf_op jit(solution)/shard_map/cycle/pallas_call | solution.py:1137
  34.3 0.0 collective-permute-done.8.other_start
  34.3 0.4 %collective-permute-start.9 = (f32[600,128]{1,0:T(8,128)S(1)}, f32[600,128]{1,0:T(8,128)S(1)}, u32[]{:S(2)}, u32[]{:S(2)}) collective-permute-start(f32[600,128]{1,0:T(8,128)S(1)} %get-tuple-element.33.own0), channel_id=1, source_target_pairs={{0,16},{16,0},{1,17},{17,1},{2,18},{18,2},{3,19},{19,3},{4,20},{20... | collective-permute-start | bytes 921608 | tf_op jit(solution)/shard_map/ppermute | solution.py:1179
  34.8 0.1 collective-permute-start.10
  34.9 0.7 %early.1 = (f32[16,128]{1,0:T(8,128)S(1)}, f32[192,160]{1,0:T(8,128)S(1)}) custom-call(f32[600,128]{1,0:T(8,128)S(1)} %get-tuple-element.33.own0, f32[528,128]{1,0:T(8,128)S(1)} %get-tuple-element.34.own1, f32[1024,128]{1,0:T(8,128)S(1)} %assemble.1.field.assembled.own_start, f32[1024,128]{1,0:T(8,128)S(1)} %collective-permute-done.8.other_start), custom_call_target="tpu_custom_call" | custom-call | flops 4000000 | bytes 4000000 | tf_op jit(solution)/shard_map/early/pallas_call | solution.py:1150
  35.6 0.8 %collective-permute-done.10.other1 = f32[528,128]{1,0:T(8,128)S(1)} collective-permute-done((f32[528,128]{1,0:T(8,128)S(1)}, f32[528,128]{1,0:T(8,128)S(1)}, u32[]{:S(2)}, u32[]{:S(2)}) %collective-permute-start.10) | collective-permute-done | bytes 270368 | tf_op jit(solution)/shard_map/ppermute | solution.py:1179
  36.4 0.0 collective-permute-done.9.other0
  36.4 0.0 copy-done
  36.4 1.5 %finish.1 = (f32[5,5,2,160]{3,2,1,0:T(2,128)}, f32[5,5,2,160]{3,2,1,0:T(2,128)}, f32[3]{0:T(128)}) custom-call(f32[600,128]{1,0:T(8,128)S(1)} %get-tuple-element.33.own0, f32[528,128]{1,0:T(8,128)S(1)} %get-tuple-element.34.own1, f32[600,128]{1,0:T(8,128)S(1)} %collective-permute-done.9.other0, f32[528,128]{1,0:T(8,128)S(1)} %collective-permute-done.10.other1, ...), custom_call_target="tpu_custom_call" | custom-call | tf_op jit(solution)/shard_map/finish/pallas_call | solution.py:1163
  (5 shorter events, 0.0 us)
Async XLA Ops:
  3.0 1.6 %collective-permute-start = (f32[104,128]{1,0:T(8,128)}, f32[104,128]{1,0:T(8,128)S(1)}, u32[]{:S(2)}, u32[]{:S(2)}) collective-permute-start(f32[104,128]{1,0:T(8,128)} %get-tuple-element.22), channel_id=1, source_target_pairs={{0,16},{16,0},{1,17},{17,1},{2,18},{18,2},{3,19},{19,3},{4,20},{20... | collective-permute-start | bytes 159752 | tf_op jit(solution)/shard_map/ppermute | solution.py:1179
  3.5 0.8 %copy-start.1 = (f32[120,128]{1,0:T(8,128)S(1)}, f32[120,128]{1,0:T(8,128)}, u32[]{:S(2)}) copy-start(f32[120,128]{1,0:T(8,128)} %get-tuple-element.23.source) | copy-start | bytes 184324
  4.6 7.5 %collective-permute-start.1 = (f32[120,128]{1,0:T(8,128)S(1)}, f32[120,128]{1,0:T(8,128)S(1)}, u32[]{:S(2)}, u32[]{:S(2)}) collective-permute-start(f32[120,128]{1,0:T(8,128)S(1)} %pad_maximum_fusion.own), channel_id=1, source_target_pairs={{0,12},{4,8},{8,4},{12,0},{16,24},{20,28},{24,16},{28,20},{1,13},{... | collective-permute-start | bytes 184328 | tf_op jit(solution)/shard_map/ppermute | solution.py:1185
  9.6 5.6 %collective-permute-start.2 = (f32[120,128]{1,0:T(8,128)S(1)}, f32[120,128]{1,0:T(8,128)S(1)}, u32[]{:S(2)}, u32[]{:S(2)}) collective-permute-start(f32[120,128]{1,0:T(8,128)S(1)} %pad_maximum_fusion.own), channel_id=1, source_target_pairs={{0,8},{4,12},{8,0},{12,4},{16,28},{20,24},{24,20},{28,16},{1,9},{5... | collective-permute-start | bytes 184328 | tf_op jit(solution)/shard_map/ppermute | solution.py:1185
  9.6 5.6 %collective-permute-start.3 = (f32[120,128]{1,0:T(8,128)S(1)}, f32[120,128]{1,0:T(8,128)S(1)}, u32[]{:S(2)}, u32[]{:S(2)}) collective-permute-start(f32[120,128]{1,0:T(8,128)S(1)} %pad_maximum_fusion.own), channel_id=1, source_target_pairs={{0,4},{4,0},{8,12},{12,8},{16,20},{20,16},{24,28},{28,24},{1,5},{5... | collective-permute-start | bytes 184328 | tf_op jit(solution)/shard_map/ppermute | solution.py:1185
  15.4 8.3 %collective-permute-start.4 = (f32[424,128]{1,0:T(8,128)S(1)}, f32[424,128]{1,0:T(8,128)S(1)}, u32[]{:S(2)}, u32[]{:S(2)}) collective-permute-start(f32[424,128]{1,0:T(8,128)S(1)} %line.1.block0), channel_id=1, source_target_pairs={{0,1},{1,0},{2,3},{3,2},{16,18},{17,19},{18,16},{19,17},{4,5},{5,4... | collective-permute-start | bytes 651272 | tf_op jit(solution)/shard_map/ppermute | solution.py:1185
  17.0 10.5 %collective-permute-start.5 = (f32[424,128]{1,0:T(8,128)S(1)}, f32[424,128]{1,0:T(8,128)S(1)}, u32[]{:S(2)}, u32[]{:S(2)}) collective-permute-start(f32[424,128]{1,0:T(8,128)S(1)} %line.1.block0), channel_id=1, source_target_pairs={{0,2},{1,3},{2,0},{3,1},{16,17},{17,16},{18,19},{19,18},{4,6},{5,7... | collective-permute-start | bytes 651272 | tf_op jit(solution)/shard_map/ppermute | solution.py:1185
  18.5 9.0 %collective-permute-start.6 = (f32[424,128]{1,0:T(8,128)S(1)}, f32[424,128]{1,0:T(8,128)S(1)}, u32[]{:S(2)}, u32[]{:S(2)}) collective-permute-start(f32[424,128]{1,0:T(8,128)S(1)} %line.1.block0), channel_id=1, source_target_pairs={{0,3},{1,2},{2,1},{3,0},{16,19},{17,18},{18,17},{19,16},{4,7},{5,6... | collective-permute-start | bytes 651272 | tf_op jit(solution)/shard_map/ppermute | solution.py:1185
  27.5 1.4 %collective-permute-start.7 = (f32[256,128]{1,0:T(8,128)S(1)}, f32[256,128]{1,0:T(8,128)S(1)}, u32[]{:S(2)}, u32[]{:S(2)}) collective-permute-start(f32[256,128]{1,0:T(8,128)S(1)} %halves.1.own_halves), channel_id=1, source_target_pairs={{0,16},{16,0},{1,17},{17,1},{2,18},{18,2},{3,19},{19,3},{4,20},{20... | collective-permute-start | bytes 393224 | tf_op jit(solution)/shard_map/ppermute | solution.py:1179
  29.0 5.4 %collective-permute-start.8 = (f32[1024,128]{1,0:T(8,128)S(1)}, f32[1024,128]{1,0:T(8,128)S(1)}, u32[]{:S(2)}, u32[]{:S(2)}) collective-permute-start(f32[1024,128]{1,0:T(8,128)S(1)} %assemble.1.field.assembled.own_start), channel_id=1, source_target_pairs={{0,16},{16,0},{1,17},{17,1},{2,18},{18,2},{3,19},{19,3},{4,20},{20... | collective-permute-start | bytes 1572872 | tf_op jit(solution)/shard_map/ppermute | solution.py:1179
  29.4 7.0 %copy-start = (f32[2,5,5,160]{3,0,2,1:T(2,128)S(1)}, f32[2,5,5,160]{3,0,2,1:T(2,128)}, u32[]{:S(2)}) copy-start(f32[2,5,5,160]{3,0,2,1:T(2,128)} %param.6) | copy-start | bytes 96004
  34.3 2.1 %collective-permute-start.9 = (f32[600,128]{1,0:T(8,128)S(1)}, f32[600,128]{1,0:T(8,128)S(1)}, u32[]{:S(2)}, u32[]{:S(2)}) collective-permute-start(f32[600,128]{1,0:T(8,128)S(1)} %get-tuple-element.33.own0), channel_id=1, source_target_pairs={{0,16},{16,0},{1,17},{17,1},{2,18},{18,2},{3,19},{19,3},{4,20},{20... | collective-permute-start | bytes 921608 | tf_op jit(solution)/shard_map/ppermute | solution.py:1179
  34.8 1.6 %collective-permute-start.10 = (f32[528,128]{1,0:T(8,128)S(1)}, f32[528,128]{1,0:T(8,128)S(1)}, u32[]{:S(2)}, u32[]{:S(2)}) collective-permute-start(f32[528,128]{1,0:T(8,128)S(1)} %get-tuple-element.34.own1), channel_id=1, source_target_pairs={{0,16},{16,0},{1,17},{17,1},{2,18},{18,2},{3,19},{19,3},{4,20},{20... | collective-permute-start | bytes 811016 | tf_op jit(solution)/shard_map/ppermute | solution.py:1179

commit v19 on v18

--- a/solution.py
+++ b/solution.py
@@ -602,7 +602,7 @@
 
 
 ORDER_X = ((3, 2), (2, 3), (1, 1))
-ORDER_Y = ((1, 2), (2, 1), (3, 3))
+ORDER_Y = ((3, 3), (1, 2), (2, 1))
 
 
 def partner(bits):

time: 38.1 us -> 37.7 us (0.990)
  waiting for transfers between devices: 15.3 us -> 14.9 us
    ppermute x6, waiting for transfers between devices: 13.5 us -> 13.1 us  [exchange_by_core(): return lax.ppermute(x, ('section', axis), pairs)]
where the time goes in v19:
time: 37.7 us; the launch traced here: 37.5 us
  waiting for transfers between devices  14.9 us (40%)
  Pallas kernels  10.5 us (28%)
  starting transfers between devices  10.5 us (28%)
  local copies, waits for them, and re-layouts  0.83 us (2%)
  between operations  0.71 us (2%)
    ppermute x6, waiting for transfers between devices, exchange_by_core(): return lax.ppermute(x, ('section', axis), pairs)  13.1 us
    ppermute x6, starting transfers between devices, exchange_by_core(): return lax.ppermute(x, ('section', axis), pairs)  9.22 us
    pallas_call x1, Pallas kernels, cycle(): pl.pallas_call(cycle_kernel, out_shape=[jax.ShapeDtypeStruct((rows, 128),...  4.9 us
    pallas_call x1, Pallas kernels, local_part(): pl.pallas_call(local_kernel, out_shape=[jax.ShapeDtypeStruct((rows, 128),...  2.35 us
    ppermute x5, waiting for transfers between devices, exchange(): lax.ppermute(x, axis, [(n, n ^ bits) for n in range(lax.axis_size(axis))])  1.84 us
    pallas_call x1, Pallas kernels, finish(): pl.pallas_call(finish_kernel, out_shape=[jax.ShapeDtypeStruct(guess.shape...  1.51 us
    ppermute x5, starting transfers between devices, exchange(): lax.ppermute(x, axis, [(n, n ^ bits) for n in range(lax.axis_size(axis))])  1.31 us
    pallas_call x4, Pallas kernels, plain_call(): pl.pallas_call(kernel, out_shape=jax.ShapeDtypeStruct((rows, 128), F32),...  1.09 us
  transfers between devices with their start and end apart: 11, of which 7 were waited for; matrix products, arithmetic and copies ran while one was open for 0% of the time, Pallas kernels for 17%

profile of v19, /device:TPU:0, one launch (start us, length us, event | category | flops | bytes accessed | tf_op | source)
XLA Modules:
  0.0 37.5 jit_solution(18060891165991495225)
XLA Ops:
  0.6 2.3 %local_part.1 = (f32[120,128]{1,0:T(8,128)}, f32[104,128]{1,0:T(8,128)}) custom-call(f32[5,5,2,160]{3,2,1,0:T(2,128)} %bitcast.6, f32[5,5,2,160]{3,2,1,0:T(2,128)} %bitcast.4, f32[5,5,160]{2,1,0:T(8,128)} %kappa_in.1, s32[6,1,1,32]{3,2,1,0:T(1,128)} %flags_in.1, f32[64,64]{1,0:T(8,128)} %constant.2.clone.rows_in), custom_call_target="tpu_custom_call" | custom-call | flops 20000000 | bytes 8000000 | tf_op jit(solution)/shard_map/local_part/pallas_call | solution.py:557
  3.0 0.5 %collective-permute-start = (f32[104,128]{1,0:T(8,128)}, f32[104,128]{1,0:T(8,128)S(1)}, u32[]{:S(2)}, u32[]{:S(2)}) collective-permute-start(f32[104,128]{1,0:T(8,128)} %get-tuple-element.22), channel_id=1, source_target_pairs={{0,16},{16,0},{1,17},{17,1},{2,18},{18,2},{3,19},{19,3},{4,20},{20... | collective-permute-start | bytes 159752 | tf_op jit(solution)/shard_map/ppermute | solution.py:1179
  3.5 0.8 %copy-done.1 = f32[120,128]{1,0:T(8,128)S(1)} copy-done((f32[120,128]{1,0:T(8,128)S(1)}, f32[120,128]{1,0:T(8,128)}, u32[]{:S(2)}) %copy-start.1) | copy-done | bytes 61464
  4.3 0.3 collective-permute-done
  4.6 5.0 %collective-permute-start.1 = (f32[120,128]{1,0:T(8,128)S(1)}, f32[120,128]{1,0:T(8,128)S(1)}, u32[]{:S(2)}, u32[]{:S(2)}) collective-permute-start(f32[120,128]{1,0:T(8,128)S(1)} %pad_maximum_fusion.own), channel_id=1, source_target_pairs={{0,12},{4,8},{8,4},{12,0},{16,24},{20,28},{24,16},{28,20},{1,13},{... | collective-permute-start | bytes 184328 | tf_op jit(solution)/shard_map/ppermute | solution.py:1185
  9.6 0.0 collective-permute-start.2
  9.6 0.6 %collective-permute-start.3 = (f32[120,128]{1,0:T(8,128)S(1)}, f32[120,128]{1,0:T(8,128)S(1)}, u32[]{:S(2)}, u32[]{:S(2)}) collective-permute-start(f32[120,128]{1,0:T(8,128)S(1)} %pad_maximum_fusion.own), channel_id=1, source_target_pairs={{0,4},{4,0},{8,12},{12,8},{16,20},{20,16},{24,28},{28,24},{1,5},{5... | collective-permute-start | bytes 184328 | tf_op jit(solution)/shard_map/ppermute | solution.py:1185
  10.3 1.8 %collective-permute-done.1.first = f32[120,128]{1,0:T(8,128)S(1)} collective-permute-done((f32[120,128]{1,0:T(8,128)S(1)}, f32[120,128]{1,0:T(8,128)S(1)}, u32[]{:S(2)}, u32[]{:S(2)}) %collective-permute-start.1) | collective-permute-done | bytes 61472 | tf_op jit(solution)/shard_map/ppermute | solution.py:1185
  12.1 3.1 %collective-permute-done.2.second = f32[120,128]{1,0:T(8,128)S(1)} collective-permute-done((f32[120,128]{1,0:T(8,128)S(1)}, f32[120,128]{1,0:T(8,128)S(1)}, u32[]{:S(2)}, u32[]{:S(2)}) %collective-permute-start.2) | collective-permute-done | bytes 61472 | tf_op jit(solution)/shard_map/ppermute | solution.py:1185
  15.2 0.0 collective-permute-done.3.third
  15.2 0.2 line.1.block0
  15.4 2.5 %collective-permute-start.4 = (f32[424,128]{1,0:T(8,128)S(1)}, f32[424,128]{1,0:T(8,128)S(1)}, u32[]{:S(2)}, u32[]{:S(2)}) collective-permute-start(f32[424,128]{1,0:T(8,128)S(1)} %line.1.block0), channel_id=1, source_target_pairs={{0,3},{1,2},{2,1},{3,0},{16,19},{17,18},{18,17},{19,16},{4,7},{5,6... | collective-permute-start | bytes 651272 | tf_op jit(solution)/shard_map/ppermute | solution.py:1185
  17.9 0.5 %collective-permute-start.5 = (f32[424,128]{1,0:T(8,128)S(1)}, f32[424,128]{1,0:T(8,128)S(1)}, u32[]{:S(2)}, u32[]{:S(2)}) collective-permute-start(f32[424,128]{1,0:T(8,128)S(1)} %line.1.block0), channel_id=1, source_target_pairs={{0,1},{1,0},{2,3},{3,2},{16,18},{17,19},{18,16},{19,17},{4,5},{5,4... | collective-permute-start | bytes 651272 | tf_op jit(solution)/shard_map/ppermute | solution.py:1185
  18.5 0.5 %collective-permute-start.6 = (f32[424,128]{1,0:T(8,128)S(1)}, f32[424,128]{1,0:T(8,128)S(1)}, u32[]{:S(2)}, u32[]{:S(2)}) collective-permute-start(f32[424,128]{1,0:T(8,128)S(1)} %line.1.block0), channel_id=1, source_target_pairs={{0,2},{1,3},{2,0},{3,1},{16,17},{17,16},{18,19},{19,18},{4,6},{5,7... | collective-permute-start | bytes 651272 | tf_op jit(solution)/shard_map/ppermute | solution.py:1185
  19.0 5.6 %collective-permute-done.4.block1 = f32[424,128]{1,0:T(8,128)S(1)} collective-permute-done((f32[424,128]{1,0:T(8,128)S(1)}, f32[424,128]{1,0:T(8,128)S(1)}, u32[]{:S(2)}, u32[]{:S(2)}) %collective-permute-start.4) | collective-permute-done | bytes 217120 | tf_op jit(solution)/shard_map/ppermute | solution.py:1185
  24.5 2.6 %collective-permute-done.5.block2 = f32[424,128]{1,0:T(8,128)S(1)} collective-permute-done((f32[424,128]{1,0:T(8,128)S(1)}, f32[424,128]{1,0:T(8,128)S(1)}, u32[]{:S(2)}, u32[]{:S(2)}) %collective-permute-start.5) | collective-permute-done | bytes 217120 | tf_op jit(solution)/shard_map/ppermute | solution.py:1185
  27.1 0.0 collective-permute-done.6.block3
  27.1 0.1 collective-permute-start.7
  27.2 0.6 %assemble.1.field.assembled.own_start = f32[1024,128]{1,0:T(8,128)S(1)} custom-call(f32[424,128]{1,0:T(8,128)S(1)} %line.1.block0, f32[424,128]{1,0:T(8,128)S(1)} %collective-permute-done.4.block1, f32[424,128]{1,0:T(8,128)S(1)} %collective-permute-done.5.block2, f32[424,128]{1,0:T(8,128)S(1)} %collective-permute-done.6.block3), custom_call_target="tpu_custom_call" | custom-call | flops 4000000 | bytes 4000000 | tf_op jit(solution)/shard_map/assemble/pallas_call | solution.py:1120
  27.8 0.8 %collective-permute-done.7.other_halves = f32[256,128]{1,0:T(8,128)S(1)} collective-permute-done((f32[256,128]{1,0:T(8,128)S(1)}, f32[256,128]{1,0:T(8,128)S(1)}, u32[]{:S(2)}, u32[]{:S(2)}) %collective-permute-start.7) | collective-permute-done | bytes 131104 | tf_op jit(solution)/shard_map/ppermute | solution.py:1179
  28.5 0.1 collective-permute-start.8
  28.7 0.3 setup.1.coefs
  29.0 0.0 copy-start
  29.0 4.9 %cycle.1 = (f32[600,128]{1,0:T(8,128)S(1)}, f32[528,128]{1,0:T(8,128)S(1)}) custom-call(f32[2704,128]{1,0:T(8,128)S(1)} %setup.1.coefs, f32[1024,128]{1,0:T(8,128)S(1)} %assemble.1.field.assembled.own_start), custom_call_target="tpu_custom_call" | custom-call | flops 40000000 | bytes 30000000 | tf_op jit(solution)/shard_map/cycle/pallas_call | solution.py:1137
  33.9 0.0 collective-permute-done.8.other_start
  33.9 0.4 %collective-permute-start.9 = (f32[600,128]{1,0:T(8,128)S(1)}, f32[600,128]{1,0:T(8,128)S(1)}, u32[]{:S(2)}, u32[]{:S(2)}) collective-permute-start(f32[600,128]{1,0:T(8,128)S(1)} %get-tuple-element.33.own0), channel_id=1, source_target_pairs={{0,16},{16,0},{1,17},{17,1},{2,18},{18,2},{3,19},{19,3},{4,20},{20... | collective-permute-start | bytes 921608 | tf_op jit(solution)/shard_map/ppermute | solution.py:1179
  34.4 0.1 collective-permute-start.10
  34.5 0.7 %early.1 = (f32[16,128]{1,0:T(8,128)S(1)}, f32[192,160]{1,0:T(8,128)S(1)}) custom-call(f32[600,128]{1,0:T(8,128)S(1)} %get-tuple-element.33.own0, f32[528,128]{1,0:T(8,128)S(1)} %get-tuple-element.34.own1, f32[1024,128]{1,0:T(8,128)S(1)} %assemble.1.field.assembled.own_start, f32[1024,128]{1,0:T(8,128)S(1)} %collective-permute-done.8.other_start), custom_call_target="tpu_custom_call" | custom-call | flops 4000000 | bytes 4000000 | tf_op jit(solution)/shard_map/early/pallas_call | solution.py:1150
  35.2 0.8 %collective-permute-done.10.other1 = f32[528,128]{1,0:T(8,128)S(1)} collective-permute-done((f32[528,128]{1,0:T(8,128)S(1)}, f32[528,128]{1,0:T(8,128)S(1)}, u32[]{:S(2)}, u32[]{:S(2)}) %collective-permute-start.10) | collective-permute-done | bytes 270368 | tf_op jit(solution)/shard_map/ppermute | solution.py:1179
  36.0 0.0 collective-permute-done.9.other0
  36.0 0.0 copy-done
  36.0 1.5 %finish.1 = (f32[5,5,2,160]{3,2,1,0:T(2,128)}, f32[5,5,2,160]{3,2,1,0:T(2,128)}, f32[3]{0:T(128)}) custom-call(f32[600,128]{1,0:T(8,128)S(1)} %get-tuple-element.33.own0, f32[528,128]{1,0:T(8,128)S(1)} %get-tuple-element.34.own1, f32[600,128]{1,0:T(8,128)S(1)} %collective-permute-done.9.other0, f32[528,128]{1,0:T(8,128)S(1)} %collective-permute-done.10.other1, ...), custom_call_target="tpu_custom_call" | custom-call | tf_op jit(solution)/shard_map/finish/pallas_call | solution.py:1163
  (5 shorter events, 0.0 us)
Async XLA Ops:
  3.0 1.6 %collective-permute-start = (f32[104,128]{1,0:T(8,128)}, f32[104,128]{1,0:T(8,128)S(1)}, u32[]{:S(2)}, u32[]{:S(2)}) collective-permute-start(f32[104,128]{1,0:T(8,128)} %get-tuple-element.22), channel_id=1, source_target_pairs={{0,16},{16,0},{1,17},{17,1},{2,18},{18,2},{3,19},{19,3},{4,20},{20... | collective-permute-start | bytes 159752 | tf_op jit(solution)/shard_map/ppermute | solution.py:1179
  3.5 0.8 %copy-start.1 = (f32[120,128]{1,0:T(8,128)S(1)}, f32[120,128]{1,0:T(8,128)}, u32[]{:S(2)}) copy-start(f32[120,128]{1,0:T(8,128)} %get-tuple-element.23.source) | copy-start | bytes 184324
  4.6 7.5 %collective-permute-start.1 = (f32[120,128]{1,0:T(8,128)S(1)}, f32[120,128]{1,0:T(8,128)S(1)}, u32[]{:S(2)}, u32[]{:S(2)}) collective-permute-start(f32[120,128]{1,0:T(8,128)S(1)} %pad_maximum_fusion.own), channel_id=1, source_target_pairs={{0,12},{4,8},{8,4},{12,0},{16,24},{20,28},{24,16},{28,20},{1,13},{... | collective-permute-start | bytes 184328 | tf_op jit(solution)/shard_map/ppermute | solution.py:1185
  9.6 5.6 %collective-permute-start.2 = (f32[120,128]{1,0:T(8,128)S(1)}, f32[120,128]{1,0:T(8,128)S(1)}, u32[]{:S(2)}, u32[]{:S(2)}) collective-permute-start(f32[120,128]{1,0:T(8,128)S(1)} %pad_maximum_fusion.own), channel_id=1, source_target_pairs={{0,8},{4,12},{8,0},{12,4},{16,28},{20,24},{24,20},{28,16},{1,9},{5... | collective-permute-start | bytes 184328 | tf_op jit(solution)/shard_map/ppermute | solution.py:1185
  9.6 5.6 %collective-permute-start.3 = (f32[120,128]{1,0:T(8,128)S(1)}, f32[120,128]{1,0:T(8,128)S(1)}, u32[]{:S(2)}, u32[]{:S(2)}) collective-permute-start(f32[120,128]{1,0:T(8,128)S(1)} %pad_maximum_fusion.own), channel_id=1, source_target_pairs={{0,4},{4,0},{8,12},{12,8},{16,20},{20,16},{24,28},{28,24},{1,5},{5... | collective-permute-start | bytes 184328 | tf_op jit(solution)/shard_map/ppermute | solution.py:1185
  15.4 9.1 %collective-permute-start.4 = (f32[424,128]{1,0:T(8,128)S(1)}, f32[424,128]{1,0:T(8,128)S(1)}, u32[]{:S(2)}, u32[]{:S(2)}) collective-permute-start(f32[424,128]{1,0:T(8,128)S(1)} %line.1.block0), channel_id=1, source_target_pairs={{0,3},{1,2},{2,1},{3,0},{16,19},{17,18},{18,17},{19,16},{4,7},{5,6... | collective-permute-start | bytes 651272 | tf_op jit(solution)/shard_map/ppermute | solution.py:1185
  17.9 9.2 %collective-permute-start.5 = (f32[424,128]{1,0:T(8,128)S(1)}, f32[424,128]{1,0:T(8,128)S(1)}, u32[]{:S(2)}, u32[]{:S(2)}) collective-permute-start(f32[424,128]{1,0:T(8,128)S(1)} %line.1.block0), channel_id=1, source_target_pairs={{0,1},{1,0},{2,3},{3,2},{16,18},{17,19},{18,16},{19,17},{4,5},{5,4... | collective-permute-start | bytes 651272 | tf_op jit(solution)/shard_map/ppermute | solution.py:1185
  18.5 8.6 %collective-permute-start.6 = (f32[424,128]{1,0:T(8,128)S(1)}, f32[424,128]{1,0:T(8,128)S(1)}, u32[]{:S(2)}, u32[]{:S(2)}) collective-permute-start(f32[424,128]{1,0:T(8,128)S(1)} %line.1.block0), channel_id=1, source_target_pairs={{0,2},{1,3},{2,0},{3,1},{16,17},{17,16},{18,19},{19,18},{4,6},{5,7... | collective-permute-start | bytes 651272 | tf_op jit(solution)/shard_map/ppermute | solution.py:1185
  27.1 1.4 %collective-permute-start.7 = (f32[256,128]{1,0:T(8,128)S(1)}, f32[256,128]{1,0:T(8,128)S(1)}, u32[]{:S(2)}, u32[]{:S(2)}) collective-permute-start(f32[256,128]{1,0:T(8,128)S(1)} %halves.1.own_halves), channel_id=1, source_target_pairs={{0,16},{16,0},{1,17},{17,1},{2,18},{18,2},{3,19},{19,3},{4,20},{20... | collective-permute-start | bytes 393224 | tf_op jit(solution)/shard_map/ppermute | solution.py:1179
  28.5 5.4 %collective-permute-start.8 = (f32[1024,128]{1,0:T(8,128)S(1)}, f32[1024,128]{1,0:T(8,128)S(1)}, u32[]{:S(2)}, u32[]{:S(2)}) collective-permute-start(f32[1024,128]{1,0:T(8,128)S(1)} %assemble.1.field.assembled.own_start), channel_id=1, source_target_pairs={{0,16},{16,0},{1,17},{17,1},{2,18},{18,2},{3,19},{19,3},{4,20},{20... | collective-permute-start | bytes 1572872 | tf_op jit(solution)/shard_map/ppermute | solution.py:1179
  29.0 7.0 %copy-start = (f32[2,5,5,160]{3,0,2,1:T(2,128)S(1)}, f32[2,5,5,160]{3,0,2,1:T(2,128)}, u32[]{:S(2)}) copy-start(f32[2,5,5,160]{3,0,2,1:T(2,128)} %param.6) | copy-start | bytes 96004
  33.9 2.1 %collective-permute-start.9 = (f32[600,128]{1,0:T(8,128)S(1)}, f32[600,128]{1,0:T(8,128)S(1)}, u32[]{:S(2)}, u32[]{:S(2)}) collective-permute-start(f32[600,128]{1,0:T(8,128)S(1)} %get-tuple-element.33.own0), channel_id=1, source_target_pairs={{0,16},{16,0},{1,17},{17,1},{2,18},{18,2},{3,19},{19,3},{4,20},{20... | collective-permute-start | bytes 921608 | tf_op jit(solution)/shard_map/ppermute | solution.py:1179
  34.4 1.6 %collective-permute-start.10 = (f32[528,128]{1,0:T(8,128)S(1)}, f32[528,128]{1,0:T(8,128)S(1)}, u32[]{:S(2)}, u32[]{:S(2)}) collective-permute-start(f32[528,128]{1,0:T(8,128)S(1)} %get-tuple-element.34.own1), channel_id=1, source_target_pairs={{0,16},{16,0},{1,17},{17,1},{2,18},{18,2},{3,19},{19,3},{4,20},{20... | collective-permute-start | bytes 811016 | tf_op jit(solution)/shard_map/ppermute | solution.py:1179

commit v20 on v19

--- a/solution.py
+++ b/solution.py
@@ -601,7 +601,7 @@
     return pieces[pl.ds(8 * h * size + r, 8, stride=size), :]
 
 
-ORDER_X = ((3, 2), (2, 3), (1, 1))
+ORDER_X = ((2, 3), (3, 2), (1, 1))
 ORDER_Y = ((3, 3), (1, 2), (2, 1))
 
 

time: 37.7 us -> 38.9 us (1.032)
  waiting for transfers between devices: 14.9 us -> 16.1 us
    ppermute x6, waiting for transfers between devices: 13.1 us -> 14.3 us  [exchange_by_core(): return lax.ppermute(x, ('section', axis), pairs)]
  transfers between devices with their start and end apart: 11 -> 11, of which waited for: 7 -> 8; matrix products, arithmetic and copies ran while one was open for 0% -> 0% of each run, Pallas kernels for 17% -> 17%
where the time goes in v20:
time: 38.9 us; the launch traced here: 38.7 us
  waiting for transfers between devices  16.1 us (41%)
  Pallas kernels  10.5 us (27%)
  starting transfers between devices  10.5 us (27%)
  local copies, waits for them, and re-layouts  0.83 us (2%)
  between operations  0.71 us (2%)
    ppermute x6, waiting for transfers between devices, exchange_by_core(): return lax.ppermute(x, ('section', axis), pairs)  14.3 us
    ppermute x6, starting transfers between devices, exchange_by_core(): return lax.ppermute(x, ('section', axis), pairs)  9.14 us
    pallas_call x1, Pallas kernels, cycle(): pl.pallas_call(cycle_kernel, out_shape=[jax.ShapeDtypeStruct((rows, 128),...  4.9 us
    pallas_call x1, Pallas kernels, local_part(): pl.pallas_call(local_kernel, out_shape=[jax.ShapeDtypeStruct((rows, 128),...  2.35 us
    ppermute x5, waiting for transfers between devices, exchange(): lax.ppermute(x, axis, [(n, n ^ bits) for n in range(lax.axis_size(axis))])  1.84 us
    pallas_call x1, Pallas kernels, finish(): pl.pallas_call(finish_kernel, out_shape=[jax.ShapeDtypeStruct(guess.shape...  1.51 us
    ppermute x5, starting transfers between devices, exchange(): lax.ppermute(x, axis, [(n, n ^ bits) for n in range(lax.axis_size(axis))])  1.31 us
    pallas_call x4, Pallas kernels, plain_call(): pl.pallas_call(kernel, out_shape=jax.ShapeDtypeStruct((rows, 128), F32),...  1.09 us
  transfers between devices with their start and end apart: 11, of which 8 were waited for; matrix products, arithmetic and copies ran while one was open for 0% of the time, Pallas kernels for 17%

profile of v20, /device:TPU:0, one launch (start us, length us, event | category | flops | bytes accessed | tf_op | source)
XLA Modules:
  0.0 38.7 jit_solution(5707474015676455035)
XLA Ops:
  0.6 2.3 %local_part.1 = (f32[120,128]{1,0:T(8,128)}, f32[104,128]{1,0:T(8,128)}) custom-call(f32[5,5,2,160]{3,2,1,0:T(2,128)} %bitcast.6, f32[5,5,2,160]{3,2,1,0:T(2,128)} %bitcast.4, f32[5,5,160]{2,1,0:T(8,128)} %kappa_in.1, s32[6,1,1,32]{3,2,1,0:T(1,128)} %flags_in.1, f32[64,64]{1,0:T(8,128)} %constant.2.clone.rows_in), custom_call_target="tpu_custom_call" | custom-call | flops 20000000 | bytes 8000000 | tf_op jit(solution)/shard_map/local_part/pallas_call | solution.py:557
  3.0 0.5 %collective-permute-start = (f32[104,128]{1,0:T(8,128)}, f32[104,128]{1,0:T(8,128)S(1)}, u32[]{:S(2)}, u32[]{:S(2)}) collective-permute-start(f32[104,128]{1,0:T(8,128)} %get-tuple-element.22), channel_id=1, source_target_pairs={{0,16},{16,0},{1,17},{17,1},{2,18},{18,2},{3,19},{19,3},{4,20},{20... | collective-permute-start | bytes 159752 | tf_op jit(solution)/shard_map/ppermute | solution.py:1179
  3.5 0.8 %copy-done.1 = f32[120,128]{1,0:T(8,128)S(1)} copy-done((f32[120,128]{1,0:T(8,128)S(1)}, f32[120,128]{1,0:T(8,128)}, u32[]{:S(2)}) %copy-start.1) | copy-done | bytes 61464
  4.3 0.3 collective-permute-done
  4.6 4.0 %collective-permute-start.1 = (f32[120,128]{1,0:T(8,128)S(1)}, f32[120,128]{1,0:T(8,128)S(1)}, u32[]{:S(2)}, u32[]{:S(2)}) collective-permute-start(f32[120,128]{1,0:T(8,128)S(1)} %pad_maximum_fusion.own), channel_id=1, source_target_pairs={{0,8},{4,12},{8,0},{12,4},{16,28},{20,24},{24,20},{28,16},{1,9},{5... | collective-permute-start | bytes 184328 | tf_op jit(solution)/shard_map/ppermute | solution.py:1185
  8.6 1.3 %collective-permute-start.2 = (f32[120,128]{1,0:T(8,128)S(1)}, f32[120,128]{1,0:T(8,128)S(1)}, u32[]{:S(2)}, u32[]{:S(2)}) collective-permute-start(f32[120,128]{1,0:T(8,128)S(1)} %pad_maximum_fusion.own), channel_id=1, source_target_pairs={{0,12},{4,8},{8,4},{12,0},{16,24},{20,28},{24,16},{28,20},{1,13},{... | collective-permute-start | bytes 184328 | tf_op jit(solution)/shard_map/ppermute | solution.py:1185
  10.0 0.2 collective-permute-start.3
  10.2 2.9 %collective-permute-done.1.first = f32[120,128]{1,0:T(8,128)S(1)} collective-permute-done((f32[120,128]{1,0:T(8,128)S(1)}, f32[120,128]{1,0:T(8,128)S(1)}, u32[]{:S(2)}, u32[]{:S(2)}) %collective-permute-start.1) | collective-permute-done | bytes 61472 | tf_op jit(solution)/shard_map/ppermute | solution.py:1185
  13.1 2.0 %collective-permute-done.2.second = f32[120,128]{1,0:T(8,128)S(1)} collective-permute-done((f32[120,128]{1,0:T(8,128)S(1)}, f32[120,128]{1,0:T(8,128)S(1)}, u32[]{:S(2)}, u32[]{:S(2)}) %collective-permute-start.2) | collective-permute-done | bytes 61472 | tf_op jit(solution)/shard_map/ppermute | solution.py:1185
  15.1 0.1 collective-permute-done.3.third
  15.2 0.2 line.1.block0
  15.4 2.6 %collective-permute-start.4 = (f32[424,128]{1,0:T(8,128)S(1)}, f32[424,128]{1,0:T(8,128)S(1)}, u32[]{:S(2)}, u32[]{:S(2)}) collective-permute-start(f32[424,128]{1,0:T(8,128)S(1)} %line.1.block0), channel_id=1, source_target_pairs={{0,3},{1,2},{2,1},{3,0},{16,19},{17,18},{18,17},{19,16},{4,7},{5,6... | collective-permute-start | bytes 651272 | tf_op jit(solution)/shard_map/ppermute | solution.py:1185
  18.0 0.5 %collective-permute-start.5 = (f32[424,128]{1,0:T(8,128)S(1)}, f32[424,128]{1,0:T(8,128)S(1)}, u32[]{:S(2)}, u32[]{:S(2)}) collective-permute-start(f32[424,128]{1,0:T(8,128)S(1)} %line.1.block0), channel_id=1, source_target_pairs={{0,1},{1,0},{2,3},{3,2},{16,18},{17,19},{18,16},{19,17},{4,5},{5,4... | collective-permute-start | bytes 651272 | tf_op jit(solution)/shard_map/ppermute | solution.py:1185
  18.5 0.5 %collective-permute-start.6 = (f32[424,128]{1,0:T(8,128)S(1)}, f32[424,128]{1,0:T(8,128)S(1)}, u32[]{:S(2)}, u32[]{:S(2)}) collective-permute-start(f32[424,128]{1,0:T(8,128)S(1)} %line.1.block0), channel_id=1, source_target_pairs={{0,2},{1,3},{2,0},{3,1},{16,17},{17,16},{18,19},{19,18},{4,6},{5,7... | collective-permute-start | bytes 651272 | tf_op jit(solution)/shard_map/ppermute | solution.py:1185
  19.0 5.7 %collective-permute-done.4.block1 = f32[424,128]{1,0:T(8,128)S(1)} collective-permute-done((f32[424,128]{1,0:T(8,128)S(1)}, f32[424,128]{1,0:T(8,128)S(1)}, u32[]{:S(2)}, u32[]{:S(2)}) %collective-permute-start.4) | collective-permute-done | bytes 217120 | tf_op jit(solution)/shard_map/ppermute | solution.py:1185
  24.7 3.6 %collective-permute-done.5.block2 = f32[424,128]{1,0:T(8,128)S(1)} collective-permute-done((f32[424,128]{1,0:T(8,128)S(1)}, f32[424,128]{1,0:T(8,128)S(1)}, u32[]{:S(2)}, u32[]{:S(2)}) %collective-permute-start.5) | collective-permute-done | bytes 217120 | tf_op jit(solution)/shard_map/ppermute | solution.py:1185
  28.2 0.0 collective-permute-done.6.block3
  28.3 0.1 collective-permute-start.7
  28.4 0.6 %assemble.1.field.assembled.own_start = f32[1024,128]{1,0:T(8,128)S(1)} custom-call(f32[424,128]{1,0:T(8,128)S(1)} %line.1.block0, f32[424,128]{1,0:T(8,128)S(1)} %collective-permute-done.4.block1, f32[424,128]{1,0:T(8,128)S(1)} %collective-permute-done.5.block2, f32[424,128]{1,0:T(8,128)S(1)} %collective-permute-done.6.block3), custom_call_target="tpu_custom_call" | custom-call | flops 4000000 | bytes 4000000 | tf_op jit(solution)/shard_map/assemble/pallas_call | solution.py:1120
  28.9 0.8 %collective-permute-done.7.other_halves = f32[256,128]{1,0:T(8,128)S(1)} collective-permute-done((f32[256,128]{1,0:T(8,128)S(1)}, f32[256,128]{1,0:T(8,128)S(1)}, u32[]{:S(2)}, u32[]{:S(2)}) %collective-permute-start.7) | collective-permute-done | bytes 131104 | tf_op jit(solution)/shard_map/ppermute | solution.py:1179
  29.7 0.1 collective-permute-start.8
  29.8 0.3 setup.1.coefs
  30.2 0.0 copy-start
  30.2 4.9 %cycle.1 = (f32[600,128]{1,0:T(8,128)S(1)}, f32[528,128]{1,0:T(8,128)S(1)}) custom-call(f32[2704,128]{1,0:T(8,128)S(1)} %setup.1.coefs, f32[1024,128]{1,0:T(8,128)S(1)} %assemble.1.field.assembled.own_start), custom_call_target="tpu_custom_call" | custom-call | flops 40000000 | bytes 30000000 | tf_op jit(solution)/shard_map/cycle/pallas_call | solution.py:1137
  35.1 0.0 collective-permute-done.8.other_start
  35.1 0.4 %collective-permute-start.9 = (f32[600,128]{1,0:T(8,128)S(1)}, f32[600,128]{1,0:T(8,128)S(1)}, u32[]{:S(2)}, u32[]{:S(2)}) collective-permute-start(f32[600,128]{1,0:T(8,128)S(1)} %get-tuple-element.33.own0), channel_id=1, source_target_pairs={{0,16},{16,0},{1,17},{17,1},{2,18},{18,2},{3,19},{19,3},{4,20},{20... | collective-permute-start | bytes 921608 | tf_op jit(solution)/shard_map/ppermute | solution.py:1179
  35.5 0.1 collective-permute-start.10
  35.7 0.7 %early.1 = (f32[16,128]{1,0:T(8,128)S(1)}, f32[192,160]{1,0:T(8,128)S(1)}) custom-call(f32[600,128]{1,0:T(8,128)S(1)} %get-tuple-element.33.own0, f32[528,128]{1,0:T(8,128)S(1)} %get-tuple-element.34.own1, f32[1024,128]{1,0:T(8,128)S(1)} %assemble.1.field.assembled.own_start, f32[1024,128]{1,0:T(8,128)S(1)} %collective-permute-done.8.other_start), custom_call_target="tpu_custom_call" | custom-call | flops 4000000 | bytes 4000000 | tf_op jit(solution)/shard_map/early/pallas_call | solution.py:1150
  36.3 0.8 %collective-permute-done.10.other1 = f32[528,128]{1,0:T(8,128)S(1)} collective-permute-done((f32[528,128]{1,0:T(8,128)S(1)}, f32[528,128]{1,0:T(8,128)S(1)}, u32[]{:S(2)}, u32[]{:S(2)}) %collective-permute-start.10) | collective-permute-done | bytes 270368 | tf_op jit(solution)/shard_map/ppermute | solution.py:1179
  37.1 0.0 collective-permute-done.9.other0
  37.1 0.0 copy-done
  37.1 1.5 %finish.1 = (f32[5,5,2,160]{3,2,1,0:T(2,128)}, f32[5,5,2,160]{3,2,1,0:T(2,128)}, f32[3]{0:T(128)}) custom-call(f32[600,128]{1,0:T(8,128)S(1)} %get-tuple-element.33.own0, f32[528,128]{1,0:T(8,128)S(1)} %get-tuple-element.34.own1, f32[600,128]{1,0:T(8,128)S(1)} %collective-permute-done.9.other0, f32[528,128]{1,0:T(8,128)S(1)} %collective-permute-done.10.other1, ...), custom_call_target="tpu_custom_call" | custom-call | tf_op jit(solution)/shard_map/finish/pallas_call | solution.py:1163
  (5 shorter events, 0.0 us)
Async XLA Ops:
  3.0 1.6 %collective-permute-start = (f32[104,128]{1,0:T(8,128)}, f32[104,128]{1,0:T(8,128)S(1)}, u32[]{:S(2)}, u32[]{:S(2)}) collective-permute-start(f32[104,128]{1,0:T(8,128)} %get-tuple-element.22), channel_id=1, source_target_pairs={{0,16},{16,0},{1,17},{17,1},{2,18},{18,2},{3,19},{19,3},{4,20},{20... | collective-permute-start | bytes 159752 | tf_op jit(solution)/shard_map/ppermute | solution.py:1179
  3.5 0.8 %copy-start.1 = (f32[120,128]{1,0:T(8,128)S(1)}, f32[120,128]{1,0:T(8,128)}, u32[]{:S(2)}) copy-start(f32[120,128]{1,0:T(8,128)} %get-tuple-element.23.source) | copy-start | bytes 184324
  4.6 8.5 %collective-permute-start.1 = (f32[120,128]{1,0:T(8,128)S(1)}, f32[120,128]{1,0:T(8,128)S(1)}, u32[]{:S(2)}, u32[]{:S(2)}) collective-permute-start(f32[120,128]{1,0:T(8,128)S(1)} %pad_maximum_fusion.own), channel_id=1, source_target_pairs={{0,8},{4,12},{8,0},{12,4},{16,28},{20,24},{24,20},{28,16},{1,9},{5... | collective-permute-start | bytes 184328 | tf_op jit(solution)/shard_map/ppermute | solution.py:1185
  8.6 6.5 %collective-permute-start.2 = (f32[120,128]{1,0:T(8,128)S(1)}, f32[120,128]{1,0:T(8,128)S(1)}, u32[]{:S(2)}, u32[]{:S(2)}) collective-permute-start(f32[120,128]{1,0:T(8,128)S(1)} %pad_maximum_fusion.own), channel_id=1, source_target_pairs={{0,12},{4,8},{8,4},{12,0},{16,24},{20,28},{24,16},{28,20},{1,13},{... | collective-permute-start | bytes 184328 | tf_op jit(solution)/shard_map/ppermute | solution.py:1185
  10.0 5.3 %collective-permute-start.3 = (f32[120,128]{1,0:T(8,128)S(1)}, f32[120,128]{1,0:T(8,128)S(1)}, u32[]{:S(2)}, u32[]{:S(2)}) collective-permute-start(f32[120,128]{1,0:T(8,128)S(1)} %pad_maximum_fusion.own), channel_id=1, source_target_pairs={{0,4},{4,0},{8,12},{12,8},{16,20},{20,16},{24,28},{28,24},{1,5},{5... | collective-permute-start | bytes 184328 | tf_op jit(solution)/shard_map/ppermute | solution.py:1185
  15.4 9.3 %collective-permute-start.4 = (f32[424,128]{1,0:T(8,128)S(1)}, f32[424,128]{1,0:T(8,128)S(1)}, u32[]{:S(2)}, u32[]{:S(2)}) collective-permute-start(f32[424,128]{1,0:T(8,128)S(1)} %line.1.block0), channel_id=1, source_target_pairs={{0,3},{1,2},{2,1},{3,0},{16,19},{17,18},{18,17},{19,16},{4,7},{5,6... | collective-permute-start | bytes 651272 | tf_op jit(solution)/shard_map/ppermute | solution.py:1185
  18.0 10.3 %collective-permute-start.5 = (f32[424,128]{1,0:T(8,128)S(1)}, f32[424,128]{1,0:T(8,128)S(1)}, u32[]{:S(2)}, u32[]{:S(2)}) collective-permute-start(f32[424,128]{1,0:T(8,128)S(1)} %line.1.block0), channel_id=1, source_target_pairs={{0,1},{1,0},{2,3},{3,2},{16,18},{17,19},{18,16},{19,17},{4,5},{5,4... | collective-permute-start | bytes 651272 | tf_op jit(solution)/shard_map/ppermute | solution.py:1185
  18.5 9.7 %collective-permute-start.6 = (f32[424,128]{1,0:T(8,128)S(1)}, f32[424,128]{1,0:T(8,128)S(1)}, u32[]{:S(2)}, u32[]{:S(2)}) collective-permute-start(f32[424,128]{1,0:T(8,128)S(1)} %line.1.block0), channel_id=1, source_target_pairs={{0,2},{1,3},{2,0},{3,1},{16,17},{17,16},{18,19},{19,18},{4,6},{5,7... | collective-permute-start | bytes 651272 | tf_op jit(solution)/shard_map/ppermute | solution.py:1185
  28.3 1.4 %collective-permute-start.7 = (f32[256,128]{1,0:T(8,128)S(1)}, f32[256,128]{1,0:T(8,128)S(1)}, u32[]{:S(2)}, u32[]{:S(2)}) collective-permute-start(f32[256,128]{1,0:T(8,128)S(1)} %halves.1.own_halves), channel_id=1, source_target_pairs={{0,16},{16,0},{1,17},{17,1},{2,18},{18,2},{3,19},{19,3},{4,20},{20... | collective-permute-start | bytes 393224 | tf_op jit(solution)/shard_map/ppermute | solution.py:1179
  29.7 5.4 %collective-permute-start.8 = (f32[1024,128]{1,0:T(8,128)S(1)}, f32[1024,128]{1,0:T(8,128)S(1)}, u32[]{:S(2)}, u32[]{:S(2)}) collective-permute-start(f32[1024,128]{1,0:T(8,128)S(1)} %assemble.1.field.assembled.own_start), channel_id=1, source_target_pairs={{0,16},{16,0},{1,17},{17,1},{2,18},{18,2},{3,19},{19,3},{4,20},{20... | collective-permute-start | bytes 1572872 | tf_op jit(solution)/shard_map/ppermute | solution.py:1179
  30.2 7.0 %copy-start = (f32[2,5,5,160]{3,0,2,1:T(2,128)S(1)}, f32[2,5,5,160]{3,0,2,1:T(2,128)}, u32[]{:S(2)}) copy-start(f32[2,5,5,160]{3,0,2,1:T(2,128)} %param.6) | copy-start | bytes 96004
  35.1 2.1 %collective-permute-start.9 = (f32[600,128]{1,0:T(8,128)S(1)}, f32[600,128]{1,0:T(8,128)S(1)}, u32[]{:S(2)}, u32[]{:S(2)}) collective-permute-start(f32[600,128]{1,0:T(8,128)S(1)} %get-tuple-element.33.own0), channel_id=1, source_target_pairs={{0,16},{16,0},{1,17},{17,1},{2,18},{18,2},{3,19},{19,3},{4,20},{20... | collective-permute-start | bytes 921608 | tf_op jit(solution)/shard_map/ppermute | solution.py:1179
  35.5 1.6 %collective-permute-start.10 = (f32[528,128]{1,0:T(8,128)S(1)}, f32[528,128]{1,0:T(8,128)S(1)}, u32[]{:S(2)}, u32[]{:S(2)}) collective-permute-start(f32[528,128]{1,0:T(8,128)S(1)} %get-tuple-element.34.own1), channel_id=1, source_target_pairs={{0,16},{16,0},{1,17},{17,1},{2,18},{18,2},{3,19},{19,3},{4,20},{20... | collective-permute-start | bytes 811016 | tf_op jit(solution)/shard_map/ppermute | solution.py:1179

commit v21 on v19

--- a/solution.py
+++ b/solution.py
@@ -354,9 +354,9 @@
 FACE_X = HALF + 25
 KAPPA = FACE_X + 15
 PIECE = KAPPA + 16
-LINE_KAPPA = 4 * HALF
-LINE_Y = LINE_KAPPA + 4 * 16
-LINE = LINE_Y + 104
+LINE = 4 * HALF
+REST_Y = 4 * 16
+REST = REST_Y + 104
 FIELD = 1000
 F32 = jnp.float32
 
@@ -676,7 +676,7 @@
     return choose(iota(row.shape, 1) // EZ, [turned[(g - 2 * slot - 1) % 4] for g in range(4)])
 
 
-def line_kernel(first, second, third, own, line, faces, sorted_pieces):
+def line_kernel(first, second, third, own, line, rest, faces, sorted_pieces):
     sorted_pieces[:PIECE, :] = own[...]
     for bits, piece in zip(ORDER_X, (first, second, third)):
         sorted_pieces[pl.ds(pl.multiple_of(partner(bits) * PIECE, 8), PIECE), :] = piece[...]
@@ -702,8 +702,8 @@
                 faces[r + 4 : r + 5, :] = ends[1][node : node + 1]
     for a, piece in enumerate(pieces):
         line[HALF * a : HALF * a + HALF, :] = piece[:HALF, :]
-        line[LINE_KAPPA + 16 * a : LINE_KAPPA + 16 * a + 16, :] = piece[KAPPA:, :]
-        line[LINE_Y + 25 * a : LINE_Y + 25 * a + 25, :] = piece[HALF:FACE_X, :]
+        rest[16 * a : 16 * a + 16, :] = piece[KAPPA:, :]
+        rest[REST_Y + 25 * a : REST_Y + 25 * a + 25, :] = piece[HALF:FACE_X, :]
         flags = [flag_lanes(piece[61:62, :], slot) for slot in range(2)]
         gains = [face_gains(flags[d], 0, d, 5) for d in range(2)]
         next_first = even if a % 2 == 0 else jnp.logical_not(even)
@@ -717,21 +717,20 @@
                 side = odd[:5] if node >= HALF else jnp.logical_not(odd[:5])
                 r = HALF * a + node % HALF
                 line[r : r + 5, :] = line[r : r + 5, :] + jnp.where(side, term[5 * k : 5 * k + 5], 0.0)
-    line[LINE_Y + 100 :, :] = jnp.zeros((4, 128), F32)
+    rest[REST_Y + 100 :, :] = jnp.zeros((4, 128), F32)
 
 
 def halves_kernel(block0, block1, block2, block3, out):
-    place_pieces((block0, block1, block2, block3), out, LINE_KAPPA, 16, 16)
+    place_pieces((block0, block1, block2, block3), out, 0, 16, 16)
 
 
 def widen(low, high, odd):
     return jnp.where(odd, pltpu.roll(high, 32, 1), low), jnp.where(odd, high, pltpu.roll(low, 96, 1))
 
 
-def assemble_kernel(block0, block1, block2, block3, field, pieces, edges, traces):
-    blocks = (block0, block1, block2, block3)
-    place_pieces(blocks, pieces, 0, HALF, HALF)
-    place_pieces(blocks, edges, LINE_Y, 25, 32)
+def assemble_kernel(block0, block1, block2, block3, rest0, rest1, rest2, rest3, field, pieces, edges, traces):
+    place_pieces((block0, block1, block2, block3), pieces, 0, HALF, HALF)
+    place_pieces((rest0, rest1, rest2, rest3), edges, REST_Y, 25, 32)
     lanes = Lanes()
     for source, size, rows, target, apart in ((edges, 32, 25, traces, 25), (pieces, HALF, HALF, field, HALF)):
         for r in range(rows):
@@ -1117,11 +1116,13 @@
 
 
 def plain_call(kernel, name, rows, scratch, operands, cost=1_000_000):
+    many = isinstance(rows, tuple)
+    shapes = [jax.ShapeDtypeStruct((r, 128), F32) for r in (rows if many else (rows,))]
     return pl.pallas_call(
         kernel,
-        out_shape=jax.ShapeDtypeStruct((rows, 128), F32),
+        out_shape=shapes if many else shapes[0],
         in_specs=[VMEM] * len(operands),
-        out_specs=VMEM,
+        out_specs=[VMEM] * len(shapes) if many else VMEM,
         scratch_shapes=[pltpu.VMEM((r, 128), F32) for r in scratch],
         compiler_params=limit(16),
         cost_estimate=pl.CostEstimate(flops=cost, bytes_accessed=cost, transcendentals=0),
@@ -1191,12 +1192,15 @@
     got, mine, kappa_piece = lax.optimization_barrier((exchange(theirs, "section", 1), *part(mine)))
     piece = jnp.concatenate([mine + got, kappa_piece])
     pieces = [exchange_by_core(piece, "gx", bits) for bits in ORDER_X] + [piece]
-    line = plain_call(line_kernel, "line", LINE, [4 * 64, 4 * PIECE], pieces)
+    line, rest = plain_call(line_kernel, "line", (LINE, REST), [4 * 64, 4 * PIECE], pieces)
+    rests = [rest] + [exchange_by_core(rest, "gy", bits) for bits in ORDER_Y]
+    halves = plain_call(halves_kernel, "halves", COLS * 16, [], rests)
+    other_halves = exchange(halves, "section", 1)
     blocks = [line] + [exchange_by_core(line, "gy", bits) for bits in ORDER_Y]
-    halves = plain_call(halves_kernel, "halves", COLS * 16, [], blocks)
-    other_halves = exchange(halves, "section", 1)
-    start = plain_call(assemble_kernel, "assemble", 128 * 8, [COLS * HALF, COLS * 32, 50 * 8], blocks, 4_000_000)
-    start, other_halves = lax.optimization_barrier((start, other_halves))
+    blocks, other_halves = lax.optimization_barrier((blocks, other_halves))
+    start = plain_call(
+        assemble_kernel, "assemble", 128 * 8, [COLS * HALF, COLS * 32, 50 * 8], blocks + rests, 4_000_000
+    )
     coefs = plain_call(setup_kernel, "setup", REGISTERS * 8, [128 * 8], (start, halves, other_halves))
     other_start = exchange(start, "section", 1)
     own, other_start = lax.optimization_barrier((cycle(coefs, start), other_start))

time: 37.7 us -> 37.9 us (level)
  starting transfers between devices: 10.5 us -> 14.7 us
  waiting for transfers between devices: 14.9 us -> 10.9 us
    ppermute x6 -> x9, starting transfers between devices: 9.22 us -> 13.4 us  [exchange_by_core(): return lax.ppermute(x, ('section', axis), pairs)]
    ppermute x6 -> x9, waiting for transfers between devices: 13.1 us -> 9.77 us  [exchange_by_core(): return lax.ppermute(x, ('section', axis), pairs)]
    ppermute x5, waiting for transfers between devices: 1.84 us -> 1.13 us  [exchange(): lax.ppermute(x, axis, [(n, n ^ bits) for n in range(lax.axis_size(axis))])]
  transfers between devices with their start and end apart: 11 -> 14, of which waited for: 7 -> 8; matrix products, arithmetic and copies ran while one was open for 0% -> 0% of each run, Pallas kernels for 17% -> 16%
where the time goes in v21:
time: 37.9 us; the launch traced here: 37.7 us
  starting transfers between devices  14.7 us (39%)
  waiting for transfers between devices  10.9 us (29%)
  Pallas kernels  10.5 us (28%)
  local copies, waits for them, and re-layouts  0.83 us (2%)
  between operations  0.72 us (2%)
    ppermute x9, starting transfers between devices, exchange_by_core(): return lax.ppermute(x, ('section', axis), pairs)  13.4 us
    ppermute x9, waiting for transfers between devices, exchange_by_core(): return lax.ppermute(x, ('section', axis), pairs)  9.77 us
    pallas_call x1, Pallas kernels, cycle(): pl.pallas_call(cycle_kernel, out_shape=[jax.ShapeDtypeStruct((rows, 128),...  4.9 us
    pallas_call x1, Pallas kernels, local_part(): pl.pallas_call(local_kernel, out_shape=[jax.ShapeDtypeStruct((rows, 128),...  2.34 us
    pallas_call x1, Pallas kernels, finish(): pl.pallas_call(finish_kernel, out_shape=[jax.ShapeDtypeStruct(guess.shape...  1.51 us
    ppermute x5, starting transfers between devices, exchange(): lax.ppermute(x, axis, [(n, n ^ bits) for n in range(lax.axis_size(axis))])  1.29 us
    ppermute x5, waiting for transfers between devices, exchange(): lax.ppermute(x, axis, [(n, n ^ bits) for n in range(lax.axis_size(axis))])  1.13 us
    pallas_call x4, Pallas kernels, plain_call(): pl.pallas_call(kernel, out_shape=shapes if many else shapes[0], in_specs=...  1.08 us
  transfers between devices with their start and end apart: 14, of which 8 were waited for; matrix products, arithmetic and copies ran while one was open for 0% of the time, Pallas kernels for 16%

profile of v21, /device:TPU:0, one launch (start us, length us, event | category | flops | bytes accessed | tf_op | source)
XLA Modules:
  0.0 37.7 jit_solution(2564415752429444751)
XLA Ops:
  0.6 2.3 %local_part.1 = (f32[120,128]{1,0:T(8,128)}, f32[104,128]{1,0:T(8,128)}) custom-call(f32[5,5,2,160]{3,2,1,0:T(2,128)} %bitcast.6, f32[5,5,2,160]{3,2,1,0:T(2,128)} %bitcast.4, f32[5,5,160]{2,1,0:T(8,128)} %kappa_in.1, s32[6,1,1,32]{3,2,1,0:T(1,128)} %flags_in.1, f32[64,64]{1,0:T(8,128)} %constant.2.clone.rows_in), custom_call_target="tpu_custom_call" | custom-call | flops 20000000 | bytes 8000000 | tf_op jit(solution)/shard_map/local_part/pallas_call | solution.py:557
  3.0 0.5 %collective-permute-start = (f32[104,128]{1,0:T(8,128)}, f32[104,128]{1,0:T(8,128)S(1)}, u32[]{:S(2)}, u32[]{:S(2)}) collective-permute-start(f32[104,128]{1,0:T(8,128)} %get-tuple-element.27), channel_id=1, source_target_pairs={{0,16},{16,0},{1,17},{17,1},{2,18},{18,2},{3,19},{19,3},{4,20},{20... | collective-permute-start | bytes 159752 | tf_op jit(solution)/shard_map/ppermute | solution.py:1180
  3.5 0.8 %copy-done.1 = f32[120,128]{1,0:T(8,128)S(1)} copy-done((f32[120,128]{1,0:T(8,128)S(1)}, f32[120,128]{1,0:T(8,128)}, u32[]{:S(2)}) %copy-start.1) | copy-done | bytes 61464
  4.3 0.3 collective-permute-done
  4.6 5.0 %collective-permute-start.1 = (f32[120,128]{1,0:T(8,128)S(1)}, f32[120,128]{1,0:T(8,128)S(1)}, u32[]{:S(2)}, u32[]{:S(2)}) collective-permute-start(f32[120,128]{1,0:T(8,128)S(1)} %pad_maximum_fusion.own), channel_id=1, source_target_pairs={{0,12},{4,8},{8,4},{12,0},{16,24},{20,28},{24,16},{28,20},{1,13},{... | collective-permute-start | bytes 184328 | tf_op jit(solution)/shard_map/ppermute | solution.py:1186
  9.6 0.0 collective-permute-start.2
  9.6 0.6 %collective-permute-start.3 = (f32[120,128]{1,0:T(8,128)S(1)}, f32[120,128]{1,0:T(8,128)S(1)}, u32[]{:S(2)}, u32[]{:S(2)}) collective-permute-start(f32[120,128]{1,0:T(8,128)S(1)} %pad_maximum_fusion.own), channel_id=1, source_target_pairs={{0,4},{4,0},{8,12},{12,8},{16,20},{20,16},{24,28},{28,24},{1,5},{5... | collective-permute-start | bytes 184328 | tf_op jit(solution)/shard_map/ppermute | solution.py:1186
  10.3 1.8 %collective-permute-done.1.first = f32[120,128]{1,0:T(8,128)S(1)} collective-permute-done((f32[120,128]{1,0:T(8,128)S(1)}, f32[120,128]{1,0:T(8,128)S(1)}, u32[]{:S(2)}, u32[]{:S(2)}) %collective-permute-start.1) | collective-permute-done | bytes 61472 | tf_op jit(solution)/shard_map/ppermute | solution.py:1186
  12.1 3.1 %collective-permute-done.2.second = f32[120,128]{1,0:T(8,128)S(1)} collective-permute-done((f32[120,128]{1,0:T(8,128)S(1)}, f32[120,128]{1,0:T(8,128)S(1)}, u32[]{:S(2)}, u32[]{:S(2)}) %collective-permute-start.2) | collective-permute-done | bytes 61472 | tf_op jit(solution)/shard_map/ppermute | solution.py:1186
  15.2 0.0 collective-permute-done.3.third
  15.2 0.2 line.1
  15.4 2.5 %collective-permute-start.7 = (f32[168,128]{1,0:T(8,128)S(1)}, f32[168,128]{1,0:T(8,128)S(1)}, u32[]{:S(2)}, u32[]{:S(2)}) collective-permute-start(f32[168,128]{1,0:T(8,128)S(1)} %get-tuple-element.35.block0.rest0), channel_id=1, source_target_pairs={{0,3},{1,2},{2,1},{3,0},{16,19},{17,18},{18,17},{19,16},{4,7},{5,6... | collective-permute-start | bytes 258056 | tf_op jit(solution)/shard_map/ppermute | solution.py:1186
  17.9 0.5 %collective-permute-start.8 = (f32[168,128]{1,0:T(8,128)S(1)}, f32[168,128]{1,0:T(8,128)S(1)}, u32[]{:S(2)}, u32[]{:S(2)}) collective-permute-start(f32[168,128]{1,0:T(8,128)S(1)} %get-tuple-element.35.block0.rest0), channel_id=1, source_target_pairs={{0,1},{1,0},{2,3},{3,2},{16,18},{17,19},{18,16},{19,17},{4,5},{5,4... | collective-permute-start | bytes 258056 | tf_op jit(solution)/shard_map/ppermute | solution.py:1186
  18.5 0.5 %collective-permute-start.9 = (f32[168,128]{1,0:T(8,128)S(1)}, f32[168,128]{1,0:T(8,128)S(1)}, u32[]{:S(2)}, u32[]{:S(2)}) collective-permute-start(f32[168,128]{1,0:T(8,128)S(1)} %get-tuple-element.35.block0.rest0), channel_id=1, source_target_pairs={{0,2},{1,3},{2,0},{3,1},{16,17},{17,16},{18,19},{19,18},{4,6},{5,7... | collective-permute-start | bytes 258056 | tf_op jit(solution)/shard_map/ppermute | solution.py:1186
  19.0 2.4 %collective-permute-start.4 = (f32[256,128]{1,0:T(8,128)S(1)}, f32[256,128]{1,0:T(8,128)S(1)}, u32[]{:S(2)}, u32[]{:S(2)}) collective-permute-start(f32[256,128]{1,0:T(8,128)S(1)} %get-tuple-element.36.block0), channel_id=1, source_target_pairs={{0,3},{1,2},{2,1},{3,0},{16,19},{17,18},{18,17},{19,16},{4,7},{5,6... | collective-permute-start | bytes 393224 | tf_op jit(solution)/shard_map/ppermute | solution.py:1186
  21.4 0.5 %collective-permute-start.5 = (f32[256,128]{1,0:T(8,128)S(1)}, f32[256,128]{1,0:T(8,128)S(1)}, u32[]{:S(2)}, u32[]{:S(2)}) collective-permute-start(f32[256,128]{1,0:T(8,128)S(1)} %get-tuple-element.36.block0), channel_id=1, source_target_pairs={{0,1},{1,0},{2,3},{3,2},{16,18},{17,19},{18,16},{19,17},{4,5},{5,4... | collective-permute-start | bytes 393224 | tf_op jit(solution)/shard_map/ppermute | solution.py:1186
  22.0 1.2 %collective-permute-start.6 = (f32[256,128]{1,0:T(8,128)S(1)}, f32[256,128]{1,0:T(8,128)S(1)}, u32[]{:S(2)}, u32[]{:S(2)}) collective-permute-start(f32[256,128]{1,0:T(8,128)S(1)} %get-tuple-element.36.block0), channel_id=1, source_target_pairs={{0,2},{1,3},{2,0},{3,1},{16,17},{17,16},{18,19},{19,18},{4,6},{5,7... | collective-permute-start | bytes 393224 | tf_op jit(solution)/shard_map/ppermute | solution.py:1186
  23.2 0.3 collective-permute-done.8.block2.rest2
  23.5 3.1 %collective-permute-done.9.block3.rest3 = f32[168,128]{1,0:T(8,128)S(1)} collective-permute-done((f32[168,128]{1,0:T(8,128)S(1)}, f32[168,128]{1,0:T(8,128)S(1)}, u32[]{:S(2)}, u32[]{:S(2)}) %collective-permute-start.9) | collective-permute-done | bytes 86048 | tf_op jit(solution)/shard_map/ppermute | solution.py:1186
  26.6 0.1 collective-permute-start.10
  26.7 0.9 %collective-permute-done.5.block2 = f32[256,128]{1,0:T(8,128)S(1)} collective-permute-done((f32[256,128]{1,0:T(8,128)S(1)}, f32[256,128]{1,0:T(8,128)S(1)}, u32[]{:S(2)}, u32[]{:S(2)}) %collective-permute-start.5) | collective-permute-done | bytes 131104 | tf_op jit(solution)/shard_map/ppermute | solution.py:1186
  27.6 0.6 %collective-permute-done.6.block3 = f32[256,128]{1,0:T(8,128)S(1)} collective-permute-done((f32[256,128]{1,0:T(8,128)S(1)}, f32[256,128]{1,0:T(8,128)S(1)}, u32[]{:S(2)}, u32[]{:S(2)}) %collective-permute-start.6) | collective-permute-done | bytes 131104 | tf_op jit(solution)/shard_map/ppermute | solution.py:1186
  28.1 0.6 %assemble.1.field.assembled.own_start = f32[1024,128]{1,0:T(8,128)S(1)} custom-call(f32[256,128]{1,0:T(8,128)S(1)} %get-tuple-element.36.block0, f32[256,128]{1,0:T(8,128)S(1)} %collective-permute-done.4.block1, f32[256,128]{1,0:T(8,128)S(1)} %collective-permute-done.5.block2, f32[256,128]{1,0:T(8,128)S(1)} %collective-permute-done.6.block3, ...), custom_call_target="tpu_custom_call" | custom-call | flops 4000000 | bytes 4000000 | tf_op jit(solution)/shard_map/assemble/pallas_call | solution.py:1121
  28.7 0.1 collective-permute-start.11
  28.8 0.3 setup.1.coefs
  29.1 0.0 copy-start
  29.1 4.9 %cycle.1 = (f32[600,128]{1,0:T(8,128)S(1)}, f32[528,128]{1,0:T(8,128)S(1)}) custom-call(f32[2704,128]{1,0:T(8,128)S(1)} %setup.1.coefs, f32[1024,128]{1,0:T(8,128)S(1)} %assemble.1.field.assembled.own_start), custom_call_target="tpu_custom_call" | custom-call | flops 40000000 | bytes 30000000 | tf_op jit(solution)/shard_map/cycle/pallas_call | solution.py:1138
  34.0 0.6 %collective-permute-start.12 = (f32[600,128]{1,0:T(8,128)S(1)}, f32[600,128]{1,0:T(8,128)S(1)}, u32[]{:S(2)}, u32[]{:S(2)}) collective-permute-start(f32[600,128]{1,0:T(8,128)S(1)} %get-tuple-element.43.own0), channel_id=1, source_target_pairs={{0,16},{16,0},{1,17},{17,1},{2,18},{18,2},{3,19},{19,3},{4,20},{20... | collective-permute-start | bytes 921608 | tf_op jit(solution)/shard_map/ppermute | solution.py:1180
  34.6 0.1 collective-permute-start.13
  34.7 0.7 %early.1 = (f32[16,128]{1,0:T(8,128)S(1)}, f32[192,160]{1,0:T(8,128)S(1)}) custom-call(f32[600,128]{1,0:T(8,128)S(1)} %get-tuple-element.43.own0, f32[528,128]{1,0:T(8,128)S(1)} %get-tuple-element.44.own1, f32[1024,128]{1,0:T(8,128)S(1)} %assemble.1.field.assembled.own_start, f32[1024,128]{1,0:T(8,128)S(1)} %collective-permute-done.11.other_start), custom_call_target="tpu_custom_call" | custom-call | flops 4000000 | bytes 4000000 | tf_op jit(solution)/shard_map/early/pallas_call | solution.py:1151
  35.3 0.9 %collective-permute-done.13.other1 = f32[528,128]{1,0:T(8,128)S(1)} collective-permute-done((f32[528,128]{1,0:T(8,128)S(1)}, f32[528,128]{1,0:T(8,128)S(1)}, u32[]{:S(2)}, u32[]{:S(2)}) %collective-permute-start.13) | collective-permute-done | bytes 270368 | tf_op jit(solution)/shard_map/ppermute | solution.py:1180
  36.2 1.5 %finish.1 = (f32[5,5,2,160]{3,2,1,0:T(2,128)}, f32[5,5,2,160]{3,2,1,0:T(2,128)}, f32[3]{0:T(128)}) custom-call(f32[600,128]{1,0:T(8,128)S(1)} %get-tuple-element.43.own0, f32[528,128]{1,0:T(8,128)S(1)} %get-tuple-element.44.own1, f32[600,128]{1,0:T(8,128)S(1)} %collective-permute-done.12.other0, f32[528,128]{1,0:T(8,128)S(1)} %collective-permute-done.13.other1, ...), custom_call_target="tpu_custom_call" | custom-call | tf_op jit(solution)/shard_map/finish/pallas_call | solution.py:1164
  (11 shorter events, 0.1 us)
Async XLA Ops:
  3.0 1.6 %collective-permute-start = (f32[104,128]{1,0:T(8,128)}, f32[104,128]{1,0:T(8,128)S(1)}, u32[]{:S(2)}, u32[]{:S(2)}) collective-permute-start(f32[104,128]{1,0:T(8,128)} %get-tuple-element.27), channel_id=1, source_target_pairs={{0,16},{16,0},{1,17},{17,1},{2,18},{18,2},{3,19},{19,3},{4,20},{20... | collective-permute-start | bytes 159752 | tf_op jit(solution)/shard_map/ppermute | solution.py:1180
  3.5 0.8 %copy-start.1 = (f32[120,128]{1,0:T(8,128)S(1)}, f32[120,128]{1,0:T(8,128)}, u32[]{:S(2)}) copy-start(f32[120,128]{1,0:T(8,128)} %get-tuple-element.28.source) | copy-start | bytes 184324
  4.6 7.5 %collective-permute-start.1 = (f32[120,128]{1,0:T(8,128)S(1)}, f32[120,128]{1,0:T(8,128)S(1)}, u32[]{:S(2)}, u32[]{:S(2)}) collective-permute-start(f32[120,128]{1,0:T(8,128)S(1)} %pad_maximum_fusion.own), channel_id=1, source_target_pairs={{0,12},{4,8},{8,4},{12,0},{16,24},{20,28},{24,16},{28,20},{1,13},{... | collective-permute-start | bytes 184328 | tf_op jit(solution)/shard_map/ppermute | solution.py:1186
  9.6 5.6 %collective-permute-start.2 = (f32[120,128]{1,0:T(8,128)S(1)}, f32[120,128]{1,0:T(8,128)S(1)}, u32[]{:S(2)}, u32[]{:S(2)}) collective-permute-start(f32[120,128]{1,0:T(8,128)S(1)} %pad_maximum_fusion.own), channel_id=1, source_target_pairs={{0,8},{4,12},{8,0},{12,4},{16,28},{20,24},{24,20},{28,16},{1,9},{5... | collective-permute-start | bytes 184328 | tf_op jit(solution)/shard_map/ppermute | solution.py:1186
  9.6 5.6 %collective-permute-start.3 = (f32[120,128]{1,0:T(8,128)S(1)}, f32[120,128]{1,0:T(8,128)S(1)}, u32[]{:S(2)}, u32[]{:S(2)}) collective-permute-start(f32[120,128]{1,0:T(8,128)S(1)} %pad_maximum_fusion.own), channel_id=1, source_target_pairs={{0,4},{4,0},{8,12},{12,8},{16,20},{20,16},{24,28},{28,24},{1,5},{5... | collective-permute-start | bytes 184328 | tf_op jit(solution)/shard_map/ppermute | solution.py:1186
  15.4 6.5 %collective-permute-start.7 = (f32[168,128]{1,0:T(8,128)S(1)}, f32[168,128]{1,0:T(8,128)S(1)}, u32[]{:S(2)}, u32[]{:S(2)}) collective-permute-start(f32[168,128]{1,0:T(8,128)S(1)} %get-tuple-element.35.block0.rest0), channel_id=1, source_target_pairs={{0,3},{1,2},{2,1},{3,0},{16,19},{17,18},{18,17},{19,16},{4,7},{5,6... | collective-permute-start | bytes 258056 | tf_op jit(solution)/shard_map/ppermute | solution.py:1186
  17.9 5.6 %collective-permute-start.8 = (f32[168,128]{1,0:T(8,128)S(1)}, f32[168,128]{1,0:T(8,128)S(1)}, u32[]{:S(2)}, u32[]{:S(2)}) collective-permute-start(f32[168,128]{1,0:T(8,128)S(1)} %get-tuple-element.35.block0.rest0), channel_id=1, source_target_pairs={{0,1},{1,0},{2,3},{3,2},{16,18},{17,19},{18,16},{19,17},{4,5},{5,4... | collective-permute-start | bytes 258056 | tf_op jit(solution)/shard_map/ppermute | solution.py:1186
  18.5 8.1 %collective-permute-start.9 = (f32[168,128]{1,0:T(8,128)S(1)}, f32[168,128]{1,0:T(8,128)S(1)}, u32[]{:S(2)}, u32[]{:S(2)}) collective-permute-start(f32[168,128]{1,0:T(8,128)S(1)} %get-tuple-element.35.block0.rest0), channel_id=1, source_target_pairs={{0,2},{1,3},{2,0},{3,1},{16,17},{17,16},{18,19},{19,18},{4,6},{5,7... | collective-permute-start | bytes 258056 | tf_op jit(solution)/shard_map/ppermute | solution.py:1186
  19.0 7.7 %collective-permute-start.4 = (f32[256,128]{1,0:T(8,128)S(1)}, f32[256,128]{1,0:T(8,128)S(1)}, u32[]{:S(2)}, u32[]{:S(2)}) collective-permute-start(f32[256,128]{1,0:T(8,128)S(1)} %get-tuple-element.36.block0), channel_id=1, source_target_pairs={{0,3},{1,2},{2,1},{3,0},{16,19},{17,18},{18,17},{19,16},{4,7},{5,6... | collective-permute-start | bytes 393224 | tf_op jit(solution)/shard_map/ppermute | solution.py:1186
  21.4 6.1 %collective-permute-start.5 = (f32[256,128]{1,0:T(8,128)S(1)}, f32[256,128]{1,0:T(8,128)S(1)}, u32[]{:S(2)}, u32[]{:S(2)}) collective-permute-start(f32[256,128]{1,0:T(8,128)S(1)} %get-tuple-element.36.block0), channel_id=1, source_target_pairs={{0,1},{1,0},{2,3},{3,2},{16,18},{17,19},{18,16},{19,17},{4,5},{5,4... | collective-permute-start | bytes 393224 | tf_op jit(solution)/shard_map/ppermute | solution.py:1186
  22.0 6.2 %collective-permute-start.6 = (f32[256,128]{1,0:T(8,128)S(1)}, f32[256,128]{1,0:T(8,128)S(1)}, u32[]{:S(2)}, u32[]{:S(2)}) collective-permute-start(f32[256,128]{1,0:T(8,128)S(1)} %get-tuple-element.36.block0), channel_id=1, source_target_pairs={{0,2},{1,3},{2,0},{3,1},{16,17},{17,16},{18,19},{19,18},{4,6},{5,7... | collective-permute-start | bytes 393224 | tf_op jit(solution)/shard_map/ppermute | solution.py:1186
  26.6 1.6 %collective-permute-start.10 = (f32[256,128]{1,0:T(8,128)S(1)}, f32[256,128]{1,0:T(8,128)S(1)}, u32[]{:S(2)}, u32[]{:S(2)}) collective-permute-start(f32[256,128]{1,0:T(8,128)S(1)} %halves.1.own_halves), channel_id=1, source_target_pairs={{0,16},{16,0},{1,17},{17,1},{2,18},{18,2},{3,19},{19,3},{4,20},{20... | collective-permute-start | bytes 393224 | tf_op jit(solution)/shard_map/ppermute | solution.py:1180
  28.7 5.3 %collective-permute-start.11 = (f32[1024,128]{1,0:T(8,128)S(1)}, f32[1024,128]{1,0:T(8,128)S(1)}, u32[]{:S(2)}, u32[]{:S(2)}) collective-permute-start(f32[1024,128]{1,0:T(8,128)S(1)} %assemble.1.field.assembled.own_start), channel_id=1, source_target_pairs={{0,16},{16,0},{1,17},{17,1},{2,18},{18,2},{3,19},{19,3},{4,20},{20... | collective-permute-start | bytes 1572872 | tf_op jit(solution)/shard_map/ppermute | solution.py:1180
  29.1 7.1 %copy-start = (f32[2,5,5,160]{3,0,2,1:T(2,128)S(1)}, f32[2,5,5,160]{3,0,2,1:T(2,128)}, u32[]{:S(2)}) copy-start(f32[2,5,5,160]{3,0,2,1:T(2,128)} %param.6) | copy-start | bytes 96004
  34.0 2.2 %collective-permute-start.12 = (f32[600,128]{1,0:T(8,128)S(1)}, f32[600,128]{1,0:T(8,128)S(1)}, u32[]{:S(2)}, u32[]{:S(2)}) collective-permute-start(f32[600,128]{1,0:T(8,128)S(1)} %get-tuple-element.43.own0), channel_id=1, source_target_pairs={{0,16},{16,0},{1,17},{17,1},{2,18},{18,2},{3,19},{19,3},{4,20},{20... | collective-permute-start | bytes 921608 | tf_op jit(solution)/shard_map/ppermute | solution.py:1180
  34.6 1.6 %collective-permute-start.13 = (f32[528,128]{1,0:T(8,128)S(1)}, f32[528,128]{1,0:T(8,128)S(1)}, u32[]{:S(2)}, u32[]{:S(2)}) collective-permute-start(f32[528,128]{1,0:T(8,128)S(1)} %get-tuple-element.44.own1), channel_id=1, source_target_pairs={{0,16},{16,0},{1,17},{17,1},{2,18},{18,2},{3,19},{19,3},{4,20},{20... | collective-permute-start | bytes 811016 | tf_op jit(solution)/shard_map/ppermute | solution.py:1180

commit v22 on v21

--- a/solution.py
+++ b/solution.py
@@ -602,17 +602,18 @@
 
 
 ORDER_X = ((3, 2), (2, 3), (1, 1))
-ORDER_Y = ((3, 3), (1, 2), (2, 1))
+ORDER_Y = ((1, 2), (2, 1), (3, 3))
+ORDER_REST = ((3, 3), (1, 2), (2, 1))
 
 
 def partner(bits):
     return jnp.where(lax.axis_index("section") == 0, bits[0], bits[1])
 
 
-def place_pieces(blocks, pieces, first, size, room):
+def place_pieces(blocks, order, pieces, first, size, room):
     my_gx, my_gy = lax.axis_index("gx"), lax.axis_index("gy")
     for b, block in enumerate(blocks):
-        gy = my_gy ^ partner(ORDER_Y[b - 1]) if b else my_gy
+        gy = my_gy ^ partner(order[b - 1]) if b else my_gy
         for a in range(4):
             column = (my_gx ^ a) * 4 + gy
             start = pl.multiple_of(column * room, 8)
@@ -721,7 +722,7 @@
 
 
 def halves_kernel(block0, block1, block2, block3, out):
-    place_pieces((block0, block1, block2, block3), out, 0, 16, 16)
+    place_pieces((block0, block1, block2, block3), ORDER_REST, out, 0, 16, 16)
 
 
 def widen(low, high, odd):
@@ -729,8 +730,8 @@
 
 
 def assemble_kernel(block0, block1, block2, block3, rest0, rest1, rest2, rest3, field, pieces, edges, traces):
-    place_pieces((block0, block1, block2, block3), pieces, 0, HALF, HALF)
-    place_pieces((rest0, rest1, rest2, rest3), edges, REST_Y, 25, 32)
+    place_pieces((block0, block1, block2, block3), ORDER_Y, pieces, 0, HALF, HALF)
+    place_pieces((rest0, rest1, rest2, rest3), ORDER_REST, edges, REST_Y, 25, 32)
     lanes = Lanes()
     for source, size, rows, target, apart in ((edges, 32, 25, traces, 25), (pieces, HALF, HALF, field, HALF)):
         for r in range(rows):
@@ -1193,7 +1194,7 @@
     piece = jnp.concatenate([mine + got, kappa_piece])
     pieces = [exchange_by_core(piece, "gx", bits) for bits in ORDER_X] + [piece]
     line, rest = plain_call(line_kernel, "line", (LINE, REST), [4 * 64, 4 * PIECE], pieces)
-    rests = [rest] + [exchange_by_core(rest, "gy", bits) for bits in ORDER_Y]
+    rests = [rest] + [exchange_by_core(rest, "gy", bits) for bits in ORDER_REST]
     halves = plain_call(halves_kernel, "halves", COLS * 16, [], rests)
     other_halves = exchange(halves, "section", 1)
     blocks = [line] + [exchange_by_core(line, "gy", bits) for bits in ORDER_Y]

time: 37.9 us -> 38.1 us (level)
  starting transfers between devices: 14.7 us -> 15.1 us
    ppermute x9, starting transfers between devices: 13.4 us -> 13.9 us  [exchange_by_core(): return lax.ppermute(x, ('section', axis), pairs)]
  transfers between devices with their start and end apart: 14 -> 14, of which waited for: 8 -> 7; matrix products, arithmetic and copies ran while one was open for 0% -> 0% of each run, Pallas kernels for 16% -> 16%
where the time goes in v22:
time: 38.1 us; the launch traced here: 37.9 us
  starting transfers between devices  15.1 us (40%)
  waiting for transfers between devices  10.7 us (28%)
  Pallas kernels  10.5 us (28%)
  local copies, waits for them, and re-layouts  0.83 us (2%)
  between operations  0.72 us (2%)
    ppermute x9, starting transfers between devices, exchange_by_core(): return lax.ppermute(x, ('section', axis), pairs)  13.9 us
    ppermute x9, waiting for transfers between devices, exchange_by_core(): return lax.ppermute(x, ('section', axis), pairs)  9.54 us
    pallas_call x1, Pallas kernels, cycle(): pl.pallas_call(cycle_kernel, out_shape=[jax.ShapeDtypeStruct((rows, 128),...  4.9 us
    pallas_call x1, Pallas kernels, local_part(): pl.pallas_call(local_kernel, out_shape=[jax.ShapeDtypeStruct((rows, 128),...  2.34 us
    pallas_call x1, Pallas kernels, finish(): pl.pallas_call(finish_kernel, out_shape=[jax.ShapeDtypeStruct(guess.shape...  1.51 us
    ppermute x5, starting transfers between devices, exchange(): lax.ppermute(x, axis, [(n, n ^ bits) for n in range(lax.axis_size(axis))])  1.29 us
    ppermute x5, waiting for transfers between devices, exchange(): lax.ppermute(x, axis, [(n, n ^ bits) for n in range(lax.axis_size(axis))])  1.13 us
    pallas_call x4, Pallas kernels, plain_call(): pl.pallas_call(kernel, out_shape=shapes if many else shapes[0], in_specs=...  1.1 us
  transfers between devices with their start and end apart: 14, of which 7 were waited for; matrix products, arithmetic and copies ran while one was open for 0% of the time, Pallas kernels for 16%

profile of v22, /device:TPU:0, one launch (start us, length us, event | category | flops | bytes accessed | tf_op | source)
XLA Modules:
  0.0 37.9 jit_solution(387342358398065870)
XLA Ops:
  0.6 2.3 %local_part.1 = (f32[120,128]{1,0:T(8,128)}, f32[104,128]{1,0:T(8,128)}) custom-call(f32[5,5,2,160]{3,2,1,0:T(2,128)} %bitcast.6, f32[5,5,2,160]{3,2,1,0:T(2,128)} %bitcast.4, f32[5,5,160]{2,1,0:T(8,128)} %kappa_in.1, s32[6,1,1,32]{3,2,1,0:T(1,128)} %flags_in.1, f32[64,64]{1,0:T(8,128)} %constant.2.clone.rows_in), custom_call_target="tpu_custom_call" | custom-call | flops 20000000 | bytes 8000000 | tf_op jit(solution)/shard_map/local_part/pallas_call | solution.py:557
  3.0 0.5 %collective-permute-start = (f32[104,128]{1,0:T(8,128)}, f32[104,128]{1,0:T(8,128)S(1)}, u32[]{:S(2)}, u32[]{:S(2)}) collective-permute-start(f32[104,128]{1,0:T(8,128)} %get-tuple-element.27), channel_id=1, source_target_pairs={{0,16},{16,0},{1,17},{17,1},{2,18},{18,2},{3,19},{19,3},{4,20},{20... | collective-permute-start | bytes 159752 | tf_op jit(solution)/shard_map/ppermute | solution.py:1181
  3.5 0.8 %copy-done.1 = f32[120,128]{1,0:T(8,128)S(1)} copy-done((f32[120,128]{1,0:T(8,128)S(1)}, f32[120,128]{1,0:T(8,128)}, u32[]{:S(2)}) %copy-start.1) | copy-done | bytes 61464
  4.3 0.3 collective-permute-done
  4.6 5.0 %collective-permute-start.1 = (f32[120,128]{1,0:T(8,128)S(1)}, f32[120,128]{1,0:T(8,128)S(1)}, u32[]{:S(2)}, u32[]{:S(2)}) collective-permute-start(f32[120,128]{1,0:T(8,128)S(1)} %pad_maximum_fusion.own), channel_id=1, source_target_pairs={{0,12},{4,8},{8,4},{12,0},{16,24},{20,28},{24,16},{28,20},{1,13},{... | collective-permute-start | bytes 184328 | tf_op jit(solution)/shard_map/ppermute | solution.py:1187
  9.6 0.0 collective-permute-start.2
  9.6 0.6 %collective-permute-start.3 = (f32[120,128]{1,0:T(8,128)S(1)}, f32[120,128]{1,0:T(8,128)S(1)}, u32[]{:S(2)}, u32[]{:S(2)}) collective-permute-start(f32[120,128]{1,0:T(8,128)S(1)} %pad_maximum_fusion.own), channel_id=1, source_target_pairs={{0,4},{4,0},{8,12},{12,8},{16,20},{20,16},{24,28},{28,24},{1,5},{5... | collective-permute-start | bytes 184328 | tf_op jit(solution)/shard_map/ppermute | solution.py:1187
  10.3 1.8 %collective-permute-done.1.first = f32[120,128]{1,0:T(8,128)S(1)} collective-permute-done((f32[120,128]{1,0:T(8,128)S(1)}, f32[120,128]{1,0:T(8,128)S(1)}, u32[]{:S(2)}, u32[]{:S(2)}) %collective-permute-start.1) | collective-permute-done | bytes 61472 | tf_op jit(solution)/shard_map/ppermute | solution.py:1187
  12.1 3.1 %collective-permute-done.2.second = f32[120,128]{1,0:T(8,128)S(1)} collective-permute-done((f32[120,128]{1,0:T(8,128)S(1)}, f32[120,128]{1,0:T(8,128)S(1)}, u32[]{:S(2)}, u32[]{:S(2)}) %collective-permute-start.2) | collective-permute-done | bytes 61472 | tf_op jit(solution)/shard_map/ppermute | solution.py:1187
  15.2 0.0 collective-permute-done.3.third
  15.2 0.2 line.1
  15.4 2.5 %collective-permute-start.7 = (f32[168,128]{1,0:T(8,128)S(1)}, f32[168,128]{1,0:T(8,128)S(1)}, u32[]{:S(2)}, u32[]{:S(2)}) collective-permute-start(f32[168,128]{1,0:T(8,128)S(1)} %get-tuple-element.35.block0.rest0), channel_id=1, source_target_pairs={{0,3},{1,2},{2,1},{3,0},{16,19},{17,18},{18,17},{19,16},{4,7},{5,6... | collective-permute-start | bytes 258056 | tf_op jit(solution)/shard_map/ppermute | solution.py:1187
  17.9 0.5 %collective-permute-start.8 = (f32[168,128]{1,0:T(8,128)S(1)}, f32[168,128]{1,0:T(8,128)S(1)}, u32[]{:S(2)}, u32[]{:S(2)}) collective-permute-start(f32[168,128]{1,0:T(8,128)S(1)} %get-tuple-element.35.block0.rest0), channel_id=1, source_target_pairs={{0,1},{1,0},{2,3},{3,2},{16,18},{17,19},{18,16},{19,17},{4,5},{5,4... | collective-permute-start | bytes 258056 | tf_op jit(solution)/shard_map/ppermute | solution.py:1187
  18.5 0.5 %collective-permute-start.9 = (f32[168,128]{1,0:T(8,128)S(1)}, f32[168,128]{1,0:T(8,128)S(1)}, u32[]{:S(2)}, u32[]{:S(2)}) collective-permute-start(f32[168,128]{1,0:T(8,128)S(1)} %get-tuple-element.35.block0.rest0), channel_id=1, source_target_pairs={{0,2},{1,3},{2,0},{3,1},{16,17},{17,16},{18,19},{19,18},{4,6},{5,7... | collective-permute-start | bytes 258056 | tf_op jit(solution)/shard_map/ppermute | solution.py:1187
  19.0 1.5 %collective-permute-start.4 = (f32[256,128]{1,0:T(8,128)S(1)}, f32[256,128]{1,0:T(8,128)S(1)}, u32[]{:S(2)}, u32[]{:S(2)}) collective-permute-start(f32[256,128]{1,0:T(8,128)S(1)} %get-tuple-element.36.block0), channel_id=1, source_target_pairs={{0,1},{1,0},{2,3},{3,2},{16,18},{17,19},{18,16},{19,17},{4,5},{5,4... | collective-permute-start | bytes 393224 | tf_op jit(solution)/shard_map/ppermute | solution.py:1187
  20.5 1.5 %collective-permute-start.5 = (f32[256,128]{1,0:T(8,128)S(1)}, f32[256,128]{1,0:T(8,128)S(1)}, u32[]{:S(2)}, u32[]{:S(2)}) collective-permute-start(f32[256,128]{1,0:T(8,128)S(1)} %get-tuple-element.36.block0), channel_id=1, source_target_pairs={{0,2},{1,3},{2,0},{3,1},{16,17},{17,16},{18,19},{19,18},{4,6},{5,7... | collective-permute-start | bytes 393224 | tf_op jit(solution)/shard_map/ppermute | solution.py:1187
  22.0 1.6 %collective-permute-start.6 = (f32[256,128]{1,0:T(8,128)S(1)}, f32[256,128]{1,0:T(8,128)S(1)}, u32[]{:S(2)}, u32[]{:S(2)}) collective-permute-start(f32[256,128]{1,0:T(8,128)S(1)} %get-tuple-element.36.block0), channel_id=1, source_target_pairs={{0,3},{1,2},{2,1},{3,0},{16,19},{17,18},{18,17},{19,16},{4,7},{5,6... | collective-permute-start | bytes 393224 | tf_op jit(solution)/shard_map/ppermute | solution.py:1187
  23.6 0.0 collective-permute-done.8.block2.rest2
  23.7 0.1 collective-permute-start.10
  23.7 2.4 %collective-permute-done.4.block1 = f32[256,128]{1,0:T(8,128)S(1)} collective-permute-done((f32[256,128]{1,0:T(8,128)S(1)}, f32[256,128]{1,0:T(8,128)S(1)}, u32[]{:S(2)}, u32[]{:S(2)}) %collective-permute-start.4) | collective-permute-done | bytes 131104 | tf_op jit(solution)/shard_map/ppermute | solution.py:1187
  26.1 0.8 %collective-permute-done.5.block2 = f32[256,128]{1,0:T(8,128)S(1)} collective-permute-done((f32[256,128]{1,0:T(8,128)S(1)}, f32[256,128]{1,0:T(8,128)S(1)}, u32[]{:S(2)}, u32[]{:S(2)}) %collective-permute-start.5) | collective-permute-done | bytes 131104 | tf_op jit(solution)/shard_map/ppermute | solution.py:1187
  27.0 1.4 %collective-permute-done.6.block3 = f32[256,128]{1,0:T(8,128)S(1)} collective-permute-done((f32[256,128]{1,0:T(8,128)S(1)}, f32[256,128]{1,0:T(8,128)S(1)}, u32[]{:S(2)}, u32[]{:S(2)}) %collective-permute-start.6) | collective-permute-done | bytes 131104 | tf_op jit(solution)/shard_map/ppermute | solution.py:1187
  28.3 0.6 %assemble.1.field.assembled.own_start = f32[1024,128]{1,0:T(8,128)S(1)} custom-call(f32[256,128]{1,0:T(8,128)S(1)} %get-tuple-element.36.block0, f32[256,128]{1,0:T(8,128)S(1)} %collective-permute-done.4.block1, f32[256,128]{1,0:T(8,128)S(1)} %collective-permute-done.5.block2, f32[256,128]{1,0:T(8,128)S(1)} %collective-permute-done.6.block3, ...), custom_call_target="tpu_custom_call" | custom-call | flops 4000000 | bytes 4000000 | tf_op jit(solution)/shard_map/assemble/pallas_call | solution.py:1122
  28.9 0.1 collective-permute-start.11
  29.0 0.3 setup.1.coefs
  29.3 0.0 copy-start
  29.3 4.9 %cycle.1 = (f32[600,128]{1,0:T(8,128)S(1)}, f32[528,128]{1,0:T(8,128)S(1)}) custom-call(f32[2704,128]{1,0:T(8,128)S(1)} %setup.1.coefs, f32[1024,128]{1,0:T(8,128)S(1)} %assemble.1.field.assembled.own_start), custom_call_target="tpu_custom_call" | custom-call | flops 40000000 | bytes 30000000 | tf_op jit(solution)/shard_map/cycle/pallas_call | solution.py:1139
  34.2 0.6 %collective-permute-start.12 = (f32[600,128]{1,0:T(8,128)S(1)}, f32[600,128]{1,0:T(8,128)S(1)}, u32[]{:S(2)}, u32[]{:S(2)}) collective-permute-start(f32[600,128]{1,0:T(8,128)S(1)} %get-tuple-element.43.own0), channel_id=1, source_target_pairs={{0,16},{16,0},{1,17},{17,1},{2,18},{18,2},{3,19},{19,3},{4,20},{20... | collective-permute-start | bytes 921608 | tf_op jit(solution)/shard_map/ppermute | solution.py:1181
  34.8 0.1 collective-permute-start.13
  34.9 0.7 %early.1 = (f32[16,128]{1,0:T(8,128)S(1)}, f32[192,160]{1,0:T(8,128)S(1)}) custom-call(f32[600,128]{1,0:T(8,128)S(1)} %get-tuple-element.43.own0, f32[528,128]{1,0:T(8,128)S(1)} %get-tuple-element.44.own1, f32[1024,128]{1,0:T(8,128)S(1)} %assemble.1.field.assembled.own_start, f32[1024,128]{1,0:T(8,128)S(1)} %collective-permute-done.11.other_start), custom_call_target="tpu_custom_call" | custom-call | flops 4000000 | bytes 4000000 | tf_op jit(solution)/shard_map/early/pallas_call | solution.py:1152
  35.5 0.9 %collective-permute-done.13.other1 = f32[528,128]{1,0:T(8,128)S(1)} collective-permute-done((f32[528,128]{1,0:T(8,128)S(1)}, f32[528,128]{1,0:T(8,128)S(1)}, u32[]{:S(2)}, u32[]{:S(2)}) %collective-permute-start.13) | collective-permute-done | bytes 270368 | tf_op jit(solution)/shard_map/ppermute | solution.py:1181
  36.4 1.5 %finish.1 = (f32[5,5,2,160]{3,2,1,0:T(2,128)}, f32[5,5,2,160]{3,2,1,0:T(2,128)}, f32[3]{0:T(128)}) custom-call(f32[600,128]{1,0:T(8,128)S(1)} %get-tuple-element.43.own0, f32[528,128]{1,0:T(8,128)S(1)} %get-tuple-element.44.own1, f32[600,128]{1,0:T(8,128)S(1)} %collective-permute-done.12.other0, f32[528,128]{1,0:T(8,128)S(1)} %collective-permute-done.13.other1, ...), custom_call_target="tpu_custom_call" | custom-call | tf_op jit(solution)/shard_map/finish/pallas_call | solution.py:1165
  (11 shorter events, 0.1 us)
Async XLA Ops:
  3.0 1.6 %collective-permute-start = (f32[104,128]{1,0:T(8,128)}, f32[104,128]{1,0:T(8,128)S(1)}, u32[]{:S(2)}, u32[]{:S(2)}) collective-permute-start(f32[104,128]{1,0:T(8,128)} %get-tuple-element.27), channel_id=1, source_target_pairs={{0,16},{16,0},{1,17},{17,1},{2,18},{18,2},{3,19},{19,3},{4,20},{20... | collective-permute-start | bytes 159752 | tf_op jit(solution)/shard_map/ppermute | solution.py:1181
  3.5 0.8 %copy-start.1 = (f32[120,128]{1,0:T(8,128)S(1)}, f32[120,128]{1,0:T(8,128)}, u32[]{:S(2)}) copy-start(f32[120,128]{1,0:T(8,128)} %get-tuple-element.28.source) | copy-start | bytes 184324
  4.6 7.5 %collective-permute-start.1 = (f32[120,128]{1,0:T(8,128)S(1)}, f32[120,128]{1,0:T(8,128)S(1)}, u32[]{:S(2)}, u32[]{:S(2)}) collective-permute-start(f32[120,128]{1,0:T(8,128)S(1)} %pad_maximum_fusion.own), channel_id=1, source_target_pairs={{0,12},{4,8},{8,4},{12,0},{16,24},{20,28},{24,16},{28,20},{1,13},{... | collective-permute-start | bytes 184328 | tf_op jit(solution)/shard_map/ppermute | solution.py:1187
  9.6 5.6 %collective-permute-start.2 = (f32[120,128]{1,0:T(8,128)S(1)}, f32[120,128]{1,0:T(8,128)S(1)}, u32[]{:S(2)}, u32[]{:S(2)}) collective-permute-start(f32[120,128]{1,0:T(8,128)S(1)} %pad_maximum_fusion.own), channel_id=1, source_target_pairs={{0,8},{4,12},{8,0},{12,4},{16,28},{20,24},{24,20},{28,16},{1,9},{5... | collective-permute-start | bytes 184328 | tf_op jit(solution)/shard_map/ppermute | solution.py:1187
  9.6 5.6 %collective-permute-start.3 = (f32[120,128]{1,0:T(8,128)S(1)}, f32[120,128]{1,0:T(8,128)S(1)}, u32[]{:S(2)}, u32[]{:S(2)}) collective-permute-start(f32[120,128]{1,0:T(8,128)S(1)} %pad_maximum_fusion.own), channel_id=1, source_target_pairs={{0,4},{4,0},{8,12},{12,8},{16,20},{20,16},{24,28},{28,24},{1,5},{5... | collective-permute-start | bytes 184328 | tf_op jit(solution)/shard_map/ppermute | solution.py:1187
  15.4 6.6 %collective-permute-start.7 = (f32[168,128]{1,0:T(8,128)S(1)}, f32[168,128]{1,0:T(8,128)S(1)}, u32[]{:S(2)}, u32[]{:S(2)}) collective-permute-start(f32[168,128]{1,0:T(8,128)S(1)} %get-tuple-element.35.block0.rest0), channel_id=1, source_target_pairs={{0,3},{1,2},{2,1},{3,0},{16,19},{17,18},{18,17},{19,16},{4,7},{5,6... | collective-permute-start | bytes 258056 | tf_op jit(solution)/shard_map/ppermute | solution.py:1187
  17.9 5.7 %collective-permute-start.8 = (f32[168,128]{1,0:T(8,128)S(1)}, f32[168,128]{1,0:T(8,128)S(1)}, u32[]{:S(2)}, u32[]{:S(2)}) collective-permute-start(f32[168,128]{1,0:T(8,128)S(1)} %get-tuple-element.35.block0.rest0), channel_id=1, source_target_pairs={{0,1},{1,0},{2,3},{3,2},{16,18},{17,19},{18,16},{19,17},{4,5},{5,4... | collective-permute-start | bytes 258056 | tf_op jit(solution)/shard_map/ppermute | solution.py:1187
  18.5 5.2 %collective-permute-start.9 = (f32[168,128]{1,0:T(8,128)S(1)}, f32[168,128]{1,0:T(8,128)S(1)}, u32[]{:S(2)}, u32[]{:S(2)}) collective-permute-start(f32[168,128]{1,0:T(8,128)S(1)} %get-tuple-element.35.block0.rest0), channel_id=1, source_target_pairs={{0,2},{1,3},{2,0},{3,1},{16,17},{17,16},{18,19},{19,18},{4,6},{5,7... | collective-permute-start | bytes 258056 | tf_op jit(solution)/shard_map/ppermute | solution.py:1187
  19.0 7.1 %collective-permute-start.4 = (f32[256,128]{1,0:T(8,128)S(1)}, f32[256,128]{1,0:T(8,128)S(1)}, u32[]{:S(2)}, u32[]{:S(2)}) collective-permute-start(f32[256,128]{1,0:T(8,128)S(1)} %get-tuple-element.36.block0), channel_id=1, source_target_pairs={{0,1},{1,0},{2,3},{3,2},{16,18},{17,19},{18,16},{19,17},{4,5},{5,4... | collective-permute-start | bytes 393224 | tf_op jit(solution)/shard_map/ppermute | solution.py:1187
  20.5 6.5 %collective-permute-start.5 = (f32[256,128]{1,0:T(8,128)S(1)}, f32[256,128]{1,0:T(8,128)S(1)}, u32[]{:S(2)}, u32[]{:S(2)}) collective-permute-start(f32[256,128]{1,0:T(8,128)S(1)} %get-tuple-element.36.block0), channel_id=1, source_target_pairs={{0,2},{1,3},{2,0},{3,1},{16,17},{17,16},{18,19},{19,18},{4,6},{5,7... | collective-permute-start | bytes 393224 | tf_op jit(solution)/shard_map/ppermute | solution.py:1187
  22.0 6.3 %collective-permute-start.6 = (f32[256,128]{1,0:T(8,128)S(1)}, f32[256,128]{1,0:T(8,128)S(1)}, u32[]{:S(2)}, u32[]{:S(2)}) collective-permute-start(f32[256,128]{1,0:T(8,128)S(1)} %get-tuple-element.36.block0), channel_id=1, source_target_pairs={{0,3},{1,2},{2,1},{3,0},{16,19},{17,18},{18,17},{19,16},{4,7},{5,6... | collective-permute-start | bytes 393224 | tf_op jit(solution)/shard_map/ppermute | solution.py:1187
  23.7 4.7 %collective-permute-start.10 = (f32[256,128]{1,0:T(8,128)S(1)}, f32[256,128]{1,0:T(8,128)S(1)}, u32[]{:S(2)}, u32[]{:S(2)}) collective-permute-start(f32[256,128]{1,0:T(8,128)S(1)} %halves.1.own_halves), channel_id=1, source_target_pairs={{0,16},{16,0},{1,17},{17,1},{2,18},{18,2},{3,19},{19,3},{4,20},{20... | collective-permute-start | bytes 393224 | tf_op jit(solution)/shard_map/ppermute | solution.py:1181
  28.9 5.3 %collective-permute-start.11 = (f32[1024,128]{1,0:T(8,128)S(1)}, f32[1024,128]{1,0:T(8,128)S(1)}, u32[]{:S(2)}, u32[]{:S(2)}) collective-permute-start(f32[1024,128]{1,0:T(8,128)S(1)} %assemble.1.field.assembled.own_start), channel_id=1, source_target_pairs={{0,16},{16,0},{1,17},{17,1},{2,18},{18,2},{3,19},{19,3},{4,20},{20... | collective-permute-start | bytes 1572872 | tf_op jit(solution)/shard_map/ppermute | solution.py:1181
  29.3 7.1 %copy-start = (f32[2,5,5,160]{3,0,2,1:T(2,128)S(1)}, f32[2,5,5,160]{3,0,2,1:T(2,128)}, u32[]{:S(2)}) copy-start(f32[2,5,5,160]{3,0,2,1:T(2,128)} %param.6) | copy-start | bytes 96004
  34.2 2.2 %collective-permute-start.12 = (f32[600,128]{1,0:T(8,128)S(1)}, f32[600,128]{1,0:T(8,128)S(1)}, u32[]{:S(2)}, u32[]{:S(2)}) collective-permute-start(f32[600,128]{1,0:T(8,128)S(1)} %get-tuple-element.43.own0), channel_id=1, source_target_pairs={{0,16},{16,0},{1,17},{17,1},{2,18},{18,2},{3,19},{19,3},{4,20},{20... | collective-permute-start | bytes 921608 | tf_op jit(solution)/shard_map/ppermute | solution.py:1181
  34.8 1.6 %collective-permute-start.13 = (f32[528,128]{1,0:T(8,128)S(1)}, f32[528,128]{1,0:T(8,128)S(1)}, u32[]{:S(2)}, u32[]{:S(2)}) collective-permute-start(f32[528,128]{1,0:T(8,128)S(1)} %get-tuple-element.44.own1), channel_id=1, source_target_pairs={{0,16},{16,0},{1,17},{17,1},{2,18},{18,2},{3,19},{19,3},{4,20},{20... | collective-permute-start | bytes 811016 | tf_op jit(solution)/shard_map/ppermute | solution.py:1181

commit v23 on v21

--- a/solution.py
+++ b/solution.py
@@ -1202,6 +1202,7 @@
         assemble_kernel, "assemble", 128 * 8, [COLS * HALF, COLS * 32, 50 * 8], blocks + rests, 4_000_000
     )
     coefs = plain_call(setup_kernel, "setup", REGISTERS * 8, [128 * 8], (start, halves, other_halves))
+    start, coefs = lax.optimization_barrier((start, coefs))
     other_start = exchange(start, "section", 1)
     own, other_start = lax.optimization_barrier((cycle(coefs, start), other_start))
     other = [exchange(part, "section", 1) for part in own]

time: 37.9 us -> 39.8 us (1.050)
  waiting for transfers between devices: 10.9 us -> 12.4 us
  starting transfers between devices: 14.7 us -> 15.1 us
    ppermute x9, waiting for transfers between devices: 9.77 us -> 11.3 us  [exchange_by_core(): return lax.ppermute(x, ('section', axis), pairs)]
  transfers between devices with their start and end apart: 14 -> 14, of which waited for: 8 -> 7; matrix products, arithmetic and copies ran while one was open for 0% -> 0% of each run, Pallas kernels for 16% -> 14%
where the time goes in v23:
time: 39.8 us; the launch traced here: 39.6 us
  starting transfers between devices  15.1 us (38%)
  waiting for transfers between devices  12.4 us (31%)
  Pallas kernels  10.5 us (26%)
  local copies, waits for them, and re-layouts  0.83 us (2%)
  between operations  0.72 us (2%)
    ppermute x9, starting transfers between devices, exchange_by_core(): return lax.ppermute(x, ('section', axis), pairs)  13.8 us
    ppermute x9, waiting for transfers between devices, exchange_by_core(): return lax.ppermute(x, ('section', axis), pairs)  11.3 us
    pallas_call x1, Pallas kernels, cycle(): pl.pallas_call(cycle_kernel, out_shape=[jax.ShapeDtypeStruct((rows, 128),...  4.9 us
    pallas_call x1, Pallas kernels, local_part(): pl.pallas_call(local_kernel, out_shape=[jax.ShapeDtypeStruct((rows, 128),...  2.34 us
    pallas_call x1, Pallas kernels, finish(): pl.pallas_call(finish_kernel, out_shape=[jax.ShapeDtypeStruct(guess.shape...  1.51 us
    ppermute x5, starting transfers between devices, exchange(): lax.ppermute(x, axis, [(n, n ^ bits) for n in range(lax.axis_size(axis))])  1.3 us
    ppermute x5, waiting for transfers between devices, exchange(): lax.ppermute(x, axis, [(n, n ^ bits) for n in range(lax.axis_size(axis))])  1.13 us
    pallas_call x4, Pallas kernels, plain_call(): pl.pallas_call(kernel, out_shape=shapes if many else shapes[0], in_specs=...  1.09 us
  transfers between devices with their start and end apart: 14, of which 7 were waited for; matrix products, arithmetic and copies ran while one was open for 0% of the time, Pallas kernels for 14%

profile of v23, /device:TPU:0, one launch (start us, length us, event | category | flops | bytes accessed | tf_op | source)
XLA Modules:
  0.0 39.6 jit_solution(12725802277944258508)
XLA Ops:
  0.6 2.3 %local_part.1 = (f32[120,128]{1,0:T(8,128)}, f32[104,128]{1,0:T(8,128)}) custom-call(f32[5,5,2,160]{3,2,1,0:T(2,128)} %bitcast.6, f32[5,5,2,160]{3,2,1,0:T(2,128)} %bitcast.4, f32[5,5,160]{2,1,0:T(8,128)} %kappa_in.1, s32[6,1,1,32]{3,2,1,0:T(1,128)} %flags_in.1, f32[64,64]{1,0:T(8,128)} %constant.2.clone.rows_in), custom_call_target="tpu_custom_call" | custom-call | flops 20000000 | bytes 8000000 | tf_op jit(solution)/shard_map/local_part/pallas_call | solution.py:557
  3.0 0.5 %collective-permute-start = (f32[104,128]{1,0:T(8,128)}, f32[104,128]{1,0:T(8,128)S(1)}, u32[]{:S(2)}, u32[]{:S(2)}) collective-permute-start(f32[104,128]{1,0:T(8,128)} %get-tuple-element.29), channel_id=1, source_target_pairs={{0,16},{16,0},{1,17},{17,1},{2,18},{18,2},{3,19},{19,3},{4,20},{20... | collective-permute-start | bytes 159752 | tf_op jit(solution)/shard_map/ppermute | solution.py:1180
  3.5 0.8 %copy-done.1 = f32[120,128]{1,0:T(8,128)S(1)} copy-done((f32[120,128]{1,0:T(8,128)S(1)}, f32[120,128]{1,0:T(8,128)}, u32[]{:S(2)}) %copy-start.1) | copy-done | bytes 61464
  4.3 0.3 collective-permute-done
  4.6 3.0 %collective-permute-start.3 = (f32[120,128]{1,0:T(8,128)S(1)}, f32[120,128]{1,0:T(8,128)S(1)}, u32[]{:S(2)}, u32[]{:S(2)}) collective-permute-start(f32[120,128]{1,0:T(8,128)S(1)} %pad_maximum_fusion.own), channel_id=1, source_target_pairs={{0,4},{4,0},{8,12},{12,8},{16,20},{20,16},{24,28},{28,24},{1,5},{5... | collective-permute-start | bytes 184328 | tf_op jit(solution)/shard_map/ppermute | solution.py:1186
  7.6 2.6 %collective-permute-start.2 = (f32[120,128]{1,0:T(8,128)S(1)}, f32[120,128]{1,0:T(8,128)S(1)}, u32[]{:S(2)}, u32[]{:S(2)}) collective-permute-start(f32[120,128]{1,0:T(8,128)S(1)} %pad_maximum_fusion.own), channel_id=1, source_target_pairs={{0,8},{4,12},{8,0},{12,4},{16,28},{20,24},{24,20},{28,16},{1,9},{5... | collective-permute-start | bytes 184328 | tf_op jit(solution)/shard_map/ppermute | solution.py:1186
  10.2 0.0 collective-permute-start.1
  10.2 0.0 collective-permute-done.3.third
  10.2 4.6 %collective-permute-done.2.second = f32[120,128]{1,0:T(8,128)S(1)} collective-permute-done((f32[120,128]{1,0:T(8,128)S(1)}, f32[120,128]{1,0:T(8,128)S(1)}, u32[]{:S(2)}, u32[]{:S(2)}) %collective-permute-start.2) | collective-permute-done | bytes 61472 | tf_op jit(solution)/shard_map/ppermute | solution.py:1186
  14.8 1.5 %collective-permute-done.1.first = f32[120,128]{1,0:T(8,128)S(1)} collective-permute-done((f32[120,128]{1,0:T(8,128)S(1)}, f32[120,128]{1,0:T(8,128)S(1)}, u32[]{:S(2)}, u32[]{:S(2)}) %collective-permute-start.1) | collective-permute-done | bytes 61472 | tf_op jit(solution)/shard_map/ppermute | solution.py:1186
  16.3 0.2 line.1
  16.5 1.6 %collective-permute-start.9 = (f32[168,128]{1,0:T(8,128)S(1)}, f32[168,128]{1,0:T(8,128)S(1)}, u32[]{:S(2)}, u32[]{:S(2)}) collective-permute-start(f32[168,128]{1,0:T(8,128)S(1)} %get-tuple-element.37.block0.rest0), channel_id=1, source_target_pairs={{0,2},{1,3},{2,0},{3,1},{16,17},{17,16},{18,19},{19,18},{4,6},{5,7... | collective-permute-start | bytes 258056 | tf_op jit(solution)/shard_map/ppermute | solution.py:1186
  18.1 1.5 %collective-permute-start.8 = (f32[168,128]{1,0:T(8,128)S(1)}, f32[168,128]{1,0:T(8,128)S(1)}, u32[]{:S(2)}, u32[]{:S(2)}) collective-permute-start(f32[168,128]{1,0:T(8,128)S(1)} %get-tuple-element.37.block0.rest0), channel_id=1, source_target_pairs={{0,1},{1,0},{2,3},{3,2},{16,18},{17,19},{18,16},{19,17},{4,5},{5,4... | collective-permute-start | bytes 258056 | tf_op jit(solution)/shard_map/ppermute | solution.py:1186
  19.6 0.5 %collective-permute-start.7 = (f32[168,128]{1,0:T(8,128)S(1)}, f32[168,128]{1,0:T(8,128)S(1)}, u32[]{:S(2)}, u32[]{:S(2)}) collective-permute-start(f32[168,128]{1,0:T(8,128)S(1)} %get-tuple-element.37.block0.rest0), channel_id=1, source_target_pairs={{0,3},{1,2},{2,1},{3,0},{16,19},{17,18},{18,17},{19,16},{4,7},{5,6... | collective-permute-start | bytes 258056 | tf_op jit(solution)/shard_map/ppermute | solution.py:1186
  20.1 1.5 %collective-permute-start.6 = (f32[256,128]{1,0:T(8,128)S(1)}, f32[256,128]{1,0:T(8,128)S(1)}, u32[]{:S(2)}, u32[]{:S(2)}) collective-permute-start(f32[256,128]{1,0:T(8,128)S(1)} %get-tuple-element.38.block0), channel_id=1, source_target_pairs={{0,2},{1,3},{2,0},{3,1},{16,17},{17,16},{18,19},{19,18},{4,6},{5,7... | collective-permute-start | bytes 393224 | tf_op jit(solution)/shard_map/ppermute | solution.py:1186
  21.6 1.5 %collective-permute-start.5 = (f32[256,128]{1,0:T(8,128)S(1)}, f32[256,128]{1,0:T(8,128)S(1)}, u32[]{:S(2)}, u32[]{:S(2)}) collective-permute-start(f32[256,128]{1,0:T(8,128)S(1)} %get-tuple-element.38.block0), channel_id=1, source_target_pairs={{0,1},{1,0},{2,3},{3,2},{16,18},{17,19},{18,16},{19,17},{4,5},{5,4... | collective-permute-start | bytes 393224 | tf_op jit(solution)/shard_map/ppermute | solution.py:1186
  23.1 0.0 collective-permute-done.9.block3.rest3
  23.1 1.6 %collective-permute-start.4 = (f32[256,128]{1,0:T(8,128)S(1)}, f32[256,128]{1,0:T(8,128)S(1)}, u32[]{:S(2)}, u32[]{:S(2)}) collective-permute-start(f32[256,128]{1,0:T(8,128)S(1)} %get-tuple-element.38.block0), channel_id=1, source_target_pairs={{0,3},{1,2},{2,1},{3,0},{16,19},{17,18},{18,17},{19,16},{4,7},{5,6... | collective-permute-start | bytes 393224 | tf_op jit(solution)/shard_map/ppermute | solution.py:1186
  24.7 1.3 %collective-permute-done.7.block1.rest1 = f32[168,128]{1,0:T(8,128)S(1)} collective-permute-done((f32[168,128]{1,0:T(8,128)S(1)}, f32[168,128]{1,0:T(8,128)S(1)}, u32[]{:S(2)}, u32[]{:S(2)}) %collective-permute-start.7) | collective-permute-done | bytes 86048 | tf_op jit(solution)/shard_map/ppermute | solution.py:1186
  26.1 0.1 collective-permute-start.10
  26.2 2.4 %collective-permute-done.6.block3 = f32[256,128]{1,0:T(8,128)S(1)} collective-permute-done((f32[256,128]{1,0:T(8,128)S(1)}, f32[256,128]{1,0:T(8,128)S(1)}, u32[]{:S(2)}, u32[]{:S(2)}) %collective-permute-start.6) | collective-permute-done | bytes 131104 | tf_op jit(solution)/shard_map/ppermute | solution.py:1186
  28.6 1.4 %collective-permute-done.4.block1 = f32[256,128]{1,0:T(8,128)S(1)} collective-permute-done((f32[256,128]{1,0:T(8,128)S(1)}, f32[256,128]{1,0:T(8,128)S(1)}, u32[]{:S(2)}, u32[]{:S(2)}) %collective-permute-start.4) | collective-permute-done | bytes 131104 | tf_op jit(solution)/shard_map/ppermute | solution.py:1186
  30.0 0.6 %assemble.1.field.assembled.own_start = f32[1024,128]{1,0:T(8,128)S(1)} custom-call(f32[256,128]{1,0:T(8,128)S(1)} %get-tuple-element.38.block0, f32[256,128]{1,0:T(8,128)S(1)} %collective-permute-done.4.block1, f32[256,128]{1,0:T(8,128)S(1)} %collective-permute-done.5.block2, f32[256,128]{1,0:T(8,128)S(1)} %collective-permute-done.6.block3, ...), custom_call_target="tpu_custom_call" | custom-call | flops 4000000 | bytes 4000000 | tf_op jit(solution)/shard_map/assemble/pallas_call | solution.py:1121
  30.6 0.3 setup.1.coefs
  30.9 0.0 copy-start
  30.9 0.1 collective-permute-start.11
  31.0 4.9 %cycle.1 = (f32[600,128]{1,0:T(8,128)S(1)}, f32[528,128]{1,0:T(8,128)S(1)}) custom-call(f32[2704,128]{1,0:T(8,128)S(1)} %setup.1.coefs, f32[1024,128]{1,0:T(8,128)S(1)} %assemble.1.field.assembled.own_start), custom_call_target="tpu_custom_call" | custom-call | flops 40000000 | bytes 30000000 | tf_op jit(solution)/shard_map/cycle/pallas_call | solution.py:1138
  35.9 0.6 %collective-permute-start.12 = (f32[600,128]{1,0:T(8,128)S(1)}, f32[600,128]{1,0:T(8,128)S(1)}, u32[]{:S(2)}, u32[]{:S(2)}) collective-permute-start(f32[600,128]{1,0:T(8,128)S(1)} %get-tuple-element.47.own0), channel_id=1, source_target_pairs={{0,16},{16,0},{1,17},{17,1},{2,18},{18,2},{3,19},{19,3},{4,20},{20... | collective-permute-start | bytes 921608 | tf_op jit(solution)/shard_map/ppermute | solution.py:1180
  36.5 0.1 collective-permute-start.13
  36.5 0.7 %early.1 = (f32[16,128]{1,0:T(8,128)S(1)}, f32[192,160]{1,0:T(8,128)S(1)}) custom-call(f32[600,128]{1,0:T(8,128)S(1)} %get-tuple-element.47.own0, f32[528,128]{1,0:T(8,128)S(1)} %get-tuple-element.48.own1, f32[1024,128]{1,0:T(8,128)S(1)} %assemble.1.field.assembled.own_start, f32[1024,128]{1,0:T(8,128)S(1)} %collective-permute-done.11.other_start), custom_call_target="tpu_custom_call" | custom-call | flops 4000000 | bytes 4000000 | tf_op jit(solution)/shard_map/early/pallas_call | solution.py:1151
  37.2 0.9 %collective-permute-done.13.other1 = f32[528,128]{1,0:T(8,128)S(1)} collective-permute-done((f32[528,128]{1,0:T(8,128)S(1)}, f32[528,128]{1,0:T(8,128)S(1)}, u32[]{:S(2)}, u32[]{:S(2)}) %collective-permute-start.13) | collective-permute-done | bytes 270368 | tf_op jit(solution)/shard_map/ppermute | solution.py:1180
  38.1 1.5 %finish.1 = (f32[5,5,2,160]{3,2,1,0:T(2,128)}, f32[5,5,2,160]{3,2,1,0:T(2,128)}, f32[3]{0:T(128)}) custom-call(f32[600,128]{1,0:T(8,128)S(1)} %get-tuple-element.47.own0, f32[528,128]{1,0:T(8,128)S(1)} %get-tuple-element.48.own1, f32[600,128]{1,0:T(8,128)S(1)} %collective-permute-done.12.other0, f32[528,128]{1,0:T(8,128)S(1)} %collective-permute-done.13.other1, ...), custom_call_target="tpu_custom_call" | custom-call | tf_op jit(solution)/shard_map/finish/pallas_call | solution.py:1164
  (11 shorter events, 0.1 us)
Async XLA Ops:
  3.0 1.6 %collective-permute-start = (f32[104,128]{1,0:T(8,128)}, f32[104,128]{1,0:T(8,128)S(1)}, u32[]{:S(2)}, u32[]{:S(2)}) collective-permute-start(f32[104,128]{1,0:T(8,128)} %get-tuple-element.29), channel_id=1, source_target_pairs={{0,16},{16,0},{1,17},{17,1},{2,18},{18,2},{3,19},{19,3},{4,20},{20... | collective-permute-start | bytes 159752 | tf_op jit(solution)/shard_map/ppermute | solution.py:1180
  3.5 0.8 %copy-start.1 = (f32[120,128]{1,0:T(8,128)S(1)}, f32[120,128]{1,0:T(8,128)}, u32[]{:S(2)}) copy-start(f32[120,128]{1,0:T(8,128)} %get-tuple-element.30.source) | copy-start | bytes 184324
  4.6 5.6 %collective-permute-start.3 = (f32[120,128]{1,0:T(8,128)S(1)}, f32[120,128]{1,0:T(8,128)S(1)}, u32[]{:S(2)}, u32[]{:S(2)}) collective-permute-start(f32[120,128]{1,0:T(8,128)S(1)} %pad_maximum_fusion.own), channel_id=1, source_target_pairs={{0,4},{4,0},{8,12},{12,8},{16,20},{20,16},{24,28},{28,24},{1,5},{5... | collective-permute-start | bytes 184328 | tf_op jit(solution)/shard_map/ppermute | solution.py:1186
  7.6 7.2 %collective-permute-start.2 = (f32[120,128]{1,0:T(8,128)S(1)}, f32[120,128]{1,0:T(8,128)S(1)}, u32[]{:S(2)}, u32[]{:S(2)}) collective-permute-start(f32[120,128]{1,0:T(8,128)S(1)} %pad_maximum_fusion.own), channel_id=1, source_target_pairs={{0,8},{4,12},{8,0},{12,4},{16,28},{20,24},{24,20},{28,16},{1,9},{5... | collective-permute-start | bytes 184328 | tf_op jit(solution)/shard_map/ppermute | solution.py:1186
  10.2 6.1 %collective-permute-start.1 = (f32[120,128]{1,0:T(8,128)S(1)}, f32[120,128]{1,0:T(8,128)S(1)}, u32[]{:S(2)}, u32[]{:S(2)}) collective-permute-start(f32[120,128]{1,0:T(8,128)S(1)} %pad_maximum_fusion.own), channel_id=1, source_target_pairs={{0,12},{4,8},{8,4},{12,0},{16,24},{20,28},{24,16},{28,20},{1,13},{... | collective-permute-start | bytes 184328 | tf_op jit(solution)/shard_map/ppermute | solution.py:1186
  16.5 6.6 %collective-permute-start.9 = (f32[168,128]{1,0:T(8,128)S(1)}, f32[168,128]{1,0:T(8,128)S(1)}, u32[]{:S(2)}, u32[]{:S(2)}) collective-permute-start(f32[168,128]{1,0:T(8,128)S(1)} %get-tuple-element.37.block0.rest0), channel_id=1, source_target_pairs={{0,2},{1,3},{2,0},{3,1},{16,17},{17,16},{18,19},{19,18},{4,6},{5,7... | collective-permute-start | bytes 258056 | tf_op jit(solution)/shard_map/ppermute | solution.py:1186
  18.1 6.6 %collective-permute-start.8 = (f32[168,128]{1,0:T(8,128)S(1)}, f32[168,128]{1,0:T(8,128)S(1)}, u32[]{:S(2)}, u32[]{:S(2)}) collective-permute-start(f32[168,128]{1,0:T(8,128)S(1)} %get-tuple-element.37.block0.rest0), channel_id=1, source_target_pairs={{0,1},{1,0},{2,3},{3,2},{16,18},{17,19},{18,16},{19,17},{4,5},{5,4... | collective-permute-start | bytes 258056 | tf_op jit(solution)/shard_map/ppermute | solution.py:1186
  19.6 6.5 %collective-permute-start.7 = (f32[168,128]{1,0:T(8,128)S(1)}, f32[168,128]{1,0:T(8,128)S(1)}, u32[]{:S(2)}, u32[]{:S(2)}) collective-permute-start(f32[168,128]{1,0:T(8,128)S(1)} %get-tuple-element.37.block0.rest0), channel_id=1, source_target_pairs={{0,3},{1,2},{2,1},{3,0},{16,19},{17,18},{18,17},{19,16},{4,7},{5,6... | collective-permute-start | bytes 258056 | tf_op jit(solution)/shard_map/ppermute | solution.py:1186
  20.1 8.5 %collective-permute-start.6 = (f32[256,128]{1,0:T(8,128)S(1)}, f32[256,128]{1,0:T(8,128)S(1)}, u32[]{:S(2)}, u32[]{:S(2)}) collective-permute-start(f32[256,128]{1,0:T(8,128)S(1)} %get-tuple-element.38.block0), channel_id=1, source_target_pairs={{0,2},{1,3},{2,0},{3,1},{16,17},{17,16},{18,19},{19,18},{4,6},{5,7... | collective-permute-start | bytes 393224 | tf_op jit(solution)/shard_map/ppermute | solution.py:1186
  21.6 7.0 %collective-permute-start.5 = (f32[256,128]{1,0:T(8,128)S(1)}, f32[256,128]{1,0:T(8,128)S(1)}, u32[]{:S(2)}, u32[]{:S(2)}) collective-permute-start(f32[256,128]{1,0:T(8,128)S(1)} %get-tuple-element.38.block0), channel_id=1, source_target_pairs={{0,1},{1,0},{2,3},{3,2},{16,18},{17,19},{18,16},{19,17},{4,5},{5,4... | collective-permute-start | bytes 393224 | tf_op jit(solution)/shard_map/ppermute | solution.py:1186
  23.1 6.9 %collective-permute-start.4 = (f32[256,128]{1,0:T(8,128)S(1)}, f32[256,128]{1,0:T(8,128)S(1)}, u32[]{:S(2)}, u32[]{:S(2)}) collective-permute-start(f32[256,128]{1,0:T(8,128)S(1)} %get-tuple-element.38.block0), channel_id=1, source_target_pairs={{0,3},{1,2},{2,1},{3,0},{16,19},{17,18},{18,17},{19,16},{4,7},{5,6... | collective-permute-start | bytes 393224 | tf_op jit(solution)/shard_map/ppermute | solution.py:1186
  26.1 3.9 %collective-permute-start.10 = (f32[256,128]{1,0:T(8,128)S(1)}, f32[256,128]{1,0:T(8,128)S(1)}, u32[]{:S(2)}, u32[]{:S(2)}) collective-permute-start(f32[256,128]{1,0:T(8,128)S(1)} %halves.1.own_halves), channel_id=1, source_target_pairs={{0,16},{16,0},{1,17},{17,1},{2,18},{18,2},{3,19},{19,3},{4,20},{20... | collective-permute-start | bytes 393224 | tf_op jit(solution)/shard_map/ppermute | solution.py:1180
  30.9 7.2 %copy-start = (f32[2,5,5,160]{3,0,2,1:T(2,128)S(1)}, f32[2,5,5,160]{3,0,2,1:T(2,128)}, u32[]{:S(2)}) copy-start(f32[2,5,5,160]{3,0,2,1:T(2,128)} %param.6) | copy-start | bytes 96004
  30.9 5.0 %collective-permute-start.11 = (f32[1024,128]{1,0:T(8,128)S(1)}, f32[1024,128]{1,0:T(8,128)S(1)}, u32[]{:S(2)}, u32[]{:S(2)}) collective-permute-start(f32[1024,128]{1,0:T(8,128)S(1)} %assemble.1.field.assembled.own_start), channel_id=1, source_target_pairs={{0,16},{16,0},{1,17},{17,1},{2,18},{18,2},{3,19},{19,3},{4,20},{20... | collective-permute-start | bytes 1572872 | tf_op jit(solution)/shard_map/ppermute | solution.py:1180
  35.9 2.2 %collective-permute-start.12 = (f32[600,128]{1,0:T(8,128)S(1)}, f32[600,128]{1,0:T(8,128)S(1)}, u32[]{:S(2)}, u32[]{:S(2)}) collective-permute-start(f32[600,128]{1,0:T(8,128)S(1)} %get-tuple-element.47.own0), channel_id=1, source_target_pairs={{0,16},{16,0},{1,17},{17,1},{2,18},{18,2},{3,19},{19,3},{4,20},{20... | collective-permute-start | bytes 921608 | tf_op jit(solution)/shard_map/ppermute | solution.py:1180
  36.5 1.6 %collective-permute-start.13 = (f32[528,128]{1,0:T(8,128)S(1)}, f32[528,128]{1,0:T(8,128)S(1)}, u32[]{:S(2)}, u32[]{:S(2)}) collective-permute-start(f32[528,128]{1,0:T(8,128)S(1)} %get-tuple-element.48.own1), channel_id=1, source_target_pairs={{0,16},{16,0},{1,17},{17,1},{2,18},{18,2},{3,19},{19,3},{4,20},{20... | collective-permute-start | bytes 811016 | tf_op jit(solution)/shard_map/ppermute | solution.py:1180
